TPU v7x, 32 devices: a whole 2x2x4 slice. The times are simulated.
32 devices in a mesh: groups: 2 (over y), wide: 4 (over z), narrow: 2 (over x), pair: 2 (over core).
Axes of the slice: x: 2, y: 2, z: 4, core: 2. Of those that a mesh axis runs over, the one named last changes fastest.
Arguments:
- row_codes: bfloat16 [256, 7168], P(('groups', 'wide', 'narrow', 'pair')), parts along dimension 0, may hold values from -448 to 448
- row_scales: bfloat16 [256, 56], P(('groups', 'wide', 'narrow', 'pair')), parts along dimension 0, may hold values from 0.0039978027 to 0.039794922
- expert_ids: int32 [256, 2], P(('groups', 'wide', 'narrow', 'pair')), parts along dimension 0, may hold values from 0 to 3, all different within a row; in each aligned block of 8 rows (0 to 7, 8 to 15, ...) at most 5 rows name the same one
- gate_weights: float32 [256, 2], P(('groups', 'wide', 'narrow', 'pair')), parts along dimension 0, may hold values from 0.1 to 0.5
- placement: int32 [4], replicated, may hold values from 0 to 3, as said below
- w_gate: bfloat16 [4, 7168, 1024], P('wide', None, ('narrow', 'pair')), may hold values from -0.0625 to 0.0625
- w_up: bfloat16 [4, 7168, 1024], P('wide', None, ('narrow', 'pair')), may hold values from -0.0625 to 0.0625
- w_down: bfloat16 [4, 1024, 7168], P('wide', ('narrow', 'pair')), may hold values from -0.1875 to 0.1875
- shared_gate: bfloat16 [7168, 1024], P(None, ('narrow', 'pair')), may hold values from -0.0625 to 0.0625
- shared_up: bfloat16 [7168, 1024], P(None, ('narrow', 'pair')), may hold values from -0.0625 to 0.0625
- shared_down: bfloat16 [1024, 7168], P(('narrow', 'pair')), may hold values from -0.1875 to 0.1875
Outputs:
- layer_out: bfloat16 [256, 7168], P(('groups', 'wide', 'narrow', 'pair')), parts along dimension 0
There are 2 independent parts, one for each index of `groups`. A program takes and returns all parts, laid end to end along the dimension named above; an argument that names none is the same for every part. Nothing has to cross between parts.
Inputs may be any that keep to these rules, and one draw needn't show every extreme that they name: `expert_ids`: each row names 2 different experts. Among the rows of one device no expert is named by more than 5 rows, and in every draw some device names some expert exactly 5 times. `placement`: each storage index is used by exactly one expert.
All inputs are finite; a program needn't handle non-finite values.
Results may differ from a plain program's by a relative error of at most 0.012.
Values may be sent and summed in bfloat16 or wider, within the bound.
No kernel may reach another device: no remote copies, remote signals or barrier semaphores. Data moves between devices by JAX's collectives and lax.ppermute only.
A program may use at most 128 MiB of HBM per device.

v0:
```python
import jax
import jax.numpy as jnp
from jax import lax
from jax.sharding import PartitionSpec as P

CAP = 5


def dequantize(codes, scales):
    row_total, feature_width = codes.shape
    blocks = (
        codes.astype(jnp.float32).reshape(row_total, feature_width // 128, 128)
        * scales.astype(jnp.float32)[:, :, None]
    )
    return blocks.reshape(row_total, feature_width).astype(jnp.bfloat16)


def expert_forward(inputs, gate_proj, up_proj, down_proj):
    gate_act = jnp.dot(inputs, gate_proj, preferred_element_type=jnp.float32)
    up_act = jnp.dot(inputs, up_proj, preferred_element_type=jnp.float32)
    hidden = (jax.nn.silu(gate_act) * up_act).astype(jnp.bfloat16)
    return jnp.dot(hidden, down_proj, preferred_element_type=jnp.float32)


def shared_path(row_codes, row_scales, shared_gate, shared_up, shared_down):
    near_codes, near_scales = (
        lax.all_gather(row_codes, ("narrow", "pair"), axis=0, tiled=True),
        lax.all_gather(row_scales, ("narrow", "pair"), axis=0, tiled=True),
    )
    near_inputs = dequantize(near_codes, near_scales)
    return lax.psum_scatter(
        expert_forward(near_inputs, shared_gate, shared_up, shared_down).astype(jnp.bfloat16),
        ("narrow", "pair"),
        scatter_dimension=0,
        tiled=True,
    ).astype(jnp.float32)


def shards(
    row_codes,
    row_scales,
    expert_ids,
    gate_weights,
    placement,
    w_gate,
    w_up,
    w_down,
    shared_gate,
    shared_up,
    shared_down,
):
    expert_count = placement.shape[0]
    node_count = lax.axis_size("wide")
    slot_total = node_count * CAP
    picked = (
        expert_ids[:, :, None] == jnp.arange(expert_count, dtype=jnp.int32)[None, None, :]
    ).astype(jnp.int32)
    per_token = jnp.sum(picked, axis=1)
    before = jnp.cumsum(per_token, axis=0) - per_token
    slot_of = jnp.sum(picked * before[:, None, :], axis=2)
    node_of = jnp.sum(picked * placement[None, None, :], axis=2)
    dest_slot = node_of * CAP + slot_of
    one_hot = dest_slot[:, :, None] == jnp.arange(slot_total, dtype=jnp.int32)[None, None, :]
    route_map = jnp.sum(one_hot.astype(jnp.bfloat16), axis=1)
    gate_map = jnp.sum(one_hot.astype(jnp.float32) * gate_weights[:, :, None], axis=1)
    send_codes = jnp.dot(route_map.T, row_codes, preferred_element_type=jnp.float32).astype(
        jnp.bfloat16
    )
    send_scales = jnp.dot(route_map.T, row_scales, preferred_element_type=jnp.float32).astype(
        jnp.bfloat16
    )
    gate_proj = w_gate[0]
    up_proj = w_up[0]
    down_proj = w_down[0]
    came_codes, came_scales = (
        lax.all_to_all(send_codes, "wide", split_axis=0, concat_axis=0, tiled=True),
        lax.all_to_all(send_scales, "wide", split_axis=0, concat_axis=0, tiled=True),
    )
    node_codes, node_scales = (
        lax.all_gather(came_codes, ("narrow", "pair"), axis=0, tiled=True),
        lax.all_gather(came_scales, ("narrow", "pair"), axis=0, tiled=True),
    )
    node_inputs = dequantize(node_codes, node_scales)
    summed = lax.psum_scatter(
        expert_forward(node_inputs, gate_proj, up_proj, down_proj).astype(jnp.bfloat16),
        ("narrow", "pair"),
        scatter_dimension=0,
        tiled=True,
    )
    shared_sum = shared_path(row_codes, row_scales, shared_gate, shared_up, shared_down)
    returned = lax.all_to_all(summed, "wide", split_axis=0, concat_axis=0, tiled=True)
    routed = jnp.dot(gate_map, returned.astype(jnp.float32), precision=lax.Precision.HIGHEST)
    return (shared_sum + routed).astype(jnp.bfloat16)


def solution(mesh):
    return jax.shard_map(
        shards,
        mesh=mesh,
        in_specs=(
            P(("groups", "wide", "narrow", "pair"), None),
            P(("groups", "wide", "narrow", "pair"), None),
            P(("groups", "wide", "narrow", "pair"), None),
            P(("groups", "wide", "narrow", "pair"), None),
            P(),
            P("wide", None, ("narrow", "pair")),
            P("wide", None, ("narrow", "pair")),
            P("wide", ("narrow", "pair"), None),
            P(None, ("narrow", "pair")),
            P(None, ("narrow", "pair")),
            P(("narrow", "pair"), None),
        ),
        out_specs=P(("groups", "wide", "narrow", "pair"), None),
        check_vma=False,
    )
```

profile of v0, /device:TPU:0, one launch (start us, length us, event | category | flops | bytes accessed | tf_op | source)
XLA Modules:
  0.0 124.3 jit_solution(10747464732141858872)
XLA Ops:
  6.5 0.7 convert_reduce_fusion
  7.2 0.2 reduce_window_sum.11
  7.4 0.8 select_reduce_fusion.2
  8.3 1.2 convolution_convert_fusion.2
  9.6 19.2 %all_to_all.36 = bf16[4,5,7168]{2,1,0:T(8,128)(2,1)S(1)} all-to-all(bf16[4,5,7168]{2,1,0:T(8,128)(2,1)S(1)} %all_to_all.24), channel_id=1, replica_groups=mesh['groups'=2,'wide'=4,'narrow'=2,'pair'=2] {'wide'}, dimensions={0} | all-to-all | bytes 573440 | tf_op jit(solution)/shard_map/all_to_all | solution.py:76
  28.8 0.9 reshape.32
  29.7 0.9 convolution_convert_fusion.3
  30.6 0.7 reshape.41
  31.3 3.2 %all-to-all-start.1 = ((bf16[4,2,140]{2,1,0:T(2,128)(2,1)}), bf16[4,2,140]{2,1,0:T(2,128)(2,1)S(1)}, u32[]{:S(2)}, u32[]{:S(2)}) async-start(bf16[4,2,140]{2,1,0:T(2,128)(2,1)} %reshape.41), calls=%async_computation.2 | async-start | bytes 8192 | tf_op jit(solution)/shard_map/all_to_all | solution.py:77
  34.6 5.3 %all_gather.13 = bf16[32,56]{1,0:T(8,128)(2,1)S(1)} all-gather(bf16[8,56]{1,0:T(8,128)(2,1)} %param.12), channel_id=1, replica_groups=mesh['groups'=2,'wide'=4,'narrow'=2,'pair'=2] {'narrow','pair'}, dimensions={0}, use_global_device_ids=true | all-gather | bytes 4480 | tf_op jit(solution)/shard_map/all_gather | solution.py:28
  39.9 9.5 %all_gather.12 = bf16[32,7168]{1,0:T(8,128)(2,1)S(1)} all-gather(bf16[8,7168]{1,0:T(8,128)(2,1)} %param.11), channel_id=1, replica_groups=mesh['groups'=2,'wide'=4,'narrow'=2,'pair'=2] {'narrow','pair'}, dimensions={0}, use_global_device_ids=true | all-gather | bytes 573440 | tf_op jit(solution)/shard_map/all_gather | solution.py:27
  49.4 0.3 mul.67
  49.7 0.5 copy-done.2
  50.2 0.5 copy-done
  50.7 2.7 %fusion.36 = f32[32,256]{1,0:T(8,128)S(1)} fusion(bf16[7168,256]{1,0:T(8,128)(2,1)} %param.19, f32[4,8,56,128]{3,2,1,0:T(8,128)S(1)} %bitcast.43, bf16[32,7168]{1,0:T(8,128)(2,1)S(1)} %all_gather.12), kind=kOutput, calls=%fused_computation.43 | convolution fusion | flops 118128640 | bytes 5079040 | tf_op jit(solution)/shard_map/dot_general | solution.py:19
  53.5 5.2 %all-gather.1 = bf16[4,20,56]{2,1,0:T(8,128)(2,1)S(1)} all-gather(bf16[1,20,56]{2,1,0:T(8,128)(2,1)S(1)} %reshape.34), channel_id=1, replica_groups=mesh['groups'=2,'wide'=4,'narrow'=2,'pair'=2] {'narrow','pair'}, dimensions={0}, use_global_device_ids=true | all-gather | bytes 11200 | tf_op jit(solution)/shard_map/all_gather | solution.py:81
  58.7 1.4 %reshape.36 = f32[80,7168]{1,0:T(8,128)S(1)} reshape(bf16[4,20,7168]{2,1,0:T(8,128)(2,1)} %all-gather.4.cloned.1.call-done) | data formatting | bytes 3440640 | tf_op jit(solution)/shard_map/convert_element_type | solution.py:12
  60.2 0.7 mul.79
  60.8 0.5 fusion.7
  61.3 0.9 copy-done.3
  62.2 0.8 fusion.5
  63.0 5.4 %convolution_convert_fusion = bf16[80,7168]{1,0:T(8,128)(2,1)S(1)} fusion(bf16[1,256,7168]{2,1,0:T(8,128)(2,1)} %param.18, bf16[80,7168]{1,0:T(8,128)(2,1)S(1)} %fusion.7, bf16[1,7168,256]{2,1,0:T(8,128)(2,1)} %param.17, f32[80,256]{1,0:T(8,128)S(1)} %fusion.5), kind=kOutput, calls=%fused_computation | convolution fusion | flops 587898880 | bytes 9715712 | tf_op jit(solution)/shard_map/dot_general | solution.py:22
  68.4 16.4 %fusion = bf16[24,7168]{1,0:T(8,128)(2,1)S(1)} fusion(bf16[80,7168]{1,0:T(8,128)(2,1)S(1)} %convolution_convert_fusion), kind=kCustom, calls=%all-reduce-scatter | all-reduce-scatter fusion | flops 688129 | bytes 1491456
  84.8 1.3 %collective-permute-start = (bf16[12,7168]{1,0:T(8,128)(2,1)S(1)}, bf16[12,7168]{1,0:T(8,128)(2,1)S(1)}, u32[]{:S(2)}, u32[]{:S(2)}) collective-permute-start(bf16[12,7168]{1,0:T(8,128)(2,1)S(1)} %slice), channel_id=1, source_target_pairs={{0,1},{1,2},{2,3},{4,5},{5,6},{6,7},{8,9},{9,10},{10,11},{12,13},{... | collective-permute-start | bytes 516104
  86.1 6.2 %convolution_convert_fusion.1 = bf16[32,7168]{1,0:T(8,128)(2,1)} fusion(bf16[256,7168]{1,0:T(8,128)(2,1)} %param.21, bf16[7168,256]{1,0:T(8,128)(2,1)} %param.20, f32[32,256]{1,0:T(8,128)S(1)} %fusion.36, f32[4,8,56,128]{3,2,1,0:T(8,128)S(1)} %bitcast.44, bf16[32,7168]{1,0:T(8,128)(2,1)} %copy-done.2), kind=kOutput, calls=%fused_computation.1 | convolution fusion | flops 235847680 | bytes 9207808 | tf_op jit(solution)/shard_map/dot_general | solution.py:22
  92.4 0.6 dynamic-slice.4
  93.6 2.4 %concatenate = bf16[36,7168]{1,0:T(8,128)(2,1)S(1)} concatenate(bf16[12,7168]{1,0:T(8,128)(2,1)S(1)} %collective-permute-done, bf16[24,7168]{1,0:T(8,128)(2,1)S(1)} %fusion), dimensions={0} | concatenate | bytes 1032192
  96.2 0.9 all_to_all.30
  97.1 4.6 %all-to-all-start.2 = ((bf16[4,5,7168]{2,1,0:T(8,128)(2,1)}), bf16[4,5,7168]{2,1,0:T(8,128)(2,1)S(1)}, u32[]{:S(2)}, u32[]{:S(2)}) async-start(bf16[4,5,7168]{2,1,0:T(8,128)(2,1)} %all_to_all.30), calls=%async_computation.3 | async-start | bytes 917504 | tf_op jit(solution)/shard_map/all_to_all | solution.py:91
  101.7 13.5 %all-to-all-done.2 = bf16[4,5,7168]{2,1,0:T(8,128)(2,1)S(1)} async-done(((bf16[4,5,7168]{2,1,0:T(8,128)(2,1)}), bf16[4,5,7168]{2,1,0:T(8,128)(2,1)S(1)}, u32[]{:S(2)}, u32[]{:S(2)}) %all-to-all-start.2) | async-done | bytes 286752 | tf_op jit(solution)/shard_map/all_to_all | solution.py:91
  115.3 0.2 reduce-scatter.4.cloned.1.call-done
  115.6 1.8 %fusion.1 = bf16[8,7168]{1,0:T(8,128)(2,1)} fusion(f32[8,20]{1,0:T(8,128)S(1)} %select_reduce_fusion, bf16[20,7168]{1,0:T(8,128)(2,1)S(1)} %all_to_all.32, bf16[8,7168]{1,0:T(8,128)(2,1)} %reduce-scatter.4.cloned.1.call-done), kind=kOutput, calls=%fused_computation.4 | convolution fusion | flops 13934592 | bytes 516736 | tf_op jit(solution)/shard_map/dot_general | solution.py:92
  (28 shorter events, 0.8 us)
Async XLA Ops:
  6.5 52.1 %all-gather.4.cloned.1.call-start = ((), (), s32[]{:S(2)}) async-start(), calls=%async_computation.5 | async-start | bytes 1720320 | tf_op jit(solution)/shard_map/all_gather | solution.py:80
  31.3 22.0 %all-to-all-start.1 = ((bf16[4,2,140]{2,1,0:T(2,128)(2,1)}), bf16[4,2,140]{2,1,0:T(2,128)(2,1)S(1)}, u32[]{:S(2)}, u32[]{:S(2)}) async-start(bf16[4,2,140]{2,1,0:T(2,128)(2,1)} %reshape.41), calls=%async_computation.2 | async-start | bytes 8192 | tf_op jit(solution)/shard_map/all_to_all | solution.py:77
  34.5 81.0 %reduce-scatter.4.cloned.1.call-start = ((), (), s32[]{:S(2)}) async-start(), calls=%async_computation.4 | async-start | bytes 573440 | tf_op jit(solution)/shard_map/reduce_scatter | solution.py:31
  49.4 0.8 copy-start.2
  49.7 1.0 copy-start
  60.1 2.0 %copy-start.3 = (bf16[1,7168,256]{2,1,0:T(8,128)(2,1)S(1)}, bf16[1,7168,256]{2,1,0:T(8,128)(2,1)}, u32[]{:S(2)}) copy-start(bf16[1,7168,256]{2,1,0:T(8,128)(2,1)} %param.16) | copy-start | bytes 11010052
  63.0 23.2 %copy-start.1 = (f32[32,56,128]{2,1,0:T(8,128)S(1)}, f32[32,56,128]{2,1,0:T(8,128)}, u32[]{:S(2)}) copy-start(f32[32,56,128]{2,1,0:T(8,128)} %copy-done) | copy-start | bytes 2752516
  84.8 7.5 %copy-start.5 = (u32[32]{0:T(128)S(1)}, u32[32]{0:T(128)}, u32[]{:S(2)}) copy-start(u32[32]{0:T(128)} %constant.28) | copy-start | bytes 388
  84.8 8.8 %collective-permute-start = (bf16[12,7168]{1,0:T(8,128)(2,1)S(1)}, bf16[12,7168]{1,0:T(8,128)(2,1)S(1)}, u32[]{:S(2)}, u32[]{:S(2)}) collective-permute-start(bf16[12,7168]{1,0:T(8,128)(2,1)S(1)} %slice), channel_id=1, source_target_pairs={{0,1},{1,2},{2,3},{4,5},{5,6},{6,7},{8,9},{9,10},{10,11},{12,13},{... | collective-permute-start | bytes 516104
  92.3 9.4 %copy-start.4 = (f32[8,2]{0,1:T(2,128)S(1)}, f32[8,2]{0,1:T(2,128)}, u32[]{:S(2)}) copy-start(f32[8,2]{0,1:T(2,128)} %param.14) | copy-start | bytes 196
  97.1 18.1 %all-to-all-start.2 = ((bf16[4,5,7168]{2,1,0:T(8,128)(2,1)}), bf16[4,5,7168]{2,1,0:T(8,128)(2,1)S(1)}, u32[]{:S(2)}, u32[]{:S(2)}) async-start(bf16[4,5,7168]{2,1,0:T(8,128)(2,1)} %all_to_all.30), calls=%async_computation.3 | async-start | bytes 917504 | tf_op jit(solution)/shard_map/all_to_all | solution.py:91
Sparse Core Ops, SparseCore 0:
  29.8 20.0 all-gather.3
  92.5 23.0 reduce-scatter.3
where the time goes:
time: 125 us; the launch traced here: 124 us
  blocking collectives  55.6 us (44%)
  matrix products  18.9 us (15%)
  between operations  14.2 us (11%)
  waiting for transfers between devices  13.8 us (11%)
  local copies, waits for them, and re-layouts  10.3 us (8%)
  starting transfers between devices  9.19 us (7%)
  other arithmetic  2.28 us (2%)
    all_to_all x1, blocking collectives, shards(): lax.all_to_all(send_codes, 'wide', split_axis=0, concat_axis=0, tiled=True)  19.2 us
    unnamed x1, blocking collectives  16.4 us
    all_to_all x1, waiting for transfers between devices, shards(): lax.all_to_all(summed, 'wide', split_axis=0, concat_axis=0, tiled=True)  13.5 us
    dot_general x2, matrix products, expert_forward(): return jnp.dot(hidden, down_proj, preferred_element_type=jnp.float32)  11.5 us
    all_gather x1, blocking collectives, shared_path(): lax.all_gather(row_codes, ('narrow', 'pair'), axis=0, tiled=True)  9.5 us
    unnamed x20, local copies, waits for them, and re-layouts  6.72 us
    all_gather x1, blocking collectives, shared_path(): lax.all_gather(row_scales, ('narrow', 'pair'), axis=0, tiled=True)  5.31 us
    all_gather x1, blocking collectives, shards(): lax.all_gather(came_scales, ('narrow', 'pair'), axis=0, tiled=True)  5.19 us
  transfers between devices with their start and end apart: 5, of which 2 were waited for; matrix products, arithmetic and copies ran while one was open for 11% of the time, Pallas kernels for 0%

commit v1 on v0

v1 whole, which is shorter than its diff:
```python
import functools

import jax
import jax.numpy as jnp
from jax import lax
from jax.experimental import pallas as pl
from jax.experimental.pallas import tpu as pltpu
from jax.sharding import PartitionSpec as P

CAP = 5
LANES = 128
SPAN = 7
MAX_ROWS = 128

VMEM = pltpu.VMEM
VSPEC = pl.BlockSpec(memory_space=pltpu.VMEM)
SSPEC = pl.BlockSpec(memory_space=pltpu.SMEM)
ASPEC = pl.BlockSpec(memory_space=pl.ANY)
F32 = jnp.float32
BF16 = jnp.bfloat16


def put(flat, at, value, rows):
    tall = flat.shape[0] // rows
    for b in range(value.shape[1] // LANES):
        flat[pl.ds(at // LANES + b, rows, stride=tall), :] = value[
            :, b * LANES : (b + 1) * LANES
        ]


def dispatch_kernel(ids, place, weights, here, codes, scales, near, *rest):
    far, (tok, stage, count) = rest[:-3], rest[-3:]
    rows, features = codes.shape
    topk = ids.shape[1]
    tall = features // LANES
    for e in range(place.shape[0]):
        count[e] = 0
    for b in range(tall):
        block = codes[:, b * LANES : (b + 1) * LANES].astype(F32)
        tok[pl.ds(b, rows, stride=tall), :] = block * scales[:, b : b + 1].astype(F32)
    near[:rows] = tok[...].reshape(rows, tall, LANES).astype(BF16)
    stage[...] = jnp.zeros_like(stage)
    sub = lax.broadcasted_iota(jnp.int32, (rows, LANES), 0)
    lane = lax.broadcasted_iota(jnp.int32, (rows, LANES), 1)
    weight = jnp.zeros((rows, LANES), F32)
    for t in range(rows):
        for k in range(topk):
            e = ids[t, k]
            node = place[e]
            slot = count[e]
            count[e] = slot + 1
            weight = jnp.where((sub == t) & (lane == node), weights[t, k], weight)
            stage[(node ^ here[0]) * CAP + slot] = tok[t * tall : (t + 1) * tall, :]
    high = weight.astype(BF16).astype(F32)
    middle = (weight - high).astype(BF16).astype(F32)
    low = weight - high - middle
    near[rows] = jnp.concatenate(
        [high, middle, low, jnp.zeros((tall - 3 * rows, LANES), F32)], axis=0
    ).astype(BF16)
    for k, ref in enumerate(far):
        ref[...] = stage[(k + 1) * CAP : (k + 2) * CAP].astype(BF16)


def unpack(refs, blocks, rows, flat, inputs):
    tall = inputs.shape[1] // LANES
    at = 0
    for ref, count in zip(refs, blocks):
        flat[at * tall : (at + count) * tall, :] = (
            ref[:count].astype(F32).reshape(count * tall, LANES)
        )
        at += count
    if at < rows:
        flat[at * tall : rows * tall, :] = jnp.zeros(((rows - at) * tall, LANES), F32)
    for b in range(tall):
        inputs[:rows, b * LANES : (b + 1) * LANES] = flat[
            pl.ds(b, rows, stride=tall), :
        ].astype(BF16)


def silu_mul(gate, up):
    return (gate / (1.0 + jnp.exp(-gate)) * up).astype(BF16)


def near_kernel(n_narrow, n_pair, here, *refs):
    count = n_narrow * n_pair
    arrived = refs[:count]
    hbm = refs[count : count + 6]
    outs = refs[count + 6 : count + 6 + n_pair]
    kept = refs[count + 6 + n_pair : count + 9 + n_pair]
    s_gate, s_up, s_down, flat, inputs, sems = refs[count + 9 + n_pair :]
    held = (s_gate, s_up, s_down) + tuple(kept)
    copies = [
        pltpu.make_async_copy(src, dst, sems.at[i])
        for i, (src, dst) in enumerate(zip(hbm, held))
    ]
    for copy in copies:
        copy.start()
    tokens, tall = arrived[0].shape[0] - 1, arrived[0].shape[1]
    rows = count * tokens
    unpack(arrived, [tokens] * count, rows, flat, inputs)
    weight = []
    for ref in arrived:
        parts = ref[tokens].astype(F32)
        whole = (
            parts[:tokens] + parts[tokens : 2 * tokens] + parts[2 * tokens : 3 * tokens]
        )
        lane = lax.broadcasted_iota(jnp.int32, whole.shape, 1)
        weight.append(
            jnp.sum(jnp.where(lane == here[0], whole, 0.0), axis=1, keepdims=True)
        )
    weight = jnp.concatenate(weight, axis=0)
    x = inputs[:rows]
    hidden = []
    for i in (0, 3):
        copies[i].wait()
        gate = jnp.dot(x, held[i][...], preferred_element_type=F32)
        copies[i + 1].wait()
        up = jnp.dot(x, held[i + 1][...], preferred_element_type=F32)
        hidden.append(silu_mul(gate, up))
    copies[2].wait()
    copies[5].wait()
    for first in range(0, tall * LANES, SPAN * LANES):
        at = slice(first, first + SPAN * LANES)
        shared = jnp.dot(hidden[0], held[2][:, at], preferred_element_type=F32)
        routed = jnp.dot(hidden[1], held[5][:, at], preferred_element_type=F32)
        put(flat, first, shared + weight * routed, rows)
    each = n_narrow * tokens
    for c in range(n_pair):
        part = flat[c * each * tall : (c + 1) * each * tall, :]
        outs[c][...] = part.reshape(n_narrow, tokens, tall, LANES).astype(BF16)


def far_kernel(n_narrow, n_pair, per, *refs):
    count = n_narrow * n_pair * per
    arrived, rest = refs[:count], refs[count:]
    gate_w, up_w, down_w = rest[:3]
    outs = rest[3 : 3 + n_pair]
    flat, inputs = rest[3 + n_pair :]
    tall = arrived[0].shape[1]
    blocks = [ref.shape[0] for ref in arrived]
    slots = sum(blocks[:per])
    step = count if sum(blocks) <= MAX_ROWS else per
    for first in range(0, count, step):
        total = sum(blocks[first : first + step])
        rows = -(-total // 16) * 16
        unpack(arrived[first : first + step], blocks[first : first + step], rows, flat, inputs)
        x = inputs[:rows]
        gate = jnp.dot(x, gate_w[...], preferred_element_type=F32)
        up = jnp.dot(x, up_w[...], preferred_element_type=F32)
        hidden = silu_mul(gate, up)
        for at in range(0, tall * LANES, SPAN * LANES):
            value = jnp.dot(
                hidden, down_w[:, at : at + SPAN * LANES], preferred_element_type=F32
            )
            put(flat, at, value, rows)
        for i in range(step // per):
            c, j = divmod(first // per + i, n_narrow)
            part = flat[i * slots * tall : (i + 1) * slots * tall, :]
            outs[c][j] = part.reshape(slots, tall, LANES).astype(BF16)


def pair_sum_kernel(n_pair, *refs):
    parts, outs = refs[:n_pair], refs[n_pair:]
    for j, out in enumerate(outs):
        total = parts[0][j].astype(F32)
        for ref in parts[1:]:
            total = total + ref[j].astype(F32)
        out[...] = total.astype(BF16)


def narrow_sum_kernel(n_narrow, *refs):
    parts, outs = refs[:n_narrow], refs[n_narrow:]
    for k, out in enumerate(outs):
        at = slice(k * CAP, (k + 1) * CAP)
        total = parts[0][at].astype(F32)
        for ref in parts[1:]:
            total = total + ref[at].astype(F32)
        out[...] = total.astype(BF16)


def combine_kernel(n_narrow, ids, place, weights, here, *refs):
    near, rest = refs[:n_narrow], refs[n_narrow:]
    far, (out, total, stage, count) = rest[:-4], rest[-4:]
    rows, features = out.shape
    tall = features // LANES
    topk = ids.shape[1]
    for e in range(place.shape[0]):
        count[e] = 0
    stage[:CAP] = jnp.zeros((CAP, tall, LANES), F32)
    for k, ref in enumerate(far):
        stage[(k + 1) * CAP : (k + 2) * CAP] = ref[...].astype(F32)
    for t in range(rows):
        value = near[0][t].astype(F32)
        for ref in near[1:]:
            value = value + ref[t].astype(F32)
        for k in range(topk):
            e = ids[t, k]
            slot = count[e]
            count[e] = slot + 1
            value = value + weights[t, k] * stage[(place[e] ^ here[0]) * CAP + slot]
        total[t * tall : (t + 1) * tall, :] = value
    for b in range(tall):
        out[:, b * LANES : (b + 1) * LANES] = total[
            pl.ds(b, rows, stride=tall), :
        ].astype(BF16)


def swap(value, axis, offset):
    size = lax.axis_size(axis)
    return lax.ppermute(value, axis, [(i, i ^ offset) for i in range(size)])


def call(kernel, name, ins, specs, outs, scratch, flops=0, moved=0, limit=48):
    return pl.pallas_call(
        kernel,
        out_shape=outs,
        in_specs=specs,
        out_specs=jax.tree.map(lambda _: VSPEC, outs),
        scratch_shapes=scratch,
        compiler_params=pltpu.CompilerParams(vmem_limit_bytes=limit << 20),
        cost_estimate=pl.CostEstimate(flops=flops, bytes_accessed=moved, transcendentals=0),
        name=name,
    )(*ins)


def shards(
    row_codes,
    row_scales,
    expert_ids,
    gate_weights,
    placement,
    w_gate,
    w_up,
    w_down,
    shared_gate,
    shared_up,
    shared_down,
):
    n_wide = lax.axis_size("wide")
    n_narrow = lax.axis_size("narrow")
    n_pair = lax.axis_size("pair")
    tokens, features = row_codes.shape
    hidden = w_gate.shape[2]
    tall = features // LANES
    slots = (n_wide - 1) * CAP
    here = lax.axis_index("wide").astype(jnp.int32).reshape(1)
    routing = (expert_ids, placement, gate_weights, here)

    def block(*lead):
        return jax.ShapeDtypeStruct(lead + (tall, LANES), BF16)

    near, *far = call(
        dispatch_kernel,
        "dispatch",
        routing + (row_codes, row_scales),
        [SSPEC] * 4 + [VSPEC] * 2,
        [block(tokens + 1)] + [block(CAP)] * (n_wide - 1),
        [
            VMEM((tokens * tall, LANES), F32),
            VMEM((n_wide * CAP, tall, LANES), F32),
            pltpu.SMEM((placement.shape[0],), jnp.int32),
        ],
    )
    order = [k for k in range(1, n_wide)]
    far = [swap(value, "wide", k) for k, value in zip(order, far)]
    near_line = [near] + [swap(near, "narrow", j) for j in range(1, n_narrow)]
    near_all = list(near_line)
    for c in range(1, n_pair):
        near_all += [swap(value, "pair", c) for value in near_line]
    if n_wide > 4:
        far = [jnp.concatenate(far, axis=0)]
    per = len(far)
    far_line = list(far)
    for j in range(1, n_narrow):
        far_line += [swap(value, "narrow", j) for value in far]
    far_all = list(far_line)
    for c in range(1, n_pair):
        far_all += [swap(value, "pair", c) for value in far_line]

    near_rows = n_narrow * n_pair * tokens
    outs = call(
        functools.partial(near_kernel, n_narrow, n_pair),
        "near",
        [here] + near_all
        + [shared_gate, shared_up, shared_down, w_gate.reshape(features, hidden),
           w_up.reshape(features, hidden), w_down.reshape(hidden, features)],
        [SSPEC] + [VSPEC] * (n_narrow * n_pair) + [ASPEC] * 6,
        [block(n_narrow, tokens)] * n_pair
        + [VMEM((features, hidden), BF16)] * 2 + [VMEM((hidden, features), BF16)],
        [
            VMEM((features, hidden), BF16),
            VMEM((features, hidden), BF16),
            VMEM((hidden, features), BF16),
            VMEM((near_rows * tall, LANES), F32),
            VMEM((near_rows, features), BF16),
            pltpu.SemaphoreType.DMA((6,)),
        ],
        flops=12 * near_rows * features * hidden,
        moved=12 * features * hidden,
    )
    near_out, kept = outs[:n_pair], outs[n_pair:]

    far_rows = n_narrow * n_pair * slots
    pass_rows = far_rows if far_rows <= MAX_ROWS else slots
    pass_rows = -(-pass_rows // 16) * 16
    far_out = call(
        functools.partial(far_kernel, n_narrow, n_pair, per),
        "far",
        far_all + list(kept),
        [VSPEC] * (n_narrow * n_pair * per + 3),
        [block(n_narrow, slots)] * n_pair,
        [VMEM((pass_rows * tall, LANES), F32), VMEM((pass_rows, features), BF16)],
        flops=6 * far_rows * features * hidden,
        moved=6 * features * hidden,
    )

    def reduce_pair(parts, rows):
        parts = [parts[0]] + [swap(parts[c], "pair", c) for c in range(1, n_pair)]
        parts = call(
            functools.partial(pair_sum_kernel, n_pair),
            "pair_sum",
            parts,
            [VSPEC] * n_pair,
            [block(rows)] * n_narrow,
            [],
        )
        return [parts[0]] + [swap(parts[j], "narrow", j) for j in range(1, n_narrow)]

    far_back = call(
        functools.partial(narrow_sum_kernel, n_narrow),
        "narrow_sum",
        reduce_pair(far_out, slots),
        [VSPEC] * n_narrow,
        [block(CAP)] * (n_wide - 1),
        [],
    )
    far_back = [swap(value, "wide", k) for k, value in zip(order, far_back)]
    near_back = reduce_pair(near_out, tokens)
    return call(
        functools.partial(combine_kernel, n_narrow),
        "combine",
        list(routing) + near_back + far_back,
        [SSPEC] * 4 + [VSPEC] * (n_narrow + n_wide - 1),
        jax.ShapeDtypeStruct((tokens, features), BF16),
        [
            VMEM((tokens * tall, LANES), F32),
            VMEM((n_wide * CAP, tall, LANES), F32),
            pltpu.SMEM((placement.shape[0],), jnp.int32),
        ],
    )


def solution(mesh):
    rows = P(("groups", "wide", "narrow", "pair"), None)
    return jax.shard_map(
        shards,
        mesh=mesh,
        in_specs=(
            rows,
            rows,
            rows,
            rows,
            P(),
            P("wide", None, ("narrow", "pair")),
            P("wide", None, ("narrow", "pair")),
            P("wide", ("narrow", "pair"), None),
            P(None, ("narrow", "pair")),
            P(None, ("narrow", "pair")),
            P(("narrow", "pair"), None),
        ),
        out_specs=rows,
        check_vma=False,
    )
```

time: 125 us -> 65.3 us (0.52)
  blocking collectives: 55.6 us -> 0 us
  matrix products: 18.9 us -> 0 us
  Pallas kernels: 0 us -> 18.5 us
  between operations: 14.2 us -> 0.15 us
  starting transfers between devices: 9.19 us -> 18.3 us
  waiting for transfers between devices: 13.8 us -> 20.2 us
  local copies, waits for them, and re-layouts: 10.3 us -> 7.9 us
  other arithmetic: 2.28 us -> 0 us
    ppermute x0 -> x22, waiting for transfers between devices: none -> 20.2 us  [swap(): return lax.ppermute(value, axis, [(i, i ^ offset) for i in range(size)])]
    all_gather x3 -> x0, blocking collectives: 20 us -> none  [the longest x1 9.5 us: shared_path(): lax.all_gather(row_codes, ('narrow', 'pair'), axis=0, tiled=True)]
    all_to_all x1 -> x0, blocking collectives: 19.2 us -> none  [shards(): lax.all_to_all(send_codes, 'wide', split_axis=0, concat_axis=0, tiled=True)]
    dot_general x7 -> x0, matrix products: 18.9 us -> none  [the longest x2 11.5 us: expert_forward(): return jnp.dot(hidden, down_proj, preferred_element_type=jnp.float32)]
    pallas_call x0 -> x7, Pallas kernels: none -> 18.5 us  [call(): pl.pallas_call(kernel, out_shape=outs, in_specs=specs, out_specs=jax.tree...]
    ppermute x0 -> x22, starting transfers between devices: none -> 18.3 us  [swap(): return lax.ppermute(value, axis, [(i, i ^ offset) for i in range(size)])]
    unnamed x1 -> x0, blocking collectives: 16.4 us -> none
    all_to_all x2 -> x0, waiting for transfers between devices: 13.5 us -> none  [the longest x1 13.5 us: shards(): lax.all_to_all(summed, 'wide', split_axis=0, concat_axis=0, tiled=True)]
  transfers between devices with their start and end apart: 5 -> 22, of which waited for: 2 -> 8; matrix products, arithmetic and copies ran while one was open for 11% -> 0% of each run, Pallas kernels for 0% -> 17%
where the time goes in v1:
time: 65.3 us; the launch traced here: 65 us
  waiting for transfers between devices  20.2 us (31%)
  Pallas kernels  18.5 us (28%)
  starting transfers between devices  18.3 us (28%)
  local copies, waits for them, and re-layouts  7.9 us (12%)
    ppermute x22, waiting for transfers between devices, swap(): return lax.ppermute(value, axis, [(i, i ^ offset) for i in range(size)])  20.2 us
    pallas_call x7, Pallas kernels, call(): pl.pallas_call(kernel, out_shape=outs, in_specs=specs, out_specs=jax.tree...  18.5 us
    ppermute x22, starting transfers between devices, swap(): return lax.ppermute(value, axis, [(i, i ^ offset) for i in range(size)])  18.3 us
    unnamed x26, local copies, waits for them, and re-layouts  7.9 us
  transfers between devices with their start and end apart: 22, of which 8 were waited for; matrix products, arithmetic and copies ran while one was open for 0% of the time, Pallas kernels for 17%

profile of v1, /device:TPU:0, one launch (start us, length us, event | category | flops | bytes accessed | tf_op | source)
XLA Modules:
  0.0 65.0 jit_solution(9139833040116529315)
XLA Ops:
  0.0 0.8 %copy.14.ids = s32[8,2]{1,0:T(8,128)S(1)} copy(s32[8,2]{0,1:T(2,128)} %param.13) | data formatting | bytes 128 | tf_op args[2]
  0.8 0.8 %copy.15.weights = f32[8,2]{1,0:T(8,128)S(1)} copy(f32[8,2]{0,1:T(2,128)} %param.14) | data formatting | bytes 128 | tf_op args[3]
  1.5 0.9 %copy-done.4 = bf16[8,7168]{1,0:T(8,128)(2,1)S(1)} copy-done((bf16[8,7168]{1,0:T(8,128)(2,1)S(1)}, bf16[8,7168]{1,0:T(8,128)(2,1)}, u32[]{:S(2)}) %copy-start.4) | copy-done | bytes 114712
  2.4 0.7 %copy-done.5 = bf16[8,56]{1,0:T(8,128)(2,1)S(1)} copy-done((bf16[8,56]{1,0:T(8,128)(2,1)S(1)}, bf16[8,56]{1,0:T(8,128)(2,1)}, u32[]{:S(2)}) %copy-start.5) | copy-done | bytes 920
  3.1 0.7 %copy-done.6 = s32[4]{0:T(128)S(1)} copy-done((s32[4]{0:T(128)S(1)}, s32[4]{0:T(128)}, u32[]{:S(2)}) %copy-start.6) | copy-done | bytes 40
  3.7 0.9 %dispatch.1 = (bf16[9,56,128]{2,1,0:T(8,128)(2,1)S(1)}, bf16[5,56,128]{2,1,0:T(8,128)(2,1)S(1)}, bf16[5,56,128]{2,1,0:T(8,128)(2,1)S(1)}, bf16[5,56,128]{2,1,0:T(8,128)(2,1)S(1)}) custom-call(s32[8,2]{1,0:T(8,128)S(1)} %copy.14.ids, s32[4]{0:T(128)S(1)} %copy-done.6, f32[8,2]{1,0:T(8,128)S(1)} %copy.15.weights, s32[1]{0:T(128)} %bitcast.here, ...), custom_call_target="tpu_custom_call" | custom-call | tf_op jit(solution)/shard_map/dispatch/pallas_call | solution.py:214
  4.7 3.0 %collective-permute-start = (bf16[9,56,128]{2,1,0:T(8,128)(2,1)S(1)}, bf16[9,56,128]{2,1,0:T(8,128)(2,1)S(1)}, u32[]{:S(2)}, u32[]{:S(2)}) collective-permute-start(bf16[9,56,128]{2,1,0:T(8,128)(2,1)S(1)} %get-tuple-element.23.refs_0_), channel_id=1, source_target_pairs={{0,2},{2,0},{1,3},{3,1},{4,6},{6,4},{5,7},{7,5},{8,10},{10,8},{9,1... | collective-permute-start | bytes 387080 | tf_op jit(solution)/shard_map/ppermute | solution.py:210
  7.7 1.6 %collective-permute-start.5 = (bf16[5,56,128]{2,1,0:T(8,128)(2,1)S(1)}, bf16[5,56,128]{2,1,0:T(8,128)(2,1)S(1)}, u32[]{:S(2)}, u32[]{:S(2)}) collective-permute-start(bf16[5,56,128]{2,1,0:T(8,128)(2,1)S(1)} %get-tuple-element.28), channel_id=1, source_target_pairs={{0,4},{4,0},{8,12},{12,8},{1,5},{5,1},{9,13},{13,9},{2,6},{6,2},{1... | collective-permute-start | bytes 215048 | tf_op jit(solution)/shard_map/ppermute | solution.py:210
  9.2 2.6 %collective-permute-start.6 = (bf16[5,56,128]{2,1,0:T(8,128)(2,1)S(1)}, bf16[5,56,128]{2,1,0:T(8,128)(2,1)S(1)}, u32[]{:S(2)}, u32[]{:S(2)}) collective-permute-start(bf16[5,56,128]{2,1,0:T(8,128)(2,1)S(1)} %get-tuple-element.29), channel_id=1, source_target_pairs={{0,8},{4,12},{8,0},{12,4},{1,9},{5,13},{9,1},{13,5},{2,10},{6,14},... | collective-permute-start | bytes 215048 | tf_op jit(solution)/shard_map/ppermute | solution.py:210
  12.3 0.6 collective-permute-start.8
  12.9 5.1 %collective-permute-done.6.refs_1_ = bf16[5,56,128]{2,1,0:T(8,128)(2,1)S(1)} collective-permute-done((bf16[5,56,128]{2,1,0:T(8,128)(2,1)S(1)}, bf16[5,56,128]{2,1,0:T(8,128)(2,1)S(1)}, u32[]{:S(2)}, u32[]{:S(2)}) %collective-permute-start.6) | collective-permute-done | bytes 71712 | tf_op jit(solution)/shard_map/ppermute | solution.py:210
  18.0 0.5 collective-permute-start.9
  18.6 1.5 %collective-permute-start.10 = (bf16[5,56,128]{2,1,0:T(8,128)(2,1)S(1)}, bf16[5,56,128]{2,1,0:T(8,128)(2,1)S(1)}, u32[]{:S(2)}, u32[]{:S(2)}) collective-permute-start(bf16[5,56,128]{2,1,0:T(8,128)(2,1)S(1)} %collective-permute-done.7.refs_2_), channel_id=1, source_target_pairs={{0,2},{2,0},{1,3},{3,1},{4,6},{6,4},{5,7},{7,5},{8,10},{10,8},{9,1... | collective-permute-start | bytes 215048 | tf_op jit(solution)/shard_map/ppermute | solution.py:210
  20.1 0.5 collective-permute-start.12
  20.6 1.8 %collective-permute-done.9.refs_4_ = bf16[5,56,128]{2,1,0:T(8,128)(2,1)S(1)} collective-permute-done((bf16[5,56,128]{2,1,0:T(8,128)(2,1)S(1)}, bf16[5,56,128]{2,1,0:T(8,128)(2,1)S(1)}, u32[]{:S(2)}, u32[]{:S(2)}) %collective-permute-start.9) | collective-permute-done | bytes 71712 | tf_op jit(solution)/shard_map/ppermute | solution.py:210
  22.4 0.8 %collective-permute-done.10.refs_5_ = bf16[5,56,128]{2,1,0:T(8,128)(2,1)S(1)} collective-permute-done((bf16[5,56,128]{2,1,0:T(8,128)(2,1)S(1)}, bf16[5,56,128]{2,1,0:T(8,128)(2,1)S(1)}, u32[]{:S(2)}, u32[]{:S(2)}) %collective-permute-start.10) | collective-permute-done | bytes 71712 | tf_op jit(solution)/shard_map/ppermute | solution.py:210
  23.1 0.5 collective-permute-start.15
  23.7 0.6 copy-done.10
  24.3 10.5 %near.1 = (bf16[2,8,56,128]{3,2,1,0:T(8,128)(2,1)}, bf16[2,8,56,128]{3,2,1,0:T(8,128)(2,1)}, bf16[7168,256]{1,0:T(8,128)(2,1)S(1)}, bf16[7168,256]{1,0:T(8,128)(2,1)S(1)}, bf16[256,7168]{1,0:T(8,128)(2,1)S(1)}) custom-call(s32[1]{0:T(128)} %bitcast.here, bf16[9,56,128]{2,1,0:T(8,128)(2,1)} %copy-done.3, bf16[9,56,128]{2,1,0:T(8,128)(2,1)} %copy-done.8, ...), custom_call_target="tpu_custom_call" | custom-call | flops 704643072 | bytes 22020096 | tf_op jit(solution)/shard_map/near/pallas_call | solution.py:214
  34.8 1.8 %copy-done = bf16[7168,256]{1,0:T(8,128)(2,1)} copy-done((bf16[7168,256]{1,0:T(8,128)(2,1)}, bf16[7168,256]{1,0:T(8,128)(2,1)S(1)}, u32[]{:S(2)}) %copy-start) | copy-done | bytes 3670040
  36.6 1.8 %copy-done.1 = bf16[256,7168]{1,0:T(8,128)(2,1)} copy-done((bf16[256,7168]{1,0:T(8,128)(2,1)}, bf16[256,7168]{1,0:T(8,128)(2,1)S(1)}, u32[]{:S(2)}) %copy-start.1) | copy-done | bytes 3670040
  38.5 5.4 %far.1 = (bf16[2,15,56,128]{3,2,1,0:T(8,128)(2,1)S(1)}, bf16[2,15,56,128]{3,2,1,0:T(8,128)(2,1)S(1)}) custom-call(bf16[5,56,128]{2,1,0:T(8,128)(2,1)S(1)} %collective-permute-done.5.refs_0_, bf16[5,56,128]{2,1,0:T(8,128)(2,1)S(1)} %collective-permute-done.6.refs_1_, bf16[5,56,128]{2,1,0:T(8,128)(2,1)S(1)} %collective-permute-done.7.refs_2_, ...), custom_call_target="tpu_custom_call" | custom-call | flops 660602880 | bytes 11010048 | tf_op jit(solution)/shard_map/far/pallas_call | solution.py:214
  44.5 1.3 %collective-permute-done.17.refs_1_ = bf16[2,15,56,128]{3,2,1,0:T(8,128)(2,1)S(1)} collective-permute-done((bf16[2,15,56,128]{3,2,1,0:T(8,128)(2,1)S(1)}, bf16[2,15,56,128]{3,2,1,0:T(8,128)(2,1)S(1)}, u32[]{:S(2)}, u32[]{:S(2)}) %collective-permute-start.17) | collective-permute-done | bytes 430112 | tf_op jit(solution)/shard_map/ppermute | solution.py:210
  45.9 1.3 %collective-permute-start.18 = (bf16[15,56,128]{2,1,0:T(8,128)(2,1)S(1)}, bf16[15,56,128]{2,1,0:T(8,128)(2,1)S(1)}, u32[]{:S(2)}, u32[]{:S(2)}) collective-permute-start(bf16[15,56,128]{2,1,0:T(8,128)(2,1)S(1)} %get-tuple-element.37), channel_id=1, source_target_pairs={{0,2},{2,0},{1,3},{3,1},{4,6},{6,4},{5,7},{7,5},{8,10},{10,8},{9,1... | collective-permute-start | bytes 645128 | tf_op jit(solution)/shard_map/ppermute | solution.py:210
  47.2 0.8 %collective-permute-start.4 = (bf16[8,56,128]{2,1,0:T(8,128)(2,1)S(1)}, bf16[8,56,128]{2,1,0:T(8,128)(2,1)S(1)}, u32[]{:S(2)}, u32[]{:S(2)}) collective-permute-start(bf16[8,56,128]{2,1,0:T(8,128)(2,1)S(1)} %get-tuple-element.27), channel_id=1, source_target_pairs={{0,2},{2,0},{1,3},{3,1},{4,6},{6,4},{5,7},{7,5},{8,10},{10,8},{9,1... | collective-permute-start | bytes 344072 | tf_op jit(solution)/shard_map/ppermute | solution.py:210
  48.1 6.0 %collective-permute-done.18.refs_1_ = bf16[15,56,128]{2,1,0:T(8,128)(2,1)S(1)} collective-permute-done((bf16[15,56,128]{2,1,0:T(8,128)(2,1)S(1)}, bf16[15,56,128]{2,1,0:T(8,128)(2,1)S(1)}, u32[]{:S(2)}, u32[]{:S(2)}) %collective-permute-start.18) | collective-permute-done | bytes 215072 | tf_op jit(solution)/shard_map/ppermute | solution.py:210
  54.1 0.9 %collective-permute-start.19 = (bf16[5,56,128]{2,1,0:T(8,128)(2,1)S(1)}, bf16[5,56,128]{2,1,0:T(8,128)(2,1)S(1)}, u32[]{:S(2)}, u32[]{:S(2)}) collective-permute-start(bf16[5,56,128]{2,1,0:T(8,128)(2,1)S(1)} %get-tuple-element.38), channel_id=1, source_target_pairs={{0,4},{4,0},{8,12},{12,8},{1,5},{5,1},{9,13},{13,9},{2,6},{6,2},{1... | collective-permute-start | bytes 215048 | tf_op jit(solution)/shard_map/ppermute | solution.py:210
  55.1 2.4 %collective-permute-start.20 = (bf16[5,56,128]{2,1,0:T(8,128)(2,1)S(1)}, bf16[5,56,128]{2,1,0:T(8,128)(2,1)S(1)}, u32[]{:S(2)}, u32[]{:S(2)}) collective-permute-start(bf16[5,56,128]{2,1,0:T(8,128)(2,1)S(1)} %get-tuple-element.39), channel_id=1, source_target_pairs={{0,8},{4,12},{8,0},{12,4},{1,9},{5,13},{9,1},{13,5},{2,10},{6,14},... | collective-permute-start | bytes 215048 | tf_op jit(solution)/shard_map/ppermute | solution.py:210
  57.5 1.1 %collective-permute-start.21 = (bf16[5,56,128]{2,1,0:T(8,128)(2,1)S(1)}, bf16[5,56,128]{2,1,0:T(8,128)(2,1)S(1)}, u32[]{:S(2)}, u32[]{:S(2)}) collective-permute-start(bf16[5,56,128]{2,1,0:T(8,128)(2,1)S(1)} %get-tuple-element.40), channel_id=1, source_target_pairs={{0,12},{4,8},{8,4},{12,0},{1,13},{5,9},{9,5},{13,1},{2,14},{6,10},... | collective-permute-start | bytes 215048 | tf_op jit(solution)/shard_map/ppermute | solution.py:210
  58.6 3.2 %collective-permute-done.20.refs_3_ = bf16[5,56,128]{2,1,0:T(8,128)(2,1)S(1)} collective-permute-done((bf16[5,56,128]{2,1,0:T(8,128)(2,1)S(1)}, bf16[5,56,128]{2,1,0:T(8,128)(2,1)S(1)}, u32[]{:S(2)}, u32[]{:S(2)}) %collective-permute-start.20) | collective-permute-done | bytes 71712 | tf_op jit(solution)/shard_map/ppermute | solution.py:210
  61.8 1.8 %collective-permute-done.21.refs_4_ = bf16[5,56,128]{2,1,0:T(8,128)(2,1)S(1)} collective-permute-done((bf16[5,56,128]{2,1,0:T(8,128)(2,1)S(1)}, bf16[5,56,128]{2,1,0:T(8,128)(2,1)S(1)}, u32[]{:S(2)}, u32[]{:S(2)}) %collective-permute-start.21) | collective-permute-done | bytes 71712 | tf_op jit(solution)/shard_map/ppermute | solution.py:210
  63.6 1.5 %combine.1 = bf16[8,7168]{1,0:T(8,128)(2,1)} custom-call(s32[8,2]{1,0:T(8,128)S(1)} %copy.14.ids, s32[4]{0:T(128)S(1)} %copy-done.7, f32[8,2]{1,0:T(8,128)S(1)} %copy.15.weights, s32[1]{0:T(128)} %bitcast.here, bf16[8,56,128]{2,1,0:T(8,128)(2,1)S(1)} %get-tuple-element.26.refs_0_, bf16[8,56,128]{2,1,0:T(8,128)(2,1)S(1)} %collective-permute-done.4.refs_1_, ...), custom_call_target="tpu_custom_call" | custom-call | tf_op jit(solution)/shard_map/combine/pallas_call | solution.py:214
  (45 shorter events, 1.4 us)
Async XLA Ops:
  1.5 0.9 %copy-start.4 = (bf16[8,7168]{1,0:T(8,128)(2,1)S(1)}, bf16[8,7168]{1,0:T(8,128)(2,1)}, u32[]{:S(2)}) copy-start(bf16[8,7168]{1,0:T(8,128)(2,1)} %codes.1) | copy-start | bytes 344068
  2.4 0.7 %copy-start.5 = (bf16[8,56]{1,0:T(8,128)(2,1)S(1)}, bf16[8,56]{1,0:T(8,128)(2,1)}, u32[]{:S(2)}) copy-start(bf16[8,56]{1,0:T(8,128)(2,1)} %scales.1) | copy-start | bytes 2692
  4.6 19.1 %copy-start.3 = (bf16[9,56,128]{2,1,0:T(8,128)(2,1)}, bf16[9,56,128]{2,1,0:T(8,128)(2,1)S(1)}, u32[]{:S(2)}) copy-start(bf16[9,56,128]{2,1,0:T(8,128)(2,1)S(1)} %get-tuple-element.23.refs_0_) | copy-start | bytes 387076
  4.7 7.4 %collective-permute-start = (bf16[9,56,128]{2,1,0:T(8,128)(2,1)S(1)}, bf16[9,56,128]{2,1,0:T(8,128)(2,1)S(1)}, u32[]{:S(2)}, u32[]{:S(2)}) collective-permute-start(bf16[9,56,128]{2,1,0:T(8,128)(2,1)S(1)} %get-tuple-element.23.refs_0_), channel_id=1, source_target_pairs={{0,2},{2,0},{1,3},{3,1},{4,6},{6,4},{5,7},{7,5},{8,10},{10,8},{9,1... | collective-permute-start | bytes 387080 | tf_op jit(solution)/shard_map/ppermute | solution.py:210
  7.7 12.4 %collective-permute-start.1 = (bf16[9,56,128]{2,1,0:T(8,128)(2,1)S(1)}, bf16[9,56,128]{2,1,0:T(8,128)(2,1)S(1)}, u32[]{:S(2)}, u32[]{:S(2)}) collective-permute-start(bf16[9,56,128]{2,1,0:T(8,128)(2,1)S(1)} %get-tuple-element.23.refs_0_), channel_id=1, source_target_pairs={{0,1},{1,0},{2,3},{3,2},{4,5},{5,4},{6,7},{7,6},{8,9},{9,8},{10,11... | collective-permute-start | bytes 387080 | tf_op jit(solution)/shard_map/ppermute | solution.py:210
  7.7 4.6 %collective-permute-start.5 = (bf16[5,56,128]{2,1,0:T(8,128)(2,1)S(1)}, bf16[5,56,128]{2,1,0:T(8,128)(2,1)S(1)}, u32[]{:S(2)}, u32[]{:S(2)}) collective-permute-start(bf16[5,56,128]{2,1,0:T(8,128)(2,1)S(1)} %get-tuple-element.28), channel_id=1, source_target_pairs={{0,4},{4,0},{8,12},{12,8},{1,5},{5,1},{9,13},{13,9},{2,6},{6,2},{1... | collective-permute-start | bytes 215048 | tf_op jit(solution)/shard_map/ppermute | solution.py:210
  9.2 8.8 %collective-permute-start.6 = (bf16[5,56,128]{2,1,0:T(8,128)(2,1)S(1)}, bf16[5,56,128]{2,1,0:T(8,128)(2,1)S(1)}, u32[]{:S(2)}, u32[]{:S(2)}) collective-permute-start(bf16[5,56,128]{2,1,0:T(8,128)(2,1)S(1)} %get-tuple-element.29), channel_id=1, source_target_pairs={{0,8},{4,12},{8,0},{12,4},{1,9},{5,13},{9,1},{13,5},{2,10},{6,14},... | collective-permute-start | bytes 215048 | tf_op jit(solution)/shard_map/ppermute | solution.py:210
  11.8 6.7 %collective-permute-start.7 = (bf16[5,56,128]{2,1,0:T(8,128)(2,1)S(1)}, bf16[5,56,128]{2,1,0:T(8,128)(2,1)S(1)}, u32[]{:S(2)}, u32[]{:S(2)}) collective-permute-start(bf16[5,56,128]{2,1,0:T(8,128)(2,1)S(1)} %get-tuple-element.30), channel_id=1, source_target_pairs={{0,12},{4,8},{8,4},{12,0},{1,13},{5,9},{9,5},{13,1},{2,14},{6,10},... | collective-permute-start | bytes 215048 | tf_op jit(solution)/shard_map/ppermute | solution.py:210
  12.1 11.7 %copy-start.8 = (bf16[9,56,128]{2,1,0:T(8,128)(2,1)}, bf16[9,56,128]{2,1,0:T(8,128)(2,1)S(1)}, u32[]{:S(2)}) copy-start(bf16[9,56,128]{2,1,0:T(8,128)(2,1)S(1)} %collective-permute-done.refs_1_) | copy-start | bytes 387076
  12.1 11.6 %collective-permute-start.2 = (bf16[9,56,128]{2,1,0:T(8,128)(2,1)S(1)}, bf16[9,56,128]{2,1,0:T(8,128)(2,1)S(1)}, u32[]{:S(2)}, u32[]{:S(2)}) collective-permute-start(bf16[9,56,128]{2,1,0:T(8,128)(2,1)S(1)} %collective-permute-done.refs_1_), channel_id=1, source_target_pairs={{0,1},{1,0},{2,3},{3,2},{4,5},{5,4},{6,7},{7,6},{8,9},{9,8},{10,11... | collective-permute-start | bytes 387080 | tf_op jit(solution)/shard_map/ppermute | solution.py:210
  12.3 7.8 %collective-permute-start.8 = (bf16[5,56,128]{2,1,0:T(8,128)(2,1)S(1)}, bf16[5,56,128]{2,1,0:T(8,128)(2,1)S(1)}, u32[]{:S(2)}, u32[]{:S(2)}) collective-permute-start(bf16[5,56,128]{2,1,0:T(8,128)(2,1)S(1)} %collective-permute-done.5.refs_0_), channel_id=1, source_target_pairs={{0,2},{2,0},{1,3},{3,1},{4,6},{6,4},{5,7},{7,5},{8,10},{10,8},{9,1... | collective-permute-start | bytes 215048 | tf_op jit(solution)/shard_map/ppermute | solution.py:210
  18.0 4.3 %collective-permute-start.9 = (bf16[5,56,128]{2,1,0:T(8,128)(2,1)S(1)}, bf16[5,56,128]{2,1,0:T(8,128)(2,1)S(1)}, u32[]{:S(2)}, u32[]{:S(2)}) collective-permute-start(bf16[5,56,128]{2,1,0:T(8,128)(2,1)S(1)} %collective-permute-done.6.refs_1_), channel_id=1, source_target_pairs={{0,2},{2,0},{1,3},{3,1},{4,6},{6,4},{5,7},{7,5},{8,10},{10,8},{9,1... | collective-permute-start | bytes 215048 | tf_op jit(solution)/shard_map/ppermute | solution.py:210
  18.6 4.6 %collective-permute-start.10 = (bf16[5,56,128]{2,1,0:T(8,128)(2,1)S(1)}, bf16[5,56,128]{2,1,0:T(8,128)(2,1)S(1)}, u32[]{:S(2)}, u32[]{:S(2)}) collective-permute-start(bf16[5,56,128]{2,1,0:T(8,128)(2,1)S(1)} %collective-permute-done.7.refs_2_), channel_id=1, source_target_pairs={{0,2},{2,0},{1,3},{3,1},{4,6},{6,4},{5,7},{7,5},{8,10},{10,8},{9,1... | collective-permute-start | bytes 215048 | tf_op jit(solution)/shard_map/ppermute | solution.py:210
  20.1 3.7 %copy-start.9 = (bf16[9,56,128]{2,1,0:T(8,128)(2,1)}, bf16[9,56,128]{2,1,0:T(8,128)(2,1)S(1)}, u32[]{:S(2)}) copy-start(bf16[9,56,128]{2,1,0:T(8,128)(2,1)S(1)} %collective-permute-done.1.refs_2_) | copy-start | bytes 387076
  20.1 3.1 %collective-permute-start.11 = (bf16[5,56,128]{2,1,0:T(8,128)(2,1)S(1)}, bf16[5,56,128]{2,1,0:T(8,128)(2,1)S(1)}, u32[]{:S(2)}, u32[]{:S(2)}) collective-permute-start(bf16[5,56,128]{2,1,0:T(8,128)(2,1)S(1)} %collective-permute-done.5.refs_0_), channel_id=1, source_target_pairs={{0,1},{1,0},{2,3},{3,2},{4,5},{5,4},{6,7},{7,6},{8,9},{9,8},{10,11... | collective-permute-start | bytes 215048 | tf_op jit(solution)/shard_map/ppermute | solution.py:210
  20.1 18.3 %collective-permute-start.12 = (bf16[5,56,128]{2,1,0:T(8,128)(2,1)S(1)}, bf16[5,56,128]{2,1,0:T(8,128)(2,1)S(1)}, u32[]{:S(2)}, u32[]{:S(2)}) collective-permute-start(bf16[5,56,128]{2,1,0:T(8,128)(2,1)S(1)} %collective-permute-done.6.refs_1_), channel_id=1, source_target_pairs={{0,1},{1,0},{2,3},{3,2},{4,5},{5,4},{6,7},{7,6},{8,9},{9,8},{10,11... | collective-permute-start | bytes 215048 | tf_op jit(solution)/shard_map/ppermute | solution.py:210
  22.4 16.1 %collective-permute-start.13 = (bf16[5,56,128]{2,1,0:T(8,128)(2,1)S(1)}, bf16[5,56,128]{2,1,0:T(8,128)(2,1)S(1)}, u32[]{:S(2)}, u32[]{:S(2)}) collective-permute-start(bf16[5,56,128]{2,1,0:T(8,128)(2,1)S(1)} %collective-permute-done.7.refs_2_), channel_id=1, source_target_pairs={{0,1},{1,0},{2,3},{3,2},{4,5},{5,4},{6,7},{7,6},{8,9},{9,8},{10,11... | collective-permute-start | bytes 215048 | tf_op jit(solution)/shard_map/ppermute | solution.py:210
  23.1 15.3 %collective-permute-start.14 = (bf16[5,56,128]{2,1,0:T(8,128)(2,1)S(1)}, bf16[5,56,128]{2,1,0:T(8,128)(2,1)S(1)}, u32[]{:S(2)}, u32[]{:S(2)}) collective-permute-start(bf16[5,56,128]{2,1,0:T(8,128)(2,1)S(1)} %collective-permute-done.8.refs_3_), channel_id=1, source_target_pairs={{0,1},{1,0},{2,3},{3,2},{4,5},{5,4},{6,7},{7,6},{8,9},{9,8},{10,11... | collective-permute-start | bytes 215048 | tf_op jit(solution)/shard_map/ppermute | solution.py:210
  23.1 15.3 %collective-permute-start.15 = (bf16[5,56,128]{2,1,0:T(8,128)(2,1)S(1)}, bf16[5,56,128]{2,1,0:T(8,128)(2,1)S(1)}, u32[]{:S(2)}, u32[]{:S(2)}) collective-permute-start(bf16[5,56,128]{2,1,0:T(8,128)(2,1)S(1)} %collective-permute-done.9.refs_4_), channel_id=1, source_target_pairs={{0,1},{1,0},{2,3},{3,2},{4,5},{5,4},{6,7},{7,6},{8,9},{9,8},{10,11... | collective-permute-start | bytes 215048 | tf_op jit(solution)/shard_map/ppermute | solution.py:210
  23.7 14.8 %collective-permute-start.16 = (bf16[5,56,128]{2,1,0:T(8,128)(2,1)S(1)}, bf16[5,56,128]{2,1,0:T(8,128)(2,1)S(1)}, u32[]{:S(2)}, u32[]{:S(2)}) collective-permute-start(bf16[5,56,128]{2,1,0:T(8,128)(2,1)S(1)} %collective-permute-done.10.refs_5_), channel_id=1, source_target_pairs={{0,1},{1,0},{2,3},{3,2},{4,5},{5,4},{6,7},{7,6},{8,9},{9,8},{10,11... | collective-permute-start | bytes 215048 | tf_op jit(solution)/shard_map/ppermute | solution.py:210
  34.8 1.8 %copy-start = (bf16[7168,256]{1,0:T(8,128)(2,1)}, bf16[7168,256]{1,0:T(8,128)(2,1)S(1)}, u32[]{:S(2)}) copy-start(bf16[7168,256]{1,0:T(8,128)(2,1)S(1)} %get-tuple-element.32.refs_13_) | copy-start | bytes 11010052
  36.6 1.8 %copy-start.1 = (bf16[256,7168]{1,0:T(8,128)(2,1)}, bf16[256,7168]{1,0:T(8,128)(2,1)S(1)}, u32[]{:S(2)}) copy-start(bf16[256,7168]{1,0:T(8,128)(2,1)S(1)} %get-tuple-element.33.refs_14_) | copy-start | bytes 11010052
  38.4 5.5 %copy-start.11 = (bf16[2,8,56,128]{3,2,1,0:T(8,128)(2,1)S(1)}, bf16[2,8,56,128]{3,2,1,0:T(8,128)(2,1)}, u32[]{:S(2)}) copy-start(bf16[2,8,56,128]{3,2,1,0:T(8,128)(2,1)} %get-tuple-element.25) | copy-start | bytes 688132
  38.5 8.7 %copy-start.2 = (bf16[2,8,56,128]{3,2,1,0:T(8,128)(2,1)S(1)}, bf16[2,8,56,128]{3,2,1,0:T(8,128)(2,1)}, u32[]{:S(2)}) copy-start(bf16[2,8,56,128]{3,2,1,0:T(8,128)(2,1)} %get-tuple-element.24.refs_0_) | copy-start | bytes 688132
  38.5 25.1 %copy-start.7 = (s32[4]{0:T(128)S(1)}, s32[4]{0:T(128)}, u32[]{:S(2)}) copy-start(s32[4]{0:T(128)} %place.3) | copy-start | bytes 52
  43.9 1.8 %collective-permute-start.17 = (bf16[2,15,56,128]{3,2,1,0:T(8,128)(2,1)S(1)}, bf16[2,15,56,128]{3,2,1,0:T(8,128)(2,1)S(1)}, u32[]{:S(2)}, u32[]{:S(2)}) collective-permute-start(bf16[2,15,56,128]{3,2,1,0:T(8,128)(2,1)S(1)} %get-tuple-element.35), channel_id=1, source_target_pairs={{0,1},{1,0},{2,3},{3,2},{4,5},{5,4},{6,7},{7,6},{8,9},{9,8},{10,11... | collective-permute-start | bytes 1290248 | tf_op jit(solution)/shard_map/ppermute | solution.py:210
  44.0 3.2 %collective-permute-start.3 = (bf16[2,8,56,128]{3,2,1,0:T(8,128)(2,1)S(1)}, bf16[2,8,56,128]{3,2,1,0:T(8,128)(2,1)S(1)}, u32[]{:S(2)}, u32[]{:S(2)}) collective-permute-start(bf16[2,8,56,128]{3,2,1,0:T(8,128)(2,1)S(1)} %copy-done.11), channel_id=1, source_target_pairs={{0,1},{1,0},{2,3},{3,2},{4,5},{5,4},{6,7},{7,6},{8,9},{9,8},{10,11... | collective-permute-start | bytes 688136 | tf_op jit(solution)/shard_map/ppermute | solution.py:210
  45.9 8.2 %collective-permute-start.18 = (bf16[15,56,128]{2,1,0:T(8,128)(2,1)S(1)}, bf16[15,56,128]{2,1,0:T(8,128)(2,1)S(1)}, u32[]{:S(2)}, u32[]{:S(2)}) collective-permute-start(bf16[15,56,128]{2,1,0:T(8,128)(2,1)S(1)} %get-tuple-element.37), channel_id=1, source_target_pairs={{0,2},{2,0},{1,3},{3,1},{4,6},{6,4},{5,7},{7,5},{8,10},{10,8},{9,1... | collective-permute-start | bytes 645128 | tf_op jit(solution)/shard_map/ppermute | solution.py:210
  47.2 11.3 %collective-permute-start.4 = (bf16[8,56,128]{2,1,0:T(8,128)(2,1)S(1)}, bf16[8,56,128]{2,1,0:T(8,128)(2,1)S(1)}, u32[]{:S(2)}, u32[]{:S(2)}) collective-permute-start(bf16[8,56,128]{2,1,0:T(8,128)(2,1)S(1)} %get-tuple-element.27), channel_id=1, source_target_pairs={{0,2},{2,0},{1,3},{3,1},{4,6},{6,4},{5,7},{7,5},{8,10},{10,8},{9,1... | collective-permute-start | bytes 344072 | tf_op jit(solution)/shard_map/ppermute | solution.py:210
  54.1 4.5 %collective-permute-start.19 = (bf16[5,56,128]{2,1,0:T(8,128)(2,1)S(1)}, bf16[5,56,128]{2,1,0:T(8,128)(2,1)S(1)}, u32[]{:S(2)}, u32[]{:S(2)}) collective-permute-start(bf16[5,56,128]{2,1,0:T(8,128)(2,1)S(1)} %get-tuple-element.38), channel_id=1, source_target_pairs={{0,4},{4,0},{8,12},{12,8},{1,5},{5,1},{9,13},{13,9},{2,6},{6,2},{1... | collective-permute-start | bytes 215048 | tf_op jit(solution)/shard_map/ppermute | solution.py:210
  55.1 6.8 %collective-permute-start.20 = (bf16[5,56,128]{2,1,0:T(8,128)(2,1)S(1)}, bf16[5,56,128]{2,1,0:T(8,128)(2,1)S(1)}, u32[]{:S(2)}, u32[]{:S(2)}) collective-permute-start(bf16[5,56,128]{2,1,0:T(8,128)(2,1)S(1)} %get-tuple-element.39), channel_id=1, source_target_pairs={{0,8},{4,12},{8,0},{12,4},{1,9},{5,13},{9,1},{13,5},{2,10},{6,14},... | collective-permute-start | bytes 215048 | tf_op jit(solution)/shard_map/ppermute | solution.py:210
  57.5 6.1 %collective-permute-start.21 = (bf16[5,56,128]{2,1,0:T(8,128)(2,1)S(1)}, bf16[5,56,128]{2,1,0:T(8,128)(2,1)S(1)}, u32[]{:S(2)}, u32[]{:S(2)}) collective-permute-start(bf16[5,56,128]{2,1,0:T(8,128)(2,1)S(1)} %get-tuple-element.40), channel_id=1, source_target_pairs={{0,12},{4,8},{8,4},{12,0},{1,13},{5,9},{9,5},{13,1},{2,14},{6,10},... | collective-permute-start | bytes 215048 | tf_op jit(solution)/shard_map/ppermute | solution.py:210
  (2 other events, 1.3 us)

commit v2 on v1

v2 whole, which is shorter than its diff:
```python
import functools

import jax
import jax.numpy as jnp
from jax import lax
from jax.experimental import pallas as pl
from jax.experimental.pallas import tpu as pltpu
from jax.sharding import PartitionSpec as P

CAP = 5
LANES = 128
SPAN = 7
MAX_ROWS = 128

VMEM = pltpu.VMEM
VSPEC = pl.BlockSpec(memory_space=pltpu.VMEM)
SSPEC = pl.BlockSpec(memory_space=pltpu.SMEM)
ASPEC = pl.BlockSpec(memory_space=pl.ANY)
F32 = jnp.float32
BF16 = jnp.bfloat16


def put(flat, at, value, rows):
    tall = flat.shape[0] // rows
    for b in range(value.shape[1] // LANES):
        flat[pl.ds(at // LANES + b, rows, stride=tall), :] = value[
            :, b * LANES : (b + 1) * LANES
        ]


def dispatch_kernel(ids_in, place_in, weights_in, codes_in, scales_in, *refs):
    near, far = refs[0], refs[1:-10]
    route, gains = refs[-10:-8]
    ids, place, weights, codes, scales, tok, stage, sems = refs[-8:]
    copies = [
        pltpu.make_async_copy(src, dst, sems.at[i])
        for i, (src, dst) in enumerate(
            (
                (codes_in, codes),
                (scales_in, scales),
                (ids_in, ids),
                (place_in, place),
                (weights_in, weights),
            )
        )
    ]
    for copy in copies:
        copy.start()
    here = lax.axis_index("wide")
    rows, features = codes.shape
    topk = ids.shape[0]
    tall = features // LANES
    stage[...] = jnp.zeros_like(stage)
    for copy in copies:
        copy.wait()
    for b in range(tall):
        block = codes[:, b * LANES : (b + 1) * LANES].astype(F32)
        tok[pl.ds(b, rows, stride=tall), :] = block * scales[:, b : b + 1].astype(F32)
    near[:rows] = tok[...].reshape(rows, tall, LANES).astype(BF16)
    sub = lax.broadcasted_iota(jnp.int32, (rows, LANES), 0)
    lane = lax.broadcasted_iota(jnp.int32, (rows, LANES), 1)
    weight = jnp.zeros((rows, LANES), F32)
    named = []
    for t in range(rows):
        for k in range(topk):
            e = ids[k, t]
            node = place[e]
            slot = jnp.int32(0)
            for other in named[: t * topk]:
                slot = slot + jnp.where(other == e, 1, 0)
            named.append(e)
            at = (node ^ here) * CAP + slot
            route[k, t] = at
            gains[k, t] = weights[k, t]
            weight = jnp.where((sub == t) & (lane == node), weights[k, t], weight)
            stage[at] = tok[t * tall : (t + 1) * tall, :]
    high = weight.astype(BF16).astype(F32)
    middle = (weight - high).astype(BF16).astype(F32)
    low = weight - high - middle
    near[rows] = jnp.concatenate(
        [high, middle, low, jnp.zeros((tall - 3 * rows, LANES), F32)], axis=0
    ).astype(BF16)
    for k, ref in enumerate(far):
        ref[...] = stage[(k + 1) * CAP : (k + 2) * CAP].astype(BF16)


def load_kernel(count, *refs):
    srcs, outs, sems = refs[:count], refs[-count - 1 : -1], refs[-1]
    copies = [
        pltpu.make_async_copy(src, dst, sems.at[i])
        for i, (src, dst) in enumerate(zip(srcs, outs))
    ]
    for copy in copies:
        copy.start()
    for copy in copies:
        copy.wait()


def unpack(refs, blocks, rows, flat, inputs):
    tall = inputs.shape[1] // LANES
    at = 0
    for ref, count in zip(refs, blocks):
        flat[at * tall : (at + count) * tall, :] = (
            ref[:count].astype(F32).reshape(count * tall, LANES)
        )
        at += count
    if at < rows:
        flat[at * tall : rows * tall, :] = jnp.zeros(((rows - at) * tall, LANES), F32)
    for b in range(tall):
        inputs[:rows, b * LANES : (b + 1) * LANES] = flat[
            pl.ds(b, rows, stride=tall), :
        ].astype(BF16)


def silu_mul(gate, up):
    return (gate / (1.0 + jnp.exp(-gate)) * up).astype(BF16)


def near_kernel(n_narrow, n_pair, *refs):
    count = n_narrow * n_pair
    arrived = refs[:count]
    held = refs[count : count + 6]
    outs = refs[count + 6 : count + 6 + n_pair]
    flat, inputs = refs[count + 6 + n_pair :]
    here = lax.axis_index("wide")
    tokens, tall = arrived[0].shape[0] - 1, arrived[0].shape[1]
    rows = count * tokens
    unpack(arrived, [tokens] * count, rows, flat, inputs)
    weight = []
    for ref in arrived:
        parts = ref[tokens].astype(F32)
        whole = (
            parts[:tokens] + parts[tokens : 2 * tokens] + parts[2 * tokens : 3 * tokens]
        )
        lane = lax.broadcasted_iota(jnp.int32, whole.shape, 1)
        weight.append(
            jnp.sum(jnp.where(lane == here, whole, 0.0), axis=1, keepdims=True)
        )
    weight = jnp.concatenate(weight, axis=0)
    x = inputs[:rows]
    hidden = []
    for i in (0, 3):
        gate = jnp.dot(x, held[i][...], preferred_element_type=F32)
        up = jnp.dot(x, held[i + 1][...], preferred_element_type=F32)
        hidden.append(silu_mul(gate, up))
    for first in range(0, tall * LANES, SPAN * LANES):
        at = slice(first, first + SPAN * LANES)
        shared = jnp.dot(hidden[0], held[2][:, at], preferred_element_type=F32)
        routed = jnp.dot(hidden[1], held[5][:, at], preferred_element_type=F32)
        put(flat, first, shared + weight * routed, rows)
    each = n_narrow * tokens
    for c in range(n_pair):
        part = flat[c * each * tall : (c + 1) * each * tall, :]
        outs[c][...] = part.reshape(n_narrow, tokens, tall, LANES).astype(BF16)


def far_kernel(n_narrow, n_pair, per, *refs):
    count = n_narrow * n_pair * per
    arrived, rest = refs[:count], refs[count:]
    gate_w, up_w, down_w = rest[:3]
    outs = rest[3 : 3 + n_pair * per]
    flat, inputs = rest[3 + n_pair * per :]
    tall = arrived[0].shape[1]
    blocks = [ref.shape[0] for ref in arrived]
    step = count if sum(blocks) <= MAX_ROWS else per
    for first in range(0, count, step):
        group = blocks[first : first + step]
        rows = -(-sum(group) // 16) * 16
        unpack(arrived[first : first + step], group, rows, flat, inputs)
        x = inputs[:rows]
        gate = jnp.dot(x, gate_w[...], preferred_element_type=F32)
        up = jnp.dot(x, up_w[...], preferred_element_type=F32)
        hidden = silu_mul(gate, up)
        for at in range(0, tall * LANES, SPAN * LANES):
            value = jnp.dot(
                hidden, down_w[:, at : at + SPAN * LANES], preferred_element_type=F32
            )
            put(flat, at, value, rows)
        at = 0
        for i, slots in enumerate(group):
            line, k = divmod(first + i, per)
            c, j = divmod(line, n_narrow)
            part = flat[at * tall : (at + slots) * tall, :]
            outs[c * per + k][j] = part.reshape(slots, tall, LANES).astype(BF16)
            at += slots


def pair_sum_kernel(n_pair, *refs):
    parts, outs = refs[:n_pair], refs[n_pair:]
    for j, out in enumerate(outs):
        total = parts[0][j].astype(F32)
        for ref in parts[1:]:
            total = total + ref[j].astype(F32)
        out[...] = total.astype(BF16)


def narrow_sum_kernel(n_narrow, *refs):
    parts, outs = refs[:n_narrow], refs[n_narrow:]
    at = 0
    for out in outs:
        rows = slice(at, at + out.shape[0])
        total = parts[0][rows].astype(F32)
        for ref in parts[1:]:
            total = total + ref[rows].astype(F32)
        out[...] = total.astype(BF16)
        at += out.shape[0]


def combine_kernel(n_narrow, order, route, gains, *refs):
    near, rest = refs[:n_narrow], refs[n_narrow:]
    far, (out, total, stage) = rest[:-3], rest[-3:]
    rows, features = out.shape
    tall = features // LANES
    topk = route.shape[0]
    stage[:CAP] = jnp.zeros((CAP, tall, LANES), F32)
    for k, ref in zip(order, far):
        stage[k * CAP : (k + 1) * CAP] = ref[...].astype(F32)
    for t in range(rows):
        value = near[0][t].astype(F32)
        for ref in near[1:]:
            value = value + ref[t].astype(F32)
        for k in range(topk):
            value = value + gains[k, t] * stage[route[k, t]]
        total[t * tall : (t + 1) * tall, :] = value
    for b in range(tall):
        out[:, b * LANES : (b + 1) * LANES] = total[
            pl.ds(b, rows, stride=tall), :
        ].astype(BF16)


def swap(value, axis, offset):
    size = lax.axis_size(axis)
    return lax.ppermute(value, axis, [(i, i ^ offset) for i in range(size)])


def call(kernel, name, ins, specs, outs, scratch, flops=0, moved=0, limit=16):
    return pl.pallas_call(
        kernel,
        out_shape=outs,
        in_specs=specs,
        out_specs=jax.tree.map(
            lambda out: SSPEC if getattr(out, "memory_space", None) == pltpu.SMEM else VSPEC,
            outs,
        ),
        scratch_shapes=scratch,
        compiler_params=pltpu.CompilerParams(vmem_limit_bytes=limit << 20),
        cost_estimate=pl.CostEstimate(flops=flops, bytes_accessed=moved, transcendentals=0),
        name=name,
    )(*ins)


def shards(
    row_codes,
    row_scales,
    expert_ids,
    gate_weights,
    placement,
    w_gate,
    w_up,
    w_down,
    shared_gate,
    shared_up,
    shared_down,
):
    n_wide = lax.axis_size("wide")
    n_narrow = lax.axis_size("narrow")
    n_pair = lax.axis_size("pair")
    tokens, features = row_codes.shape
    hidden = w_gate.shape[2]
    tall = features // LANES
    topk = expert_ids.shape[1]
    limit = 16 if n_wide <= 4 else 48

    def block(*lead):
        return jax.ShapeDtypeStruct(lead + (tall, LANES), BF16)

    near, *far = call(
        dispatch_kernel,
        "dispatch",
        (expert_ids.T, placement, gate_weights.T, row_codes, row_scales),
        [ASPEC] * 5,
        [block(tokens + 1)]
        + [block(CAP)] * (n_wide - 1)
        + [pltpu.SMEM((topk, tokens), jnp.int32), pltpu.SMEM((topk, tokens), F32)],
        [
            pltpu.SMEM((topk, tokens), jnp.int32),
            pltpu.SMEM(placement.shape, jnp.int32),
            pltpu.SMEM((topk, tokens), F32),
            VMEM((tokens, features), BF16),
            VMEM(row_scales.shape, BF16),
            VMEM((tokens * tall, LANES), F32),
            VMEM((n_wide * CAP, tall, LANES), F32),
            pltpu.SemaphoreType.DMA((5,)),
        ],
    )
    far, (route, gains) = far[:-2], far[-2:]
    order = list(range(n_wide - 1, 0, -1))
    far = [swap(far[k - 1], "wide", k) for k in order]
    near_line = [near] + [swap(near, "narrow", j) for j in range(1, n_narrow)]

    def load(name, after, *weights):
        return call(
            functools.partial(load_kernel, len(weights)),
            name,
            list(weights) + [after],
            [ASPEC] * (len(weights) + 1),
            [VMEM(value.shape, BF16) for value in weights],
            [pltpu.SemaphoreType.DMA((len(weights),))],
            moved=2 * sum(value.size for value in weights),
        )

    shared = load("load_shared", near, shared_gate, shared_up, shared_down)
    routed = load(
        "load_routed",
        near,
        w_gate.reshape(features, hidden),
        w_up.reshape(features, hidden),
        w_down.reshape(hidden, features),
    )
    near_all = list(near_line)
    for c in range(1, n_pair):
        near_all += [swap(value, "pair", c) for value in near_line]
    if n_wide > 4:
        far = [jnp.concatenate(far, axis=0)]
    per = len(far)
    slots = far[0].shape[0]
    far_line = list(far)
    for j in range(1, n_narrow):
        far_line += [swap(value, "narrow", j) for value in far]
    far_all = list(far_line)
    for c in range(1, n_pair):
        far_all += [swap(value, "pair", c) for value in far_line]

    near_rows = n_narrow * n_pair * tokens
    near_out = call(
        functools.partial(near_kernel, n_narrow, n_pair),
        "near",
        near_all + list(shared) + list(routed),
        [VSPEC] * (n_narrow * n_pair + 6),
        [block(n_narrow, tokens)] * n_pair,
        [VMEM((near_rows * tall, LANES), F32), VMEM((near_rows, features), BF16)],
        flops=12 * near_rows * features * hidden,
        moved=12 * features * hidden,
        limit=limit,
    )

    far_rows = n_narrow * n_pair * per * slots
    pass_rows = far_rows if far_rows <= MAX_ROWS else per * slots
    pass_rows = -(-pass_rows // 16) * 16
    far_out = call(
        functools.partial(far_kernel, n_narrow, n_pair, per),
        "far",
        far_all + list(routed),
        [VSPEC] * (n_narrow * n_pair * per + 3),
        [block(n_narrow, slots)] * (n_pair * per),
        [VMEM((pass_rows * tall, LANES), F32), VMEM((pass_rows, features), BF16)],
        flops=6 * far_rows * features * hidden,
        moved=6 * features * hidden,
        limit=limit,
    )

    def reduce_pair(parts, rows):
        parts = [parts[0]] + [swap(parts[c], "pair", c) for c in range(1, n_pair)]
        parts = call(
            functools.partial(pair_sum_kernel, n_pair),
            "pair_sum",
            parts,
            [VSPEC] * n_pair,
            [block(rows)] * n_narrow,
            [],
            limit=limit,
        )
        return [parts[0]] + [swap(parts[j], "narrow", j) for j in range(1, n_narrow)]

    near_back = reduce_pair(near_out, tokens)
    far_back = []
    for k in range(per):
        far_back += call(
            functools.partial(narrow_sum_kernel, n_narrow),
            "narrow_sum",
            reduce_pair(far_out[k::per], slots),
            [VSPEC] * n_narrow,
            [block(CAP)] * (slots // CAP),
            [],
            limit=limit,
        )
    far_back = [swap(value, "wide", k) for k, value in zip(order, far_back)]
    return call(
        functools.partial(combine_kernel, n_narrow, order),
        "combine",
        [route, gains] + near_back + far_back,
        [SSPEC] * 2 + [VSPEC] * (n_narrow + n_wide - 1),
        jax.ShapeDtypeStruct((tokens, features), BF16),
        [
            VMEM((tokens * tall, LANES), F32),
            VMEM((n_wide * CAP, tall, LANES), F32),
        ],
    )


def solution(mesh):
    rows = P(("groups", "wide", "narrow", "pair"), None)
    return jax.shard_map(
        shards,
        mesh=mesh,
        in_specs=(
            rows,
            rows,
            rows,
            rows,
            P(),
            P("wide", None, ("narrow", "pair")),
            P("wide", None, ("narrow", "pair")),
            P("wide", ("narrow", "pair"), None),
            P(None, ("narrow", "pair")),
            P(None, ("narrow", "pair")),
            P(("narrow", "pair"), None),
        ),
        out_specs=rows,
        check_vma=False,
    )
```

time: 65.3 us -> 59 us (0.904)
  Pallas kernels: 18.5 us -> 9.53 us
  local copies, waits for them, and re-layouts: 7.9 us -> 13.1 us
  waiting for transfers between devices: 20.2 us -> 15.7 us
  starting transfers between devices: 18.3 us -> 20.2 us
    pallas_call x7 -> x13, Pallas kernels: 18.5 us -> 9.53 us  [call(): pl.pallas_call(kernel, out_shape=outs, in_specs=specs, out_specs=jax.tree...]
    unnamed x26 -> x22, local copies, waits for them, and re-layouts: 7.9 us -> 13.1 us
    ppermute x22 -> x26, waiting for transfers between devices: 20.2 us -> 15.7 us  [swap(): return lax.ppermute(value, axis, [(i, i ^ offset) for i in range(size)])]
    ppermute x22 -> x26, starting transfers between devices: 18.3 us -> 20.2 us  [swap(): return lax.ppermute(value, axis, [(i, i ^ offset) for i in range(size)])]
  transfers between devices with their start and end apart: 22 -> 26, of which waited for: 8 -> 10; matrix products, arithmetic and copies ran while one was open for 0% -> 0% of each run, Pallas kernels for 17% -> 13%
where the time goes in v2:
time: 59 us; the launch traced here: 58.7 us
  starting transfers between devices  20.2 us (34%)
  waiting for transfers between devices  15.7 us (27%)
  local copies, waits for them, and re-layouts  13.1 us (22%)
  Pallas kernels  9.53 us (16%)
    ppermute x26, starting transfers between devices, swap(): return lax.ppermute(value, axis, [(i, i ^ offset) for i in range(size)])  20.2 us
    ppermute x26, waiting for transfers between devices, swap(): return lax.ppermute(value, axis, [(i, i ^ offset) for i in range(size)])  15.7 us
    unnamed x22, local copies, waits for them, and re-layouts  13.1 us
    pallas_call x13, Pallas kernels, call(): pl.pallas_call(kernel, out_shape=outs, in_specs=specs, out_specs=jax.tree...  9.53 us
  transfers between devices with their start and end apart: 26, of which 10 were waited for; matrix products, arithmetic and copies ran while one was open for 0% of the time, Pallas kernels for 13%

profile of v2, /device:TPU:0, one launch (start us, length us, event | category | flops | bytes accessed | tf_op | source)
XLA Modules:
  0.0 58.7 jit_solution(17489211045319853331)
XLA Ops:
  0.0 0.9 %copy-done.6 = bf16[8,7168]{1,0:T(8,128)(2,1)S(1)} copy-done((bf16[8,7168]{1,0:T(8,128)(2,1)S(1)}, bf16[8,7168]{1,0:T(8,128)(2,1)}, u32[]{:S(2)}) %copy-start.6) | copy-done | bytes 114712
  0.9 0.7 %copy-done.7 = bf16[8,56]{1,0:T(8,128)(2,1)S(1)} copy-done((bf16[8,56]{1,0:T(8,128)(2,1)S(1)}, bf16[8,56]{1,0:T(8,128)(2,1)}, u32[]{:S(2)}) %copy-start.7) | copy-done | bytes 920
  1.6 0.7 %copy-done.8 = s32[8,2]{0,1:T(2,128)S(1)} copy-done((s32[8,2]{0,1:T(2,128)S(1)}, s32[8,2]{0,1:T(2,128)}, u32[]{:S(2)}) %copy-start.8) | copy-done | bytes 88
  3.6 1.0 %dispatch.1 = (bf16[9,56,128]{2,1,0:T(8,128)(2,1)S(1)}, bf16[5,56,128]{2,1,0:T(8,128)(2,1)S(1)}, bf16[5,56,128]{2,1,0:T(8,128)(2,1)S(1)}, bf16[5,56,128]{2,1,0:T...) custom-call(s32[2,8]{1,0:T(2,128)S(1)} %bitcast.8, s32[4]{0:T(128)S(1)} %copy-done.10, f32[2,8]{1,0:T(2,128)S(1)} %bitcast.9, ...), custom_call_target="tpu_custom_call" | custom-call | tf_op jit(solution)/shard_map/dispatch/pallas_call | solution.py:237
  4.6 3.0 %collective-permute-start = (bf16[9,56,128]{2,1,0:T(8,128)(2,1)S(1)}, bf16[9,56,128]{2,1,0:T(8,128)(2,1)S(1)}, u32[]{:S(2)}, u32[]{:S(2)}) collective-permute-start(bf16[9,56,128]{2,1,0:T(8,128)(2,1)S(1)} %get-tuple-element.35.refs_3_.refs_0_), channel_id=1, source_target_pairs={{0,2},{2,0},{1,3},{3,1},{4,6},{6,4},{5,7},{7,5},{8,10},{10,8},{9,1... | collective-permute-start | bytes 387080 | tf_op jit(solution)/shard_map/ppermute | solution.py:233
  7.6 3.6 %collective-permute-start.5 = (bf16[5,56,128]{2,1,0:T(8,128)(2,1)S(1)}, bf16[5,56,128]{2,1,0:T(8,128)(2,1)S(1)}, u32[]{:S(2)}, u32[]{:S(2)}) collective-permute-start(bf16[5,56,128]{2,1,0:T(8,128)(2,1)S(1)} %get-tuple-element.46), channel_id=1, source_target_pairs={{0,12},{4,8},{8,4},{12,0},{1,13},{5,9},{9,5},{13,1},{2,14},{6,10},... | collective-permute-start | bytes 215048 | tf_op jit(solution)/shard_map/ppermute | solution.py:233
  11.2 0.8 %collective-permute-start.7 = (bf16[5,56,128]{2,1,0:T(8,128)(2,1)S(1)}, bf16[5,56,128]{2,1,0:T(8,128)(2,1)S(1)}, u32[]{:S(2)}, u32[]{:S(2)}) collective-permute-start(bf16[5,56,128]{2,1,0:T(8,128)(2,1)S(1)} %get-tuple-element.48), channel_id=1, source_target_pairs={{0,4},{4,0},{8,12},{12,8},{1,5},{5,1},{9,13},{13,9},{2,6},{6,2},{1... | collective-permute-start | bytes 215048 | tf_op jit(solution)/shard_map/ppermute | solution.py:233
  12.0 2.4 %collective-permute-done.5.refs_0_ = bf16[5,56,128]{2,1,0:T(8,128)(2,1)S(1)} collective-permute-done((bf16[5,56,128]{2,1,0:T(8,128)(2,1)S(1)}, bf16[5,56,128]{2,1,0:T(8,128)(2,1)S(1)}, u32[]{:S(2)}, u32[]{:S(2)}) %collective-permute-start.5) | collective-permute-done | bytes 71712 | tf_op jit(solution)/shard_map/ppermute | solution.py:233
  14.4 3.4 %collective-permute-done.6.refs_1_ = bf16[5,56,128]{2,1,0:T(8,128)(2,1)S(1)} collective-permute-done((bf16[5,56,128]{2,1,0:T(8,128)(2,1)S(1)}, bf16[5,56,128]{2,1,0:T(8,128)(2,1)S(1)}, u32[]{:S(2)}, u32[]{:S(2)}) %collective-permute-start.6) | collective-permute-done | bytes 71712 | tf_op jit(solution)/shard_map/ppermute | solution.py:233
  18.4 1.5 %collective-permute-start.9 = (bf16[5,56,128]{2,1,0:T(8,128)(2,1)S(1)}, bf16[5,56,128]{2,1,0:T(8,128)(2,1)S(1)}, u32[]{:S(2)}, u32[]{:S(2)}) collective-permute-start(bf16[5,56,128]{2,1,0:T(8,128)(2,1)S(1)} %collective-permute-done.6.refs_1_), channel_id=1, source_target_pairs={{0,2},{2,0},{1,3},{3,1},{4,6},{6,4},{5,7},{7,5},{8,10},{10,8},{9,1... | collective-permute-start | bytes 215048 | tf_op jit(solution)/shard_map/ppermute | solution.py:233
  20.4 2.6 %collective-permute-done.8.refs_3_ = bf16[5,56,128]{2,1,0:T(8,128)(2,1)S(1)} collective-permute-done((bf16[5,56,128]{2,1,0:T(8,128)(2,1)S(1)}, bf16[5,56,128]{2,1,0:T(8,128)(2,1)S(1)}, u32[]{:S(2)}, u32[]{:S(2)}) %collective-permute-start.8) | collective-permute-done | bytes 71712 | tf_op jit(solution)/shard_map/ppermute | solution.py:233
  23.0 1.0 %collective-permute-done.9.refs_4_ = bf16[5,56,128]{2,1,0:T(8,128)(2,1)S(1)} collective-permute-done((bf16[5,56,128]{2,1,0:T(8,128)(2,1)S(1)}, bf16[5,56,128]{2,1,0:T(8,128)(2,1)S(1)}, u32[]{:S(2)}, u32[]{:S(2)}) %collective-permute-start.9) | collective-permute-done | bytes 71712 | tf_op jit(solution)/shard_map/ppermute | solution.py:233
  24.0 0.8 %collective-permute-done.10.refs_5_ = bf16[5,56,128]{2,1,0:T(8,128)(2,1)S(1)} collective-permute-done((bf16[5,56,128]{2,1,0:T(8,128)(2,1)S(1)}, bf16[5,56,128]{2,1,0:T(8,128)(2,1)S(1)}, u32[]{:S(2)}, u32[]{:S(2)}) %collective-permute-start.10) | collective-permute-done | bytes 71712 | tf_op jit(solution)/shard_map/ppermute | solution.py:233
  25.3 2.0 %copy-done = bf16[1,7168,256]{2,1,0:T(8,128)(2,1)S(1)} copy-done((bf16[1,7168,256]{2,1,0:T(8,128)(2,1)S(1)}, bf16[1,7168,256]{2,1,0:T(8,128)(2,1)}, u32[]{:S(2)}) %copy-start) | copy-done | bytes 3670040
  27.3 2.0 %copy-done.1 = bf16[1,7168,256]{2,1,0:T(8,128)(2,1)S(1)} copy-done((bf16[1,7168,256]{2,1,0:T(8,128)(2,1)S(1)}, bf16[1,7168,256]{2,1,0:T(8,128)(2,1)}, u32[]{:S(2)}) %copy-start.1) | copy-done | bytes 3670040
  29.3 2.0 %copy-done.2 = bf16[1,256,7168]{2,1,0:T(8,128)(2,1)S(1)} copy-done((bf16[1,256,7168]{2,1,0:T(8,128)(2,1)S(1)}, bf16[1,256,7168]{2,1,0:T(8,128)(2,1)}, u32[]{:S(2)}) %copy-start.2) | copy-done | bytes 3670040
  31.4 0.8 %load_routed.1 = (bf16[7168,256]{1,0:T(8,128)(2,1)S(1)}, bf16[7168,256]{1,0:T(8,128)(2,1)S(1)}, bf16[256,7168]{1,0:T(8,128)(2,1)S(1)}) custom-call(bf16[7168,256]{1,0:T(8,128)(2,1)S(1)} %bitcast.5, bf16[7168,256]{1,0:T(8,128)(2,1)S(1)} %bitcast.6, bf16[256,7168]{1,0:T(8,128)(2,1)S(1)} %bitcast.7, bf16[9,56,128]{2,1,0:T(8,128)(2,1)S(1)} %get-tuple-element.35.refs_3_.refs_0_), custom_call_target="tpu_custom_call" | custom-call | bytes 11010048 | tf_op jit(solution)/shard_map/load_routed/pallas_call | solution.py:237
  32.2 1.3 %copy-done.3 = bf16[7168,256]{1,0:T(8,128)(2,1)S(1)} copy-done((bf16[7168,256]{1,0:T(8,128)(2,1)S(1)}, bf16[7168,256]{1,0:T(8,128)(2,1)}, u32[]{:S(2)}) %copy-start.3) | copy-done | bytes 3670040
  33.4 1.1 %copy-done.4 = bf16[7168,256]{1,0:T(8,128)(2,1)S(1)} copy-done((bf16[7168,256]{1,0:T(8,128)(2,1)S(1)}, bf16[7168,256]{1,0:T(8,128)(2,1)}, u32[]{:S(2)}) %copy-start.4) | copy-done | bytes 3670040
  34.5 1.0 %copy-done.5 = bf16[256,7168]{1,0:T(8,128)(2,1)S(1)} copy-done((bf16[256,7168]{1,0:T(8,128)(2,1)S(1)}, bf16[256,7168]{1,0:T(8,128)(2,1)}, u32[]{:S(2)}) %copy-start.5) | copy-done | bytes 3670040
  35.6 0.8 %load_shared.1 = (bf16[7168,256]{1,0:T(8,128)(2,1)S(1)}, bf16[7168,256]{1,0:T(8,128)(2,1)S(1)}, bf16[256,7168]{1,0:T(8,128)(2,1)S(1)}) custom-call(bf16[7168,256]{1,0:T(8,128)(2,1)S(1)} %copy-done.3, bf16[7168,256]{1,0:T(8,128)(2,1)S(1)} %copy-done.4, bf16[256,7168]{1,0:T(8,128)(2,1)S(1)} %copy-done.5, bf16[9,56,128]{2,1,0:T(8,128)(2,1)S(1)} %get-tuple-element.35.refs_3_.refs_0_), custom_call_target="tpu_custom_call" | custom-call | bytes 11010048 | tf_op jit(solution)/shard_map/load_shared/pallas_call | solution.py:237
  36.4 3.8 %near.1 = (bf16[2,8,56,128]{3,2,1,0:T(8,128)(2,1)S(1)}, bf16[2,8,56,128]{3,2,1,0:T(8,128)(2,1)S(1)}) custom-call(bf16[9,56,128]{2,1,0:T(8,128)(2,1)S(1)} %get-tuple-element.35.refs_3_.refs_0_, bf16[9,56,128]{2,1,0:T(8,128)(2,1)S(1)} %collective-permute-done.refs_1_, bf16[9,56,128]{2,1,0:T(8,128)(2,1)S(1)} %collective-permute-done.1.refs_2_, ...), custom_call_target="tpu_custom_call" | custom-call | flops 704643072 | bytes 22020096 | tf_op jit(solution)/shard_map/near/pallas_call | solution.py:237
  40.3 2.2 %far.1 = (bf16[2,5,56,128]{3,2,1,0:T(8,128)(2,1)S(1)}, bf16[2,5,56,128]{3,2,1,0:T(8,128)(2,1)S(1)}, bf16[2,5,56,128]{3,2,1,0:T(8,128)(2,1)S(1)}, bf16[2,5,56,128...) custom-call(bf16[5,56,128]{2,1,0:T(8,128)(2,1)S(1)} %collective-permute-done.5.refs_0_, ...), custom_call_target="tpu_custom_call" | custom-call | flops 660602880 | bytes 11010048 | tf_op jit(solution)/shard_map/far/pallas_call | solution.py:237
  44.1 1.1 %collective-permute-start.18 = (bf16[5,56,128]{2,1,0:T(8,128)(2,1)S(1)}, bf16[5,56,128]{2,1,0:T(8,128)(2,1)S(1)}, u32[]{:S(2)}, u32[]{:S(2)}) collective-permute-start(bf16[5,56,128]{2,1,0:T(8,128)(2,1)S(1)} %get-tuple-element.52), channel_id=1, source_target_pairs={{0,2},{2,0},{1,3},{3,1},{4,6},{6,4},{5,7},{7,5},{8,10},{10,8},{9,1... | collective-permute-start | bytes 215048 | tf_op jit(solution)/shard_map/ppermute | solution.py:233
  45.2 1.1 %collective-permute-start.21 = (bf16[5,56,128]{2,1,0:T(8,128)(2,1)S(1)}, bf16[5,56,128]{2,1,0:T(8,128)(2,1)S(1)}, u32[]{:S(2)}, u32[]{:S(2)}) collective-permute-start(bf16[5,56,128]{2,1,0:T(8,128)(2,1)S(1)} %get-tuple-element.56), channel_id=1, source_target_pairs={{0,2},{2,0},{1,3},{3,1},{4,6},{6,4},{5,7},{7,5},{8,10},{10,8},{9,1... | collective-permute-start | bytes 215048 | tf_op jit(solution)/shard_map/ppermute | solution.py:233
  46.4 1.0 %collective-permute-start.24 = (bf16[5,56,128]{2,1,0:T(8,128)(2,1)S(1)}, bf16[5,56,128]{2,1,0:T(8,128)(2,1)S(1)}, u32[]{:S(2)}, u32[]{:S(2)}) collective-permute-start(bf16[5,56,128]{2,1,0:T(8,128)(2,1)S(1)} %get-tuple-element.60), channel_id=1, source_target_pairs={{0,2},{2,0},{1,3},{3,1},{4,6},{6,4},{5,7},{7,5},{8,10},{10,8},{9,1... | collective-permute-start | bytes 215048 | tf_op jit(solution)/shard_map/ppermute | solution.py:233
  47.5 1.1 %collective-permute-start.4 = (bf16[8,56,128]{2,1,0:T(8,128)(2,1)S(1)}, bf16[8,56,128]{2,1,0:T(8,128)(2,1)S(1)}, u32[]{:S(2)}, u32[]{:S(2)}) collective-permute-start(bf16[8,56,128]{2,1,0:T(8,128)(2,1)S(1)} %get-tuple-element.45), channel_id=1, source_target_pairs={{0,2},{2,0},{1,3},{3,1},{4,6},{6,4},{5,7},{7,5},{8,10},{10,8},{9,1... | collective-permute-start | bytes 344072 | tf_op jit(solution)/shard_map/ppermute | solution.py:233
  49.3 2.5 %collective-permute-start.19 = (bf16[5,56,128]{2,1,0:T(8,128)(2,1)S(1)}, bf16[5,56,128]{2,1,0:T(8,128)(2,1)S(1)}, u32[]{:S(2)}, u32[]{:S(2)}) collective-permute-start(bf16[5,56,128]{2,1,0:T(8,128)(2,1)S(1)} %narrow_sum.3), channel_id=1, source_target_pairs={{0,12},{4,8},{8,4},{12,0},{1,13},{5,9},{9,5},{13,1},{2,14},{6,10},... | collective-permute-start | bytes 215048 | tf_op jit(solution)/shard_map/ppermute | solution.py:233
  52.3 1.7 %collective-permute-start.25 = (bf16[5,56,128]{2,1,0:T(8,128)(2,1)S(1)}, bf16[5,56,128]{2,1,0:T(8,128)(2,1)S(1)}, u32[]{:S(2)}, u32[]{:S(2)}) collective-permute-start(bf16[5,56,128]{2,1,0:T(8,128)(2,1)S(1)} %narrow_sum.5), channel_id=1, source_target_pairs={{0,4},{4,0},{8,12},{12,8},{1,5},{5,1},{9,13},{13,9},{2,6},{6,2},{1... | collective-permute-start | bytes 215048 | tf_op jit(solution)/shard_map/ppermute | solution.py:233
  54.0 1.6 %collective-permute-done.19.refs_2_ = bf16[5,56,128]{2,1,0:T(8,128)(2,1)S(1)} collective-permute-done((bf16[5,56,128]{2,1,0:T(8,128)(2,1)S(1)}, bf16[5,56,128]{2,1,0:T(8,128)(2,1)S(1)}, u32[]{:S(2)}, u32[]{:S(2)}) %collective-permute-start.19) | collective-permute-done | bytes 71712 | tf_op jit(solution)/shard_map/ppermute | solution.py:233
  55.7 2.3 %collective-permute-done.22.refs_3_ = bf16[5,56,128]{2,1,0:T(8,128)(2,1)S(1)} collective-permute-done((bf16[5,56,128]{2,1,0:T(8,128)(2,1)S(1)}, bf16[5,56,128]{2,1,0:T(8,128)(2,1)S(1)}, u32[]{:S(2)}, u32[]{:S(2)}) %collective-permute-start.22) | collective-permute-done | bytes 71712 | tf_op jit(solution)/shard_map/ppermute | solution.py:233
  57.9 0.8 %combine.1 = bf16[8,7168]{1,0:T(8,128)(2,1)} custom-call(s32[2,8]{1,0:T(2,128)S(4)} %get-tuple-element.33.route, f32[2,8]{1,0:T(2,128)S(4)} %get-tuple-element.34.gains, bf16[8,56,128]{2,1,0:T(8,128)(2,1)S(1)} %get-tuple-element.44.refs_0_, bf16[8,56,128]{2,1,0:T(8,128)(2,1)S(1)} %collective-permute-done.4.refs_1_, ...), custom_call_target="tpu_custom_call" | custom-call | tf_op jit(solution)/shard_map/combine/pallas_call | solution.py:237
  (55 shorter events, 5.9 us)
Async XLA Ops:
  4.6 7.4 %collective-permute-start = (bf16[9,56,128]{2,1,0:T(8,128)(2,1)S(1)}, bf16[9,56,128]{2,1,0:T(8,128)(2,1)S(1)}, u32[]{:S(2)}, u32[]{:S(2)}) collective-permute-start(bf16[9,56,128]{2,1,0:T(8,128)(2,1)S(1)} %get-tuple-element.35.refs_3_.refs_0_), channel_id=1, source_target_pairs={{0,2},{2,0},{1,3},{3,1},{4,6},{6,4},{5,7},{7,5},{8,10},{10,8},{9,1... | collective-permute-start | bytes 387080 | tf_op jit(solution)/shard_map/ppermute | solution.py:233
  7.6 12.3 %collective-permute-start.1 = (bf16[9,56,128]{2,1,0:T(8,128)(2,1)S(1)}, bf16[9,56,128]{2,1,0:T(8,128)(2,1)S(1)}, u32[]{:S(2)}, u32[]{:S(2)}) collective-permute-start(bf16[9,56,128]{2,1,0:T(8,128)(2,1)S(1)} %get-tuple-element.35.refs_3_.refs_0_), channel_id=1, source_target_pairs={{0,1},{1,0},{2,3},{3,2},{4,5},{5,4},{6,7},{7,6},{8,9},{9,8},{10,11... | collective-permute-start | bytes 387080 | tf_op jit(solution)/shard_map/ppermute | solution.py:233
  7.6 6.8 %collective-permute-start.5 = (bf16[5,56,128]{2,1,0:T(8,128)(2,1)S(1)}, bf16[5,56,128]{2,1,0:T(8,128)(2,1)S(1)}, u32[]{:S(2)}, u32[]{:S(2)}) collective-permute-start(bf16[5,56,128]{2,1,0:T(8,128)(2,1)S(1)} %get-tuple-element.46), channel_id=1, source_target_pairs={{0,12},{4,8},{8,4},{12,0},{1,13},{5,9},{9,5},{13,1},{2,14},{6,10},... | collective-permute-start | bytes 215048 | tf_op jit(solution)/shard_map/ppermute | solution.py:233
  11.2 6.7 %collective-permute-start.6 = (bf16[5,56,128]{2,1,0:T(8,128)(2,1)S(1)}, bf16[5,56,128]{2,1,0:T(8,128)(2,1)S(1)}, u32[]{:S(2)}, u32[]{:S(2)}) collective-permute-start(bf16[5,56,128]{2,1,0:T(8,128)(2,1)S(1)} %get-tuple-element.47), channel_id=1, source_target_pairs={{0,8},{4,12},{8,0},{12,4},{1,9},{5,13},{9,1},{13,5},{2,10},{6,14},... | collective-permute-start | bytes 215048 | tf_op jit(solution)/shard_map/ppermute | solution.py:233
  11.2 7.2 %collective-permute-start.7 = (bf16[5,56,128]{2,1,0:T(8,128)(2,1)S(1)}, bf16[5,56,128]{2,1,0:T(8,128)(2,1)S(1)}, u32[]{:S(2)}, u32[]{:S(2)}) collective-permute-start(bf16[5,56,128]{2,1,0:T(8,128)(2,1)S(1)} %get-tuple-element.48), channel_id=1, source_target_pairs={{0,4},{4,0},{8,12},{12,8},{1,5},{5,1},{9,13},{13,9},{2,6},{6,2},{1... | collective-permute-start | bytes 215048 | tf_op jit(solution)/shard_map/ppermute | solution.py:233
  12.0 12.8 %collective-permute-start.2 = (bf16[9,56,128]{2,1,0:T(8,128)(2,1)S(1)}, bf16[9,56,128]{2,1,0:T(8,128)(2,1)S(1)}, u32[]{:S(2)}, u32[]{:S(2)}) collective-permute-start(bf16[9,56,128]{2,1,0:T(8,128)(2,1)S(1)} %collective-permute-done.refs_1_), channel_id=1, source_target_pairs={{0,1},{1,0},{2,3},{3,2},{4,5},{5,4},{6,7},{7,6},{8,9},{9,8},{10,11... | collective-permute-start | bytes 387080 | tf_op jit(solution)/shard_map/ppermute | solution.py:233
  14.4 6.0 %collective-permute-start.11 = (bf16[5,56,128]{2,1,0:T(8,128)(2,1)S(1)}, bf16[5,56,128]{2,1,0:T(8,128)(2,1)S(1)}, u32[]{:S(2)}, u32[]{:S(2)}) collective-permute-start(bf16[5,56,128]{2,1,0:T(8,128)(2,1)S(1)} %collective-permute-done.5.refs_0_), channel_id=1, source_target_pairs={{0,1},{1,0},{2,3},{3,2},{4,5},{5,4},{6,7},{7,6},{8,9},{9,8},{10,11... | collective-permute-start | bytes 215048 | tf_op jit(solution)/shard_map/ppermute | solution.py:233
  17.8 5.1 %collective-permute-start.8 = (bf16[5,56,128]{2,1,0:T(8,128)(2,1)S(1)}, bf16[5,56,128]{2,1,0:T(8,128)(2,1)S(1)}, u32[]{:S(2)}, u32[]{:S(2)}) collective-permute-start(bf16[5,56,128]{2,1,0:T(8,128)(2,1)S(1)} %collective-permute-done.5.refs_0_), channel_id=1, source_target_pairs={{0,2},{2,0},{1,3},{3,1},{4,6},{6,4},{5,7},{7,5},{8,10},{10,8},{9,1... | collective-permute-start | bytes 215048 | tf_op jit(solution)/shard_map/ppermute | solution.py:233
  18.4 5.6 %collective-permute-start.9 = (bf16[5,56,128]{2,1,0:T(8,128)(2,1)S(1)}, bf16[5,56,128]{2,1,0:T(8,128)(2,1)S(1)}, u32[]{:S(2)}, u32[]{:S(2)}) collective-permute-start(bf16[5,56,128]{2,1,0:T(8,128)(2,1)S(1)} %collective-permute-done.6.refs_1_), channel_id=1, source_target_pairs={{0,2},{2,0},{1,3},{3,1},{4,6},{6,4},{5,7},{7,5},{8,10},{10,8},{9,1... | collective-permute-start | bytes 215048 | tf_op jit(solution)/shard_map/ppermute | solution.py:233
  19.9 4.9 %collective-permute-start.10 = (bf16[5,56,128]{2,1,0:T(8,128)(2,1)S(1)}, bf16[5,56,128]{2,1,0:T(8,128)(2,1)S(1)}, u32[]{:S(2)}, u32[]{:S(2)}) collective-permute-start(bf16[5,56,128]{2,1,0:T(8,128)(2,1)S(1)} %collective-permute-done.7.refs_2_), channel_id=1, source_target_pairs={{0,2},{2,0},{1,3},{3,1},{4,6},{6,4},{5,7},{7,5},{8,10},{10,8},{9,1... | collective-permute-start | bytes 215048 | tf_op jit(solution)/shard_map/ppermute | solution.py:233
  20.4 19.8 %collective-permute-start.12 = (bf16[5,56,128]{2,1,0:T(8,128)(2,1)S(1)}, bf16[5,56,128]{2,1,0:T(8,128)(2,1)S(1)}, u32[]{:S(2)}, u32[]{:S(2)}) collective-permute-start(bf16[5,56,128]{2,1,0:T(8,128)(2,1)S(1)} %collective-permute-done.6.refs_1_), channel_id=1, source_target_pairs={{0,1},{1,0},{2,3},{3,2},{4,5},{5,4},{6,7},{7,6},{8,9},{9,8},{10,11... | collective-permute-start | bytes 215048 | tf_op jit(solution)/shard_map/ppermute | solution.py:233
  23.0 17.3 %collective-permute-start.13 = (bf16[5,56,128]{2,1,0:T(8,128)(2,1)S(1)}, bf16[5,56,128]{2,1,0:T(8,128)(2,1)S(1)}, u32[]{:S(2)}, u32[]{:S(2)}) collective-permute-start(bf16[5,56,128]{2,1,0:T(8,128)(2,1)S(1)} %collective-permute-done.7.refs_2_), channel_id=1, source_target_pairs={{0,1},{1,0},{2,3},{3,2},{4,5},{5,4},{6,7},{7,6},{8,9},{9,8},{10,11... | collective-permute-start | bytes 215048 | tf_op jit(solution)/shard_map/ppermute | solution.py:233
  24.0 16.3 %collective-permute-start.14 = (bf16[5,56,128]{2,1,0:T(8,128)(2,1)S(1)}, bf16[5,56,128]{2,1,0:T(8,128)(2,1)S(1)}, u32[]{:S(2)}, u32[]{:S(2)}) collective-permute-start(bf16[5,56,128]{2,1,0:T(8,128)(2,1)S(1)} %collective-permute-done.8.refs_3_), channel_id=1, source_target_pairs={{0,1},{1,0},{2,3},{3,2},{4,5},{5,4},{6,7},{7,6},{8,9},{9,8},{10,11... | collective-permute-start | bytes 215048 | tf_op jit(solution)/shard_map/ppermute | solution.py:233
  24.8 15.5 %collective-permute-start.15 = (bf16[5,56,128]{2,1,0:T(8,128)(2,1)S(1)}, bf16[5,56,128]{2,1,0:T(8,128)(2,1)S(1)}, u32[]{:S(2)}, u32[]{:S(2)}) collective-permute-start(bf16[5,56,128]{2,1,0:T(8,128)(2,1)S(1)} %collective-permute-done.9.refs_4_), channel_id=1, source_target_pairs={{0,1},{1,0},{2,3},{3,2},{4,5},{5,4},{6,7},{7,6},{8,9},{9,8},{10,11... | collective-permute-start | bytes 215048 | tf_op jit(solution)/shard_map/ppermute | solution.py:233
  24.8 15.5 %collective-permute-start.16 = (bf16[5,56,128]{2,1,0:T(8,128)(2,1)S(1)}, bf16[5,56,128]{2,1,0:T(8,128)(2,1)S(1)}, u32[]{:S(2)}, u32[]{:S(2)}) collective-permute-start(bf16[5,56,128]{2,1,0:T(8,128)(2,1)S(1)} %collective-permute-done.10.refs_5_), channel_id=1, source_target_pairs={{0,1},{1,0},{2,3},{3,2},{4,5},{5,4},{6,7},{7,6},{8,9},{9,8},{10,11... | collective-permute-start | bytes 215048 | tf_op jit(solution)/shard_map/ppermute | solution.py:233
  25.3 2.0 %copy-start = (bf16[1,7168,256]{2,1,0:T(8,128)(2,1)S(1)}, bf16[1,7168,256]{2,1,0:T(8,128)(2,1)}, u32[]{:S(2)}) copy-start(bf16[1,7168,256]{2,1,0:T(8,128)(2,1)} %param.16) | copy-start | bytes 11010052
  27.3 2.0 %copy-start.1 = (bf16[1,7168,256]{2,1,0:T(8,128)(2,1)S(1)}, bf16[1,7168,256]{2,1,0:T(8,128)(2,1)}, u32[]{:S(2)}) copy-start(bf16[1,7168,256]{2,1,0:T(8,128)(2,1)} %param.17) | copy-start | bytes 11010052
  29.3 2.0 %copy-start.2 = (bf16[1,256,7168]{2,1,0:T(8,128)(2,1)S(1)}, bf16[1,256,7168]{2,1,0:T(8,128)(2,1)}, u32[]{:S(2)}) copy-start(bf16[1,256,7168]{2,1,0:T(8,128)(2,1)} %param.18) | copy-start | bytes 11010052
  31.4 2.0 %copy-start.3 = (bf16[7168,256]{1,0:T(8,128)(2,1)S(1)}, bf16[7168,256]{1,0:T(8,128)(2,1)}, u32[]{:S(2)}) copy-start(bf16[7168,256]{1,0:T(8,128)(2,1)} %refs_0_.1) | copy-start | bytes 11010052
  31.4 3.2 %copy-start.4 = (bf16[7168,256]{1,0:T(8,128)(2,1)S(1)}, bf16[7168,256]{1,0:T(8,128)(2,1)}, u32[]{:S(2)}) copy-start(bf16[7168,256]{1,0:T(8,128)(2,1)} %refs_1_.1) | copy-start | bytes 11010052
  31.4 4.2 %copy-start.5 = (bf16[256,7168]{1,0:T(8,128)(2,1)S(1)}, bf16[256,7168]{1,0:T(8,128)(2,1)}, u32[]{:S(2)}) copy-start(bf16[256,7168]{1,0:T(8,128)(2,1)} %refs_2_.1) | copy-start | bytes 11010052
  40.2 7.3 %collective-permute-start.3 = (bf16[2,8,56,128]{3,2,1,0:T(8,128)(2,1)S(1)}, bf16[2,8,56,128]{3,2,1,0:T(8,128)(2,1)S(1)}, u32[]{:S(2)}, u32[]{:S(2)}) collective-permute-start(bf16[2,8,56,128]{3,2,1,0:T(8,128)(2,1)S(1)} %get-tuple-element.43), channel_id=1, source_target_pairs={{0,1},{1,0},{2,3},{3,2},{4,5},{5,4},{6,7},{7,6},{8,9},{9,8},{10,11... | collective-permute-start | bytes 688136 | tf_op jit(solution)/shard_map/ppermute | solution.py:233
  42.5 1.5 %collective-permute-start.17 = (bf16[2,5,56,128]{3,2,1,0:T(8,128)(2,1)S(1)}, bf16[2,5,56,128]{3,2,1,0:T(8,128)(2,1)S(1)}, u32[]{:S(2)}, u32[]{:S(2)}) collective-permute-start(bf16[2,5,56,128]{3,2,1,0:T(8,128)(2,1)S(1)} %get-tuple-element.50), channel_id=1, source_target_pairs={{0,1},{1,0},{2,3},{3,2},{4,5},{5,4},{6,7},{7,6},{8,9},{9,8},{10,11... | collective-permute-start | bytes 430088 | tf_op jit(solution)/shard_map/ppermute | solution.py:233
  43.1 2.1 %collective-permute-start.20 = (bf16[2,5,56,128]{3,2,1,0:T(8,128)(2,1)S(1)}, bf16[2,5,56,128]{3,2,1,0:T(8,128)(2,1)S(1)}, u32[]{:S(2)}, u32[]{:S(2)}) collective-permute-start(bf16[2,5,56,128]{3,2,1,0:T(8,128)(2,1)S(1)} %get-tuple-element.54), channel_id=1, source_target_pairs={{0,1},{1,0},{2,3},{3,2},{4,5},{5,4},{6,7},{7,6},{8,9},{9,8},{10,11... | collective-permute-start | bytes 430088 | tf_op jit(solution)/shard_map/ppermute | solution.py:233
  43.2 3.2 %collective-permute-start.23 = (bf16[2,5,56,128]{3,2,1,0:T(8,128)(2,1)S(1)}, bf16[2,5,56,128]{3,2,1,0:T(8,128)(2,1)S(1)}, u32[]{:S(2)}, u32[]{:S(2)}) collective-permute-start(bf16[2,5,56,128]{3,2,1,0:T(8,128)(2,1)S(1)} %get-tuple-element.58), channel_id=1, source_target_pairs={{0,1},{1,0},{2,3},{3,2},{4,5},{5,4},{6,7},{7,6},{8,9},{9,8},{10,11... | collective-permute-start | bytes 430088 | tf_op jit(solution)/shard_map/ppermute | solution.py:233
  44.1 5.1 %collective-permute-start.18 = (bf16[5,56,128]{2,1,0:T(8,128)(2,1)S(1)}, bf16[5,56,128]{2,1,0:T(8,128)(2,1)S(1)}, u32[]{:S(2)}, u32[]{:S(2)}) collective-permute-start(bf16[5,56,128]{2,1,0:T(8,128)(2,1)S(1)} %get-tuple-element.52), channel_id=1, source_target_pairs={{0,2},{2,0},{1,3},{3,1},{4,6},{6,4},{5,7},{7,5},{8,10},{10,8},{9,1... | collective-permute-start | bytes 215048 | tf_op jit(solution)/shard_map/ppermute | solution.py:233
  45.2 6.6 %collective-permute-start.21 = (bf16[5,56,128]{2,1,0:T(8,128)(2,1)S(1)}, bf16[5,56,128]{2,1,0:T(8,128)(2,1)S(1)}, u32[]{:S(2)}, u32[]{:S(2)}) collective-permute-start(bf16[5,56,128]{2,1,0:T(8,128)(2,1)S(1)} %get-tuple-element.56), channel_id=1, source_target_pairs={{0,2},{2,0},{1,3},{3,1},{4,6},{6,4},{5,7},{7,5},{8,10},{10,8},{9,1... | collective-permute-start | bytes 215048 | tf_op jit(solution)/shard_map/ppermute | solution.py:233
  46.4 5.9 %collective-permute-start.24 = (bf16[5,56,128]{2,1,0:T(8,128)(2,1)S(1)}, bf16[5,56,128]{2,1,0:T(8,128)(2,1)S(1)}, u32[]{:S(2)}, u32[]{:S(2)}) collective-permute-start(bf16[5,56,128]{2,1,0:T(8,128)(2,1)S(1)} %get-tuple-element.60), channel_id=1, source_target_pairs={{0,2},{2,0},{1,3},{3,1},{4,6},{6,4},{5,7},{7,5},{8,10},{10,8},{9,1... | collective-permute-start | bytes 215048 | tf_op jit(solution)/shard_map/ppermute | solution.py:233
  47.5 10.4 %collective-permute-start.4 = (bf16[8,56,128]{2,1,0:T(8,128)(2,1)S(1)}, bf16[8,56,128]{2,1,0:T(8,128)(2,1)S(1)}, u32[]{:S(2)}, u32[]{:S(2)}) collective-permute-start(bf16[8,56,128]{2,1,0:T(8,128)(2,1)S(1)} %get-tuple-element.45), channel_id=1, source_target_pairs={{0,2},{2,0},{1,3},{3,1},{4,6},{6,4},{5,7},{7,5},{8,10},{10,8},{9,1... | collective-permute-start | bytes 344072 | tf_op jit(solution)/shard_map/ppermute | solution.py:233
  49.3 6.4 %collective-permute-start.19 = (bf16[5,56,128]{2,1,0:T(8,128)(2,1)S(1)}, bf16[5,56,128]{2,1,0:T(8,128)(2,1)S(1)}, u32[]{:S(2)}, u32[]{:S(2)}) collective-permute-start(bf16[5,56,128]{2,1,0:T(8,128)(2,1)S(1)} %narrow_sum.3), channel_id=1, source_target_pairs={{0,12},{4,8},{8,4},{12,0},{1,13},{5,9},{9,5},{13,1},{2,14},{6,10},... | collective-permute-start | bytes 215048 | tf_op jit(solution)/shard_map/ppermute | solution.py:233
  51.8 6.1 %collective-permute-start.22 = (bf16[5,56,128]{2,1,0:T(8,128)(2,1)S(1)}, bf16[5,56,128]{2,1,0:T(8,128)(2,1)S(1)}, u32[]{:S(2)}, u32[]{:S(2)}) collective-permute-start(bf16[5,56,128]{2,1,0:T(8,128)(2,1)S(1)} %narrow_sum.4), channel_id=1, source_target_pairs={{0,8},{4,12},{8,0},{12,4},{1,9},{5,13},{9,1},{13,5},{2,10},{6,14},... | collective-permute-start | bytes 215048 | tf_op jit(solution)/shard_map/ppermute | solution.py:233
  52.3 5.6 %collective-permute-start.25 = (bf16[5,56,128]{2,1,0:T(8,128)(2,1)S(1)}, bf16[5,56,128]{2,1,0:T(8,128)(2,1)S(1)}, u32[]{:S(2)}, u32[]{:S(2)}) collective-permute-start(bf16[5,56,128]{2,1,0:T(8,128)(2,1)S(1)} %narrow_sum.5), channel_id=1, source_target_pairs={{0,4},{4,0},{8,12},{12,8},{1,5},{5,1},{9,13},{13,9},{2,6},{6,2},{1... | collective-permute-start | bytes 215048 | tf_op jit(solution)/shard_map/ppermute | solution.py:233
  (5 other events, 3.6 us)

commit v3 on v2

--- a/solution.py
+++ b/solution.py
@@ -233,6 +233,14 @@
     return lax.ppermute(value, axis, [(i, i ^ offset) for i in range(size)])
 
 
+def in_hbm(*values):
+    return [pltpu.with_memory_space_constraint(value, pltpu.HBM) for value in values]
+
+
+def after(values, *others):
+    return list(lax.optimization_barrier((tuple(values), others))[0])
+
+
 def call(kernel, name, ins, specs, outs, scratch, flops=0, moved=0, limit=16):
     return pl.pallas_call(
         kernel,
@@ -277,7 +285,7 @@
     near, *far = call(
         dispatch_kernel,
         "dispatch",
-        (expert_ids.T, placement, gate_weights.T, row_codes, row_scales),
+        in_hbm(expert_ids.T, placement, gate_weights.T, row_codes, row_scales),
         [ASPEC] * 5,
         [block(tokens + 1)]
         + [block(CAP)] * (n_wide - 1)
@@ -298,11 +306,11 @@
     far = [swap(far[k - 1], "wide", k) for k in order]
     near_line = [near] + [swap(near, "narrow", j) for j in range(1, n_narrow)]
 
-    def load(name, after, *weights):
+    def load(name, first, *weights):
         return call(
             functools.partial(load_kernel, len(weights)),
             name,
-            list(weights) + [after],
+            in_hbm(*weights) + [first],
             [ASPEC] * (len(weights) + 1),
             [VMEM(value.shape, BF16) for value in weights],
             [pltpu.SemaphoreType.DMA((len(weights),))],
@@ -317,19 +325,20 @@
         w_up.reshape(features, hidden),
         w_down.reshape(hidden, features),
     )
-    near_all = list(near_line)
-    for c in range(1, n_pair):
-        near_all += [swap(value, "pair", c) for value in near_line]
     if n_wide > 4:
         far = [jnp.concatenate(far, axis=0)]
     per = len(far)
     slots = far[0].shape[0]
-    far_line = list(far)
+    far = after(far, shared[0])
+    far_side = []
     for j in range(1, n_narrow):
-        far_line += [swap(value, "narrow", j) for value in far]
-    far_all = list(far_line)
+        far_side += [swap(value, "narrow", j) for value in far]
+    far_side = after(far_side, routed[0])
+    near_line = after(near_line, *far)
+    near_all = list(near_line)
     for c in range(1, n_pair):
-        far_all += [swap(value, "pair", c) for value in far_line]
+        near_all += [swap(value, "pair", c) for value in near_line]
+    near_all = after(near_all, *far_side)
 
     near_rows = n_narrow * n_pair * tokens
     near_out = call(
@@ -343,6 +352,25 @@
         moved=12 * features * hidden,
         limit=limit,
     )
+
+    def reduce_pair(parts, rows):
+        parts = [parts[0]] + [swap(parts[c], "pair", c) for c in range(1, n_pair)]
+        parts = call(
+            functools.partial(pair_sum_kernel, n_pair),
+            "pair_sum",
+            parts,
+            [VSPEC] * n_pair,
+            [block(rows)] * n_narrow,
+            [],
+            limit=limit,
+        )
+        return [parts[0]] + [swap(parts[j], "narrow", j) for j in range(1, n_narrow)]
+
+    near_back = reduce_pair(near_out, tokens)
+    far_line = list(far) + far_side
+    far_all = list(far_line)
+    for c in range(1, n_pair):
+        far_all += [swap(value, "pair", c) for value in far_line]
 
     far_rows = n_narrow * n_pair * per * slots
     pass_rows = far_rows if far_rows <= MAX_ROWS else per * slots
@@ -359,20 +387,6 @@
         limit=limit,
     )
 
-    def reduce_pair(parts, rows):
-        parts = [parts[0]] + [swap(parts[c], "pair", c) for c in range(1, n_pair)]
-        parts = call(
-            functools.partial(pair_sum_kernel, n_pair),
-            "pair_sum",
-            parts,
-            [VSPEC] * n_pair,
-            [block(rows)] * n_narrow,
-            [],
-            limit=limit,
-        )
-        return [parts[0]] + [swap(parts[j], "narrow", j) for j in range(1, n_narrow)]
-
-    near_back = reduce_pair(near_out, tokens)
     far_back = []
     for k in range(per):
         far_back += call(

time: 59 us -> 47.4 us (0.80)
  local copies, waits for them, and re-layouts: 13.1 us -> 0 us
  waiting for transfers between devices: 15.7 us -> 8.27 us
  Pallas kernels: 9.53 us -> 16.8 us
  starting transfers between devices: 20.2 us -> 22.1 us
    unnamed x22 -> x0, local copies, waits for them, and re-layouts: 13.1 us -> none
    ppermute x26, waiting for transfers between devices: 15.7 us -> 8.27 us  [swap(): return lax.ppermute(value, axis, [(i, i ^ offset) for i in range(size)])]
    pallas_call x13, Pallas kernels: 9.53 us -> 16.8 us  [call(): pl.pallas_call(kernel, out_shape=outs, in_specs=specs, out_specs=jax.tree...]
    ppermute x26, starting transfers between devices: 20.2 us -> 22.1 us  [swap(): return lax.ppermute(value, axis, [(i, i ^ offset) for i in range(size)])]
  transfers between devices with their start and end apart: 26 -> 26, of which waited for: 10 -> 8; matrix products, arithmetic and copies ran while one was open for 0% -> 0% of each run, Pallas kernels for 13% -> 31%
where the time goes in v3:
time: 47.4 us; the launch traced here: 47.3 us
  starting transfers between devices  22.1 us (47%)
  Pallas kernels  16.8 us (35%)
  waiting for transfers between devices  8.27 us (17%)
    ppermute x26, starting transfers between devices, swap(): return lax.ppermute(value, axis, [(i, i ^ offset) for i in range(size)])  22.1 us
    pallas_call x13, Pallas kernels, call(): pl.pallas_call(kernel, out_shape=outs, in_specs=specs, out_specs=jax.tree...  16.8 us
    ppermute x26, waiting for transfers between devices, swap(): return lax.ppermute(value, axis, [(i, i ^ offset) for i in range(size)])  8.27 us
  transfers between devices with their start and end apart: 26, of which 8 were waited for; matrix products, arithmetic and copies ran while one was open for 0% of the time, Pallas kernels for 31%

profile of v3, /device:TPU:0, one launch (start us, length us, event | category | flops | bytes accessed | tf_op | source)
XLA Modules:
  0.0 47.3 jit_solution(17420810574123469686)
XLA Ops:
  0.0 1.2 %dispatch.1 = (bf16[9,56,128]{2,1,0:T(8,128)(2,1)S(1)}, bf16[5,56,128]{2,1,0:T(8,128)(2,1)S(1)}, bf16[5,56,128]{2,1,0:T(8,128)(2,1)S(1)}, bf16[5,56,128]{2,1,0:T...) custom-call(s32[2,8]{1,0:T(2,128)} %bitcast.8, s32[4]{0:T(128)} %place_in.1, f32[2,8]{1,0:T(2,128)} %bitcast.9, ...), custom_call_target="tpu_custom_call" | custom-call | tf_op jit(solution)/shard_map/dispatch/pallas_call | solution.py:245
  1.2 3.0 %collective-permute-start = (bf16[9,56,128]{2,1,0:T(8,128)(2,1)S(1)}, bf16[9,56,128]{2,1,0:T(8,128)(2,1)S(1)}, u32[]{:S(2)}, u32[]{:S(2)}) collective-permute-start(bf16[9,56,128]{2,1,0:T(8,128)(2,1)S(1)} %get-tuple-element.61.refs_3_.refs_0_), channel_id=1, source_target_pairs={{0,2},{2,0},{1,3},{3,1},{4,6},{6,4},{5,7},{7,5},{8,10},{10,8},{9,1... | collective-permute-start | bytes 387080 | tf_op jit(solution)/shard_map/ppermute | solution.py:233
  4.2 3.6 %collective-permute-start.1 = (bf16[5,56,128]{2,1,0:T(8,128)(2,1)S(1)}, bf16[5,56,128]{2,1,0:T(8,128)(2,1)S(1)}, u32[]{:S(2)}, u32[]{:S(2)}) collective-permute-start(bf16[5,56,128]{2,1,0:T(8,128)(2,1)S(1)} %get-tuple-element.48), channel_id=1, source_target_pairs={{0,12},{4,8},{8,4},{12,0},{1,13},{5,9},{9,5},{13,1},{2,14},{6,10},... | collective-permute-start | bytes 215048 | tf_op jit(solution)/shard_map/ppermute | solution.py:233
  7.8 0.8 %collective-permute-start.3 = (bf16[5,56,128]{2,1,0:T(8,128)(2,1)S(1)}, bf16[5,56,128]{2,1,0:T(8,128)(2,1)S(1)}, u32[]{:S(2)}, u32[]{:S(2)}) collective-permute-start(bf16[5,56,128]{2,1,0:T(8,128)(2,1)S(1)} %get-tuple-element.50), channel_id=1, source_target_pairs={{0,4},{4,0},{8,12},{12,8},{1,5},{5,1},{9,13},{13,9},{2,6},{6,2},{1... | collective-permute-start | bytes 215048 | tf_op jit(solution)/shard_map/ppermute | solution.py:233
  8.6 4.2 %load_shared.1 = (bf16[7168,256]{1,0:T(8,128)(2,1)S(1)}, bf16[7168,256]{1,0:T(8,128)(2,1)S(1)}, bf16[256,7168]{1,0:T(8,128)(2,1)S(1)}) custom-call(bf16[7168,256]{1,0:T(8,128)(2,1)} %refs_0_.1, bf16[7168,256]{1,0:T(8,128)(2,1)} %refs_1_.1, bf16[256,7168]{1,0:T(8,128)(2,1)} %refs_2_.1, bf16[9,56,128]{2,1,0:T(8,128)(2,1)S(1)} %get-tuple-element.61.refs_3_.refs_0_), custom_call_target="tpu_custom_call" | custom-call | bytes 11010048 | tf_op jit(solution)/shard_map/load_shared/pallas_call | solution.py:245
  12.9 0.8 %collective-permute-done.2.refs_1_ = bf16[5,56,128]{2,1,0:T(8,128)(2,1)S(1)} collective-permute-done((bf16[5,56,128]{2,1,0:T(8,128)(2,1)S(1)}, bf16[5,56,128]{2,1,0:T(8,128)(2,1)S(1)}, u32[]{:S(2)}, u32[]{:S(2)}) %collective-permute-start.2) | collective-permute-done | bytes 71712 | tf_op jit(solution)/shard_map/ppermute | solution.py:233
  13.7 0.4 collective-permute-start.6
  14.1 0.5 %collective-permute-start.5 = (bf16[9,56,128]{2,1,0:T(8,128)(2,1)S(1)}, bf16[9,56,128]{2,1,0:T(8,128)(2,1)S(1)}, u32[]{:S(2)}, u32[]{:S(2)}) collective-permute-start(bf16[9,56,128]{2,1,0:T(8,128)(2,1)S(1)} %collective-permute-done.refs_1_), channel_id=1, source_target_pairs={{0,1},{1,0},{2,3},{3,2},{4,5},{5,4},{6,7},{7,6},{8,9},{9,8},{10,11... | collective-permute-start | bytes 387080 | tf_op jit(solution)/shard_map/ppermute | solution.py:233
  14.7 1.6 %collective-permute-start.7 = (bf16[5,56,128]{2,1,0:T(8,128)(2,1)S(1)}, bf16[5,56,128]{2,1,0:T(8,128)(2,1)S(1)}, u32[]{:S(2)}, u32[]{:S(2)}) collective-permute-start(bf16[5,56,128]{2,1,0:T(8,128)(2,1)S(1)} %collective-permute-done.2.refs_1_), channel_id=1, source_target_pairs={{0,2},{2,0},{1,3},{3,1},{4,6},{6,4},{5,7},{7,5},{8,10},{10,8},{9,1... | collective-permute-start | bytes 215048 | tf_op jit(solution)/shard_map/ppermute | solution.py:233
  16.2 0.4 collective-permute-start.8
  16.7 2.1 %collective-permute-done.6.refs_3_ = bf16[5,56,128]{2,1,0:T(8,128)(2,1)S(1)} collective-permute-done((bf16[5,56,128]{2,1,0:T(8,128)(2,1)S(1)}, bf16[5,56,128]{2,1,0:T(8,128)(2,1)S(1)}, u32[]{:S(2)}, u32[]{:S(2)}) %collective-permute-start.6) | collective-permute-done | bytes 71712 | tf_op jit(solution)/shard_map/ppermute | solution.py:233
  18.8 4.2 %load_routed.1 = (bf16[7168,256]{1,0:T(8,128)(2,1)S(1)}, bf16[7168,256]{1,0:T(8,128)(2,1)S(1)}, bf16[256,7168]{1,0:T(8,128)(2,1)S(1)}) custom-call(bf16[7168,256]{1,0:T(8,128)(2,1)} %bitcast.5, bf16[7168,256]{1,0:T(8,128)(2,1)} %bitcast.6, bf16[256,7168]{1,0:T(8,128)(2,1)} %bitcast.7, bf16[9,56,128]{2,1,0:T(8,128)(2,1)S(1)} %get-tuple-element.61.refs_3_.refs_0_), custom_call_target="tpu_custom_call" | custom-call | bytes 11010048 | tf_op jit(solution)/shard_map/load_routed/pallas_call | solution.py:245
  23.0 0.6 %collective-permute-start.12 = (bf16[5,56,128]{2,1,0:T(8,128)(2,1)S(1)}, bf16[5,56,128]{2,1,0:T(8,128)(2,1)S(1)}, u32[]{:S(2)}, u32[]{:S(2)}) collective-permute-start(bf16[5,56,128]{2,1,0:T(8,128)(2,1)S(1)} %collective-permute-done.2.refs_1_), channel_id=1, source_target_pairs={{0,1},{1,0},{2,3},{3,2},{4,5},{5,4},{6,7},{7,6},{8,9},{9,8},{10,11... | collective-permute-start | bytes 215048 | tf_op jit(solution)/shard_map/ppermute | solution.py:233
  23.7 0.4 collective-permute-start.14
  24.2 0.4 collective-permute-start.16
  24.6 3.8 %near.1 = (bf16[2,8,56,128]{3,2,1,0:T(8,128)(2,1)S(1)}, bf16[2,8,56,128]{3,2,1,0:T(8,128)(2,1)S(1)}) custom-call(bf16[9,56,128]{2,1,0:T(8,128)(2,1)S(1)} %get-tuple-element.61.refs_3_.refs_0_, bf16[9,56,128]{2,1,0:T(8,128)(2,1)S(1)} %collective-permute-done.refs_1_, bf16[9,56,128]{2,1,0:T(8,128)(2,1)S(1)} %collective-permute-done.4.refs_2_, ...), custom_call_target="tpu_custom_call" | custom-call | flops 704643072 | bytes 22020096 | tf_op jit(solution)/shard_map/near/pallas_call | solution.py:245
  28.5 0.2 collective-permute-start.9
  28.7 2.3 %far.1 = (bf16[2,5,56,128]{3,2,1,0:T(8,128)(2,1)S(1)}, bf16[2,5,56,128]{3,2,1,0:T(8,128)(2,1)S(1)}, bf16[2,5,56,128]{3,2,1,0:T(8,128)(2,1)S(1)}, bf16[2,5,56,128...) custom-call(bf16[5,56,128]{2,1,0:T(8,128)(2,1)S(1)} %collective-permute-done.1.refs_0_, ...), custom_call_target="tpu_custom_call" | custom-call | flops 660602880 | bytes 11010048 | tf_op jit(solution)/shard_map/far/pallas_call | solution.py:245
  31.0 0.5 %collective-permute-start.17 = (bf16[2,5,56,128]{3,2,1,0:T(8,128)(2,1)S(1)}, bf16[2,5,56,128]{3,2,1,0:T(8,128)(2,1)S(1)}, u32[]{:S(2)}, u32[]{:S(2)}) collective-permute-start(bf16[2,5,56,128]{3,2,1,0:T(8,128)(2,1)S(1)} %get-tuple-element.74), channel_id=1, source_target_pairs={{0,1},{1,0},{2,3},{3,2},{4,5},{5,4},{6,7},{7,6},{8,9},{9,8},{10,11... | collective-permute-start | bytes 430088 | tf_op jit(solution)/shard_map/ppermute | solution.py:233
  31.6 0.4 collective-permute-start.23
  32.0 0.5 %collective-permute-done.17.refs_1_ = bf16[2,5,56,128]{3,2,1,0:T(8,128)(2,1)S(1)} collective-permute-done((bf16[2,5,56,128]{3,2,1,0:T(8,128)(2,1)S(1)}, bf16[2,5,56,128]{3,2,1,0:T(8,128)(2,1)S(1)}, u32[]{:S(2)}, u32[]{:S(2)}) %collective-permute-start.17) | collective-permute-done | bytes 143392 | tf_op jit(solution)/shard_map/ppermute | solution.py:233
  32.6 0.2 collective-permute-done.20.refs_1_
  32.9 1.9 %collective-permute-start.21 = (bf16[5,56,128]{2,1,0:T(8,128)(2,1)S(1)}, bf16[5,56,128]{2,1,0:T(8,128)(2,1)S(1)}, u32[]{:S(2)}, u32[]{:S(2)}) collective-permute-start(bf16[5,56,128]{2,1,0:T(8,128)(2,1)S(1)} %get-tuple-element.80), channel_id=1, source_target_pairs={{0,2},{2,0},{1,3},{3,1},{4,6},{6,4},{5,7},{7,5},{8,10},{10,8},{9,1... | collective-permute-start | bytes 215048 | tf_op jit(solution)/shard_map/ppermute | solution.py:233
  34.8 0.3 collective-permute-start.24
  35.2 1.9 %collective-permute-start.10 = (bf16[8,56,128]{2,1,0:T(8,128)(2,1)S(1)}, bf16[8,56,128]{2,1,0:T(8,128)(2,1)S(1)}, u32[]{:S(2)}, u32[]{:S(2)}) collective-permute-start(bf16[8,56,128]{2,1,0:T(8,128)(2,1)S(1)} %get-tuple-element.72), channel_id=1, source_target_pairs={{0,2},{2,0},{1,3},{3,1},{4,6},{6,4},{5,7},{7,5},{8,10},{10,8},{9,1... | collective-permute-start | bytes 344072 | tf_op jit(solution)/shard_map/ppermute | solution.py:233
  37.0 0.6 %collective-permute-done.18.refs_1_ = bf16[5,56,128]{2,1,0:T(8,128)(2,1)S(1)} collective-permute-done((bf16[5,56,128]{2,1,0:T(8,128)(2,1)S(1)}, bf16[5,56,128]{2,1,0:T(8,128)(2,1)S(1)}, u32[]{:S(2)}, u32[]{:S(2)}) %collective-permute-start.18) | collective-permute-done | bytes 71712 | tf_op jit(solution)/shard_map/ppermute | solution.py:233
  37.7 2.8 %collective-permute-start.19 = (bf16[5,56,128]{2,1,0:T(8,128)(2,1)S(1)}, bf16[5,56,128]{2,1,0:T(8,128)(2,1)S(1)}, u32[]{:S(2)}, u32[]{:S(2)}) collective-permute-start(bf16[5,56,128]{2,1,0:T(8,128)(2,1)S(1)} %narrow_sum.3), channel_id=1, source_target_pairs={{0,12},{4,8},{8,4},{12,0},{1,13},{5,9},{9,5},{13,1},{2,14},{6,10},... | collective-permute-start | bytes 215048 | tf_op jit(solution)/shard_map/ppermute | solution.py:233
  40.6 0.1 collective-permute-done.24.refs_1_
  40.8 1.9 %collective-permute-start.25 = (bf16[5,56,128]{2,1,0:T(8,128)(2,1)S(1)}, bf16[5,56,128]{2,1,0:T(8,128)(2,1)S(1)}, u32[]{:S(2)}, u32[]{:S(2)}) collective-permute-start(bf16[5,56,128]{2,1,0:T(8,128)(2,1)S(1)} %narrow_sum.5), channel_id=1, source_target_pairs={{0,4},{4,0},{8,12},{12,8},{1,5},{5,1},{9,13},{13,9},{2,6},{6,2},{1... | collective-permute-start | bytes 215048 | tf_op jit(solution)/shard_map/ppermute | solution.py:233
  42.7 1.3 %collective-permute-done.19.refs_2_ = bf16[5,56,128]{2,1,0:T(8,128)(2,1)S(1)} collective-permute-done((bf16[5,56,128]{2,1,0:T(8,128)(2,1)S(1)}, bf16[5,56,128]{2,1,0:T(8,128)(2,1)S(1)}, u32[]{:S(2)}, u32[]{:S(2)}) %collective-permute-start.19) | collective-permute-done | bytes 71712 | tf_op jit(solution)/shard_map/ppermute | solution.py:233
  44.0 2.5 %collective-permute-done.22.refs_3_ = bf16[5,56,128]{2,1,0:T(8,128)(2,1)S(1)} collective-permute-done((bf16[5,56,128]{2,1,0:T(8,128)(2,1)S(1)}, bf16[5,56,128]{2,1,0:T(8,128)(2,1)S(1)}, u32[]{:S(2)}, u32[]{:S(2)}) %collective-permute-start.22) | collective-permute-done | bytes 71712 | tf_op jit(solution)/shard_map/ppermute | solution.py:233
  46.5 0.8 %combine.1 = bf16[8,7168]{1,0:T(8,128)(2,1)} custom-call(s32[2,8]{1,0:T(2,128)S(4)} %get-tuple-element.45.route, f32[2,8]{1,0:T(2,128)S(4)} %get-tuple-element.46.gains, bf16[8,56,128]{2,1,0:T(8,128)(2,1)S(1)} %get-tuple-element.71.refs_0_, bf16[8,56,128]{2,1,0:T(8,128)(2,1)S(1)} %collective-permute-done.10.refs_1_, ...), custom_call_target="tpu_custom_call" | custom-call | tf_op jit(solution)/shard_map/combine/pallas_call | solution.py:245
  (33 shorter events, 0.7 us)
Async XLA Ops:
  1.2 12.9 %collective-permute-start = (bf16[9,56,128]{2,1,0:T(8,128)(2,1)S(1)}, bf16[9,56,128]{2,1,0:T(8,128)(2,1)S(1)}, u32[]{:S(2)}, u32[]{:S(2)}) collective-permute-start(bf16[9,56,128]{2,1,0:T(8,128)(2,1)S(1)} %get-tuple-element.61.refs_3_.refs_0_), channel_id=1, source_target_pairs={{0,2},{2,0},{1,3},{3,1},{4,6},{6,4},{5,7},{7,5},{8,10},{10,8},{9,1... | collective-permute-start | bytes 387080 | tf_op jit(solution)/shard_map/ppermute | solution.py:233
  4.2 8.6 %collective-permute-start.1 = (bf16[5,56,128]{2,1,0:T(8,128)(2,1)S(1)}, bf16[5,56,128]{2,1,0:T(8,128)(2,1)S(1)}, u32[]{:S(2)}, u32[]{:S(2)}) collective-permute-start(bf16[5,56,128]{2,1,0:T(8,128)(2,1)S(1)} %get-tuple-element.48), channel_id=1, source_target_pairs={{0,12},{4,8},{8,4},{12,0},{1,13},{5,9},{9,5},{13,1},{2,14},{6,10},... | collective-permute-start | bytes 215048 | tf_op jit(solution)/shard_map/ppermute | solution.py:233
  7.8 5.8 %collective-permute-start.2 = (bf16[5,56,128]{2,1,0:T(8,128)(2,1)S(1)}, bf16[5,56,128]{2,1,0:T(8,128)(2,1)S(1)}, u32[]{:S(2)}, u32[]{:S(2)}) collective-permute-start(bf16[5,56,128]{2,1,0:T(8,128)(2,1)S(1)} %get-tuple-element.49), channel_id=1, source_target_pairs={{0,8},{4,12},{8,0},{12,4},{1,9},{5,13},{9,1},{13,5},{2,10},{6,14},... | collective-permute-start | bytes 215048 | tf_op jit(solution)/shard_map/ppermute | solution.py:233
  7.8 5.9 %collective-permute-start.3 = (bf16[5,56,128]{2,1,0:T(8,128)(2,1)S(1)}, bf16[5,56,128]{2,1,0:T(8,128)(2,1)S(1)}, u32[]{:S(2)}, u32[]{:S(2)}) collective-permute-start(bf16[5,56,128]{2,1,0:T(8,128)(2,1)S(1)} %get-tuple-element.50), channel_id=1, source_target_pairs={{0,4},{4,0},{8,12},{12,8},{1,5},{5,1},{9,13},{13,9},{2,6},{6,2},{1... | collective-permute-start | bytes 215048 | tf_op jit(solution)/shard_map/ppermute | solution.py:233
  13.7 5.1 %collective-permute-start.6 = (bf16[5,56,128]{2,1,0:T(8,128)(2,1)S(1)}, bf16[5,56,128]{2,1,0:T(8,128)(2,1)S(1)}, u32[]{:S(2)}, u32[]{:S(2)}) collective-permute-start(bf16[5,56,128]{2,1,0:T(8,128)(2,1)S(1)} %collective-permute-done.1.refs_0_), channel_id=1, source_target_pairs={{0,2},{2,0},{1,3},{3,1},{4,6},{6,4},{5,7},{7,5},{8,10},{10,8},{9,1... | collective-permute-start | bytes 215048 | tf_op jit(solution)/shard_map/ppermute | solution.py:233
  14.1 10.0 %collective-permute-start.4 = (bf16[9,56,128]{2,1,0:T(8,128)(2,1)S(1)}, bf16[9,56,128]{2,1,0:T(8,128)(2,1)S(1)}, u32[]{:S(2)}, u32[]{:S(2)}) collective-permute-start(bf16[9,56,128]{2,1,0:T(8,128)(2,1)S(1)} %get-tuple-element.61.refs_3_.refs_0_), channel_id=1, source_target_pairs={{0,1},{1,0},{2,3},{3,2},{4,5},{5,4},{6,7},{7,6},{8,9},{9,8},{10,11... | collective-permute-start | bytes 387080 | tf_op jit(solution)/shard_map/ppermute | solution.py:233
  14.1 10.1 %collective-permute-start.5 = (bf16[9,56,128]{2,1,0:T(8,128)(2,1)S(1)}, bf16[9,56,128]{2,1,0:T(8,128)(2,1)S(1)}, u32[]{:S(2)}, u32[]{:S(2)}) collective-permute-start(bf16[9,56,128]{2,1,0:T(8,128)(2,1)S(1)} %collective-permute-done.refs_1_), channel_id=1, source_target_pairs={{0,1},{1,0},{2,3},{3,2},{4,5},{5,4},{6,7},{7,6},{8,9},{9,8},{10,11... | collective-permute-start | bytes 387080 | tf_op jit(solution)/shard_map/ppermute | solution.py:233
  14.7 8.4 %collective-permute-start.7 = (bf16[5,56,128]{2,1,0:T(8,128)(2,1)S(1)}, bf16[5,56,128]{2,1,0:T(8,128)(2,1)S(1)}, u32[]{:S(2)}, u32[]{:S(2)}) collective-permute-start(bf16[5,56,128]{2,1,0:T(8,128)(2,1)S(1)} %collective-permute-done.2.refs_1_), channel_id=1, source_target_pairs={{0,2},{2,0},{1,3},{3,1},{4,6},{6,4},{5,7},{7,5},{8,10},{10,8},{9,1... | collective-permute-start | bytes 215048 | tf_op jit(solution)/shard_map/ppermute | solution.py:233
  16.2 7.4 %collective-permute-start.8 = (bf16[5,56,128]{2,1,0:T(8,128)(2,1)S(1)}, bf16[5,56,128]{2,1,0:T(8,128)(2,1)S(1)}, u32[]{:S(2)}, u32[]{:S(2)}) collective-permute-start(bf16[5,56,128]{2,1,0:T(8,128)(2,1)S(1)} %collective-permute-done.3.refs_2_), channel_id=1, source_target_pairs={{0,2},{2,0},{1,3},{3,1},{4,6},{6,4},{5,7},{7,5},{8,10},{10,8},{9,1... | collective-permute-start | bytes 215048 | tf_op jit(solution)/shard_map/ppermute | solution.py:233
  18.8 4.9 %collective-permute-start.11 = (bf16[5,56,128]{2,1,0:T(8,128)(2,1)S(1)}, bf16[5,56,128]{2,1,0:T(8,128)(2,1)S(1)}, u32[]{:S(2)}, u32[]{:S(2)}) collective-permute-start(bf16[5,56,128]{2,1,0:T(8,128)(2,1)S(1)} %collective-permute-done.1.refs_0_), channel_id=1, source_target_pairs={{0,1},{1,0},{2,3},{3,2},{4,5},{5,4},{6,7},{7,6},{8,9},{9,8},{10,11... | collective-permute-start | bytes 215048 | tf_op jit(solution)/shard_map/ppermute | solution.py:233
  23.0 5.5 %collective-permute-start.12 = (bf16[5,56,128]{2,1,0:T(8,128)(2,1)S(1)}, bf16[5,56,128]{2,1,0:T(8,128)(2,1)S(1)}, u32[]{:S(2)}, u32[]{:S(2)}) collective-permute-start(bf16[5,56,128]{2,1,0:T(8,128)(2,1)S(1)} %collective-permute-done.2.refs_1_), channel_id=1, source_target_pairs={{0,1},{1,0},{2,3},{3,2},{4,5},{5,4},{6,7},{7,6},{8,9},{9,8},{10,11... | collective-permute-start | bytes 215048 | tf_op jit(solution)/shard_map/ppermute | solution.py:233
  23.6 5.0 %collective-permute-start.13 = (bf16[5,56,128]{2,1,0:T(8,128)(2,1)S(1)}, bf16[5,56,128]{2,1,0:T(8,128)(2,1)S(1)}, u32[]{:S(2)}, u32[]{:S(2)}) collective-permute-start(bf16[5,56,128]{2,1,0:T(8,128)(2,1)S(1)} %collective-permute-done.3.refs_2_), channel_id=1, source_target_pairs={{0,1},{1,0},{2,3},{3,2},{4,5},{5,4},{6,7},{7,6},{8,9},{9,8},{10,11... | collective-permute-start | bytes 215048 | tf_op jit(solution)/shard_map/ppermute | solution.py:233
  23.7 5.0 %collective-permute-start.14 = (bf16[5,56,128]{2,1,0:T(8,128)(2,1)S(1)}, bf16[5,56,128]{2,1,0:T(8,128)(2,1)S(1)}, u32[]{:S(2)}, u32[]{:S(2)}) collective-permute-start(bf16[5,56,128]{2,1,0:T(8,128)(2,1)S(1)} %collective-permute-done.6.refs_3_), channel_id=1, source_target_pairs={{0,1},{1,0},{2,3},{3,2},{4,5},{5,4},{6,7},{7,6},{8,9},{9,8},{10,11... | collective-permute-start | bytes 215048 | tf_op jit(solution)/shard_map/ppermute | solution.py:233
  24.1 4.5 %collective-permute-start.15 = (bf16[5,56,128]{2,1,0:T(8,128)(2,1)S(1)}, bf16[5,56,128]{2,1,0:T(8,128)(2,1)S(1)}, u32[]{:S(2)}, u32[]{:S(2)}) collective-permute-start(bf16[5,56,128]{2,1,0:T(8,128)(2,1)S(1)} %collective-permute-done.7.refs_4_), channel_id=1, source_target_pairs={{0,1},{1,0},{2,3},{3,2},{4,5},{5,4},{6,7},{7,6},{8,9},{9,8},{10,11... | collective-permute-start | bytes 215048 | tf_op jit(solution)/shard_map/ppermute | solution.py:233
  24.2 4.5 %collective-permute-start.16 = (bf16[5,56,128]{2,1,0:T(8,128)(2,1)S(1)}, bf16[5,56,128]{2,1,0:T(8,128)(2,1)S(1)}, u32[]{:S(2)}, u32[]{:S(2)}) collective-permute-start(bf16[5,56,128]{2,1,0:T(8,128)(2,1)S(1)} %collective-permute-done.8.refs_5_), channel_id=1, source_target_pairs={{0,1},{1,0},{2,3},{3,2},{4,5},{5,4},{6,7},{7,6},{8,9},{9,8},{10,11... | collective-permute-start | bytes 215048 | tf_op jit(solution)/shard_map/ppermute | solution.py:233
  28.5 6.6 %collective-permute-start.9 = (bf16[2,8,56,128]{3,2,1,0:T(8,128)(2,1)S(1)}, bf16[2,8,56,128]{3,2,1,0:T(8,128)(2,1)S(1)}, u32[]{:S(2)}, u32[]{:S(2)}) collective-permute-start(bf16[2,8,56,128]{3,2,1,0:T(8,128)(2,1)S(1)} %get-tuple-element.70), channel_id=1, source_target_pairs={{0,1},{1,0},{2,3},{3,2},{4,5},{5,4},{6,7},{7,6},{8,9},{9,8},{10,11... | collective-permute-start | bytes 688136 | tf_op jit(solution)/shard_map/ppermute | solution.py:233
  31.0 1.5 %collective-permute-start.17 = (bf16[2,5,56,128]{3,2,1,0:T(8,128)(2,1)S(1)}, bf16[2,5,56,128]{3,2,1,0:T(8,128)(2,1)S(1)}, u32[]{:S(2)}, u32[]{:S(2)}) collective-permute-start(bf16[2,5,56,128]{3,2,1,0:T(8,128)(2,1)S(1)} %get-tuple-element.74), channel_id=1, source_target_pairs={{0,1},{1,0},{2,3},{3,2},{4,5},{5,4},{6,7},{7,6},{8,9},{9,8},{10,11... | collective-permute-start | bytes 430088 | tf_op jit(solution)/shard_map/ppermute | solution.py:233
  31.5 1.4 %collective-permute-start.20 = (bf16[2,5,56,128]{3,2,1,0:T(8,128)(2,1)S(1)}, bf16[2,5,56,128]{3,2,1,0:T(8,128)(2,1)S(1)}, u32[]{:S(2)}, u32[]{:S(2)}) collective-permute-start(bf16[2,5,56,128]{3,2,1,0:T(8,128)(2,1)S(1)} %get-tuple-element.78), channel_id=1, source_target_pairs={{0,1},{1,0},{2,3},{3,2},{4,5},{5,4},{6,7},{7,6},{8,9},{9,8},{10,11... | collective-permute-start | bytes 430088 | tf_op jit(solution)/shard_map/ppermute | solution.py:233
  31.6 3.2 %collective-permute-start.23 = (bf16[2,5,56,128]{3,2,1,0:T(8,128)(2,1)S(1)}, bf16[2,5,56,128]{3,2,1,0:T(8,128)(2,1)S(1)}, u32[]{:S(2)}, u32[]{:S(2)}) collective-permute-start(bf16[2,5,56,128]{3,2,1,0:T(8,128)(2,1)S(1)} %get-tuple-element.82), channel_id=1, source_target_pairs={{0,1},{1,0},{2,3},{3,2},{4,5},{5,4},{6,7},{7,6},{8,9},{9,8},{10,11... | collective-permute-start | bytes 430088 | tf_op jit(solution)/shard_map/ppermute | solution.py:233
  32.5 5.1 %collective-permute-start.18 = (bf16[5,56,128]{2,1,0:T(8,128)(2,1)S(1)}, bf16[5,56,128]{2,1,0:T(8,128)(2,1)S(1)}, u32[]{:S(2)}, u32[]{:S(2)}) collective-permute-start(bf16[5,56,128]{2,1,0:T(8,128)(2,1)S(1)} %get-tuple-element.76), channel_id=1, source_target_pairs={{0,2},{2,0},{1,3},{3,1},{4,6},{6,4},{5,7},{7,5},{8,10},{10,8},{9,1... | collective-permute-start | bytes 215048 | tf_op jit(solution)/shard_map/ppermute | solution.py:233
  32.9 7.6 %collective-permute-start.21 = (bf16[5,56,128]{2,1,0:T(8,128)(2,1)S(1)}, bf16[5,56,128]{2,1,0:T(8,128)(2,1)S(1)}, u32[]{:S(2)}, u32[]{:S(2)}) collective-permute-start(bf16[5,56,128]{2,1,0:T(8,128)(2,1)S(1)} %get-tuple-element.80), channel_id=1, source_target_pairs={{0,2},{2,0},{1,3},{3,1},{4,6},{6,4},{5,7},{7,5},{8,10},{10,8},{9,1... | collective-permute-start | bytes 215048 | tf_op jit(solution)/shard_map/ppermute | solution.py:233
  34.8 5.9 %collective-permute-start.24 = (bf16[5,56,128]{2,1,0:T(8,128)(2,1)S(1)}, bf16[5,56,128]{2,1,0:T(8,128)(2,1)S(1)}, u32[]{:S(2)}, u32[]{:S(2)}) collective-permute-start(bf16[5,56,128]{2,1,0:T(8,128)(2,1)S(1)} %get-tuple-element.84), channel_id=1, source_target_pairs={{0,2},{2,0},{1,3},{3,1},{4,6},{6,4},{5,7},{7,5},{8,10},{10,8},{9,1... | collective-permute-start | bytes 215048 | tf_op jit(solution)/shard_map/ppermute | solution.py:233
  35.2 11.3 %collective-permute-start.10 = (bf16[8,56,128]{2,1,0:T(8,128)(2,1)S(1)}, bf16[8,56,128]{2,1,0:T(8,128)(2,1)S(1)}, u32[]{:S(2)}, u32[]{:S(2)}) collective-permute-start(bf16[8,56,128]{2,1,0:T(8,128)(2,1)S(1)} %get-tuple-element.72), channel_id=1, source_target_pairs={{0,2},{2,0},{1,3},{3,1},{4,6},{6,4},{5,7},{7,5},{8,10},{10,8},{9,1... | collective-permute-start | bytes 344072 | tf_op jit(solution)/shard_map/ppermute | solution.py:233
  37.7 6.3 %collective-permute-start.19 = (bf16[5,56,128]{2,1,0:T(8,128)(2,1)S(1)}, bf16[5,56,128]{2,1,0:T(8,128)(2,1)S(1)}, u32[]{:S(2)}, u32[]{:S(2)}) collective-permute-start(bf16[5,56,128]{2,1,0:T(8,128)(2,1)S(1)} %narrow_sum.3), channel_id=1, source_target_pairs={{0,12},{4,8},{8,4},{12,0},{1,13},{5,9},{9,5},{13,1},{2,14},{6,10},... | collective-permute-start | bytes 215048 | tf_op jit(solution)/shard_map/ppermute | solution.py:233
  40.5 6.0 %collective-permute-start.22 = (bf16[5,56,128]{2,1,0:T(8,128)(2,1)S(1)}, bf16[5,56,128]{2,1,0:T(8,128)(2,1)S(1)}, u32[]{:S(2)}, u32[]{:S(2)}) collective-permute-start(bf16[5,56,128]{2,1,0:T(8,128)(2,1)S(1)} %narrow_sum.4), channel_id=1, source_target_pairs={{0,8},{4,12},{8,0},{12,4},{1,9},{5,13},{9,1},{13,5},{2,10},{6,14},... | collective-permute-start | bytes 215048 | tf_op jit(solution)/shard_map/ppermute | solution.py:233
  40.8 5.7 %collective-permute-start.25 = (bf16[5,56,128]{2,1,0:T(8,128)(2,1)S(1)}, bf16[5,56,128]{2,1,0:T(8,128)(2,1)S(1)}, u32[]{:S(2)}, u32[]{:S(2)}) collective-permute-start(bf16[5,56,128]{2,1,0:T(8,128)(2,1)S(1)} %narrow_sum.5), channel_id=1, source_target_pairs={{0,4},{4,0},{8,12},{12,8},{1,5},{5,1},{9,13},{13,9},{2,6},{6,2},{1... | collective-permute-start | bytes 215048 | tf_op jit(solution)/shard_map/ppermute | solution.py:233

commit v4 on v3

--- a/solution.py
+++ b/solution.py
@@ -29,6 +29,7 @@
 
 
 def dispatch_kernel(ids_in, place_in, weights_in, codes_in, scales_in, *refs):
+    refs = refs[6:]
     near, far = refs[0], refs[1:-10]
     route, gains = refs[-10:-8]
     ids, place, weights, codes, scales, tok, stage, sems = refs[-8:]
@@ -84,18 +85,6 @@
         ref[...] = stage[(k + 1) * CAP : (k + 2) * CAP].astype(BF16)
 
 
-def load_kernel(count, *refs):
-    srcs, outs, sems = refs[:count], refs[-count - 1 : -1], refs[-1]
-    copies = [
-        pltpu.make_async_copy(src, dst, sems.at[i])
-        for i, (src, dst) in enumerate(zip(srcs, outs))
-    ]
-    for copy in copies:
-        copy.start()
-    for copy in copies:
-        copy.wait()
-
-
 def unpack(refs, blocks, rows, flat, inputs):
     tall = inputs.shape[1] // LANES
     at = 0
@@ -282,11 +271,18 @@
     def block(*lead):
         return jax.ShapeDtypeStruct(lead + (tall, LANES), BF16)
 
+    shared = [shared_gate, shared_up, shared_down]
+    routed = [
+        w_gate.reshape(features, hidden),
+        w_up.reshape(features, hidden),
+        w_down.reshape(hidden, features),
+    ]
     near, *far = call(
         dispatch_kernel,
         "dispatch",
-        in_hbm(expert_ids.T, placement, gate_weights.T, row_codes, row_scales),
-        [ASPEC] * 5,
+        in_hbm(expert_ids.T, placement, gate_weights.T, row_codes, row_scales)
+        + in_hbm(*shared, *routed),
+        [ASPEC] * 11,
         [block(tokens + 1)]
         + [block(CAP)] * (n_wide - 1)
         + [pltpu.SMEM((topk, tokens), jnp.int32), pltpu.SMEM((topk, tokens), F32)],
@@ -306,39 +302,17 @@
     far = [swap(far[k - 1], "wide", k) for k in order]
     near_line = [near] + [swap(near, "narrow", j) for j in range(1, n_narrow)]
 
-    def load(name, first, *weights):
-        return call(
-            functools.partial(load_kernel, len(weights)),
-            name,
-            in_hbm(*weights) + [first],
-            [ASPEC] * (len(weights) + 1),
-            [VMEM(value.shape, BF16) for value in weights],
-            [pltpu.SemaphoreType.DMA((len(weights),))],
-            moved=2 * sum(value.size for value in weights),
-        )
-
-    shared = load("load_shared", near, shared_gate, shared_up, shared_down)
-    routed = load(
-        "load_routed",
-        near,
-        w_gate.reshape(features, hidden),
-        w_up.reshape(features, hidden),
-        w_down.reshape(hidden, features),
-    )
     if n_wide > 4:
         far = [jnp.concatenate(far, axis=0)]
     per = len(far)
     slots = far[0].shape[0]
-    far = after(far, shared[0])
     far_side = []
     for j in range(1, n_narrow):
         far_side += [swap(value, "narrow", j) for value in far]
-    far_side = after(far_side, routed[0])
     near_line = after(near_line, *far)
     near_all = list(near_line)
     for c in range(1, n_pair):
         near_all += [swap(value, "pair", c) for value in near_line]
-    near_all = after(near_all, *far_side)
 
     near_rows = n_narrow * n_pair * tokens
     near_out = call(
@@ -367,7 +341,7 @@
         return [parts[0]] + [swap(parts[j], "narrow", j) for j in range(1, n_narrow)]
 
     near_back = reduce_pair(near_out, tokens)
-    far_line = list(far) + far_side
+    far_line = list(far) + after(far_side, near_out[0])
     far_all = list(far_line)
     for c in range(1, n_pair):
         far_all += [swap(value, "pair", c) for value in far_line]

time: 47.4 us -> 42 us (0.89)
  Pallas kernels: 16.8 us -> 8.56 us
  waiting for transfers between devices: 8.27 us -> 10.7 us
    pallas_call x13 -> x11, Pallas kernels: 16.8 us -> 8.56 us  [call(): pl.pallas_call(kernel, out_shape=outs, in_specs=specs, out_specs=jax.tree...]
    ppermute x26, waiting for transfers between devices: 8.27 us -> 10.7 us  [swap(): return lax.ppermute(value, axis, [(i, i ^ offset) for i in range(size)])]
  transfers between devices with their start and end apart: 26 -> 26, of which waited for: 8 -> 12; matrix products, arithmetic and copies ran while one was open for 0% -> 0% of each run, Pallas kernels for 31% -> 15%
where the time goes in v4:
time: 42 us; the launch traced here: 41.9 us
  starting transfers between devices  22.5 us (54%)
  waiting for transfers between devices  10.7 us (25%)
  Pallas kernels  8.56 us (20%)
    ppermute x26, starting transfers between devices, swap(): return lax.ppermute(value, axis, [(i, i ^ offset) for i in range(size)])  22.5 us
    ppermute x26, waiting for transfers between devices, swap(): return lax.ppermute(value, axis, [(i, i ^ offset) for i in range(size)])  10.7 us
    pallas_call x11, Pallas kernels, call(): pl.pallas_call(kernel, out_shape=outs, in_specs=specs, out_specs=jax.tree...  8.56 us
  transfers between devices with their start and end apart: 26, of which 12 were waited for; matrix products, arithmetic and copies ran while one was open for 0% of the time, Pallas kernels for 15%

profile of v4, /device:TPU:0, one launch (start us, length us, event | category | flops | bytes accessed | tf_op | source)
XLA Modules:
  0.0 41.9 jit_solution(5069663642379364346)
XLA Ops:
  0.0 1.4 %dispatch.1 = (bf16[9,56,128]{2,1,0:T(8,128)(2,1)S(1)}, bf16[5,56,128]{2,1,0:T(8,128)(2,1)S(1)}, bf16[5,56,128]{2,1,0:T(8,128)(2,1)S(1)}, bf16[5,56,128]{2,1,0:T...) custom-call(s32[2,8]{1,0:T(2,128)} %bitcast.14, s32[4]{0:T(128)} %place_in.1, f32[2,8]{1,0:T(2,128)} %bitcast.15, ...), custom_call_target="tpu_custom_call" | custom-call | tf_op jit(solution)/shard_map/dispatch/pallas_call | solution.py:234
  1.4 3.0 %collective-permute-start = (bf16[9,56,128]{2,1,0:T(8,128)(2,1)S(1)}, bf16[9,56,128]{2,1,0:T(8,128)(2,1)S(1)}, u32[]{:S(2)}, u32[]{:S(2)}) collective-permute-start(bf16[9,56,128]{2,1,0:T(8,128)(2,1)S(1)} %get-tuple-element.38.refs_0_), channel_id=1, source_target_pairs={{0,2},{2,0},{1,3},{3,1},{4,6},{6,4},{5,7},{7,5},{8,10},{10,8},{9,1... | collective-permute-start | bytes 387080 | tf_op jit(solution)/shard_map/ppermute | solution.py:222
  4.4 3.6 %collective-permute-start.1 = (bf16[5,56,128]{2,1,0:T(8,128)(2,1)S(1)}, bf16[5,56,128]{2,1,0:T(8,128)(2,1)S(1)}, u32[]{:S(2)}, u32[]{:S(2)}) collective-permute-start(bf16[5,56,128]{2,1,0:T(8,128)(2,1)S(1)} %get-tuple-element.35), channel_id=1, source_target_pairs={{0,12},{4,8},{8,4},{12,0},{1,13},{5,9},{9,5},{13,1},{2,14},{6,10},... | collective-permute-start | bytes 215048 | tf_op jit(solution)/shard_map/ppermute | solution.py:222
  8.0 0.8 %collective-permute-start.3 = (bf16[5,56,128]{2,1,0:T(8,128)(2,1)S(1)}, bf16[5,56,128]{2,1,0:T(8,128)(2,1)S(1)}, u32[]{:S(2)}, u32[]{:S(2)}) collective-permute-start(bf16[5,56,128]{2,1,0:T(8,128)(2,1)S(1)} %get-tuple-element.37), channel_id=1, source_target_pairs={{0,4},{4,0},{8,12},{12,8},{1,5},{5,1},{9,13},{13,9},{2,6},{6,2},{1... | collective-permute-start | bytes 215048 | tf_op jit(solution)/shard_map/ppermute | solution.py:222
  8.8 2.6 %collective-permute-done.1.refs_0_ = bf16[5,56,128]{2,1,0:T(8,128)(2,1)S(1)} collective-permute-done((bf16[5,56,128]{2,1,0:T(8,128)(2,1)S(1)}, bf16[5,56,128]{2,1,0:T(8,128)(2,1)S(1)}, u32[]{:S(2)}, u32[]{:S(2)}) %collective-permute-start.1) | collective-permute-done | bytes 71712 | tf_op jit(solution)/shard_map/ppermute | solution.py:222
  11.4 2.4 %collective-permute-done.2.refs_1_ = bf16[5,56,128]{2,1,0:T(8,128)(2,1)S(1)} collective-permute-done((bf16[5,56,128]{2,1,0:T(8,128)(2,1)S(1)}, bf16[5,56,128]{2,1,0:T(8,128)(2,1)S(1)}, u32[]{:S(2)}, u32[]{:S(2)}) %collective-permute-start.2) | collective-permute-done | bytes 71712 | tf_op jit(solution)/shard_map/ppermute | solution.py:222
  13.9 0.5 %collective-permute-start.5 = (bf16[9,56,128]{2,1,0:T(8,128)(2,1)S(1)}, bf16[9,56,128]{2,1,0:T(8,128)(2,1)S(1)}, u32[]{:S(2)}, u32[]{:S(2)}) collective-permute-start(bf16[9,56,128]{2,1,0:T(8,128)(2,1)S(1)} %collective-permute-done.refs_1_), channel_id=1, source_target_pairs={{0,1},{1,0},{2,3},{3,2},{4,5},{5,4},{6,7},{7,6},{8,9},{9,8},{10,11... | collective-permute-start | bytes 387080 | tf_op jit(solution)/shard_map/ppermute | solution.py:222
  14.4 0.4 %collective-permute-start.8 = (bf16[5,56,128]{2,1,0:T(8,128)(2,1)S(1)}, bf16[5,56,128]{2,1,0:T(8,128)(2,1)S(1)}, u32[]{:S(2)}, u32[]{:S(2)}) collective-permute-start(bf16[5,56,128]{2,1,0:T(8,128)(2,1)S(1)} %collective-permute-done.1.refs_0_), channel_id=1, source_target_pairs={{0,2},{2,0},{1,3},{3,1},{4,6},{6,4},{5,7},{7,5},{8,10},{10,8},{9,1... | collective-permute-start | bytes 215048 | tf_op jit(solution)/shard_map/ppermute | solution.py:222
  14.8 1.6 %collective-permute-start.9 = (bf16[5,56,128]{2,1,0:T(8,128)(2,1)S(1)}, bf16[5,56,128]{2,1,0:T(8,128)(2,1)S(1)}, u32[]{:S(2)}, u32[]{:S(2)}) collective-permute-start(bf16[5,56,128]{2,1,0:T(8,128)(2,1)S(1)} %collective-permute-done.2.refs_1_), channel_id=1, source_target_pairs={{0,2},{2,0},{1,3},{3,1},{4,6},{6,4},{5,7},{7,5},{8,10},{10,8},{9,1... | collective-permute-start | bytes 215048 | tf_op jit(solution)/shard_map/ppermute | solution.py:222
  16.4 0.4 %collective-permute-start.10 = (bf16[5,56,128]{2,1,0:T(8,128)(2,1)S(1)}, bf16[5,56,128]{2,1,0:T(8,128)(2,1)S(1)}, u32[]{:S(2)}, u32[]{:S(2)}) collective-permute-start(bf16[5,56,128]{2,1,0:T(8,128)(2,1)S(1)} %collective-permute-done.3.refs_2_), channel_id=1, source_target_pairs={{0,2},{2,0},{1,3},{3,1},{4,6},{6,4},{5,7},{7,5},{8,10},{10,8},{9,1... | collective-permute-start | bytes 215048 | tf_op jit(solution)/shard_map/ppermute | solution.py:222
  16.9 0.5 %collective-permute-start.12 = (bf16[5,56,128]{2,1,0:T(8,128)(2,1)S(1)}, bf16[5,56,128]{2,1,0:T(8,128)(2,1)S(1)}, u32[]{:S(2)}, u32[]{:S(2)}) collective-permute-start(bf16[5,56,128]{2,1,0:T(8,128)(2,1)S(1)} %collective-permute-done.2.refs_1_), channel_id=1, source_target_pairs={{0,1},{1,0},{2,3},{3,2},{4,5},{5,4},{6,7},{7,6},{8,9},{9,8},{10,11... | collective-permute-start | bytes 215048 | tf_op jit(solution)/shard_map/ppermute | solution.py:222
  17.4 3.9 %near.1 = (bf16[2,8,56,128]{3,2,1,0:T(8,128)(2,1)S(1)}, bf16[2,8,56,128]{3,2,1,0:T(8,128)(2,1)S(1)}) custom-call(bf16[9,56,128]{2,1,0:T(8,128)(2,1)S(1)} %get-tuple-element.38.refs_0_, bf16[9,56,128]{2,1,0:T(8,128)(2,1)S(1)} %collective-permute-done.refs_1_, bf16[9,56,128]{2,1,0:T(8,128)(2,1)S(1)} %collective-permute-done.4.refs_2_, ...), custom_call_target="tpu_custom_call" | custom-call | flops 704643072 | bytes 22020096 | tf_op jit(solution)/shard_map/near/pallas_call | solution.py:234
  21.7 0.2 collective-permute-start.14
  21.9 0.3 collective-permute-start.15
  22.2 0.2 collective-permute-start.16
  22.4 0.3 collective-permute-start.6
  23.2 0.3 collective-permute-done.16.refs_11_
  23.4 2.3 %far.1 = (bf16[2,5,56,128]{3,2,1,0:T(8,128)(2,1)S(1)}, bf16[2,5,56,128]{3,2,1,0:T(8,128)(2,1)S(1)}, bf16[2,5,56,128]{3,2,1,0:T(8,128)(2,1)S(1)}, bf16[2,5,56,128...) custom-call(bf16[5,56,128]{2,1,0:T(8,128)(2,1)S(1)} %collective-permute-done.1.refs_0_, ...), custom_call_target="tpu_custom_call" | custom-call | flops 660602880 | bytes 11010048 | tf_op jit(solution)/shard_map/far/pallas_call | solution.py:234
  25.8 0.3 collective-permute-start.17
  26.1 0.3 collective-permute-start.20
  26.3 0.2 collective-permute-start.23
  26.6 0.6 %collective-permute-done.17.refs_1_ = bf16[2,5,56,128]{3,2,1,0:T(8,128)(2,1)S(1)} collective-permute-done((bf16[2,5,56,128]{3,2,1,0:T(8,128)(2,1)S(1)}, bf16[2,5,56,128]{3,2,1,0:T(8,128)(2,1)S(1)}, u32[]{:S(2)}, u32[]{:S(2)}) %collective-permute-start.17) | collective-permute-done | bytes 143392 | tf_op jit(solution)/shard_map/ppermute | solution.py:222
  27.2 1.5 %collective-permute-start.18 = (bf16[5,56,128]{2,1,0:T(8,128)(2,1)S(1)}, bf16[5,56,128]{2,1,0:T(8,128)(2,1)S(1)}, u32[]{:S(2)}, u32[]{:S(2)}) collective-permute-start(bf16[5,56,128]{2,1,0:T(8,128)(2,1)S(1)} %get-tuple-element.50), channel_id=1, source_target_pairs={{0,2},{2,0},{1,3},{3,1},{4,6},{6,4},{5,7},{7,5},{8,10},{10,8},{9,1... | collective-permute-start | bytes 215048 | tf_op jit(solution)/shard_map/ppermute | solution.py:222
  28.8 0.6 %collective-permute-start.21 = (bf16[5,56,128]{2,1,0:T(8,128)(2,1)S(1)}, bf16[5,56,128]{2,1,0:T(8,128)(2,1)S(1)}, u32[]{:S(2)}, u32[]{:S(2)}) collective-permute-start(bf16[5,56,128]{2,1,0:T(8,128)(2,1)S(1)} %get-tuple-element.54), channel_id=1, source_target_pairs={{0,2},{2,0},{1,3},{3,1},{4,6},{6,4},{5,7},{7,5},{8,10},{10,8},{9,1... | collective-permute-start | bytes 215048 | tf_op jit(solution)/shard_map/ppermute | solution.py:222
  29.5 1.5 %collective-permute-start.24 = (bf16[5,56,128]{2,1,0:T(8,128)(2,1)S(1)}, bf16[5,56,128]{2,1,0:T(8,128)(2,1)S(1)}, u32[]{:S(2)}, u32[]{:S(2)}) collective-permute-start(bf16[5,56,128]{2,1,0:T(8,128)(2,1)S(1)} %get-tuple-element.58), channel_id=1, source_target_pairs={{0,2},{2,0},{1,3},{3,1},{4,6},{6,4},{5,7},{7,5},{8,10},{10,8},{9,1... | collective-permute-start | bytes 215048 | tf_op jit(solution)/shard_map/ppermute | solution.py:222
  31.1 0.6 %collective-permute-start.7 = (bf16[8,56,128]{2,1,0:T(8,128)(2,1)S(1)}, bf16[8,56,128]{2,1,0:T(8,128)(2,1)S(1)}, u32[]{:S(2)}, u32[]{:S(2)}) collective-permute-start(bf16[8,56,128]{2,1,0:T(8,128)(2,1)S(1)} %get-tuple-element.43), channel_id=1, source_target_pairs={{0,2},{2,0},{1,3},{3,1},{4,6},{6,4},{5,7},{7,5},{8,10},{10,8},{9,1... | collective-permute-start | bytes 344072 | tf_op jit(solution)/shard_map/ppermute | solution.py:222
  31.9 2.8 %collective-permute-start.19 = (bf16[5,56,128]{2,1,0:T(8,128)(2,1)S(1)}, bf16[5,56,128]{2,1,0:T(8,128)(2,1)S(1)}, u32[]{:S(2)}, u32[]{:S(2)}) collective-permute-start(bf16[5,56,128]{2,1,0:T(8,128)(2,1)S(1)} %narrow_sum.3), channel_id=1, source_target_pairs={{0,12},{4,8},{8,4},{12,0},{1,13},{5,9},{9,5},{13,1},{2,14},{6,10},... | collective-permute-start | bytes 215048 | tf_op jit(solution)/shard_map/ppermute | solution.py:222
  34.7 0.7 %collective-permute-start.22 = (bf16[5,56,128]{2,1,0:T(8,128)(2,1)S(1)}, bf16[5,56,128]{2,1,0:T(8,128)(2,1)S(1)}, u32[]{:S(2)}, u32[]{:S(2)}) collective-permute-start(bf16[5,56,128]{2,1,0:T(8,128)(2,1)S(1)} %narrow_sum.4), channel_id=1, source_target_pairs={{0,8},{4,12},{8,0},{12,4},{1,9},{5,13},{9,1},{13,5},{2,10},{6,14},... | collective-permute-start | bytes 215048 | tf_op jit(solution)/shard_map/ppermute | solution.py:222
  35.5 1.7 %collective-permute-start.25 = (bf16[5,56,128]{2,1,0:T(8,128)(2,1)S(1)}, bf16[5,56,128]{2,1,0:T(8,128)(2,1)S(1)}, u32[]{:S(2)}, u32[]{:S(2)}) collective-permute-start(bf16[5,56,128]{2,1,0:T(8,128)(2,1)S(1)} %narrow_sum.5), channel_id=1, source_target_pairs={{0,4},{4,0},{8,12},{12,8},{1,5},{5,1},{9,13},{13,9},{2,6},{6,2},{1... | collective-permute-start | bytes 215048 | tf_op jit(solution)/shard_map/ppermute | solution.py:222
  37.3 1.0 %collective-permute-done.19.refs_2_ = bf16[5,56,128]{2,1,0:T(8,128)(2,1)S(1)} collective-permute-done((bf16[5,56,128]{2,1,0:T(8,128)(2,1)S(1)}, bf16[5,56,128]{2,1,0:T(8,128)(2,1)S(1)}, u32[]{:S(2)}, u32[]{:S(2)}) %collective-permute-start.19) | collective-permute-done | bytes 71712 | tf_op jit(solution)/shard_map/ppermute | solution.py:222
  38.3 2.7 %collective-permute-done.22.refs_3_ = bf16[5,56,128]{2,1,0:T(8,128)(2,1)S(1)} collective-permute-done((bf16[5,56,128]{2,1,0:T(8,128)(2,1)S(1)}, bf16[5,56,128]{2,1,0:T(8,128)(2,1)S(1)}, u32[]{:S(2)}, u32[]{:S(2)}) %collective-permute-start.22) | collective-permute-done | bytes 71712 | tf_op jit(solution)/shard_map/ppermute | solution.py:222
  41.1 0.8 %combine.1 = bf16[8,7168]{1,0:T(8,128)(2,1)} custom-call(s32[2,8]{1,0:T(2,128)S(4)} %get-tuple-element.32.route, f32[2,8]{1,0:T(2,128)S(4)} %get-tuple-element.33.gains, bf16[8,56,128]{2,1,0:T(8,128)(2,1)S(1)} %get-tuple-element.42.refs_0_, bf16[8,56,128]{2,1,0:T(8,128)(2,1)S(1)} %collective-permute-done.7.refs_1_, ...), custom_call_target="tpu_custom_call" | custom-call | tf_op jit(solution)/shard_map/combine/pallas_call | solution.py:234
  (43 shorter events, 1.4 us)
Async XLA Ops:
  0.0 17.4 %copy-start = (bf16[1,7168,256]{2,1,0:T(8,128)(2,1)S(1)}, bf16[1,7168,256]{2,1,0:T(8,128)(2,1)}, u32[]{:S(2)}) copy-start(bf16[1,7168,256]{2,1,0:T(8,128)(2,1)} %param.16) | copy-start | bytes 11010052
  0.0 17.4 %copy-start.1 = (bf16[1,7168,256]{2,1,0:T(8,128)(2,1)S(1)}, bf16[1,7168,256]{2,1,0:T(8,128)(2,1)}, u32[]{:S(2)}) copy-start(bf16[1,7168,256]{2,1,0:T(8,128)(2,1)} %param.17) | copy-start | bytes 11010052
  0.0 17.4 %copy-start.2 = (bf16[1,256,7168]{2,1,0:T(8,128)(2,1)S(1)}, bf16[1,256,7168]{2,1,0:T(8,128)(2,1)}, u32[]{:S(2)}) copy-start(bf16[1,256,7168]{2,1,0:T(8,128)(2,1)} %param.18) | copy-start | bytes 11010052
  0.0 17.4 %copy-start.3 = (bf16[7168,256]{1,0:T(8,128)(2,1)S(1)}, bf16[7168,256]{1,0:T(8,128)(2,1)}, u32[]{:S(2)}) copy-start(bf16[7168,256]{1,0:T(8,128)(2,1)} %refs_4_.1) | copy-start | bytes 11010052
  0.0 17.4 %copy-start.4 = (bf16[7168,256]{1,0:T(8,128)(2,1)S(1)}, bf16[7168,256]{1,0:T(8,128)(2,1)}, u32[]{:S(2)}) copy-start(bf16[7168,256]{1,0:T(8,128)(2,1)} %refs_5_.1) | copy-start | bytes 11010052
  0.0 17.4 %copy-start.5 = (bf16[256,7168]{1,0:T(8,128)(2,1)S(1)}, bf16[256,7168]{1,0:T(8,128)(2,1)}, u32[]{:S(2)}) copy-start(bf16[256,7168]{1,0:T(8,128)(2,1)} %refs_6_.1) | copy-start | bytes 11010052
  1.4 12.5 %collective-permute-start = (bf16[9,56,128]{2,1,0:T(8,128)(2,1)S(1)}, bf16[9,56,128]{2,1,0:T(8,128)(2,1)S(1)}, u32[]{:S(2)}, u32[]{:S(2)}) collective-permute-start(bf16[9,56,128]{2,1,0:T(8,128)(2,1)S(1)} %get-tuple-element.38.refs_0_), channel_id=1, source_target_pairs={{0,2},{2,0},{1,3},{3,1},{4,6},{6,4},{5,7},{7,5},{8,10},{10,8},{9,1... | collective-permute-start | bytes 387080 | tf_op jit(solution)/shard_map/ppermute | solution.py:222
  4.4 7.0 %collective-permute-start.1 = (bf16[5,56,128]{2,1,0:T(8,128)(2,1)S(1)}, bf16[5,56,128]{2,1,0:T(8,128)(2,1)S(1)}, u32[]{:S(2)}, u32[]{:S(2)}) collective-permute-start(bf16[5,56,128]{2,1,0:T(8,128)(2,1)S(1)} %get-tuple-element.35), channel_id=1, source_target_pairs={{0,12},{4,8},{8,4},{12,0},{1,13},{5,9},{9,5},{13,1},{2,14},{6,10},... | collective-permute-start | bytes 215048 | tf_op jit(solution)/shard_map/ppermute | solution.py:222
  8.0 5.8 %collective-permute-start.2 = (bf16[5,56,128]{2,1,0:T(8,128)(2,1)S(1)}, bf16[5,56,128]{2,1,0:T(8,128)(2,1)S(1)}, u32[]{:S(2)}, u32[]{:S(2)}) collective-permute-start(bf16[5,56,128]{2,1,0:T(8,128)(2,1)S(1)} %get-tuple-element.36), channel_id=1, source_target_pairs={{0,8},{4,12},{8,0},{12,4},{1,9},{5,13},{9,1},{13,5},{2,10},{6,14},... | collective-permute-start | bytes 215048 | tf_op jit(solution)/shard_map/ppermute | solution.py:222
  8.0 5.9 %collective-permute-start.3 = (bf16[5,56,128]{2,1,0:T(8,128)(2,1)S(1)}, bf16[5,56,128]{2,1,0:T(8,128)(2,1)S(1)}, u32[]{:S(2)}, u32[]{:S(2)}) collective-permute-start(bf16[5,56,128]{2,1,0:T(8,128)(2,1)S(1)} %get-tuple-element.37), channel_id=1, source_target_pairs={{0,4},{4,0},{8,12},{12,8},{1,5},{5,1},{9,13},{13,9},{2,6},{6,2},{1... | collective-permute-start | bytes 215048 | tf_op jit(solution)/shard_map/ppermute | solution.py:222
  13.9 3.0 %collective-permute-start.4 = (bf16[9,56,128]{2,1,0:T(8,128)(2,1)S(1)}, bf16[9,56,128]{2,1,0:T(8,128)(2,1)S(1)}, u32[]{:S(2)}, u32[]{:S(2)}) collective-permute-start(bf16[9,56,128]{2,1,0:T(8,128)(2,1)S(1)} %get-tuple-element.38.refs_0_), channel_id=1, source_target_pairs={{0,1},{1,0},{2,3},{3,2},{4,5},{5,4},{6,7},{7,6},{8,9},{9,8},{10,11... | collective-permute-start | bytes 387080 | tf_op jit(solution)/shard_map/ppermute | solution.py:222
  13.9 3.0 %collective-permute-start.5 = (bf16[9,56,128]{2,1,0:T(8,128)(2,1)S(1)}, bf16[9,56,128]{2,1,0:T(8,128)(2,1)S(1)}, u32[]{:S(2)}, u32[]{:S(2)}) collective-permute-start(bf16[9,56,128]{2,1,0:T(8,128)(2,1)S(1)} %collective-permute-done.refs_1_), channel_id=1, source_target_pairs={{0,1},{1,0},{2,3},{3,2},{4,5},{5,4},{6,7},{7,6},{8,9},{9,8},{10,11... | collective-permute-start | bytes 387080 | tf_op jit(solution)/shard_map/ppermute | solution.py:222
  14.4 6.9 %collective-permute-start.8 = (bf16[5,56,128]{2,1,0:T(8,128)(2,1)S(1)}, bf16[5,56,128]{2,1,0:T(8,128)(2,1)S(1)}, u32[]{:S(2)}, u32[]{:S(2)}) collective-permute-start(bf16[5,56,128]{2,1,0:T(8,128)(2,1)S(1)} %collective-permute-done.1.refs_0_), channel_id=1, source_target_pairs={{0,2},{2,0},{1,3},{3,1},{4,6},{6,4},{5,7},{7,5},{8,10},{10,8},{9,1... | collective-permute-start | bytes 215048 | tf_op jit(solution)/shard_map/ppermute | solution.py:222
  14.8 6.6 %collective-permute-start.9 = (bf16[5,56,128]{2,1,0:T(8,128)(2,1)S(1)}, bf16[5,56,128]{2,1,0:T(8,128)(2,1)S(1)}, u32[]{:S(2)}, u32[]{:S(2)}) collective-permute-start(bf16[5,56,128]{2,1,0:T(8,128)(2,1)S(1)} %collective-permute-done.2.refs_1_), channel_id=1, source_target_pairs={{0,2},{2,0},{1,3},{3,1},{4,6},{6,4},{5,7},{7,5},{8,10},{10,8},{9,1... | collective-permute-start | bytes 215048 | tf_op jit(solution)/shard_map/ppermute | solution.py:222
  16.4 5.2 %collective-permute-start.10 = (bf16[5,56,128]{2,1,0:T(8,128)(2,1)S(1)}, bf16[5,56,128]{2,1,0:T(8,128)(2,1)S(1)}, u32[]{:S(2)}, u32[]{:S(2)}) collective-permute-start(bf16[5,56,128]{2,1,0:T(8,128)(2,1)S(1)} %collective-permute-done.3.refs_2_), channel_id=1, source_target_pairs={{0,2},{2,0},{1,3},{3,1},{4,6},{6,4},{5,7},{7,5},{8,10},{10,8},{9,1... | collective-permute-start | bytes 215048 | tf_op jit(solution)/shard_map/ppermute | solution.py:222
  16.9 5.3 %collective-permute-start.11 = (bf16[5,56,128]{2,1,0:T(8,128)(2,1)S(1)}, bf16[5,56,128]{2,1,0:T(8,128)(2,1)S(1)}, u32[]{:S(2)}, u32[]{:S(2)}) collective-permute-start(bf16[5,56,128]{2,1,0:T(8,128)(2,1)S(1)} %collective-permute-done.1.refs_0_), channel_id=1, source_target_pairs={{0,1},{1,0},{2,3},{3,2},{4,5},{5,4},{6,7},{7,6},{8,9},{9,8},{10,11... | collective-permute-start | bytes 215048 | tf_op jit(solution)/shard_map/ppermute | solution.py:222
  16.9 5.5 %collective-permute-start.12 = (bf16[5,56,128]{2,1,0:T(8,128)(2,1)S(1)}, bf16[5,56,128]{2,1,0:T(8,128)(2,1)S(1)}, u32[]{:S(2)}, u32[]{:S(2)}) collective-permute-start(bf16[5,56,128]{2,1,0:T(8,128)(2,1)S(1)} %collective-permute-done.2.refs_1_), channel_id=1, source_target_pairs={{0,1},{1,0},{2,3},{3,2},{4,5},{5,4},{6,7},{7,6},{8,9},{9,8},{10,11... | collective-permute-start | bytes 215048 | tf_op jit(solution)/shard_map/ppermute | solution.py:222
  21.3 1.4 %collective-permute-start.13 = (bf16[5,56,128]{2,1,0:T(8,128)(2,1)S(1)}, bf16[5,56,128]{2,1,0:T(8,128)(2,1)S(1)}, u32[]{:S(2)}, u32[]{:S(2)}) collective-permute-start(bf16[5,56,128]{2,1,0:T(8,128)(2,1)S(1)} %collective-permute-done.3.refs_2_), channel_id=1, source_target_pairs={{0,1},{1,0},{2,3},{3,2},{4,5},{5,4},{6,7},{7,6},{8,9},{9,8},{10,11... | collective-permute-start | bytes 215048 | tf_op jit(solution)/shard_map/ppermute | solution.py:222
  21.7 1.3 %collective-permute-start.14 = (bf16[5,56,128]{2,1,0:T(8,128)(2,1)S(1)}, bf16[5,56,128]{2,1,0:T(8,128)(2,1)S(1)}, u32[]{:S(2)}, u32[]{:S(2)}) collective-permute-start(bf16[5,56,128]{2,1,0:T(8,128)(2,1)S(1)} %collective-permute-done.8.refs_3_), channel_id=1, source_target_pairs={{0,1},{1,0},{2,3},{3,2},{4,5},{5,4},{6,7},{7,6},{8,9},{9,8},{10,11... | collective-permute-start | bytes 215048 | tf_op jit(solution)/shard_map/ppermute | solution.py:222
  21.9 1.3 %collective-permute-start.15 = (bf16[5,56,128]{2,1,0:T(8,128)(2,1)S(1)}, bf16[5,56,128]{2,1,0:T(8,128)(2,1)S(1)}, u32[]{:S(2)}, u32[]{:S(2)}) collective-permute-start(bf16[5,56,128]{2,1,0:T(8,128)(2,1)S(1)} %collective-permute-done.9.refs_4_), channel_id=1, source_target_pairs={{0,1},{1,0},{2,3},{3,2},{4,5},{5,4},{6,7},{7,6},{8,9},{9,8},{10,11... | collective-permute-start | bytes 215048 | tf_op jit(solution)/shard_map/ppermute | solution.py:222
  22.2 1.3 %collective-permute-start.16 = (bf16[5,56,128]{2,1,0:T(8,128)(2,1)S(1)}, bf16[5,56,128]{2,1,0:T(8,128)(2,1)S(1)}, u32[]{:S(2)}, u32[]{:S(2)}) collective-permute-start(bf16[5,56,128]{2,1,0:T(8,128)(2,1)S(1)} %collective-permute-done.10.refs_5_), channel_id=1, source_target_pairs={{0,1},{1,0},{2,3},{3,2},{4,5},{5,4},{6,7},{7,6},{8,9},{9,8},{10,11... | collective-permute-start | bytes 215048 | tf_op jit(solution)/shard_map/ppermute | solution.py:222
  22.4 8.6 %collective-permute-start.6 = (bf16[2,8,56,128]{3,2,1,0:T(8,128)(2,1)S(1)}, bf16[2,8,56,128]{3,2,1,0:T(8,128)(2,1)S(1)}, u32[]{:S(2)}, u32[]{:S(2)}) collective-permute-start(bf16[2,8,56,128]{3,2,1,0:T(8,128)(2,1)S(1)} %get-tuple-element.41), channel_id=1, source_target_pairs={{0,1},{1,0},{2,3},{3,2},{4,5},{5,4},{6,7},{7,6},{8,9},{9,8},{10,11... | collective-permute-start | bytes 688136 | tf_op jit(solution)/shard_map/ppermute | solution.py:222
  25.8 1.4 %collective-permute-start.17 = (bf16[2,5,56,128]{3,2,1,0:T(8,128)(2,1)S(1)}, bf16[2,5,56,128]{3,2,1,0:T(8,128)(2,1)S(1)}, u32[]{:S(2)}, u32[]{:S(2)}) collective-permute-start(bf16[2,5,56,128]{3,2,1,0:T(8,128)(2,1)S(1)} %get-tuple-element.48), channel_id=1, source_target_pairs={{0,1},{1,0},{2,3},{3,2},{4,5},{5,4},{6,7},{7,6},{8,9},{9,8},{10,11... | collective-permute-start | bytes 430088 | tf_op jit(solution)/shard_map/ppermute | solution.py:222
  26.1 2.7 %collective-permute-start.20 = (bf16[2,5,56,128]{3,2,1,0:T(8,128)(2,1)S(1)}, bf16[2,5,56,128]{3,2,1,0:T(8,128)(2,1)S(1)}, u32[]{:S(2)}, u32[]{:S(2)}) collective-permute-start(bf16[2,5,56,128]{3,2,1,0:T(8,128)(2,1)S(1)} %get-tuple-element.52), channel_id=1, source_target_pairs={{0,1},{1,0},{2,3},{3,2},{4,5},{5,4},{6,7},{7,6},{8,9},{9,8},{10,11... | collective-permute-start | bytes 430088 | tf_op jit(solution)/shard_map/ppermute | solution.py:222
  26.3 3.1 %collective-permute-start.23 = (bf16[2,5,56,128]{3,2,1,0:T(8,128)(2,1)S(1)}, bf16[2,5,56,128]{3,2,1,0:T(8,128)(2,1)S(1)}, u32[]{:S(2)}, u32[]{:S(2)}) collective-permute-start(bf16[2,5,56,128]{3,2,1,0:T(8,128)(2,1)S(1)} %get-tuple-element.56), channel_id=1, source_target_pairs={{0,1},{1,0},{2,3},{3,2},{4,5},{5,4},{6,7},{7,6},{8,9},{9,8},{10,11... | collective-permute-start | bytes 430088 | tf_op jit(solution)/shard_map/ppermute | solution.py:222
  27.2 4.6 %collective-permute-start.18 = (bf16[5,56,128]{2,1,0:T(8,128)(2,1)S(1)}, bf16[5,56,128]{2,1,0:T(8,128)(2,1)S(1)}, u32[]{:S(2)}, u32[]{:S(2)}) collective-permute-start(bf16[5,56,128]{2,1,0:T(8,128)(2,1)S(1)} %get-tuple-element.50), channel_id=1, source_target_pairs={{0,2},{2,0},{1,3},{3,1},{4,6},{6,4},{5,7},{7,5},{8,10},{10,8},{9,1... | collective-permute-start | bytes 215048 | tf_op jit(solution)/shard_map/ppermute | solution.py:222
  28.8 5.9 %collective-permute-start.21 = (bf16[5,56,128]{2,1,0:T(8,128)(2,1)S(1)}, bf16[5,56,128]{2,1,0:T(8,128)(2,1)S(1)}, u32[]{:S(2)}, u32[]{:S(2)}) collective-permute-start(bf16[5,56,128]{2,1,0:T(8,128)(2,1)S(1)} %get-tuple-element.54), channel_id=1, source_target_pairs={{0,2},{2,0},{1,3},{3,1},{4,6},{6,4},{5,7},{7,5},{8,10},{10,8},{9,1... | collective-permute-start | bytes 215048 | tf_op jit(solution)/shard_map/ppermute | solution.py:222
  29.5 6.0 %collective-permute-start.24 = (bf16[5,56,128]{2,1,0:T(8,128)(2,1)S(1)}, bf16[5,56,128]{2,1,0:T(8,128)(2,1)S(1)}, u32[]{:S(2)}, u32[]{:S(2)}) collective-permute-start(bf16[5,56,128]{2,1,0:T(8,128)(2,1)S(1)} %get-tuple-element.58), channel_id=1, source_target_pairs={{0,2},{2,0},{1,3},{3,1},{4,6},{6,4},{5,7},{7,5},{8,10},{10,8},{9,1... | collective-permute-start | bytes 215048 | tf_op jit(solution)/shard_map/ppermute | solution.py:222
  31.1 6.2 %collective-permute-start.7 = (bf16[8,56,128]{2,1,0:T(8,128)(2,1)S(1)}, bf16[8,56,128]{2,1,0:T(8,128)(2,1)S(1)}, u32[]{:S(2)}, u32[]{:S(2)}) collective-permute-start(bf16[8,56,128]{2,1,0:T(8,128)(2,1)S(1)} %get-tuple-element.43), channel_id=1, source_target_pairs={{0,2},{2,0},{1,3},{3,1},{4,6},{6,4},{5,7},{7,5},{8,10},{10,8},{9,1... | collective-permute-start | bytes 344072 | tf_op jit(solution)/shard_map/ppermute | solution.py:222
  31.9 6.5 %collective-permute-start.19 = (bf16[5,56,128]{2,1,0:T(8,128)(2,1)S(1)}, bf16[5,56,128]{2,1,0:T(8,128)(2,1)S(1)}, u32[]{:S(2)}, u32[]{:S(2)}) collective-permute-start(bf16[5,56,128]{2,1,0:T(8,128)(2,1)S(1)} %narrow_sum.3), channel_id=1, source_target_pairs={{0,12},{4,8},{8,4},{12,0},{1,13},{5,9},{9,5},{13,1},{2,14},{6,10},... | collective-permute-start | bytes 215048 | tf_op jit(solution)/shard_map/ppermute | solution.py:222
  34.7 6.3 %collective-permute-start.22 = (bf16[5,56,128]{2,1,0:T(8,128)(2,1)S(1)}, bf16[5,56,128]{2,1,0:T(8,128)(2,1)S(1)}, u32[]{:S(2)}, u32[]{:S(2)}) collective-permute-start(bf16[5,56,128]{2,1,0:T(8,128)(2,1)S(1)} %narrow_sum.4), channel_id=1, source_target_pairs={{0,8},{4,12},{8,0},{12,4},{1,9},{5,13},{9,1},{13,5},{2,10},{6,14},... | collective-permute-start | bytes 215048 | tf_op jit(solution)/shard_map/ppermute | solution.py:222
  35.5 5.6 %collective-permute-start.25 = (bf16[5,56,128]{2,1,0:T(8,128)(2,1)S(1)}, bf16[5,56,128]{2,1,0:T(8,128)(2,1)S(1)}, u32[]{:S(2)}, u32[]{:S(2)}) collective-permute-start(bf16[5,56,128]{2,1,0:T(8,128)(2,1)S(1)} %narrow_sum.5), channel_id=1, source_target_pairs={{0,4},{4,0},{8,12},{12,8},{1,5},{5,1},{9,13},{13,9},{2,6},{6,2},{1... | collective-permute-start | bytes 215048 | tf_op jit(solution)/shard_map/ppermute | solution.py:222

commit v5 on v4

--- a/solution.py
+++ b/solution.py
@@ -105,38 +105,45 @@
     return (gate / (1.0 + jnp.exp(-gate)) * up).astype(BF16)
 
 
-def near_kernel(n_narrow, n_pair, *refs):
-    count = n_narrow * n_pair
-    arrived = refs[:count]
-    held = refs[count : count + 6]
-    outs = refs[count + 6 : count + 6 + n_pair]
-    flat, inputs = refs[count + 6 + n_pair :]
+def near_shared_kernel(*refs):
+    count = len(refs) - 7
+    arrived, (gate_w, up_w, down_w), outs = refs[:count], refs[count : count + 3], refs[-4:]
+    inputs, weight, value, flat = outs
     here = lax.axis_index("wide")
     tokens, tall = arrived[0].shape[0] - 1, arrived[0].shape[1]
     rows = count * tokens
     unpack(arrived, [tokens] * count, rows, flat, inputs)
-    weight = []
-    for ref in arrived:
+    for i, ref in enumerate(arrived):
         parts = ref[tokens].astype(F32)
         whole = (
             parts[:tokens] + parts[tokens : 2 * tokens] + parts[2 * tokens : 3 * tokens]
         )
         lane = lax.broadcasted_iota(jnp.int32, whole.shape, 1)
-        weight.append(
-            jnp.sum(jnp.where(lane == here, whole, 0.0), axis=1, keepdims=True)
-        )
-    weight = jnp.concatenate(weight, axis=0)
-    x = inputs[:rows]
-    hidden = []
-    for i in (0, 3):
-        gate = jnp.dot(x, held[i][...], preferred_element_type=F32)
-        up = jnp.dot(x, held[i + 1][...], preferred_element_type=F32)
-        hidden.append(silu_mul(gate, up))
+        gain = jnp.sum(jnp.where(lane == here, whole, 0.0), axis=1, keepdims=True)
+        weight[i * tokens : (i + 1) * tokens, :] = jnp.broadcast_to(gain, whole.shape)
+    x = inputs[...]
+    gate = jnp.dot(x, gate_w[...], preferred_element_type=F32)
+    up = jnp.dot(x, up_w[...], preferred_element_type=F32)
+    hidden = silu_mul(gate, up)
     for first in range(0, tall * LANES, SPAN * LANES):
         at = slice(first, first + SPAN * LANES)
-        shared = jnp.dot(hidden[0], held[2][:, at], preferred_element_type=F32)
-        routed = jnp.dot(hidden[1], held[5][:, at], preferred_element_type=F32)
-        put(flat, first, shared + weight * routed, rows)
+        value[:, at] = jnp.dot(hidden, down_w[:, at], preferred_element_type=F32)
+
+
+def near_routed_kernel(n_narrow, n_pair, inputs, weight, value, gate_w, up_w, down_w, *refs):
+    outs, flat = refs[:n_pair], refs[n_pair]
+    rows, features = inputs.shape
+    tall = features // LANES
+    tokens = rows // (n_narrow * n_pair)
+    x = inputs[...]
+    gate = jnp.dot(x, gate_w[...], preferred_element_type=F32)
+    up = jnp.dot(x, up_w[...], preferred_element_type=F32)
+    hidden = silu_mul(gate, up)
+    gain = weight[:, :1]
+    for first in range(0, features, SPAN * LANES):
+        at = slice(first, first + SPAN * LANES)
+        routed = jnp.dot(hidden, down_w[:, at], preferred_element_type=F32)
+        put(flat, first, value[:, at] + gain * routed, rows)
     each = n_narrow * tokens
     for c in range(n_pair):
         part = flat[c * each * tall : (c + 1) * each * tall, :]
@@ -300,47 +307,48 @@
     far, (route, gains) = far[:-2], far[-2:]
     order = list(range(n_wide - 1, 0, -1))
     far = [swap(far[k - 1], "wide", k) for k in order]
-    near_line = [near] + [swap(near, "narrow", j) for j in range(1, n_narrow)]
-
+    beside = ("narrow", "pair")
+    near_all = [
+        swap(near, beside, j * n_pair + c) if j + c else near
+        for c in range(n_pair)
+        for j in range(n_narrow)
+    ]
     if n_wide > 4:
         far = [jnp.concatenate(far, axis=0)]
     per = len(far)
     slots = far[0].shape[0]
+
+    near_rows = n_narrow * n_pair * tokens
+    near_mid = call(
+        near_shared_kernel,
+        "near_shared",
+        near_all + shared,
+        [VSPEC] * (n_narrow * n_pair + 3),
+        [
+            jax.ShapeDtypeStruct((near_rows, features), BF16),
+            jax.ShapeDtypeStruct((near_rows, LANES), F32),
+            jax.ShapeDtypeStruct((near_rows, features), F32),
+        ],
+        [VMEM((near_rows * tall, LANES), F32)],
+        flops=6 * near_rows * features * hidden,
+        moved=6 * features * hidden,
+        limit=limit,
+    )
+    far = after(far, near_mid[1])
     far_side = []
     for j in range(1, n_narrow):
         far_side += [swap(value, "narrow", j) for value in far]
-    near_line = after(near_line, *far)
-    near_all = list(near_line)
-    for c in range(1, n_pair):
-        near_all += [swap(value, "pair", c) for value in near_line]
-
-    near_rows = n_narrow * n_pair * tokens
     near_out = call(
-        functools.partial(near_kernel, n_narrow, n_pair),
-        "near",
-        near_all + list(shared) + list(routed),
-        [VSPEC] * (n_narrow * n_pair + 6),
+        functools.partial(near_routed_kernel, n_narrow, n_pair),
+        "near_routed",
+        after(near_mid, *far) + routed,
+        [VSPEC] * 6,
         [block(n_narrow, tokens)] * n_pair,
-        [VMEM((near_rows * tall, LANES), F32), VMEM((near_rows, features), BF16)],
-        flops=12 * near_rows * features * hidden,
-        moved=12 * features * hidden,
+        [VMEM((near_rows * tall, LANES), F32)],
+        flops=6 * near_rows * features * hidden,
+        moved=6 * features * hidden,
         limit=limit,
     )
-
-    def reduce_pair(parts, rows):
-        parts = [parts[0]] + [swap(parts[c], "pair", c) for c in range(1, n_pair)]
-        parts = call(
-            functools.partial(pair_sum_kernel, n_pair),
-            "pair_sum",
-            parts,
-            [VSPEC] * n_pair,
-            [block(rows)] * n_narrow,
-            [],
-            limit=limit,
-        )
-        return [parts[0]] + [swap(parts[j], "narrow", j) for j in range(1, n_narrow)]
-
-    near_back = reduce_pair(near_out, tokens)
     far_line = list(far) + after(far_side, near_out[0])
     far_all = list(far_line)
     for c in range(1, n_pair):
@@ -361,6 +369,19 @@
         limit=limit,
     )
 
+    def reduce_pair(parts, rows):
+        parts = [parts[0]] + [swap(parts[c], "pair", c) for c in range(1, n_pair)]
+        parts = call(
+            functools.partial(pair_sum_kernel, n_pair),
+            "pair_sum",
+            parts,
+            [VSPEC] * n_pair,
+            [block(rows)] * n_narrow,
+            [],
+            limit=limit,
+        )
+        return [parts[0]] + [swap(parts[j], "narrow", j) for j in range(1, n_narrow)]
+
     far_back = []
     for k in range(per):
         far_back += call(
@@ -372,6 +393,7 @@
             [],
             limit=limit,
         )
+    near_back = reduce_pair(near_out, tokens)
     far_back = [swap(value, "wide", k) for k, value in zip(order, far_back)]
     return call(
         functools.partial(combine_kernel, n_narrow, order),

time: 42 us -> 42 us (level)
  waiting for transfers between devices: 10.7 us -> 9.24 us
  starting transfers between devices: 22.5 us -> 23.8 us
    ppermute x26, waiting for transfers between devices: 10.7 us -> 9.24 us  [swap(): return lax.ppermute(value, axis, [(i, i ^ offset) for i in range(size)])]
    ppermute x26, starting transfers between devices: 22.5 us -> 23.8 us  [swap(): return lax.ppermute(value, axis, [(i, i ^ offset) for i in range(size)])]
    pallas_call x11 -> x12, Pallas kernels: 8.56 us -> 8.66 us  [call(): pl.pallas_call(kernel, out_shape=outs, in_specs=specs, out_specs=jax.tree...]
  transfers between devices with their start and end apart: 26 -> 26, of which waited for: 12 -> 12; matrix products, arithmetic and copies ran while one was open for 0% -> 0% of each run, Pallas kernels for 15% -> 16%
where the time goes in v5:
time: 42 us; the launch traced here: 41.9 us
  starting transfers between devices  23.8 us (57%)
  waiting for transfers between devices  9.24 us (22%)
  Pallas kernels  8.66 us (21%)
    ppermute x26, starting transfers between devices, swap(): return lax.ppermute(value, axis, [(i, i ^ offset) for i in range(size)])  23.8 us
    ppermute x26, waiting for transfers between devices, swap(): return lax.ppermute(value, axis, [(i, i ^ offset) for i in range(size)])  9.24 us
    pallas_call x12, Pallas kernels, call(): pl.pallas_call(kernel, out_shape=outs, in_specs=specs, out_specs=jax.tree...  8.66 us
  transfers between devices with their start and end apart: 26, of which 12 were waited for; matrix products, arithmetic and copies ran while one was open for 0% of the time, Pallas kernels for 16%

profile of v5, /device:TPU:0, one launch (start us, length us, event | category | flops | bytes accessed | tf_op | source)
XLA Modules:
  0.0 41.9 jit_solution(3756130943724670467)
XLA Ops:
  0.0 1.4 %dispatch.1 = (bf16[9,56,128]{2,1,0:T(8,128)(2,1)S(1)}, bf16[5,56,128]{2,1,0:T(8,128)(2,1)S(1)}, bf16[5,56,128]{2,1,0:T(8,128)(2,1)S(1)}, bf16[5,56,128]{2,1,0:T...) custom-call(s32[2,8]{1,0:T(2,128)} %bitcast.14, s32[4]{0:T(128)} %place_in.1, f32[2,8]{1,0:T(2,128)} %bitcast.15, ...), custom_call_target="tpu_custom_call" | custom-call | tf_op jit(solution)/shard_map/dispatch/pallas_call | solution.py:241
  1.4 3.0 %collective-permute-start = (bf16[9,56,128]{2,1,0:T(8,128)(2,1)S(1)}, bf16[9,56,128]{2,1,0:T(8,128)(2,1)S(1)}, u32[]{:S(2)}, u32[]{:S(2)}) collective-permute-start(bf16[9,56,128]{2,1,0:T(8,128)(2,1)S(1)} %get-tuple-element.41.refs_0_), channel_id=1, source_target_pairs={{0,2},{1,3},{2,0},{3,1},{4,6},{5,7},{6,4},{7,5},{8,10},{9,11},{10,... | collective-permute-start | bytes 387080 | tf_op jit(solution)/shard_map/ppermute | solution.py:229
  4.4 0.2 collective-permute-start.2
  4.6 4.0 %collective-permute-start.3 = (bf16[5,56,128]{2,1,0:T(8,128)(2,1)S(1)}, bf16[5,56,128]{2,1,0:T(8,128)(2,1)S(1)}, u32[]{:S(2)}, u32[]{:S(2)}) collective-permute-start(bf16[5,56,128]{2,1,0:T(8,128)(2,1)S(1)} %get-tuple-element.45), channel_id=1, source_target_pairs={{0,12},{4,8},{8,4},{12,0},{1,13},{5,9},{9,5},{13,1},{2,14},{6,10},... | collective-permute-start | bytes 215048 | tf_op jit(solution)/shard_map/ppermute | solution.py:229
  8.7 1.7 %collective-permute-start.5 = (bf16[5,56,128]{2,1,0:T(8,128)(2,1)S(1)}, bf16[5,56,128]{2,1,0:T(8,128)(2,1)S(1)}, u32[]{:S(2)}, u32[]{:S(2)}) collective-permute-start(bf16[5,56,128]{2,1,0:T(8,128)(2,1)S(1)} %get-tuple-element.47), channel_id=1, source_target_pairs={{0,4},{4,0},{8,12},{12,8},{1,5},{5,1},{9,13},{13,9},{2,6},{6,2},{1... | collective-permute-start | bytes 215048 | tf_op jit(solution)/shard_map/ppermute | solution.py:229
  10.4 2.0 %near_shared.1 = (bf16[32,7168]{1,0:T(8,128)(2,1)S(1)}, f32[32,128]{1,0:T(8,128)S(1)}, f32[32,7168]{1,0:T(8,128)S(1)}) custom-call(bf16[9,56,128]{2,1,0:T(8,128)(2,1)S(1)} %get-tuple-element.41.refs_0_, bf16[9,56,128]{2,1,0:T(8,128)(2,1)S(1)} %collective-permute-done.refs_1_, bf16[9,56,128]{2,1,0:T(8,128)(2,1)S(1)} %collective-permute-done.1.refs_2_, ...), custom_call_target="tpu_custom_call" | custom-call | flops 352321536 | bytes 11010048 | tf_op jit(solution)/shard_map/near_shared/pallas_call | solution.py:241
  12.5 2.4 %collective-permute-done.4.refs_1_ = bf16[5,56,128]{2,1,0:T(8,128)(2,1)S(1)} collective-permute-done((bf16[5,56,128]{2,1,0:T(8,128)(2,1)S(1)}, bf16[5,56,128]{2,1,0:T(8,128)(2,1)S(1)}, u32[]{:S(2)}, u32[]{:S(2)}) %collective-permute-start.4) | collective-permute-done | bytes 71712 | tf_op jit(solution)/shard_map/ppermute | solution.py:229
  14.9 1.7 %collective-permute-start.8 = (bf16[5,56,128]{2,1,0:T(8,128)(2,1)S(1)}, bf16[5,56,128]{2,1,0:T(8,128)(2,1)S(1)}, u32[]{:S(2)}, u32[]{:S(2)}) collective-permute-start(bf16[5,56,128]{2,1,0:T(8,128)(2,1)S(1)} %collective-permute-done.3.refs_0_), channel_id=1, source_target_pairs={{0,2},{2,0},{1,3},{3,1},{4,6},{6,4},{5,7},{7,5},{8,10},{10,8},{9,1... | collective-permute-start | bytes 215048 | tf_op jit(solution)/shard_map/ppermute | solution.py:229
  16.5 0.4 collective-permute-start.9
  16.9 1.7 %collective-permute-start.10 = (bf16[5,56,128]{2,1,0:T(8,128)(2,1)S(1)}, bf16[5,56,128]{2,1,0:T(8,128)(2,1)S(1)}, u32[]{:S(2)}, u32[]{:S(2)}) collective-permute-start(bf16[5,56,128]{2,1,0:T(8,128)(2,1)S(1)} %collective-permute-done.5.refs_2_), channel_id=1, source_target_pairs={{0,2},{2,0},{1,3},{3,1},{4,6},{6,4},{5,7},{7,5},{8,10},{10,8},{9,1... | collective-permute-start | bytes 215048 | tf_op jit(solution)/shard_map/ppermute | solution.py:229
  18.6 0.5 %collective-permute-start.12 = (bf16[5,56,128]{2,1,0:T(8,128)(2,1)S(1)}, bf16[5,56,128]{2,1,0:T(8,128)(2,1)S(1)}, u32[]{:S(2)}, u32[]{:S(2)}) collective-permute-start(bf16[5,56,128]{2,1,0:T(8,128)(2,1)S(1)} %collective-permute-done.4.refs_1_), channel_id=1, source_target_pairs={{0,1},{1,0},{2,3},{3,2},{4,5},{5,4},{6,7},{7,6},{8,9},{9,8},{10,11... | collective-permute-start | bytes 215048 | tf_op jit(solution)/shard_map/ppermute | solution.py:229
  19.1 2.0 %near_routed.1 = (bf16[2,8,56,128]{3,2,1,0:T(8,128)(2,1)S(1)}, bf16[2,8,56,128]{3,2,1,0:T(8,128)(2,1)S(1)}) custom-call(bf16[32,7168]{1,0:T(8,128)(2,1)S(1)} %get-tuple-element.51.inputs, f32[32,128]{1,0:T(8,128)S(1)} %get-tuple-element.52.weight, f32[32,7168]{1,0:T(8,128)S(1)} %get-tuple-element.53.value, bf16[7168,256]{1,0:T(8,128)(2,1)S(1)} %bitcast.6, ...), custom_call_target="tpu_custom_call" | custom-call | flops 352321536 | bytes 11010048 | tf_op jit(solution)/shard_map/near_routed/pallas_call | solution.py:241
  21.3 0.8 %collective-permute-done.10.refs_5_ = bf16[5,56,128]{2,1,0:T(8,128)(2,1)S(1)} collective-permute-done((bf16[5,56,128]{2,1,0:T(8,128)(2,1)S(1)}, bf16[5,56,128]{2,1,0:T(8,128)(2,1)S(1)}, u32[]{:S(2)}, u32[]{:S(2)}) %collective-permute-start.10) | collective-permute-done | bytes 71712 | tf_op jit(solution)/shard_map/ppermute | solution.py:229
  22.1 0.5 %collective-permute-start.15 = (bf16[5,56,128]{2,1,0:T(8,128)(2,1)S(1)}, bf16[5,56,128]{2,1,0:T(8,128)(2,1)S(1)}, u32[]{:S(2)}, u32[]{:S(2)}) collective-permute-start(bf16[5,56,128]{2,1,0:T(8,128)(2,1)S(1)} %collective-permute-done.9.refs_4_), channel_id=1, source_target_pairs={{0,1},{1,0},{2,3},{3,2},{4,5},{5,4},{6,7},{7,6},{8,9},{9,8},{10,11... | collective-permute-start | bytes 215048 | tf_op jit(solution)/shard_map/ppermute | solution.py:229
  22.6 0.5 %collective-permute-start.6 = (bf16[2,8,56,128]{3,2,1,0:T(8,128)(2,1)S(1)}, bf16[2,8,56,128]{3,2,1,0:T(8,128)(2,1)S(1)}, u32[]{:S(2)}, u32[]{:S(2)}) collective-permute-start(bf16[2,8,56,128]{3,2,1,0:T(8,128)(2,1)S(1)} %get-tuple-element.55), channel_id=1, source_target_pairs={{0,1},{1,0},{2,3},{3,2},{4,5},{5,4},{6,7},{7,6},{8,9},{9,8},{10,11... | collective-permute-start | bytes 688136 | tf_op jit(solution)/shard_map/ppermute | solution.py:229
  23.1 0.2 collective-permute-done.14.refs_9_
  23.5 0.4 collective-permute-done.16.refs_11_
  23.8 2.2 %far.1 = (bf16[2,5,56,128]{3,2,1,0:T(8,128)(2,1)S(1)}, bf16[2,5,56,128]{3,2,1,0:T(8,128)(2,1)S(1)}, bf16[2,5,56,128]{3,2,1,0:T(8,128)(2,1)S(1)}, bf16[2,5,56,128...) custom-call(bf16[5,56,128]{2,1,0:T(8,128)(2,1)S(1)} %collective-permute-done.3.refs_0_, ...), custom_call_target="tpu_custom_call" | custom-call | flops 660602880 | bytes 11010048 | tf_op jit(solution)/shard_map/far/pallas_call | solution.py:241
  26.1 0.2 collective-permute-start.17
  26.3 0.4 collective-permute-start.20
  26.8 0.7 %collective-permute-done.17.refs_1_ = bf16[2,5,56,128]{3,2,1,0:T(8,128)(2,1)S(1)} collective-permute-done((bf16[2,5,56,128]{3,2,1,0:T(8,128)(2,1)S(1)}, bf16[2,5,56,128]{3,2,1,0:T(8,128)(2,1)S(1)}, u32[]{:S(2)}, u32[]{:S(2)}) %collective-permute-start.17) | collective-permute-done | bytes 143392 | tf_op jit(solution)/shard_map/ppermute | solution.py:229
  27.5 1.1 %collective-permute-start.18 = (bf16[5,56,128]{2,1,0:T(8,128)(2,1)S(1)}, bf16[5,56,128]{2,1,0:T(8,128)(2,1)S(1)}, u32[]{:S(2)}, u32[]{:S(2)}) collective-permute-start(bf16[5,56,128]{2,1,0:T(8,128)(2,1)S(1)} %get-tuple-element.64), channel_id=1, source_target_pairs={{0,2},{2,0},{1,3},{3,1},{4,6},{6,4},{5,7},{7,5},{8,10},{10,8},{9,1... | collective-permute-start | bytes 215048 | tf_op jit(solution)/shard_map/ppermute | solution.py:229
  28.7 1.0 %collective-permute-start.21 = (bf16[5,56,128]{2,1,0:T(8,128)(2,1)S(1)}, bf16[5,56,128]{2,1,0:T(8,128)(2,1)S(1)}, u32[]{:S(2)}, u32[]{:S(2)}) collective-permute-start(bf16[5,56,128]{2,1,0:T(8,128)(2,1)S(1)} %get-tuple-element.68), channel_id=1, source_target_pairs={{0,2},{2,0},{1,3},{3,1},{4,6},{6,4},{5,7},{7,5},{8,10},{10,8},{9,1... | collective-permute-start | bytes 215048 | tf_op jit(solution)/shard_map/ppermute | solution.py:229
  29.8 1.1 %collective-permute-start.24 = (bf16[5,56,128]{2,1,0:T(8,128)(2,1)S(1)}, bf16[5,56,128]{2,1,0:T(8,128)(2,1)S(1)}, u32[]{:S(2)}, u32[]{:S(2)}) collective-permute-start(bf16[5,56,128]{2,1,0:T(8,128)(2,1)S(1)} %get-tuple-element.72), channel_id=1, source_target_pairs={{0,2},{2,0},{1,3},{3,1},{4,6},{6,4},{5,7},{7,5},{8,10},{10,8},{9,1... | collective-permute-start | bytes 215048 | tf_op jit(solution)/shard_map/ppermute | solution.py:229
  31.0 1.0 %collective-permute-start.7 = (bf16[8,56,128]{2,1,0:T(8,128)(2,1)S(1)}, bf16[8,56,128]{2,1,0:T(8,128)(2,1)S(1)}, u32[]{:S(2)}, u32[]{:S(2)}) collective-permute-start(bf16[8,56,128]{2,1,0:T(8,128)(2,1)S(1)} %get-tuple-element.57), channel_id=1, source_target_pairs={{0,2},{2,0},{1,3},{3,1},{4,6},{6,4},{5,7},{7,5},{8,10},{10,8},{9,1... | collective-permute-start | bytes 344072 | tf_op jit(solution)/shard_map/ppermute | solution.py:229
  32.0 0.6 %collective-permute-done.18.refs_1_ = bf16[5,56,128]{2,1,0:T(8,128)(2,1)S(1)} collective-permute-done((bf16[5,56,128]{2,1,0:T(8,128)(2,1)S(1)}, bf16[5,56,128]{2,1,0:T(8,128)(2,1)S(1)}, u32[]{:S(2)}, u32[]{:S(2)}) %collective-permute-start.18) | collective-permute-done | bytes 71712 | tf_op jit(solution)/shard_map/ppermute | solution.py:229
  32.7 2.3 %collective-permute-start.19 = (bf16[5,56,128]{2,1,0:T(8,128)(2,1)S(1)}, bf16[5,56,128]{2,1,0:T(8,128)(2,1)S(1)}, u32[]{:S(2)}, u32[]{:S(2)}) collective-permute-start(bf16[5,56,128]{2,1,0:T(8,128)(2,1)S(1)} %narrow_sum.3), channel_id=1, source_target_pairs={{0,12},{4,8},{8,4},{12,0},{1,13},{5,9},{9,5},{13,1},{2,14},{6,10},... | collective-permute-start | bytes 215048 | tf_op jit(solution)/shard_map/ppermute | solution.py:229
  35.0 0.6 %collective-permute-start.22 = (bf16[5,56,128]{2,1,0:T(8,128)(2,1)S(1)}, bf16[5,56,128]{2,1,0:T(8,128)(2,1)S(1)}, u32[]{:S(2)}, u32[]{:S(2)}) collective-permute-start(bf16[5,56,128]{2,1,0:T(8,128)(2,1)S(1)} %narrow_sum.4), channel_id=1, source_target_pairs={{0,8},{4,12},{8,0},{12,4},{1,9},{5,13},{9,1},{13,5},{2,10},{6,14},... | collective-permute-start | bytes 215048 | tf_op jit(solution)/shard_map/ppermute | solution.py:229
  35.7 1.6 %collective-permute-start.25 = (bf16[5,56,128]{2,1,0:T(8,128)(2,1)S(1)}, bf16[5,56,128]{2,1,0:T(8,128)(2,1)S(1)}, u32[]{:S(2)}, u32[]{:S(2)}) collective-permute-start(bf16[5,56,128]{2,1,0:T(8,128)(2,1)S(1)} %narrow_sum.5), channel_id=1, source_target_pairs={{0,4},{4,0},{8,12},{12,8},{1,5},{5,1},{9,13},{13,9},{2,6},{6,2},{1... | collective-permute-start | bytes 215048 | tf_op jit(solution)/shard_map/ppermute | solution.py:229
  37.5 2.1 %collective-permute-done.19.refs_2_ = bf16[5,56,128]{2,1,0:T(8,128)(2,1)S(1)} collective-permute-done((bf16[5,56,128]{2,1,0:T(8,128)(2,1)S(1)}, bf16[5,56,128]{2,1,0:T(8,128)(2,1)S(1)}, u32[]{:S(2)}, u32[]{:S(2)}) %collective-permute-start.19) | collective-permute-done | bytes 71712 | tf_op jit(solution)/shard_map/ppermute | solution.py:229
  39.6 1.5 %collective-permute-done.22.refs_3_ = bf16[5,56,128]{2,1,0:T(8,128)(2,1)S(1)} collective-permute-done((bf16[5,56,128]{2,1,0:T(8,128)(2,1)S(1)}, bf16[5,56,128]{2,1,0:T(8,128)(2,1)S(1)}, u32[]{:S(2)}, u32[]{:S(2)}) %collective-permute-start.22) | collective-permute-done | bytes 71712 | tf_op jit(solution)/shard_map/ppermute | solution.py:229
  41.1 0.8 %combine.1 = bf16[8,7168]{1,0:T(8,128)(2,1)} custom-call(s32[2,8]{1,0:T(2,128)S(4)} %get-tuple-element.39.route, f32[2,8]{1,0:T(2,128)S(4)} %get-tuple-element.40.gains, bf16[8,56,128]{2,1,0:T(8,128)(2,1)S(1)} %get-tuple-element.56.refs_0_, bf16[8,56,128]{2,1,0:T(8,128)(2,1)S(1)} %collective-permute-done.7.refs_1_, ...), custom_call_target="tpu_custom_call" | custom-call | tf_op jit(solution)/shard_map/combine/pallas_call | solution.py:241
  (44 shorter events, 1.1 us)
Async XLA Ops:
  0.0 10.4 %copy-start.3 = (bf16[7168,256]{1,0:T(8,128)(2,1)S(1)}, bf16[7168,256]{1,0:T(8,128)(2,1)}, u32[]{:S(2)}) copy-start(bf16[7168,256]{1,0:T(8,128)(2,1)} %refs_4_.1) | copy-start | bytes 11010052
  0.0 10.4 %copy-start.4 = (bf16[7168,256]{1,0:T(8,128)(2,1)S(1)}, bf16[7168,256]{1,0:T(8,128)(2,1)}, u32[]{:S(2)}) copy-start(bf16[7168,256]{1,0:T(8,128)(2,1)} %refs_5_.1) | copy-start | bytes 11010052
  0.0 10.4 %copy-start.5 = (bf16[256,7168]{1,0:T(8,128)(2,1)S(1)}, bf16[256,7168]{1,0:T(8,128)(2,1)}, u32[]{:S(2)}) copy-start(bf16[256,7168]{1,0:T(8,128)(2,1)} %refs_6_.1) | copy-start | bytes 11010052
  1.4 7.3 %collective-permute-start = (bf16[9,56,128]{2,1,0:T(8,128)(2,1)S(1)}, bf16[9,56,128]{2,1,0:T(8,128)(2,1)S(1)}, u32[]{:S(2)}, u32[]{:S(2)}) collective-permute-start(bf16[9,56,128]{2,1,0:T(8,128)(2,1)S(1)} %get-tuple-element.41.refs_0_), channel_id=1, source_target_pairs={{0,2},{1,3},{2,0},{3,1},{4,6},{5,7},{6,4},{7,5},{8,10},{9,11},{10,... | collective-permute-start | bytes 387080 | tf_op jit(solution)/shard_map/ppermute | solution.py:229
  4.4 6.0 %collective-permute-start.1 = (bf16[9,56,128]{2,1,0:T(8,128)(2,1)S(1)}, bf16[9,56,128]{2,1,0:T(8,128)(2,1)S(1)}, u32[]{:S(2)}, u32[]{:S(2)}) collective-permute-start(bf16[9,56,128]{2,1,0:T(8,128)(2,1)S(1)} %get-tuple-element.41.refs_0_), channel_id=1, source_target_pairs={{0,1},{1,0},{2,3},{3,2},{4,5},{5,4},{6,7},{7,6},{8,9},{9,8},{10,11... | collective-permute-start | bytes 387080 | tf_op jit(solution)/shard_map/ppermute | solution.py:229
  4.4 6.0 %collective-permute-start.2 = (bf16[9,56,128]{2,1,0:T(8,128)(2,1)S(1)}, bf16[9,56,128]{2,1,0:T(8,128)(2,1)S(1)}, u32[]{:S(2)}, u32[]{:S(2)}) collective-permute-start(bf16[9,56,128]{2,1,0:T(8,128)(2,1)S(1)} %get-tuple-element.41.refs_0_), channel_id=1, source_target_pairs={{0,3},{1,2},{2,1},{3,0},{4,7},{5,6},{6,5},{7,4},{8,11},{9,10},{10,... | collective-permute-start | bytes 387080 | tf_op jit(solution)/shard_map/ppermute | solution.py:229
  4.6 7.9 %collective-permute-start.3 = (bf16[5,56,128]{2,1,0:T(8,128)(2,1)S(1)}, bf16[5,56,128]{2,1,0:T(8,128)(2,1)S(1)}, u32[]{:S(2)}, u32[]{:S(2)}) collective-permute-start(bf16[5,56,128]{2,1,0:T(8,128)(2,1)S(1)} %get-tuple-element.45), channel_id=1, source_target_pairs={{0,12},{4,8},{8,4},{12,0},{1,13},{5,9},{9,5},{13,1},{2,14},{6,10},... | collective-permute-start | bytes 215048 | tf_op jit(solution)/shard_map/ppermute | solution.py:229
  8.6 6.2 %collective-permute-start.4 = (bf16[5,56,128]{2,1,0:T(8,128)(2,1)S(1)}, bf16[5,56,128]{2,1,0:T(8,128)(2,1)S(1)}, u32[]{:S(2)}, u32[]{:S(2)}) collective-permute-start(bf16[5,56,128]{2,1,0:T(8,128)(2,1)S(1)} %get-tuple-element.46), channel_id=1, source_target_pairs={{0,8},{4,12},{8,0},{12,4},{1,9},{5,13},{9,1},{13,5},{2,10},{6,14},... | collective-permute-start | bytes 215048 | tf_op jit(solution)/shard_map/ppermute | solution.py:229
  8.6 10.4 %copy-start = (bf16[1,7168,256]{2,1,0:T(8,128)(2,1)S(1)}, bf16[1,7168,256]{2,1,0:T(8,128)(2,1)}, u32[]{:S(2)}) copy-start(bf16[1,7168,256]{2,1,0:T(8,128)(2,1)} %param.16) | copy-start | bytes 11010052
  8.6 10.4 %copy-start.1 = (bf16[1,7168,256]{2,1,0:T(8,128)(2,1)S(1)}, bf16[1,7168,256]{2,1,0:T(8,128)(2,1)}, u32[]{:S(2)}) copy-start(bf16[1,7168,256]{2,1,0:T(8,128)(2,1)} %param.17) | copy-start | bytes 11010052
  8.7 10.4 %copy-start.2 = (bf16[1,256,7168]{2,1,0:T(8,128)(2,1)S(1)}, bf16[1,256,7168]{2,1,0:T(8,128)(2,1)}, u32[]{:S(2)}) copy-start(bf16[1,256,7168]{2,1,0:T(8,128)(2,1)} %param.18) | copy-start | bytes 11010052
  8.7 6.2 %collective-permute-start.5 = (bf16[5,56,128]{2,1,0:T(8,128)(2,1)S(1)}, bf16[5,56,128]{2,1,0:T(8,128)(2,1)S(1)}, u32[]{:S(2)}, u32[]{:S(2)}) collective-permute-start(bf16[5,56,128]{2,1,0:T(8,128)(2,1)S(1)} %get-tuple-element.47), channel_id=1, source_target_pairs={{0,4},{4,0},{8,12},{12,8},{1,5},{5,1},{9,13},{13,9},{2,6},{6,2},{1... | collective-permute-start | bytes 215048 | tf_op jit(solution)/shard_map/ppermute | solution.py:229
  14.9 6.3 %collective-permute-start.8 = (bf16[5,56,128]{2,1,0:T(8,128)(2,1)S(1)}, bf16[5,56,128]{2,1,0:T(8,128)(2,1)S(1)}, u32[]{:S(2)}, u32[]{:S(2)}) collective-permute-start(bf16[5,56,128]{2,1,0:T(8,128)(2,1)S(1)} %collective-permute-done.3.refs_0_), channel_id=1, source_target_pairs={{0,2},{2,0},{1,3},{3,1},{4,6},{6,4},{5,7},{7,5},{8,10},{10,8},{9,1... | collective-permute-start | bytes 215048 | tf_op jit(solution)/shard_map/ppermute | solution.py:229
  16.5 4.7 %collective-permute-start.9 = (bf16[5,56,128]{2,1,0:T(8,128)(2,1)S(1)}, bf16[5,56,128]{2,1,0:T(8,128)(2,1)S(1)}, u32[]{:S(2)}, u32[]{:S(2)}) collective-permute-start(bf16[5,56,128]{2,1,0:T(8,128)(2,1)S(1)} %collective-permute-done.4.refs_1_), channel_id=1, source_target_pairs={{0,2},{2,0},{1,3},{3,1},{4,6},{6,4},{5,7},{7,5},{8,10},{10,8},{9,1... | collective-permute-start | bytes 215048 | tf_op jit(solution)/shard_map/ppermute | solution.py:229
  16.9 5.2 %collective-permute-start.10 = (bf16[5,56,128]{2,1,0:T(8,128)(2,1)S(1)}, bf16[5,56,128]{2,1,0:T(8,128)(2,1)S(1)}, u32[]{:S(2)}, u32[]{:S(2)}) collective-permute-start(bf16[5,56,128]{2,1,0:T(8,128)(2,1)S(1)} %collective-permute-done.5.refs_2_), channel_id=1, source_target_pairs={{0,2},{2,0},{1,3},{3,1},{4,6},{6,4},{5,7},{7,5},{8,10},{10,8},{9,1... | collective-permute-start | bytes 215048 | tf_op jit(solution)/shard_map/ppermute | solution.py:229
  18.6 4.0 %collective-permute-start.11 = (bf16[5,56,128]{2,1,0:T(8,128)(2,1)S(1)}, bf16[5,56,128]{2,1,0:T(8,128)(2,1)S(1)}, u32[]{:S(2)}, u32[]{:S(2)}) collective-permute-start(bf16[5,56,128]{2,1,0:T(8,128)(2,1)S(1)} %collective-permute-done.3.refs_0_), channel_id=1, source_target_pairs={{0,1},{1,0},{2,3},{3,2},{4,5},{5,4},{6,7},{7,6},{8,9},{9,8},{10,11... | collective-permute-start | bytes 215048 | tf_op jit(solution)/shard_map/ppermute | solution.py:229
  18.6 4.0 %collective-permute-start.12 = (bf16[5,56,128]{2,1,0:T(8,128)(2,1)S(1)}, bf16[5,56,128]{2,1,0:T(8,128)(2,1)S(1)}, u32[]{:S(2)}, u32[]{:S(2)}) collective-permute-start(bf16[5,56,128]{2,1,0:T(8,128)(2,1)S(1)} %collective-permute-done.4.refs_1_), channel_id=1, source_target_pairs={{0,1},{1,0},{2,3},{3,2},{4,5},{5,4},{6,7},{7,6},{8,9},{9,8},{10,11... | collective-permute-start | bytes 215048 | tf_op jit(solution)/shard_map/ppermute | solution.py:229
  21.1 1.9 %collective-permute-start.13 = (bf16[5,56,128]{2,1,0:T(8,128)(2,1)S(1)}, bf16[5,56,128]{2,1,0:T(8,128)(2,1)S(1)}, u32[]{:S(2)}, u32[]{:S(2)}) collective-permute-start(bf16[5,56,128]{2,1,0:T(8,128)(2,1)S(1)} %collective-permute-done.5.refs_2_), channel_id=1, source_target_pairs={{0,1},{1,0},{2,3},{3,2},{4,5},{5,4},{6,7},{7,6},{8,9},{9,8},{10,11... | collective-permute-start | bytes 215048 | tf_op jit(solution)/shard_map/ppermute | solution.py:229
  22.0 1.3 %collective-permute-start.14 = (bf16[5,56,128]{2,1,0:T(8,128)(2,1)S(1)}, bf16[5,56,128]{2,1,0:T(8,128)(2,1)S(1)}, u32[]{:S(2)}, u32[]{:S(2)}) collective-permute-start(bf16[5,56,128]{2,1,0:T(8,128)(2,1)S(1)} %collective-permute-done.8.refs_3_), channel_id=1, source_target_pairs={{0,1},{1,0},{2,3},{3,2},{4,5},{5,4},{6,7},{7,6},{8,9},{9,8},{10,11... | collective-permute-start | bytes 215048 | tf_op jit(solution)/shard_map/ppermute | solution.py:229
  22.1 1.4 %collective-permute-start.15 = (bf16[5,56,128]{2,1,0:T(8,128)(2,1)S(1)}, bf16[5,56,128]{2,1,0:T(8,128)(2,1)S(1)}, u32[]{:S(2)}, u32[]{:S(2)}) collective-permute-start(bf16[5,56,128]{2,1,0:T(8,128)(2,1)S(1)} %collective-permute-done.9.refs_4_), channel_id=1, source_target_pairs={{0,1},{1,0},{2,3},{3,2},{4,5},{5,4},{6,7},{7,6},{8,9},{9,8},{10,11... | collective-permute-start | bytes 215048 | tf_op jit(solution)/shard_map/ppermute | solution.py:229
  22.6 1.3 %collective-permute-start.16 = (bf16[5,56,128]{2,1,0:T(8,128)(2,1)S(1)}, bf16[5,56,128]{2,1,0:T(8,128)(2,1)S(1)}, u32[]{:S(2)}, u32[]{:S(2)}) collective-permute-start(bf16[5,56,128]{2,1,0:T(8,128)(2,1)S(1)} %collective-permute-done.10.refs_5_), channel_id=1, source_target_pairs={{0,1},{1,0},{2,3},{3,2},{4,5},{5,4},{6,7},{7,6},{8,9},{9,8},{10,11... | collective-permute-start | bytes 215048 | tf_op jit(solution)/shard_map/ppermute | solution.py:229
  22.6 8.3 %collective-permute-start.6 = (bf16[2,8,56,128]{3,2,1,0:T(8,128)(2,1)S(1)}, bf16[2,8,56,128]{3,2,1,0:T(8,128)(2,1)S(1)}, u32[]{:S(2)}, u32[]{:S(2)}) collective-permute-start(bf16[2,8,56,128]{3,2,1,0:T(8,128)(2,1)S(1)} %get-tuple-element.55), channel_id=1, source_target_pairs={{0,1},{1,0},{2,3},{3,2},{4,5},{5,4},{6,7},{7,6},{8,9},{9,8},{10,11... | collective-permute-start | bytes 688136 | tf_op jit(solution)/shard_map/ppermute | solution.py:229
  26.1 1.4 %collective-permute-start.17 = (bf16[2,5,56,128]{3,2,1,0:T(8,128)(2,1)S(1)}, bf16[2,5,56,128]{3,2,1,0:T(8,128)(2,1)S(1)}, u32[]{:S(2)}, u32[]{:S(2)}) collective-permute-start(bf16[2,5,56,128]{3,2,1,0:T(8,128)(2,1)S(1)} %get-tuple-element.62), channel_id=1, source_target_pairs={{0,1},{1,0},{2,3},{3,2},{4,5},{5,4},{6,7},{7,6},{8,9},{9,8},{10,11... | collective-permute-start | bytes 430088 | tf_op jit(solution)/shard_map/ppermute | solution.py:229
  26.3 2.4 %collective-permute-start.20 = (bf16[2,5,56,128]{3,2,1,0:T(8,128)(2,1)S(1)}, bf16[2,5,56,128]{3,2,1,0:T(8,128)(2,1)S(1)}, u32[]{:S(2)}, u32[]{:S(2)}) collective-permute-start(bf16[2,5,56,128]{3,2,1,0:T(8,128)(2,1)S(1)} %get-tuple-element.66), channel_id=1, source_target_pairs={{0,1},{1,0},{2,3},{3,2},{4,5},{5,4},{6,7},{7,6},{8,9},{9,8},{10,11... | collective-permute-start | bytes 430088 | tf_op jit(solution)/shard_map/ppermute | solution.py:229
  26.6 3.1 %collective-permute-start.23 = (bf16[2,5,56,128]{3,2,1,0:T(8,128)(2,1)S(1)}, bf16[2,5,56,128]{3,2,1,0:T(8,128)(2,1)S(1)}, u32[]{:S(2)}, u32[]{:S(2)}) collective-permute-start(bf16[2,5,56,128]{3,2,1,0:T(8,128)(2,1)S(1)} %get-tuple-element.70), channel_id=1, source_target_pairs={{0,1},{1,0},{2,3},{3,2},{4,5},{5,4},{6,7},{7,6},{8,9},{9,8},{10,11... | collective-permute-start | bytes 430088 | tf_op jit(solution)/shard_map/ppermute | solution.py:229
  27.5 5.1 %collective-permute-start.18 = (bf16[5,56,128]{2,1,0:T(8,128)(2,1)S(1)}, bf16[5,56,128]{2,1,0:T(8,128)(2,1)S(1)}, u32[]{:S(2)}, u32[]{:S(2)}) collective-permute-start(bf16[5,56,128]{2,1,0:T(8,128)(2,1)S(1)} %get-tuple-element.64), channel_id=1, source_target_pairs={{0,2},{2,0},{1,3},{3,1},{4,6},{6,4},{5,7},{7,5},{8,10},{10,8},{9,1... | collective-permute-start | bytes 215048 | tf_op jit(solution)/shard_map/ppermute | solution.py:229
  28.7 6.3 %collective-permute-start.21 = (bf16[5,56,128]{2,1,0:T(8,128)(2,1)S(1)}, bf16[5,56,128]{2,1,0:T(8,128)(2,1)S(1)}, u32[]{:S(2)}, u32[]{:S(2)}) collective-permute-start(bf16[5,56,128]{2,1,0:T(8,128)(2,1)S(1)} %get-tuple-element.68), channel_id=1, source_target_pairs={{0,2},{2,0},{1,3},{3,1},{4,6},{6,4},{5,7},{7,5},{8,10},{10,8},{9,1... | collective-permute-start | bytes 215048 | tf_op jit(solution)/shard_map/ppermute | solution.py:229
  29.8 5.9 %collective-permute-start.24 = (bf16[5,56,128]{2,1,0:T(8,128)(2,1)S(1)}, bf16[5,56,128]{2,1,0:T(8,128)(2,1)S(1)}, u32[]{:S(2)}, u32[]{:S(2)}) collective-permute-start(bf16[5,56,128]{2,1,0:T(8,128)(2,1)S(1)} %get-tuple-element.72), channel_id=1, source_target_pairs={{0,2},{2,0},{1,3},{3,1},{4,6},{6,4},{5,7},{7,5},{8,10},{10,8},{9,1... | collective-permute-start | bytes 215048 | tf_op jit(solution)/shard_map/ppermute | solution.py:229
  31.0 6.5 %collective-permute-start.7 = (bf16[8,56,128]{2,1,0:T(8,128)(2,1)S(1)}, bf16[8,56,128]{2,1,0:T(8,128)(2,1)S(1)}, u32[]{:S(2)}, u32[]{:S(2)}) collective-permute-start(bf16[8,56,128]{2,1,0:T(8,128)(2,1)S(1)} %get-tuple-element.57), channel_id=1, source_target_pairs={{0,2},{2,0},{1,3},{3,1},{4,6},{6,4},{5,7},{7,5},{8,10},{10,8},{9,1... | collective-permute-start | bytes 344072 | tf_op jit(solution)/shard_map/ppermute | solution.py:229
  32.7 6.9 %collective-permute-start.19 = (bf16[5,56,128]{2,1,0:T(8,128)(2,1)S(1)}, bf16[5,56,128]{2,1,0:T(8,128)(2,1)S(1)}, u32[]{:S(2)}, u32[]{:S(2)}) collective-permute-start(bf16[5,56,128]{2,1,0:T(8,128)(2,1)S(1)} %narrow_sum.3), channel_id=1, source_target_pairs={{0,12},{4,8},{8,4},{12,0},{1,13},{5,9},{9,5},{13,1},{2,14},{6,10},... | collective-permute-start | bytes 215048 | tf_op jit(solution)/shard_map/ppermute | solution.py:229
  35.0 6.1 %collective-permute-start.22 = (bf16[5,56,128]{2,1,0:T(8,128)(2,1)S(1)}, bf16[5,56,128]{2,1,0:T(8,128)(2,1)S(1)}, u32[]{:S(2)}, u32[]{:S(2)}) collective-permute-start(bf16[5,56,128]{2,1,0:T(8,128)(2,1)S(1)} %narrow_sum.4), channel_id=1, source_target_pairs={{0,8},{4,12},{8,0},{12,4},{1,9},{5,13},{9,1},{13,5},{2,10},{6,14},... | collective-permute-start | bytes 215048 | tf_op jit(solution)/shard_map/ppermute | solution.py:229
  35.7 5.3 %collective-permute-start.25 = (bf16[5,56,128]{2,1,0:T(8,128)(2,1)S(1)}, bf16[5,56,128]{2,1,0:T(8,128)(2,1)S(1)}, u32[]{:S(2)}, u32[]{:S(2)}) collective-permute-start(bf16[5,56,128]{2,1,0:T(8,128)(2,1)S(1)} %narrow_sum.5), channel_id=1, source_target_pairs={{0,4},{4,0},{8,12},{12,8},{1,5},{5,1},{9,13},{13,9},{2,6},{6,2},{1... | collective-permute-start | bytes 215048 | tf_op jit(solution)/shard_map/ppermute | solution.py:229

commit v6 on v5

--- a/solution.py
+++ b/solution.py
@@ -20,8 +20,8 @@
 BF16 = jnp.bfloat16
 
 
-def put(flat, at, value, rows):
-    tall = flat.shape[0] // rows
+def put(flat, at, value, tall):
+    rows = value.shape[0]
     for b in range(value.shape[1] // LANES):
         flat[pl.ds(at // LANES + b, rows, stride=tall), :] = value[
             :, b * LANES : (b + 1) * LANES
@@ -85,7 +85,7 @@
         ref[...] = stage[(k + 1) * CAP : (k + 2) * CAP].astype(BF16)
 
 
-def unpack(refs, blocks, rows, flat, inputs):
+def unpack(refs, blocks, rows, flat, inputs, first=0):
     tall = inputs.shape[1] // LANES
     at = 0
     for ref, count in zip(refs, blocks):
@@ -96,7 +96,7 @@
     if at < rows:
         flat[at * tall : rows * tall, :] = jnp.zeros(((rows - at) * tall, LANES), F32)
     for b in range(tall):
-        inputs[:rows, b * LANES : (b + 1) * LANES] = flat[
+        inputs[first : first + rows, b * LANES : (b + 1) * LANES] = flat[
             pl.ds(b, rows, stride=tall), :
         ].astype(BF16)
 
@@ -130,49 +130,46 @@
         value[:, at] = jnp.dot(hidden, down_w[:, at], preferred_element_type=F32)
 
 
-def near_routed_kernel(n_narrow, n_pair, inputs, weight, value, gate_w, up_w, down_w, *refs):
-    outs, flat = refs[:n_pair], refs[n_pair]
-    rows, features = inputs.shape
-    tall = features // LANES
-    tokens = rows // (n_narrow * n_pair)
-    x = inputs[...]
-    gate = jnp.dot(x, gate_w[...], preferred_element_type=F32)
-    up = jnp.dot(x, up_w[...], preferred_element_type=F32)
-    hidden = silu_mul(gate, up)
-    gain = weight[:, :1]
-    for first in range(0, features, SPAN * LANES):
-        at = slice(first, first + SPAN * LANES)
-        routed = jnp.dot(hidden, down_w[:, at], preferred_element_type=F32)
-        put(flat, first, value[:, at] + gain * routed, rows)
-    each = n_narrow * tokens
-    for c in range(n_pair):
-        part = flat[c * each * tall : (c + 1) * each * tall, :]
-        outs[c][...] = part.reshape(n_narrow, tokens, tall, LANES).astype(BF16)
-
-
-def far_kernel(n_narrow, n_pair, per, *refs):
+def routed_kernel(n_narrow, n_pair, per, *refs):
     count = n_narrow * n_pair * per
     arrived, rest = refs[:count], refs[count:]
-    gate_w, up_w, down_w = rest[:3]
-    outs = rest[3 : 3 + n_pair * per]
-    flat, inputs = rest[3 + n_pair * per :]
+    near, weight, value, gate_w, up_w, down_w = rest[:6]
+    near_outs, outs = rest[6 : 6 + n_pair], rest[6 + n_pair : -2]
+    flat, inputs = rest[-2:]
     tall = arrived[0].shape[1]
+    near_rows = near.shape[0]
+    each = near_rows // n_pair
     blocks = [ref.shape[0] for ref in arrived]
     step = count if sum(blocks) <= MAX_ROWS else per
     for first in range(0, count, step):
         group = blocks[first : first + step]
+        head = 0 if first else near_rows
         rows = -(-sum(group) // 16) * 16
-        unpack(arrived[first : first + step], group, rows, flat, inputs)
-        x = inputs[:rows]
+        unpack(arrived[first : first + step], group, rows, flat, inputs, head)
+        if head:
+            inputs[:head] = near[...]
+        x = inputs[: head + rows]
         gate = jnp.dot(x, gate_w[...], preferred_element_type=F32)
         up = jnp.dot(x, up_w[...], preferred_element_type=F32)
         hidden = silu_mul(gate, up)
         for at in range(0, tall * LANES, SPAN * LANES):
-            value = jnp.dot(
+            part = jnp.dot(
                 hidden, down_w[:, at : at + SPAN * LANES], preferred_element_type=F32
             )
-            put(flat, at, value, rows)
-        at = 0
+            if head:
+                part = jnp.concatenate(
+                    [
+                        value[:, at : at + SPAN * LANES] + weight[:, :1] * part[:head],
+                        part[head:],
+                    ],
+                    axis=0,
+                )
+            put(flat, at, part, tall)
+        if head:
+            for c in range(n_pair):
+                part = flat[c * each * tall : (c + 1) * each * tall, :]
+                near_outs[c][...] = part.reshape(near_outs[c].shape).astype(BF16)
+        at = head
         for i, slots in enumerate(group):
             line, k = divmod(first + i, per)
             c, j = divmod(line, n_narrow)
@@ -204,13 +201,18 @@
 
 def combine_kernel(n_narrow, order, route, gains, *refs):
     near, rest = refs[:n_narrow], refs[n_narrow:]
-    far, (out, total, stage) = rest[:-3], rest[-3:]
+    far, direct = rest[: len(order)], rest[len(order) : -3]
+    out, total, stage = rest[-3:]
     rows, features = out.shape
     tall = features // LANES
     topk = route.shape[0]
     stage[:CAP] = jnp.zeros((CAP, tall, LANES), F32)
     for k, ref in zip(order, far):
         stage[k * CAP : (k + 1) * CAP] = ref[...].astype(F32)
+    arrived = direct[0][...].astype(F32)
+    for ref in direct[1:]:
+        arrived = arrived + ref[...].astype(F32)
+    stage[CAP : 2 * CAP] = arrived
     for t in range(rows):
         value = near[0][t].astype(F32)
         for ref in near[1:]:
@@ -305,18 +307,23 @@
         ],
     )
     far, (route, gains) = far[:-2], far[-2:]
-    order = list(range(n_wide - 1, 0, -1))
-    far = [swap(far[k - 1], "wide", k) for k in order]
-    beside = ("narrow", "pair")
-    near_all = [
-        swap(near, beside, j * n_pair + c) if j + c else near
-        for c in range(n_pair)
-        for j in range(n_narrow)
-    ]
+    order = list(range(n_wide - 1, 1, -1))
+    across = ("wide", "narrow")
+    bundles = [swap(far[k - 1], "wide", k) for k in order]
+    direct = [swap(far[0], across, n_narrow + j) for j in range(n_narrow)]
+    near_line = [near] + [swap(near, "narrow", j) for j in range(1, n_narrow)]
+    bundles = after(bundles, *direct)
     if n_wide > 4:
-        far = [jnp.concatenate(far, axis=0)]
-    per = len(far)
-    slots = far[0].shape[0]
+        bundles = [jnp.concatenate(bundles, axis=0)]
+    lines = [list(bundles)]
+    for j in range(1, n_narrow):
+        lines.append([swap(value, "narrow", j) for value in bundles])
+    per = len(bundles) + 1
+    slots = [value.shape[0] for value in bundles] + [CAP]
+    near_line = after(near_line, *bundles)
+    near_all = list(near_line)
+    for c in range(1, n_pair):
+        near_all += [swap(value, "pair", c) for value in near_line]
 
     near_rows = n_narrow * n_pair * tokens
     near_mid = call(
@@ -334,72 +341,70 @@
         moved=6 * features * hidden,
         limit=limit,
     )
-    far = after(far, near_mid[1])
-    far_side = []
-    for j in range(1, n_narrow):
-        far_side += [swap(value, "narrow", j) for value in far]
-    near_out = call(
-        functools.partial(near_routed_kernel, n_narrow, n_pair),
-        "near_routed",
-        after(near_mid, *far) + routed,
-        [VSPEC] * 6,
-        [block(n_narrow, tokens)] * n_pair,
-        [VMEM((near_rows * tall, LANES), F32)],
-        flops=6 * near_rows * features * hidden,
+    side = after([value for line in lines[1:] for value in line], near_mid[1])
+    far_line = []
+    for j in range(n_narrow):
+        far_line += lines[0] if j == 0 else side[(j - 1) * (per - 1) : j * (per - 1)]
+        far_line.append(direct[j])
+    far_all = list(far_line)
+    for c in range(1, n_pair):
+        far_all += [swap(value, "pair", c) for value in far_line]
+
+    far_rows = n_narrow * n_pair * sum(slots)
+    pass_rows = far_rows if far_rows <= MAX_ROWS else sum(slots)
+    pass_rows = near_rows + -(-pass_rows // 16) * 16
+    outs = call(
+        functools.partial(routed_kernel, n_narrow, n_pair, per),
+        "routed",
+        far_all + list(near_mid) + routed,
+        [VSPEC] * (n_narrow * n_pair * per + 6),
+        [block(n_narrow, tokens)] * n_pair
+        + [block(n_narrow, count) for count in slots] * n_pair,
+        [VMEM((pass_rows * tall, LANES), F32), VMEM((pass_rows, features), BF16)],
+        flops=6 * (near_rows + far_rows) * features * hidden,
         moved=6 * features * hidden,
         limit=limit,
     )
-    far_line = list(far) + after(far_side, near_out[0])
-    far_all = list(far_line)
-    for c in range(1, n_pair):
-        far_all += [swap(value, "pair", c) for value in far_line]
-
-    far_rows = n_narrow * n_pair * per * slots
-    pass_rows = far_rows if far_rows <= MAX_ROWS else per * slots
-    pass_rows = -(-pass_rows // 16) * 16
-    far_out = call(
-        functools.partial(far_kernel, n_narrow, n_pair, per),
-        "far",
-        far_all + list(routed),
-        [VSPEC] * (n_narrow * n_pair * per + 3),
-        [block(n_narrow, slots)] * (n_pair * per),
-        [VMEM((pass_rows * tall, LANES), F32), VMEM((pass_rows, features), BF16)],
-        flops=6 * far_rows * features * hidden,
-        moved=6 * features * hidden,
-        limit=limit,
-    )
-
-    def reduce_pair(parts, rows):
-        parts = [parts[0]] + [swap(parts[c], "pair", c) for c in range(1, n_pair)]
-        parts = call(
+    near_out, far_out = outs[:n_pair], outs[n_pair:]
+
+    def reduce_pair(parts, *first):
+        rows = parts[0].shape[1]
+        return call(
             functools.partial(pair_sum_kernel, n_pair),
             "pair_sum",
-            parts,
+            after([parts[0]] + [swap(parts[c], "pair", c) for c in range(1, n_pair)], *first),
             [VSPEC] * n_pair,
             [block(rows)] * n_narrow,
             [],
             limit=limit,
         )
+
+    def send_narrow(parts):
         return [parts[0]] + [swap(parts[j], "narrow", j) for j in range(1, n_narrow)]
 
     far_back = []
-    for k in range(per):
+    for k in range(per - 1):
         far_back += call(
             functools.partial(narrow_sum_kernel, n_narrow),
             "narrow_sum",
-            reduce_pair(far_out[k::per], slots),
+            send_narrow(reduce_pair(far_out[k::per])),
             [VSPEC] * n_narrow,
-            [block(CAP)] * (slots // CAP),
+            [block(CAP)] * (slots[k] // CAP),
             [],
             limit=limit,
         )
-    near_back = reduce_pair(near_out, tokens)
+    sums = far_back
     far_back = [swap(value, "wide", k) for k, value in zip(order, far_back)]
+    direct_back = reduce_pair(far_out[per - 1 :: per], sums[0])
+    near_back = send_narrow(reduce_pair(near_out))
+    direct_back = [
+        swap(value, across, n_narrow + j) for j, value in enumerate(direct_back)
+    ]
     return call(
         functools.partial(combine_kernel, n_narrow, order),
         "combine",
-        [route, gains] + near_back + far_back,
-        [SSPEC] * 2 + [VSPEC] * (n_narrow + n_wide - 1),
+        [route, gains] + near_back + far_back + direct_back,
+        [SSPEC] * 2 + [VSPEC] * (2 * n_narrow + len(order)),
         jax.ShapeDtypeStruct((tokens, features), BF16),
         [
             VMEM((tokens * tall, LANES), F32),

time: 42 us -> 43.5 us (1.036)
  waiting for transfers between devices: 9.24 us -> 14.4 us
  Pallas kernels: 8.66 us -> 6.69 us
  starting transfers between devices: 23.8 us -> 22.2 us
    ppermute x26, waiting for transfers between devices: 9.24 us -> 14.4 us  [swap(): return lax.ppermute(value, axis, [(i, i ^ offset) for i in range(size)])]
    pallas_call x12 -> x10, Pallas kernels: 8.66 us -> 6.69 us  [call(): pl.pallas_call(kernel, out_shape=outs, in_specs=specs, out_specs=jax.tree...]
    ppermute x26, starting transfers between devices: 23.8 us -> 22.2 us  [swap(): return lax.ppermute(value, axis, [(i, i ^ offset) for i in range(size)])]
  transfers between devices with their start and end apart: 26 -> 26, of which waited for: 12 -> 14; matrix products, arithmetic and copies ran while one was open for 0% -> 0% of each run, Pallas kernels for 16% -> 5%
where the time goes in v6:
time: 43.5 us; the launch traced here: 43.4 us
  starting transfers between devices  22.2 us (51%)
  waiting for transfers between devices  14.4 us (33%)
  Pallas kernels  6.69 us (15%)
    ppermute x26, starting transfers between devices, swap(): return lax.ppermute(value, axis, [(i, i ^ offset) for i in range(size)])  22.2 us
    ppermute x26, waiting for transfers between devices, swap(): return lax.ppermute(value, axis, [(i, i ^ offset) for i in range(size)])  14.4 us
    pallas_call x10, Pallas kernels, call(): pl.pallas_call(kernel, out_shape=outs, in_specs=specs, out_specs=jax.tree...  6.69 us
  transfers between devices with their start and end apart: 26, of which 14 were waited for; matrix products, arithmetic and copies ran while one was open for 0% of the time, Pallas kernels for 5%

profile of v6, /device:TPU:0, one launch (start us, length us, event | category | flops | bytes accessed | tf_op | source)
XLA Modules:
  0.0 43.4 jit_solution(4277597993767332652)
XLA Ops:
  0.0 1.4 %dispatch.1 = (bf16[9,56,128]{2,1,0:T(8,128)(2,1)S(1)}, bf16[5,56,128]{2,1,0:T(8,128)(2,1)S(1)}, bf16[5,56,128]{2,1,0:T(8,128)(2,1)S(1)}, bf16[5,56,128]{2,1,0:T...) custom-call(s32[2,8]{1,0:T(2,128)} %bitcast.11, s32[4]{0:T(128)} %place_in.1, f32[2,8]{1,0:T(2,128)} %bitcast.12, ...), custom_call_target="tpu_custom_call" | custom-call | tf_op jit(solution)/shard_map/dispatch/pallas_call | solution.py:243
  1.4 3.0 %collective-permute-start.6 = (bf16[9,56,128]{2,1,0:T(8,128)(2,1)S(1)}, bf16[9,56,128]{2,1,0:T(8,128)(2,1)S(1)}, u32[]{:S(2)}, u32[]{:S(2)}) collective-permute-start(bf16[9,56,128]{2,1,0:T(8,128)(2,1)S(1)} %get-tuple-element.52.refs_0_), channel_id=1, source_target_pairs={{0,2},{2,0},{1,3},{3,1},{4,6},{6,4},{5,7},{7,5},{8,10},{10,8},{9,1... | collective-permute-start | bytes 387080 | tf_op jit(solution)/shard_map/ppermute | solution.py:231
  4.4 3.6 %collective-permute-start = (bf16[5,56,128]{2,1,0:T(8,128)(2,1)S(1)}, bf16[5,56,128]{2,1,0:T(8,128)(2,1)S(1)}, u32[]{:S(2)}, u32[]{:S(2)}) collective-permute-start(bf16[5,56,128]{2,1,0:T(8,128)(2,1)S(1)} %get-tuple-element.46), channel_id=1, source_target_pairs={{0,12},{4,8},{8,4},{12,0},{1,13},{5,9},{9,5},{13,1},{2,14},{6,10},... | collective-permute-start | bytes 215048 | tf_op jit(solution)/shard_map/ppermute | solution.py:231
  8.0 0.5 %collective-permute-start.3 = (bf16[5,56,128]{2,1,0:T(8,128)(2,1)S(1)}, bf16[5,56,128]{2,1,0:T(8,128)(2,1)S(1)}, u32[]{:S(2)}, u32[]{:S(2)}) collective-permute-start(bf16[5,56,128]{2,1,0:T(8,128)(2,1)S(1)} %get-tuple-element.48), channel_id=1, source_target_pairs={{0,6},{2,4},{4,2},{6,0},{8,14},{10,12},{12,10},{14,8},{1,7},{3,5},... | collective-permute-start | bytes 215048 | tf_op jit(solution)/shard_map/ppermute | solution.py:231
  8.5 1.5 %collective-permute-start.2 = (bf16[5,56,128]{2,1,0:T(8,128)(2,1)S(1)}, bf16[5,56,128]{2,1,0:T(8,128)(2,1)S(1)}, u32[]{:S(2)}, u32[]{:S(2)}) collective-permute-start(bf16[5,56,128]{2,1,0:T(8,128)(2,1)S(1)} %get-tuple-element.48), channel_id=1, source_target_pairs={{0,4},{2,6},{4,0},{6,2},{8,12},{10,14},{12,8},{14,10},{1,5},{3,7},... | collective-permute-start | bytes 215048 | tf_op jit(solution)/shard_map/ppermute | solution.py:231
  10.1 1.3 %collective-permute-done.refs_0_ = bf16[5,56,128]{2,1,0:T(8,128)(2,1)S(1)} collective-permute-done((bf16[5,56,128]{2,1,0:T(8,128)(2,1)S(1)}, bf16[5,56,128]{2,1,0:T(8,128)(2,1)S(1)}, u32[]{:S(2)}, u32[]{:S(2)}) %collective-permute-start) | collective-permute-done | bytes 71712 | tf_op jit(solution)/shard_map/ppermute | solution.py:231
  11.4 2.4 %collective-permute-done.1.refs_1_ = bf16[5,56,128]{2,1,0:T(8,128)(2,1)S(1)} collective-permute-done((bf16[5,56,128]{2,1,0:T(8,128)(2,1)S(1)}, bf16[5,56,128]{2,1,0:T(8,128)(2,1)S(1)}, u32[]{:S(2)}, u32[]{:S(2)}) %collective-permute-start.1) | collective-permute-done | bytes 71712 | tf_op jit(solution)/shard_map/ppermute | solution.py:231
  13.8 0.9 %collective-permute-done.3.refs_5_ = bf16[5,56,128]{2,1,0:T(8,128)(2,1)S(1)} collective-permute-done((bf16[5,56,128]{2,1,0:T(8,128)(2,1)S(1)}, bf16[5,56,128]{2,1,0:T(8,128)(2,1)S(1)}, u32[]{:S(2)}, u32[]{:S(2)}) %collective-permute-start.3) | collective-permute-done | bytes 71712 | tf_op jit(solution)/shard_map/ppermute | solution.py:231
  14.7 0.6 %collective-permute-done.2.refs_2_ = bf16[5,56,128]{2,1,0:T(8,128)(2,1)S(1)} collective-permute-done((bf16[5,56,128]{2,1,0:T(8,128)(2,1)S(1)}, bf16[5,56,128]{2,1,0:T(8,128)(2,1)S(1)}, u32[]{:S(2)}, u32[]{:S(2)}) %collective-permute-start.2) | collective-permute-done | bytes 71712 | tf_op jit(solution)/shard_map/ppermute | solution.py:231
  15.3 0.5 %collective-permute-start.8 = (bf16[9,56,128]{2,1,0:T(8,128)(2,1)S(1)}, bf16[9,56,128]{2,1,0:T(8,128)(2,1)S(1)}, u32[]{:S(2)}, u32[]{:S(2)}) collective-permute-start(bf16[9,56,128]{2,1,0:T(8,128)(2,1)S(1)} %collective-permute-done.6.refs_1_), channel_id=1, source_target_pairs={{0,1},{1,0},{2,3},{3,2},{4,5},{5,4},{6,7},{7,6},{8,9},{9,8},{10,11... | collective-permute-start | bytes 387080 | tf_op jit(solution)/shard_map/ppermute | solution.py:231
  15.8 0.8 %collective-permute-start.4 = (bf16[5,56,128]{2,1,0:T(8,128)(2,1)S(1)}, bf16[5,56,128]{2,1,0:T(8,128)(2,1)S(1)}, u32[]{:S(2)}, u32[]{:S(2)}) collective-permute-start(bf16[5,56,128]{2,1,0:T(8,128)(2,1)S(1)} %collective-permute-done.refs_0_), channel_id=1, source_target_pairs={{0,2},{2,0},{1,3},{3,1},{4,6},{6,4},{5,7},{7,5},{8,10},{10,8},{9,1... | collective-permute-start | bytes 215048 | tf_op jit(solution)/shard_map/ppermute | solution.py:231
  16.5 1.3 %collective-permute-start.5 = (bf16[5,56,128]{2,1,0:T(8,128)(2,1)S(1)}, bf16[5,56,128]{2,1,0:T(8,128)(2,1)S(1)}, u32[]{:S(2)}, u32[]{:S(2)}) collective-permute-start(bf16[5,56,128]{2,1,0:T(8,128)(2,1)S(1)} %collective-permute-done.1.refs_1_), channel_id=1, source_target_pairs={{0,2},{2,0},{1,3},{3,1},{4,6},{6,4},{5,7},{7,5},{8,10},{10,8},{9,1... | collective-permute-start | bytes 215048 | tf_op jit(solution)/shard_map/ppermute | solution.py:231
  17.8 0.5 %collective-permute-start.9 = (bf16[5,56,128]{2,1,0:T(8,128)(2,1)S(1)}, bf16[5,56,128]{2,1,0:T(8,128)(2,1)S(1)}, u32[]{:S(2)}, u32[]{:S(2)}) collective-permute-start(bf16[5,56,128]{2,1,0:T(8,128)(2,1)S(1)} %collective-permute-done.refs_0_), channel_id=1, source_target_pairs={{0,1},{1,0},{2,3},{3,2},{4,5},{5,4},{6,7},{7,6},{8,9},{9,8},{10,11... | collective-permute-start | bytes 215048 | tf_op jit(solution)/shard_map/ppermute | solution.py:231
  18.4 2.0 %near_shared.1 = (bf16[32,7168]{1,0:T(8,128)(2,1)S(1)}, f32[32,128]{1,0:T(8,128)S(1)}, f32[32,7168]{1,0:T(8,128)S(1)}) custom-call(bf16[9,56,128]{2,1,0:T(8,128)(2,1)S(1)} %get-tuple-element.52.refs_0_, bf16[9,56,128]{2,1,0:T(8,128)(2,1)S(1)} %collective-permute-done.6.refs_1_, bf16[9,56,128]{2,1,0:T(8,128)(2,1)S(1)} %collective-permute-done.7.refs_2_, ...), custom_call_target="tpu_custom_call" | custom-call | flops 352321536 | bytes 11010048 | tf_op jit(solution)/shard_map/near_shared/pallas_call | solution.py:243
  21.0 0.5 %collective-permute-done.5.refs_4_ = bf16[5,56,128]{2,1,0:T(8,128)(2,1)S(1)} collective-permute-done((bf16[5,56,128]{2,1,0:T(8,128)(2,1)S(1)}, bf16[5,56,128]{2,1,0:T(8,128)(2,1)S(1)}, u32[]{:S(2)}, u32[]{:S(2)}) %collective-permute-start.5) | collective-permute-done | bytes 71712 | tf_op jit(solution)/shard_map/ppermute | solution.py:231
  21.4 0.5 %collective-permute-start.13 = (bf16[5,56,128]{2,1,0:T(8,128)(2,1)S(1)}, bf16[5,56,128]{2,1,0:T(8,128)(2,1)S(1)}, u32[]{:S(2)}, u32[]{:S(2)}) collective-permute-start(bf16[5,56,128]{2,1,0:T(8,128)(2,1)S(1)} %collective-permute-done.5.refs_4_), channel_id=1, source_target_pairs={{0,1},{1,0},{2,3},{3,2},{4,5},{5,4},{6,7},{7,6},{8,9},{9,8},{10,11... | collective-permute-start | bytes 215048 | tf_op jit(solution)/shard_map/ppermute | solution.py:231
  22.0 0.7 %collective-permute-done.12.refs_9_ = bf16[5,56,128]{2,1,0:T(8,128)(2,1)S(1)} collective-permute-done((bf16[5,56,128]{2,1,0:T(8,128)(2,1)S(1)}, bf16[5,56,128]{2,1,0:T(8,128)(2,1)S(1)}, u32[]{:S(2)}, u32[]{:S(2)}) %collective-permute-start.12) | collective-permute-done | bytes 71712 | tf_op jit(solution)/shard_map/ppermute | solution.py:231
  22.9 2.3 %routed.1 = (bf16[2,8,56,128]{3,2,1,0:T(8,128)(2,1)S(1)}, bf16[2,8,56,128]{3,2,1,0:T(8,128)(2,1)S(1)}, bf16[2,5,56,128]{3,2,1,0:T(8,128)(2,1)S(1)}, bf16[2,5,56,...) custom-call(bf16[5,56,128]{2,1,0:T(8,128)(2,1)S(1)} %collective-perm, ...), custom_call_target="tpu_custom_call" | custom-call | flops 1012924416 | bytes 11010048 | tf_op jit(solution)/shard_map/routed/pallas_call | solution.py:243
  25.2 0.4 collective-permute-start.15
  26.3 0.7 %collective-permute-done.17.refs_1_ = bf16[2,5,56,128]{3,2,1,0:T(8,128)(2,1)S(1)} collective-permute-done((bf16[2,5,56,128]{3,2,1,0:T(8,128)(2,1)S(1)}, bf16[2,5,56,128]{3,2,1,0:T(8,128)(2,1)S(1)}, u32[]{:S(2)}, u32[]{:S(2)}) %collective-permute-start.17) | collective-permute-done | bytes 143392 | tf_op jit(solution)/shard_map/ppermute | solution.py:231
  27.0 1.0 %collective-permute-start.18 = (bf16[5,56,128]{2,1,0:T(8,128)(2,1)S(1)}, bf16[5,56,128]{2,1,0:T(8,128)(2,1)S(1)}, u32[]{:S(2)}, u32[]{:S(2)}) collective-permute-start(bf16[5,56,128]{2,1,0:T(8,128)(2,1)S(1)} %get-tuple-element.70), channel_id=1, source_target_pairs={{0,2},{2,0},{1,3},{3,1},{4,6},{6,4},{5,7},{7,5},{8,10},{10,8},{9,1... | collective-permute-start | bytes 215048 | tf_op jit(solution)/shard_map/ppermute | solution.py:231
  28.1 1.1 %collective-permute-start.21 = (bf16[5,56,128]{2,1,0:T(8,128)(2,1)S(1)}, bf16[5,56,128]{2,1,0:T(8,128)(2,1)S(1)}, u32[]{:S(2)}, u32[]{:S(2)}) collective-permute-start(bf16[5,56,128]{2,1,0:T(8,128)(2,1)S(1)} %get-tuple-element.76), channel_id=1, source_target_pairs={{0,2},{2,0},{1,3},{3,1},{4,6},{6,4},{5,7},{7,5},{8,10},{10,8},{9,1... | collective-permute-start | bytes 215048 | tf_op jit(solution)/shard_map/ppermute | solution.py:231
  29.3 1.0 %collective-permute-start.16 = (bf16[8,56,128]{2,1,0:T(8,128)(2,1)S(1)}, bf16[8,56,128]{2,1,0:T(8,128)(2,1)S(1)}, u32[]{:S(2)}, u32[]{:S(2)}) collective-permute-start(bf16[8,56,128]{2,1,0:T(8,128)(2,1)S(1)} %get-tuple-element.64), channel_id=1, source_target_pairs={{0,2},{2,0},{1,3},{3,1},{4,6},{6,4},{5,7},{7,5},{8,10},{10,8},{9,1... | collective-permute-start | bytes 344072 | tf_op jit(solution)/shard_map/ppermute | solution.py:231
  30.3 1.8 %collective-permute-done.18.refs_1_ = bf16[5,56,128]{2,1,0:T(8,128)(2,1)S(1)} collective-permute-done((bf16[5,56,128]{2,1,0:T(8,128)(2,1)S(1)}, bf16[5,56,128]{2,1,0:T(8,128)(2,1)S(1)}, u32[]{:S(2)}, u32[]{:S(2)}) %collective-permute-start.18) | collective-permute-done | bytes 71712 | tf_op jit(solution)/shard_map/ppermute | solution.py:231
  32.1 2.3 %collective-permute-start.19 = (bf16[5,56,128]{2,1,0:T(8,128)(2,1)S(1)}, bf16[5,56,128]{2,1,0:T(8,128)(2,1)S(1)}, u32[]{:S(2)}, u32[]{:S(2)}) collective-permute-start(bf16[5,56,128]{2,1,0:T(8,128)(2,1)S(1)} %narrow_sum.2), channel_id=1, source_target_pairs={{0,12},{4,8},{8,4},{12,0},{1,13},{5,9},{9,5},{13,1},{2,14},{6,10},... | collective-permute-start | bytes 215048 | tf_op jit(solution)/shard_map/ppermute | solution.py:231
  34.9 1.9 %collective-permute-start.24 = (bf16[5,56,128]{2,1,0:T(8,128)(2,1)S(1)}, bf16[5,56,128]{2,1,0:T(8,128)(2,1)S(1)}, u32[]{:S(2)}, u32[]{:S(2)}) collective-permute-start(bf16[5,56,128]{2,1,0:T(8,128)(2,1)S(1)} %get-tuple-element.81), channel_id=1, source_target_pairs={{0,4},{2,6},{4,0},{6,2},{8,12},{10,14},{12,8},{14,10},{1,5},{3,7},... | collective-permute-start | bytes 215048 | tf_op jit(solution)/shard_map/ppermute | solution.py:231
  36.8 0.7 %collective-permute-start.25 = (bf16[5,56,128]{2,1,0:T(8,128)(2,1)S(1)}, bf16[5,56,128]{2,1,0:T(8,128)(2,1)S(1)}, u32[]{:S(2)}, u32[]{:S(2)}) collective-permute-start(bf16[5,56,128]{2,1,0:T(8,128)(2,1)S(1)} %get-tuple-element.82), channel_id=1, source_target_pairs={{0,6},{2,4},{4,2},{6,0},{8,14},{10,12},{12,10},{14,8},{1,7},{3,5},... | collective-permute-start | bytes 215048 | tf_op jit(solution)/shard_map/ppermute | solution.py:231
  37.6 1.2 %collective-permute-done.19.refs_2_ = bf16[5,56,128]{2,1,0:T(8,128)(2,1)S(1)} collective-permute-done((bf16[5,56,128]{2,1,0:T(8,128)(2,1)S(1)}, bf16[5,56,128]{2,1,0:T(8,128)(2,1)S(1)}, u32[]{:S(2)}, u32[]{:S(2)}) %collective-permute-start.19) | collective-permute-done | bytes 71712 | tf_op jit(solution)/shard_map/ppermute | solution.py:231
  38.7 2.2 %collective-permute-done.22.refs_3_ = bf16[5,56,128]{2,1,0:T(8,128)(2,1)S(1)} collective-permute-done((bf16[5,56,128]{2,1,0:T(8,128)(2,1)S(1)}, bf16[5,56,128]{2,1,0:T(8,128)(2,1)S(1)}, u32[]{:S(2)}, u32[]{:S(2)}) %collective-permute-start.22) | collective-permute-done | bytes 71712 | tf_op jit(solution)/shard_map/ppermute | solution.py:231
  40.9 0.4 collective-permute-done.24.refs_4_
  41.3 1.2 %collective-permute-done.25.refs_5_ = bf16[5,56,128]{2,1,0:T(8,128)(2,1)S(1)} collective-permute-done((bf16[5,56,128]{2,1,0:T(8,128)(2,1)S(1)}, bf16[5,56,128]{2,1,0:T(8,128)(2,1)S(1)}, u32[]{:S(2)}, u32[]{:S(2)}) %collective-permute-start.25) | collective-permute-done | bytes 71712 | tf_op jit(solution)/shard_map/ppermute | solution.py:231
  42.6 0.8 %combine.1 = bf16[8,7168]{1,0:T(8,128)(2,1)} custom-call(s32[2,8]{1,0:T(2,128)S(4)} %get-tuple-element.44.route, f32[2,8]{1,0:T(2,128)S(4)} %get-tuple-element.45.gains, bf16[8,56,128]{2,1,0:T(8,128)(2,1)S(1)} %get-tuple-element.63.refs_0_, bf16[8,56,128]{2,1,0:T(8,128)(2,1)S(1)} %collective-permute-done.16.refs_1_, ...), custom_call_target="tpu_custom_call" | custom-call | tf_op jit(solution)/shard_map/combine/pallas_call | solution.py:243
  (42 shorter events, 2.0 us)
Async XLA Ops:
  0.0 18.4 %copy-start = (bf16[7168,256]{1,0:T(8,128)(2,1)S(1)}, bf16[7168,256]{1,0:T(8,128)(2,1)}, u32[]{:S(2)}) copy-start(bf16[7168,256]{1,0:T(8,128)(2,1)} %refs_4_.1) | copy-start | bytes 11010052
  0.0 18.4 %copy-start.1 = (bf16[7168,256]{1,0:T(8,128)(2,1)S(1)}, bf16[7168,256]{1,0:T(8,128)(2,1)}, u32[]{:S(2)}) copy-start(bf16[7168,256]{1,0:T(8,128)(2,1)} %refs_5_.1) | copy-start | bytes 11010052
  0.0 18.4 %copy-start.2 = (bf16[256,7168]{1,0:T(8,128)(2,1)S(1)}, bf16[256,7168]{1,0:T(8,128)(2,1)}, u32[]{:S(2)}) copy-start(bf16[256,7168]{1,0:T(8,128)(2,1)} %refs_6_.1) | copy-start | bytes 11010052
  1.4 13.9 %collective-permute-start.6 = (bf16[9,56,128]{2,1,0:T(8,128)(2,1)S(1)}, bf16[9,56,128]{2,1,0:T(8,128)(2,1)S(1)}, u32[]{:S(2)}, u32[]{:S(2)}) collective-permute-start(bf16[9,56,128]{2,1,0:T(8,128)(2,1)S(1)} %get-tuple-element.52.refs_0_), channel_id=1, source_target_pairs={{0,2},{2,0},{1,3},{3,1},{4,6},{6,4},{5,7},{7,5},{8,10},{10,8},{9,1... | collective-permute-start | bytes 387080 | tf_op jit(solution)/shard_map/ppermute | solution.py:231
  4.4 7.0 %collective-permute-start = (bf16[5,56,128]{2,1,0:T(8,128)(2,1)S(1)}, bf16[5,56,128]{2,1,0:T(8,128)(2,1)S(1)}, u32[]{:S(2)}, u32[]{:S(2)}) collective-permute-start(bf16[5,56,128]{2,1,0:T(8,128)(2,1)S(1)} %get-tuple-element.46), channel_id=1, source_target_pairs={{0,12},{4,8},{8,4},{12,0},{1,13},{5,9},{9,5},{13,1},{2,14},{6,10},... | collective-permute-start | bytes 215048 | tf_op jit(solution)/shard_map/ppermute | solution.py:231
  8.0 5.8 %collective-permute-start.1 = (bf16[5,56,128]{2,1,0:T(8,128)(2,1)S(1)}, bf16[5,56,128]{2,1,0:T(8,128)(2,1)S(1)}, u32[]{:S(2)}, u32[]{:S(2)}) collective-permute-start(bf16[5,56,128]{2,1,0:T(8,128)(2,1)S(1)} %get-tuple-element.47), channel_id=1, source_target_pairs={{0,8},{4,12},{8,0},{12,4},{1,9},{5,13},{9,1},{13,5},{2,10},{6,14},... | collective-permute-start | bytes 215048 | tf_op jit(solution)/shard_map/ppermute | solution.py:231
  8.0 14.9 %copy-start.3 = (bf16[1,7168,256]{2,1,0:T(8,128)(2,1)S(1)}, bf16[1,7168,256]{2,1,0:T(8,128)(2,1)}, u32[]{:S(2)}) copy-start(bf16[1,7168,256]{2,1,0:T(8,128)(2,1)} %param.16) | copy-start | bytes 11010052
  8.0 14.9 %copy-start.4 = (bf16[1,7168,256]{2,1,0:T(8,128)(2,1)S(1)}, bf16[1,7168,256]{2,1,0:T(8,128)(2,1)}, u32[]{:S(2)}) copy-start(bf16[1,7168,256]{2,1,0:T(8,128)(2,1)} %param.17) | copy-start | bytes 11010052
  8.0 14.9 %copy-start.5 = (bf16[1,256,7168]{2,1,0:T(8,128)(2,1)S(1)}, bf16[1,256,7168]{2,1,0:T(8,128)(2,1)}, u32[]{:S(2)}) copy-start(bf16[1,256,7168]{2,1,0:T(8,128)(2,1)} %param.18) | copy-start | bytes 11010052
  8.0 6.7 %collective-permute-start.3 = (bf16[5,56,128]{2,1,0:T(8,128)(2,1)S(1)}, bf16[5,56,128]{2,1,0:T(8,128)(2,1)S(1)}, u32[]{:S(2)}, u32[]{:S(2)}) collective-permute-start(bf16[5,56,128]{2,1,0:T(8,128)(2,1)S(1)} %get-tuple-element.48), channel_id=1, source_target_pairs={{0,6},{2,4},{4,2},{6,0},{8,14},{10,12},{12,10},{14,8},{1,7},{3,5},... | collective-permute-start | bytes 215048 | tf_op jit(solution)/shard_map/ppermute | solution.py:231
  8.5 6.7 %collective-permute-start.2 = (bf16[5,56,128]{2,1,0:T(8,128)(2,1)S(1)}, bf16[5,56,128]{2,1,0:T(8,128)(2,1)S(1)}, u32[]{:S(2)}, u32[]{:S(2)}) collective-permute-start(bf16[5,56,128]{2,1,0:T(8,128)(2,1)S(1)} %get-tuple-element.48), channel_id=1, source_target_pairs={{0,4},{2,6},{4,0},{6,2},{8,12},{10,14},{12,8},{14,10},{1,5},{3,7},... | collective-permute-start | bytes 215048 | tf_op jit(solution)/shard_map/ppermute | solution.py:231
  15.3 2.5 %collective-permute-start.7 = (bf16[9,56,128]{2,1,0:T(8,128)(2,1)S(1)}, bf16[9,56,128]{2,1,0:T(8,128)(2,1)S(1)}, u32[]{:S(2)}, u32[]{:S(2)}) collective-permute-start(bf16[9,56,128]{2,1,0:T(8,128)(2,1)S(1)} %get-tuple-element.52.refs_0_), channel_id=1, source_target_pairs={{0,1},{1,0},{2,3},{3,2},{4,5},{5,4},{6,7},{7,6},{8,9},{9,8},{10,11... | collective-permute-start | bytes 387080 | tf_op jit(solution)/shard_map/ppermute | solution.py:231
  15.3 3.1 %collective-permute-start.8 = (bf16[9,56,128]{2,1,0:T(8,128)(2,1)S(1)}, bf16[9,56,128]{2,1,0:T(8,128)(2,1)S(1)}, u32[]{:S(2)}, u32[]{:S(2)}) collective-permute-start(bf16[9,56,128]{2,1,0:T(8,128)(2,1)S(1)} %collective-permute-done.6.refs_1_), channel_id=1, source_target_pairs={{0,1},{1,0},{2,3},{3,2},{4,5},{5,4},{6,7},{7,6},{8,9},{9,8},{10,11... | collective-permute-start | bytes 387080 | tf_op jit(solution)/shard_map/ppermute | solution.py:231
  15.8 4.9 %collective-permute-start.4 = (bf16[5,56,128]{2,1,0:T(8,128)(2,1)S(1)}, bf16[5,56,128]{2,1,0:T(8,128)(2,1)S(1)}, u32[]{:S(2)}, u32[]{:S(2)}) collective-permute-start(bf16[5,56,128]{2,1,0:T(8,128)(2,1)S(1)} %collective-permute-done.refs_0_), channel_id=1, source_target_pairs={{0,2},{2,0},{1,3},{3,1},{4,6},{6,4},{5,7},{7,5},{8,10},{10,8},{9,1... | collective-permute-start | bytes 215048 | tf_op jit(solution)/shard_map/ppermute | solution.py:231
  16.5 4.9 %collective-permute-start.5 = (bf16[5,56,128]{2,1,0:T(8,128)(2,1)S(1)}, bf16[5,56,128]{2,1,0:T(8,128)(2,1)S(1)}, u32[]{:S(2)}, u32[]{:S(2)}) collective-permute-start(bf16[5,56,128]{2,1,0:T(8,128)(2,1)S(1)} %collective-permute-done.1.refs_1_), channel_id=1, source_target_pairs={{0,2},{2,0},{1,3},{3,1},{4,6},{6,4},{5,7},{7,5},{8,10},{10,8},{9,1... | collective-permute-start | bytes 215048 | tf_op jit(solution)/shard_map/ppermute | solution.py:231
  17.8 3.6 %collective-permute-start.14 = (bf16[5,56,128]{2,1,0:T(8,128)(2,1)S(1)}, bf16[5,56,128]{2,1,0:T(8,128)(2,1)S(1)}, u32[]{:S(2)}, u32[]{:S(2)}) collective-permute-start(bf16[5,56,128]{2,1,0:T(8,128)(2,1)S(1)} %collective-permute-done.3.refs_5_), channel_id=1, source_target_pairs={{0,1},{1,0},{2,3},{3,2},{4,5},{5,4},{6,7},{7,6},{8,9},{9,8},{10,11... | collective-permute-start | bytes 215048 | tf_op jit(solution)/shard_map/ppermute | solution.py:231
  17.8 4.2 %collective-permute-start.9 = (bf16[5,56,128]{2,1,0:T(8,128)(2,1)S(1)}, bf16[5,56,128]{2,1,0:T(8,128)(2,1)S(1)}, u32[]{:S(2)}, u32[]{:S(2)}) collective-permute-start(bf16[5,56,128]{2,1,0:T(8,128)(2,1)S(1)} %collective-permute-done.refs_0_), channel_id=1, source_target_pairs={{0,1},{1,0},{2,3},{3,2},{4,5},{5,4},{6,7},{7,6},{8,9},{9,8},{10,11... | collective-permute-start | bytes 215048 | tf_op jit(solution)/shard_map/ppermute | solution.py:231
  18.3 3.6 %collective-permute-start.10 = (bf16[5,56,128]{2,1,0:T(8,128)(2,1)S(1)}, bf16[5,56,128]{2,1,0:T(8,128)(2,1)S(1)}, u32[]{:S(2)}, u32[]{:S(2)}) collective-permute-start(bf16[5,56,128]{2,1,0:T(8,128)(2,1)S(1)} %collective-permute-done.1.refs_1_), channel_id=1, source_target_pairs={{0,1},{1,0},{2,3},{3,2},{4,5},{5,4},{6,7},{7,6},{8,9},{9,8},{10,11... | collective-permute-start | bytes 215048 | tf_op jit(solution)/shard_map/ppermute | solution.py:231
  20.7 1.3 %collective-permute-start.11 = (bf16[5,56,128]{2,1,0:T(8,128)(2,1)S(1)}, bf16[5,56,128]{2,1,0:T(8,128)(2,1)S(1)}, u32[]{:S(2)}, u32[]{:S(2)}) collective-permute-start(bf16[5,56,128]{2,1,0:T(8,128)(2,1)S(1)} %collective-permute-done.2.refs_2_), channel_id=1, source_target_pairs={{0,1},{1,0},{2,3},{3,2},{4,5},{5,4},{6,7},{7,6},{8,9},{9,8},{10,11... | collective-permute-start | bytes 215048 | tf_op jit(solution)/shard_map/ppermute | solution.py:231
  21.4 1.3 %collective-permute-start.12 = (bf16[5,56,128]{2,1,0:T(8,128)(2,1)S(1)}, bf16[5,56,128]{2,1,0:T(8,128)(2,1)S(1)}, u32[]{:S(2)}, u32[]{:S(2)}) collective-permute-start(bf16[5,56,128]{2,1,0:T(8,128)(2,1)S(1)} %collective-permute-done.4.refs_3_), channel_id=1, source_target_pairs={{0,1},{1,0},{2,3},{3,2},{4,5},{5,4},{6,7},{7,6},{8,9},{9,8},{10,11... | collective-permute-start | bytes 215048 | tf_op jit(solution)/shard_map/ppermute | solution.py:231
  21.4 1.4 %collective-permute-start.13 = (bf16[5,56,128]{2,1,0:T(8,128)(2,1)S(1)}, bf16[5,56,128]{2,1,0:T(8,128)(2,1)S(1)}, u32[]{:S(2)}, u32[]{:S(2)}) collective-permute-start(bf16[5,56,128]{2,1,0:T(8,128)(2,1)S(1)} %collective-permute-done.5.refs_4_), channel_id=1, source_target_pairs={{0,1},{1,0},{2,3},{3,2},{4,5},{5,4},{6,7},{7,6},{8,9},{9,8},{10,11... | collective-permute-start | bytes 215048 | tf_op jit(solution)/shard_map/ppermute | solution.py:231
  25.2 4.0 %collective-permute-start.15 = (bf16[2,8,56,128]{3,2,1,0:T(8,128)(2,1)S(1)}, bf16[2,8,56,128]{3,2,1,0:T(8,128)(2,1)S(1)}, u32[]{:S(2)}, u32[]{:S(2)}) collective-permute-start(bf16[2,8,56,128]{3,2,1,0:T(8,128)(2,1)S(1)} %get-tuple-element.60), channel_id=1, source_target_pairs={{0,1},{1,0},{2,3},{3,2},{4,5},{5,4},{6,7},{7,6},{8,9},{9,8},{10,11... | collective-permute-start | bytes 688136 | tf_op jit(solution)/shard_map/ppermute | solution.py:231
  25.6 1.4 %collective-permute-start.17 = (bf16[2,5,56,128]{3,2,1,0:T(8,128)(2,1)S(1)}, bf16[2,5,56,128]{3,2,1,0:T(8,128)(2,1)S(1)}, u32[]{:S(2)}, u32[]{:S(2)}) collective-permute-start(bf16[2,5,56,128]{3,2,1,0:T(8,128)(2,1)S(1)} %get-tuple-element.66), channel_id=1, source_target_pairs={{0,1},{1,0},{2,3},{3,2},{4,5},{5,4},{6,7},{7,6},{8,9},{9,8},{10,11... | collective-permute-start | bytes 430088 | tf_op jit(solution)/shard_map/ppermute | solution.py:231
  25.8 2.3 %collective-permute-start.20 = (bf16[2,5,56,128]{3,2,1,0:T(8,128)(2,1)S(1)}, bf16[2,5,56,128]{3,2,1,0:T(8,128)(2,1)S(1)}, u32[]{:S(2)}, u32[]{:S(2)}) collective-permute-start(bf16[2,5,56,128]{3,2,1,0:T(8,128)(2,1)S(1)} %get-tuple-element.72), channel_id=1, source_target_pairs={{0,1},{1,0},{2,3},{3,2},{4,5},{5,4},{6,7},{7,6},{8,9},{9,8},{10,11... | collective-permute-start | bytes 430088 | tf_op jit(solution)/shard_map/ppermute | solution.py:231
  26.1 8.7 %collective-permute-start.23 = (bf16[2,5,56,128]{3,2,1,0:T(8,128)(2,1)S(1)}, bf16[2,5,56,128]{3,2,1,0:T(8,128)(2,1)S(1)}, u32[]{:S(2)}, u32[]{:S(2)}) collective-permute-start(bf16[2,5,56,128]{3,2,1,0:T(8,128)(2,1)S(1)} %get-tuple-element.78), channel_id=1, source_target_pairs={{0,1},{1,0},{2,3},{3,2},{4,5},{5,4},{6,7},{7,6},{8,9},{9,8},{10,11... | collective-permute-start | bytes 430088 | tf_op jit(solution)/shard_map/ppermute | solution.py:231
  27.0 5.1 %collective-permute-start.18 = (bf16[5,56,128]{2,1,0:T(8,128)(2,1)S(1)}, bf16[5,56,128]{2,1,0:T(8,128)(2,1)S(1)}, u32[]{:S(2)}, u32[]{:S(2)}) collective-permute-start(bf16[5,56,128]{2,1,0:T(8,128)(2,1)S(1)} %get-tuple-element.70), channel_id=1, source_target_pairs={{0,2},{2,0},{1,3},{3,1},{4,6},{6,4},{5,7},{7,5},{8,10},{10,8},{9,1... | collective-permute-start | bytes 215048 | tf_op jit(solution)/shard_map/ppermute | solution.py:231
  28.1 6.4 %collective-permute-start.21 = (bf16[5,56,128]{2,1,0:T(8,128)(2,1)S(1)}, bf16[5,56,128]{2,1,0:T(8,128)(2,1)S(1)}, u32[]{:S(2)}, u32[]{:S(2)}) collective-permute-start(bf16[5,56,128]{2,1,0:T(8,128)(2,1)S(1)} %get-tuple-element.76), channel_id=1, source_target_pairs={{0,2},{2,0},{1,3},{3,1},{4,6},{6,4},{5,7},{7,5},{8,10},{10,8},{9,1... | collective-permute-start | bytes 215048 | tf_op jit(solution)/shard_map/ppermute | solution.py:231
  29.3 13.3 %collective-permute-start.16 = (bf16[8,56,128]{2,1,0:T(8,128)(2,1)S(1)}, bf16[8,56,128]{2,1,0:T(8,128)(2,1)S(1)}, u32[]{:S(2)}, u32[]{:S(2)}) collective-permute-start(bf16[8,56,128]{2,1,0:T(8,128)(2,1)S(1)} %get-tuple-element.64), channel_id=1, source_target_pairs={{0,2},{2,0},{1,3},{3,1},{4,6},{6,4},{5,7},{7,5},{8,10},{10,8},{9,1... | collective-permute-start | bytes 344072 | tf_op jit(solution)/shard_map/ppermute | solution.py:231
  32.1 6.6 %collective-permute-start.19 = (bf16[5,56,128]{2,1,0:T(8,128)(2,1)S(1)}, bf16[5,56,128]{2,1,0:T(8,128)(2,1)S(1)}, u32[]{:S(2)}, u32[]{:S(2)}) collective-permute-start(bf16[5,56,128]{2,1,0:T(8,128)(2,1)S(1)} %narrow_sum.2), channel_id=1, source_target_pairs={{0,12},{4,8},{8,4},{12,0},{1,13},{5,9},{9,5},{13,1},{2,14},{6,10},... | collective-permute-start | bytes 215048 | tf_op jit(solution)/shard_map/ppermute | solution.py:231
  34.5 6.4 %collective-permute-start.22 = (bf16[5,56,128]{2,1,0:T(8,128)(2,1)S(1)}, bf16[5,56,128]{2,1,0:T(8,128)(2,1)S(1)}, u32[]{:S(2)}, u32[]{:S(2)}) collective-permute-start(bf16[5,56,128]{2,1,0:T(8,128)(2,1)S(1)} %narrow_sum.3), channel_id=1, source_target_pairs={{0,8},{4,12},{8,0},{12,4},{1,9},{5,13},{9,1},{13,5},{2,10},{6,14},... | collective-permute-start | bytes 215048 | tf_op jit(solution)/shard_map/ppermute | solution.py:231
  34.9 6.4 %collective-permute-start.24 = (bf16[5,56,128]{2,1,0:T(8,128)(2,1)S(1)}, bf16[5,56,128]{2,1,0:T(8,128)(2,1)S(1)}, u32[]{:S(2)}, u32[]{:S(2)}) collective-permute-start(bf16[5,56,128]{2,1,0:T(8,128)(2,1)S(1)} %get-tuple-element.81), channel_id=1, source_target_pairs={{0,4},{2,6},{4,0},{6,2},{8,12},{10,14},{12,8},{14,10},{1,5},{3,7},... | collective-permute-start | bytes 215048 | tf_op jit(solution)/shard_map/ppermute | solution.py:231
  36.8 5.8 %collective-permute-start.25 = (bf16[5,56,128]{2,1,0:T(8,128)(2,1)S(1)}, bf16[5,56,128]{2,1,0:T(8,128)(2,1)S(1)}, u32[]{:S(2)}, u32[]{:S(2)}) collective-permute-start(bf16[5,56,128]{2,1,0:T(8,128)(2,1)S(1)} %get-tuple-element.82), channel_id=1, source_target_pairs={{0,6},{2,4},{4,2},{6,0},{8,14},{10,12},{12,10},{14,8},{1,7},{3,5},... | collective-permute-start | bytes 215048 | tf_op jit(solution)/shard_map/ppermute | solution.py:231

commit v7 on v6

--- a/solution.py
+++ b/solution.py
@@ -10,6 +10,7 @@
 CAP = 5
 LANES = 128
 SPAN = 7
+HALVES = 2
 MAX_ROWS = 128
 
 VMEM = pltpu.VMEM
@@ -178,12 +179,14 @@
             at += slots
 
 
-def pair_sum_kernel(n_pair, *refs):
+def pair_sum_kernel(n_pair, cuts, *refs):
     parts, outs = refs[:n_pair], refs[n_pair:]
-    for j, out in enumerate(outs):
-        total = parts[0][j].astype(F32)
+    for i, out in enumerate(outs):
+        j, cut = divmod(i, cuts)
+        rows = slice(cut * out.shape[0], (cut + 1) * out.shape[0])
+        total = parts[0][j, rows].astype(F32)
         for ref in parts[1:]:
-            total = total + ref[j].astype(F32)
+            total = total + ref[j, rows].astype(F32)
         out[...] = total.astype(BF16)
 
 
@@ -199,26 +202,40 @@
         at += out.shape[0]
 
 
-def combine_kernel(n_narrow, order, route, gains, *refs):
-    near, rest = refs[:n_narrow], refs[n_narrow:]
-    far, direct = rest[: len(order)], rest[len(order) : -3]
-    out, total, stage = rest[-3:]
+def far_combine_kernel(order, route, gains, *refs):
+    far, (total, stage) = refs[: len(order)], refs[-2:]
+    topk, rows = route.shape
+    tall = stage.shape[1]
+    stage[: 2 * CAP] = jnp.zeros((2 * CAP, tall, LANES), F32)
+    for k, ref in zip(order, far):
+        stage[k * CAP : (k + 1) * CAP] = ref[...].astype(F32)
+    for t in range(rows):
+        value = gains[0, t] * stage[route[0, t]]
+        for k in range(1, topk):
+            value = value + gains[k, t] * stage[route[k, t]]
+        total[t] = value
+
+
+def combine_kernel(n_narrow, route, gains, far, *refs):
+    near, direct = refs[: HALVES * n_narrow], refs[HALVES * n_narrow : -3]
+    out, total, stage = refs[-3:]
     rows, features = out.shape
     tall = features // LANES
     topk = route.shape[0]
-    stage[:CAP] = jnp.zeros((CAP, tall, LANES), F32)
-    for k, ref in zip(order, far):
-        stage[k * CAP : (k + 1) * CAP] = ref[...].astype(F32)
+    stage[0] = jnp.zeros((tall, LANES), F32)
     arrived = direct[0][...].astype(F32)
     for ref in direct[1:]:
         arrived = arrived + ref[...].astype(F32)
-    stage[CAP : 2 * CAP] = arrived
+    stage[1:] = arrived
     for t in range(rows):
-        value = near[0][t].astype(F32)
-        for ref in near[1:]:
-            value = value + ref[t].astype(F32)
+        value = far[t]
+        cut, row = divmod(t, rows // HALVES)
+        for ref in near[cut * n_narrow : (cut + 1) * n_narrow]:
+            value = value + ref[row].astype(F32)
         for k in range(topk):
-            value = value + gains[k, t] * stage[route[k, t]]
+            slot = route[k, t] - CAP
+            slot = jnp.where((slot >= 0) & (slot < CAP), slot + 1, 0)
+            value = value + gains[k, t] * stage[slot]
         total[t * tall : (t + 1) * tall, :] = value
     for b in range(tall):
         out[:, b * LANES : (b + 1) * LANES] = total[
@@ -367,14 +384,14 @@
     )
     near_out, far_out = outs[:n_pair], outs[n_pair:]
 
-    def reduce_pair(parts, *first):
+    def reduce_pair(parts, *first, cuts=1):
         rows = parts[0].shape[1]
         return call(
-            functools.partial(pair_sum_kernel, n_pair),
+            functools.partial(pair_sum_kernel, n_pair, cuts),
             "pair_sum",
             after([parts[0]] + [swap(parts[c], "pair", c) for c in range(1, n_pair)], *first),
             [VSPEC] * n_pair,
-            [block(rows)] * n_narrow,
+            [block(rows // cuts)] * (n_narrow * cuts),
             [],
             limit=limit,
         )
@@ -395,21 +412,29 @@
         )
     sums = far_back
     far_back = [swap(value, "wide", k) for k, value in zip(order, far_back)]
-    direct_back = reduce_pair(far_out[per - 1 :: per], sums[0])
-    near_back = send_narrow(reduce_pair(near_out))
+    direct_back = reduce_pair(far_out[per - 1 :: per])
+    near_parts = reduce_pair(near_out, cuts=HALVES)
+    near_back = []
+    for cut in range(HALVES):
+        near_back += send_narrow(near_parts[cut::HALVES])
     direct_back = [
         swap(value, across, n_narrow + j) for j, value in enumerate(direct_back)
     ]
+    far_sum = call(
+        functools.partial(far_combine_kernel, order),
+        "far_combine",
+        [route, gains] + far_back + in_hbm(*shared, *routed),
+        [SSPEC] * 2 + [VSPEC] * len(order) + [ASPEC] * 6,
+        jax.ShapeDtypeStruct((tokens, tall, LANES), F32),
+        [VMEM((n_wide * CAP, tall, LANES), F32)],
+    )
     return call(
-        functools.partial(combine_kernel, n_narrow, order),
+        functools.partial(combine_kernel, n_narrow),
         "combine",
-        [route, gains] + near_back + far_back + direct_back,
-        [SSPEC] * 2 + [VSPEC] * (2 * n_narrow + len(order)),
+        [route, gains, far_sum] + near_back + direct_back,
+        [SSPEC] * 2 + [VSPEC] * (1 + (HALVES + 1) * n_narrow),
         jax.ShapeDtypeStruct((tokens, features), BF16),
-        [
-            VMEM((tokens * tall, LANES), F32),
-            VMEM((n_wide * CAP, tall, LANES), F32),
-        ],
+        [VMEM((tokens * tall, LANES), F32), VMEM((CAP + 1, tall, LANES), F32)],
     )
 
 

time: 43.5 us -> 43.8 us (level)
  starting transfers between devices: 22.2 us -> 23.1 us
  waiting for transfers between devices: 14.4 us -> 13.7 us
    ppermute x26 -> x27, starting transfers between devices: 22.2 us -> 23.1 us  [swap(): return lax.ppermute(value, axis, [(i, i ^ offset) for i in range(size)])]
    ppermute x26 -> x27, waiting for transfers between devices: 14.4 us -> 13.7 us  [swap(): return lax.ppermute(value, axis, [(i, i ^ offset) for i in range(size)])]
    pallas_call x10 -> x11, Pallas kernels: 6.69 us -> 6.81 us  [call(): pl.pallas_call(kernel, out_shape=outs, in_specs=specs, out_specs=jax.tree...]
  transfers between devices with their start and end apart: 26 -> 27, of which waited for: 14 -> 15; matrix products, arithmetic and copies ran while one was open for 0% -> 0% of each run, Pallas kernels for 5% -> 5%
where the time goes in v7:
time: 43.8 us; the launch traced here: 43.7 us
  starting transfers between devices  23.1 us (53%)
  waiting for transfers between devices  13.7 us (31%)
  Pallas kernels  6.81 us (16%)
    ppermute x27, starting transfers between devices, swap(): return lax.ppermute(value, axis, [(i, i ^ offset) for i in range(size)])  23.1 us
    ppermute x27, waiting for transfers between devices, swap(): return lax.ppermute(value, axis, [(i, i ^ offset) for i in range(size)])  13.7 us
    pallas_call x11, Pallas kernels, call(): pl.pallas_call(kernel, out_shape=outs, in_specs=specs, out_specs=jax.tree...  6.81 us
  transfers between devices with their start and end apart: 27, of which 15 were waited for; matrix products, arithmetic and copies ran while one was open for 0% of the time, Pallas kernels for 5%

profile of v7, /device:TPU:0, one launch (start us, length us, event | category | flops | bytes accessed | tf_op | source)
XLA Modules:
  0.0 43.7 jit_solution(16694760504450309990)
XLA Ops:
  0.0 1.4 %dispatch.1 = (bf16[9,56,128]{2,1,0:T(8,128)(2,1)S(1)}, bf16[5,56,128]{2,1,0:T(8,128)(2,1)S(1)}, bf16[5,56,128]{2,1,0:T(8,128)(2,1)S(1)}, bf16[5,56,128]{2,1,0:T...) custom-call(s32[2,8]{1,0:T(2,128)} %bitcast.14, s32[4]{0:T(128)} %place_in.1, f32[2,8]{1,0:T(2,128)} %bitcast.15, ...), custom_call_target="tpu_custom_call" | custom-call | tf_op jit(solution)/shard_map/dispatch/pallas_call | solution.py:260
  1.4 3.0 %collective-permute-start.6 = (bf16[9,56,128]{2,1,0:T(8,128)(2,1)S(1)}, bf16[9,56,128]{2,1,0:T(8,128)(2,1)S(1)}, u32[]{:S(2)}, u32[]{:S(2)}) collective-permute-start(bf16[9,56,128]{2,1,0:T(8,128)(2,1)S(1)} %get-tuple-element.54.refs_0_), channel_id=1, source_target_pairs={{0,2},{2,0},{1,3},{3,1},{4,6},{6,4},{5,7},{7,5},{8,10},{10,8},{9,1... | collective-permute-start | bytes 387080 | tf_op jit(solution)/shard_map/ppermute | solution.py:248
  4.4 3.6 %collective-permute-start = (bf16[5,56,128]{2,1,0:T(8,128)(2,1)S(1)}, bf16[5,56,128]{2,1,0:T(8,128)(2,1)S(1)}, u32[]{:S(2)}, u32[]{:S(2)}) collective-permute-start(bf16[5,56,128]{2,1,0:T(8,128)(2,1)S(1)} %get-tuple-element.48), channel_id=1, source_target_pairs={{0,12},{4,8},{8,4},{12,0},{1,13},{5,9},{9,5},{13,1},{2,14},{6,10},... | collective-permute-start | bytes 215048 | tf_op jit(solution)/shard_map/ppermute | solution.py:248
  8.0 0.5 %collective-permute-start.3 = (bf16[5,56,128]{2,1,0:T(8,128)(2,1)S(1)}, bf16[5,56,128]{2,1,0:T(8,128)(2,1)S(1)}, u32[]{:S(2)}, u32[]{:S(2)}) collective-permute-start(bf16[5,56,128]{2,1,0:T(8,128)(2,1)S(1)} %get-tuple-element.50), channel_id=1, source_target_pairs={{0,6},{2,4},{4,2},{6,0},{8,14},{10,12},{12,10},{14,8},{1,7},{3,5},... | collective-permute-start | bytes 215048 | tf_op jit(solution)/shard_map/ppermute | solution.py:248
  8.5 1.5 %collective-permute-start.2 = (bf16[5,56,128]{2,1,0:T(8,128)(2,1)S(1)}, bf16[5,56,128]{2,1,0:T(8,128)(2,1)S(1)}, u32[]{:S(2)}, u32[]{:S(2)}) collective-permute-start(bf16[5,56,128]{2,1,0:T(8,128)(2,1)S(1)} %get-tuple-element.50), channel_id=1, source_target_pairs={{0,4},{2,6},{4,0},{6,2},{8,12},{10,14},{12,8},{14,10},{1,5},{3,7},... | collective-permute-start | bytes 215048 | tf_op jit(solution)/shard_map/ppermute | solution.py:248
  10.1 1.3 %collective-permute-done.refs_0_ = bf16[5,56,128]{2,1,0:T(8,128)(2,1)S(1)} collective-permute-done((bf16[5,56,128]{2,1,0:T(8,128)(2,1)S(1)}, bf16[5,56,128]{2,1,0:T(8,128)(2,1)S(1)}, u32[]{:S(2)}, u32[]{:S(2)}) %collective-permute-start) | collective-permute-done | bytes 71712 | tf_op jit(solution)/shard_map/ppermute | solution.py:248
  11.4 2.4 %collective-permute-done.1.refs_1_ = bf16[5,56,128]{2,1,0:T(8,128)(2,1)S(1)} collective-permute-done((bf16[5,56,128]{2,1,0:T(8,128)(2,1)S(1)}, bf16[5,56,128]{2,1,0:T(8,128)(2,1)S(1)}, u32[]{:S(2)}, u32[]{:S(2)}) %collective-permute-start.1) | collective-permute-done | bytes 71712 | tf_op jit(solution)/shard_map/ppermute | solution.py:248
  13.8 0.9 %collective-permute-done.3.refs_5_ = bf16[5,56,128]{2,1,0:T(8,128)(2,1)S(1)} collective-permute-done((bf16[5,56,128]{2,1,0:T(8,128)(2,1)S(1)}, bf16[5,56,128]{2,1,0:T(8,128)(2,1)S(1)}, u32[]{:S(2)}, u32[]{:S(2)}) %collective-permute-start.3) | collective-permute-done | bytes 71712 | tf_op jit(solution)/shard_map/ppermute | solution.py:248
  14.7 0.6 %collective-permute-done.2.refs_2_ = bf16[5,56,128]{2,1,0:T(8,128)(2,1)S(1)} collective-permute-done((bf16[5,56,128]{2,1,0:T(8,128)(2,1)S(1)}, bf16[5,56,128]{2,1,0:T(8,128)(2,1)S(1)}, u32[]{:S(2)}, u32[]{:S(2)}) %collective-permute-start.2) | collective-permute-done | bytes 71712 | tf_op jit(solution)/shard_map/ppermute | solution.py:248
  15.3 0.5 %collective-permute-start.8 = (bf16[9,56,128]{2,1,0:T(8,128)(2,1)S(1)}, bf16[9,56,128]{2,1,0:T(8,128)(2,1)S(1)}, u32[]{:S(2)}, u32[]{:S(2)}) collective-permute-start(bf16[9,56,128]{2,1,0:T(8,128)(2,1)S(1)} %collective-permute-done.6.refs_1_), channel_id=1, source_target_pairs={{0,1},{1,0},{2,3},{3,2},{4,5},{5,4},{6,7},{7,6},{8,9},{9,8},{10,11... | collective-permute-start | bytes 387080 | tf_op jit(solution)/shard_map/ppermute | solution.py:248
  15.8 0.8 %collective-permute-start.4 = (bf16[5,56,128]{2,1,0:T(8,128)(2,1)S(1)}, bf16[5,56,128]{2,1,0:T(8,128)(2,1)S(1)}, u32[]{:S(2)}, u32[]{:S(2)}) collective-permute-start(bf16[5,56,128]{2,1,0:T(8,128)(2,1)S(1)} %collective-permute-done.refs_0_), channel_id=1, source_target_pairs={{0,2},{2,0},{1,3},{3,1},{4,6},{6,4},{5,7},{7,5},{8,10},{10,8},{9,1... | collective-permute-start | bytes 215048 | tf_op jit(solution)/shard_map/ppermute | solution.py:248
  16.5 1.3 %collective-permute-start.5 = (bf16[5,56,128]{2,1,0:T(8,128)(2,1)S(1)}, bf16[5,56,128]{2,1,0:T(8,128)(2,1)S(1)}, u32[]{:S(2)}, u32[]{:S(2)}) collective-permute-start(bf16[5,56,128]{2,1,0:T(8,128)(2,1)S(1)} %collective-permute-done.1.refs_1_), channel_id=1, source_target_pairs={{0,2},{2,0},{1,3},{3,1},{4,6},{6,4},{5,7},{7,5},{8,10},{10,8},{9,1... | collective-permute-start | bytes 215048 | tf_op jit(solution)/shard_map/ppermute | solution.py:248
  17.8 0.5 %collective-permute-start.9 = (bf16[5,56,128]{2,1,0:T(8,128)(2,1)S(1)}, bf16[5,56,128]{2,1,0:T(8,128)(2,1)S(1)}, u32[]{:S(2)}, u32[]{:S(2)}) collective-permute-start(bf16[5,56,128]{2,1,0:T(8,128)(2,1)S(1)} %collective-permute-done.refs_0_), channel_id=1, source_target_pairs={{0,1},{1,0},{2,3},{3,2},{4,5},{5,4},{6,7},{7,6},{8,9},{9,8},{10,11... | collective-permute-start | bytes 215048 | tf_op jit(solution)/shard_map/ppermute | solution.py:248
  18.4 2.0 %near_shared.1 = (bf16[32,7168]{1,0:T(8,128)(2,1)S(1)}, f32[32,128]{1,0:T(8,128)S(1)}, f32[32,7168]{1,0:T(8,128)S(1)}) custom-call(bf16[9,56,128]{2,1,0:T(8,128)(2,1)S(1)} %get-tuple-element.54.refs_0_, bf16[9,56,128]{2,1,0:T(8,128)(2,1)S(1)} %collective-permute-done.6.refs_1_, bf16[9,56,128]{2,1,0:T(8,128)(2,1)S(1)} %collective-permute-done.7.refs_2_, ...), custom_call_target="tpu_custom_call" | custom-call | flops 352321536 | bytes 11010048 | tf_op jit(solution)/shard_map/near_shared/pallas_call | solution.py:260
  20.9 0.5 %collective-permute-done.5.refs_4_ = bf16[5,56,128]{2,1,0:T(8,128)(2,1)S(1)} collective-permute-done((bf16[5,56,128]{2,1,0:T(8,128)(2,1)S(1)}, bf16[5,56,128]{2,1,0:T(8,128)(2,1)S(1)}, u32[]{:S(2)}, u32[]{:S(2)}) %collective-permute-start.5) | collective-permute-done | bytes 71712 | tf_op jit(solution)/shard_map/ppermute | solution.py:248
  21.4 0.5 %collective-permute-start.13 = (bf16[5,56,128]{2,1,0:T(8,128)(2,1)S(1)}, bf16[5,56,128]{2,1,0:T(8,128)(2,1)S(1)}, u32[]{:S(2)}, u32[]{:S(2)}) collective-permute-start(bf16[5,56,128]{2,1,0:T(8,128)(2,1)S(1)} %collective-permute-done.5.refs_4_), channel_id=1, source_target_pairs={{0,1},{1,0},{2,3},{3,2},{4,5},{5,4},{6,7},{7,6},{8,9},{9,8},{10,11... | collective-permute-start | bytes 215048 | tf_op jit(solution)/shard_map/ppermute | solution.py:248
  22.0 0.7 %collective-permute-done.12.refs_9_ = bf16[5,56,128]{2,1,0:T(8,128)(2,1)S(1)} collective-permute-done((bf16[5,56,128]{2,1,0:T(8,128)(2,1)S(1)}, bf16[5,56,128]{2,1,0:T(8,128)(2,1)S(1)}, u32[]{:S(2)}, u32[]{:S(2)}) %collective-permute-start.12) | collective-permute-done | bytes 71712 | tf_op jit(solution)/shard_map/ppermute | solution.py:248
  22.9 2.4 %routed.1 = (bf16[2,8,56,128]{3,2,1,0:T(8,128)(2,1)S(1)}, bf16[2,8,56,128]{3,2,1,0:T(8,128)(2,1)S(1)}, bf16[2,5,56,128]{3,2,1,0:T(8,128)(2,1)S(1)}, bf16[2,5,56,...) custom-call(bf16[5,56,128]{2,1,0:T(8,128)(2,1)S(1)} %collective-perm, ...), custom_call_target="tpu_custom_call" | custom-call | flops 1012924416 | bytes 11010048 | tf_op jit(solution)/shard_map/routed/pallas_call | solution.py:260
  25.2 0.4 collective-permute-start.15
  25.8 0.4 collective-permute-start.21
  26.7 1.0 %collective-permute-start.16 = (bf16[5,56,128]{2,1,0:T(8,128)(2,1)S(1)}, bf16[5,56,128]{2,1,0:T(8,128)(2,1)S(1)}, u32[]{:S(2)}, u32[]{:S(2)}) collective-permute-start(bf16[5,56,128]{2,1,0:T(8,128)(2,1)S(1)} %get-tuple-element.66), channel_id=1, source_target_pairs={{0,2},{2,0},{1,3},{3,1},{4,6},{6,4},{5,7},{7,5},{8,10},{10,8},{9,1... | collective-permute-start | bytes 215048 | tf_op jit(solution)/shard_map/ppermute | solution.py:248
  27.8 1.1 %collective-permute-start.19 = (bf16[5,56,128]{2,1,0:T(8,128)(2,1)S(1)}, bf16[5,56,128]{2,1,0:T(8,128)(2,1)S(1)}, u32[]{:S(2)}, u32[]{:S(2)}) collective-permute-start(bf16[5,56,128]{2,1,0:T(8,128)(2,1)S(1)} %get-tuple-element.72), channel_id=1, source_target_pairs={{0,2},{2,0},{1,3},{3,1},{4,6},{6,4},{5,7},{7,5},{8,10},{10,8},{9,1... | collective-permute-start | bytes 215048 | tf_op jit(solution)/shard_map/ppermute | solution.py:248
  28.9 2.9 %collective-permute-done.16.refs_1_ = bf16[5,56,128]{2,1,0:T(8,128)(2,1)S(1)} collective-permute-done((bf16[5,56,128]{2,1,0:T(8,128)(2,1)S(1)}, bf16[5,56,128]{2,1,0:T(8,128)(2,1)S(1)}, u32[]{:S(2)}, u32[]{:S(2)}) %collective-permute-start.16) | collective-permute-done | bytes 71712 | tf_op jit(solution)/shard_map/ppermute | solution.py:248
  31.9 2.3 %collective-permute-start.17 = (bf16[5,56,128]{2,1,0:T(8,128)(2,1)S(1)}, bf16[5,56,128]{2,1,0:T(8,128)(2,1)S(1)}, u32[]{:S(2)}, u32[]{:S(2)}) collective-permute-start(bf16[5,56,128]{2,1,0:T(8,128)(2,1)S(1)} %narrow_sum.2), channel_id=1, source_target_pairs={{0,12},{4,8},{8,4},{12,0},{1,13},{5,9},{9,5},{13,1},{2,14},{6,10},... | collective-permute-start | bytes 215048 | tf_op jit(solution)/shard_map/ppermute | solution.py:248
  34.6 1.9 %collective-permute-start.25 = (bf16[5,56,128]{2,1,0:T(8,128)(2,1)S(1)}, bf16[5,56,128]{2,1,0:T(8,128)(2,1)S(1)}, u32[]{:S(2)}, u32[]{:S(2)}) collective-permute-start(bf16[5,56,128]{2,1,0:T(8,128)(2,1)S(1)} %get-tuple-element.85), channel_id=1, source_target_pairs={{0,4},{2,6},{4,0},{6,2},{8,12},{10,14},{12,8},{14,10},{1,5},{3,7},... | collective-permute-start | bytes 215048 | tf_op jit(solution)/shard_map/ppermute | solution.py:248
  36.5 0.5 %collective-permute-start.26 = (bf16[5,56,128]{2,1,0:T(8,128)(2,1)S(1)}, bf16[5,56,128]{2,1,0:T(8,128)(2,1)S(1)}, u32[]{:S(2)}, u32[]{:S(2)}) collective-permute-start(bf16[5,56,128]{2,1,0:T(8,128)(2,1)S(1)} %get-tuple-element.86), channel_id=1, source_target_pairs={{0,6},{2,4},{4,2},{6,0},{8,14},{10,12},{12,10},{14,8},{1,7},{3,5},... | collective-permute-start | bytes 215048 | tf_op jit(solution)/shard_map/ppermute | solution.py:248
  37.1 1.2 %collective-permute-start.22 = (bf16[4,56,128]{2,1,0:T(8,128)(2,1)S(1)}, bf16[4,56,128]{2,1,0:T(8,128)(2,1)S(1)}, u32[]{:S(2)}, u32[]{:S(2)}) collective-permute-start(bf16[4,56,128]{2,1,0:T(8,128)(2,1)S(1)} %get-tuple-element.78), channel_id=1, source_target_pairs={{0,2},{2,0},{1,3},{3,1},{4,6},{6,4},{5,7},{7,5},{8,10},{10,8},{9,1... | collective-permute-start | bytes 172040 | tf_op jit(solution)/shard_map/ppermute | solution.py:248
  38.4 1.0 %collective-permute-start.23 = (bf16[4,56,128]{2,1,0:T(8,128)(2,1)S(1)}, bf16[4,56,128]{2,1,0:T(8,128)(2,1)S(1)}, u32[]{:S(2)}, u32[]{:S(2)}) collective-permute-start(bf16[4,56,128]{2,1,0:T(8,128)(2,1)S(1)} %get-tuple-element.80), channel_id=1, source_target_pairs={{0,2},{2,0},{1,3},{3,1},{4,6},{6,4},{5,7},{7,5},{8,10},{10,8},{9,1... | collective-permute-start | bytes 172040 | tf_op jit(solution)/shard_map/ppermute | solution.py:248
  39.4 1.3 %collective-permute-done.20.refs_1_ = bf16[5,56,128]{2,1,0:T(8,128)(2,1)S(1)} collective-permute-done((bf16[5,56,128]{2,1,0:T(8,128)(2,1)S(1)}, bf16[5,56,128]{2,1,0:T(8,128)(2,1)S(1)}, u32[]{:S(2)}, u32[]{:S(2)}) %collective-permute-start.20) | collective-permute-done | bytes 71712 | tf_op jit(solution)/shard_map/ppermute | solution.py:248
  41.1 1.3 %collective-permute-done.26.refs_5_ = bf16[5,56,128]{2,1,0:T(8,128)(2,1)S(1)} collective-permute-done((bf16[5,56,128]{2,1,0:T(8,128)(2,1)S(1)}, bf16[5,56,128]{2,1,0:T(8,128)(2,1)S(1)}, u32[]{:S(2)}, u32[]{:S(2)}) %collective-permute-start.26) | collective-permute-done | bytes 71712 | tf_op jit(solution)/shard_map/ppermute | solution.py:248
  42.3 0.6 %collective-permute-done.23.refs_3_ = bf16[4,56,128]{2,1,0:T(8,128)(2,1)S(1)} collective-permute-done((bf16[4,56,128]{2,1,0:T(8,128)(2,1)S(1)}, bf16[4,56,128]{2,1,0:T(8,128)(2,1)S(1)}, u32[]{:S(2)}, u32[]{:S(2)}) %collective-permute-start.23) | collective-permute-done | bytes 57376 | tf_op jit(solution)/shard_map/ppermute | solution.py:248
  42.9 0.8 %combine.1 = bf16[8,7168]{1,0:T(8,128)(2,1)} custom-call(s32[2,8]{1,0:T(2,128)S(4)} %get-tuple-element.46.route, f32[2,8]{1,0:T(2,128)S(4)} %get-tuple-element.47.gains, f32[8,56,128]{2,1,0:T(8,128)S(1)} %far_combine.1.far, bf16[4,56,128]{2,1,0:T(8,128)(2,1)S(1)} %get-tuple-element.77.refs_0_, bf16[4,56,128]{2,1,0:T(8,128)(2,1)S(1)} %collective-permute-done.22.refs_1_, ...), custom_call_target="tpu_custom_call" | custom-call | tf_op jit(solution)/shard_map/combine/pallas_call | solution.py:260
  (45 shorter events, 2.5 us)
Async XLA Ops:
  0.0 18.4 %copy-start = (bf16[7168,256]{1,0:T(8,128)(2,1)S(1)}, bf16[7168,256]{1,0:T(8,128)(2,1)}, u32[]{:S(2)}) copy-start(bf16[7168,256]{1,0:T(8,128)(2,1)} %refs_2_.3) | copy-start | bytes 11010052
  0.0 18.4 %copy-start.1 = (bf16[7168,256]{1,0:T(8,128)(2,1)S(1)}, bf16[7168,256]{1,0:T(8,128)(2,1)}, u32[]{:S(2)}) copy-start(bf16[7168,256]{1,0:T(8,128)(2,1)} %refs_3_.1) | copy-start | bytes 11010052
  0.0 18.4 %copy-start.2 = (bf16[256,7168]{1,0:T(8,128)(2,1)S(1)}, bf16[256,7168]{1,0:T(8,128)(2,1)}, u32[]{:S(2)}) copy-start(bf16[256,7168]{1,0:T(8,128)(2,1)} %refs_4_.3) | copy-start | bytes 11010052
  1.4 13.9 %collective-permute-start.6 = (bf16[9,56,128]{2,1,0:T(8,128)(2,1)S(1)}, bf16[9,56,128]{2,1,0:T(8,128)(2,1)S(1)}, u32[]{:S(2)}, u32[]{:S(2)}) collective-permute-start(bf16[9,56,128]{2,1,0:T(8,128)(2,1)S(1)} %get-tuple-element.54.refs_0_), channel_id=1, source_target_pairs={{0,2},{2,0},{1,3},{3,1},{4,6},{6,4},{5,7},{7,5},{8,10},{10,8},{9,1... | collective-permute-start | bytes 387080 | tf_op jit(solution)/shard_map/ppermute | solution.py:248
  4.4 7.0 %collective-permute-start = (bf16[5,56,128]{2,1,0:T(8,128)(2,1)S(1)}, bf16[5,56,128]{2,1,0:T(8,128)(2,1)S(1)}, u32[]{:S(2)}, u32[]{:S(2)}) collective-permute-start(bf16[5,56,128]{2,1,0:T(8,128)(2,1)S(1)} %get-tuple-element.48), channel_id=1, source_target_pairs={{0,12},{4,8},{8,4},{12,0},{1,13},{5,9},{9,5},{13,1},{2,14},{6,10},... | collective-permute-start | bytes 215048 | tf_op jit(solution)/shard_map/ppermute | solution.py:248
  8.0 5.8 %collective-permute-start.1 = (bf16[5,56,128]{2,1,0:T(8,128)(2,1)S(1)}, bf16[5,56,128]{2,1,0:T(8,128)(2,1)S(1)}, u32[]{:S(2)}, u32[]{:S(2)}) collective-permute-start(bf16[5,56,128]{2,1,0:T(8,128)(2,1)S(1)} %get-tuple-element.49), channel_id=1, source_target_pairs={{0,8},{4,12},{8,0},{12,4},{1,9},{5,13},{9,1},{13,5},{2,10},{6,14},... | collective-permute-start | bytes 215048 | tf_op jit(solution)/shard_map/ppermute | solution.py:248
  8.0 14.9 %copy-start.4 = (bf16[1,7168,256]{2,1,0:T(8,128)(2,1)S(1)}, bf16[1,7168,256]{2,1,0:T(8,128)(2,1)}, u32[]{:S(2)}) copy-start(bf16[1,7168,256]{2,1,0:T(8,128)(2,1)} %param.17) | copy-start | bytes 11010052
  8.0 14.9 %copy-start.5 = (bf16[1,256,7168]{2,1,0:T(8,128)(2,1)S(1)}, bf16[1,256,7168]{2,1,0:T(8,128)(2,1)}, u32[]{:S(2)}) copy-start(bf16[1,256,7168]{2,1,0:T(8,128)(2,1)} %param.18) | copy-start | bytes 11010052
  8.0 6.7 %collective-permute-start.3 = (bf16[5,56,128]{2,1,0:T(8,128)(2,1)S(1)}, bf16[5,56,128]{2,1,0:T(8,128)(2,1)S(1)}, u32[]{:S(2)}, u32[]{:S(2)}) collective-permute-start(bf16[5,56,128]{2,1,0:T(8,128)(2,1)S(1)} %get-tuple-element.50), channel_id=1, source_target_pairs={{0,6},{2,4},{4,2},{6,0},{8,14},{10,12},{12,10},{14,8},{1,7},{3,5},... | collective-permute-start | bytes 215048 | tf_op jit(solution)/shard_map/ppermute | solution.py:248
  8.5 6.7 %collective-permute-start.2 = (bf16[5,56,128]{2,1,0:T(8,128)(2,1)S(1)}, bf16[5,56,128]{2,1,0:T(8,128)(2,1)S(1)}, u32[]{:S(2)}, u32[]{:S(2)}) collective-permute-start(bf16[5,56,128]{2,1,0:T(8,128)(2,1)S(1)} %get-tuple-element.50), channel_id=1, source_target_pairs={{0,4},{2,6},{4,0},{6,2},{8,12},{10,14},{12,8},{14,10},{1,5},{3,7},... | collective-permute-start | bytes 215048 | tf_op jit(solution)/shard_map/ppermute | solution.py:248
  15.3 2.5 %collective-permute-start.7 = (bf16[9,56,128]{2,1,0:T(8,128)(2,1)S(1)}, bf16[9,56,128]{2,1,0:T(8,128)(2,1)S(1)}, u32[]{:S(2)}, u32[]{:S(2)}) collective-permute-start(bf16[9,56,128]{2,1,0:T(8,128)(2,1)S(1)} %get-tuple-element.54.refs_0_), channel_id=1, source_target_pairs={{0,1},{1,0},{2,3},{3,2},{4,5},{5,4},{6,7},{7,6},{8,9},{9,8},{10,11... | collective-permute-start | bytes 387080 | tf_op jit(solution)/shard_map/ppermute | solution.py:248
  15.3 3.1 %collective-permute-start.8 = (bf16[9,56,128]{2,1,0:T(8,128)(2,1)S(1)}, bf16[9,56,128]{2,1,0:T(8,128)(2,1)S(1)}, u32[]{:S(2)}, u32[]{:S(2)}) collective-permute-start(bf16[9,56,128]{2,1,0:T(8,128)(2,1)S(1)} %collective-permute-done.6.refs_1_), channel_id=1, source_target_pairs={{0,1},{1,0},{2,3},{3,2},{4,5},{5,4},{6,7},{7,6},{8,9},{9,8},{10,11... | collective-permute-start | bytes 387080 | tf_op jit(solution)/shard_map/ppermute | solution.py:248
  15.8 4.9 %collective-permute-start.4 = (bf16[5,56,128]{2,1,0:T(8,128)(2,1)S(1)}, bf16[5,56,128]{2,1,0:T(8,128)(2,1)S(1)}, u32[]{:S(2)}, u32[]{:S(2)}) collective-permute-start(bf16[5,56,128]{2,1,0:T(8,128)(2,1)S(1)} %collective-permute-done.refs_0_), channel_id=1, source_target_pairs={{0,2},{2,0},{1,3},{3,1},{4,6},{6,4},{5,7},{7,5},{8,10},{10,8},{9,1... | collective-permute-start | bytes 215048 | tf_op jit(solution)/shard_map/ppermute | solution.py:248
  16.5 4.9 %collective-permute-start.5 = (bf16[5,56,128]{2,1,0:T(8,128)(2,1)S(1)}, bf16[5,56,128]{2,1,0:T(8,128)(2,1)S(1)}, u32[]{:S(2)}, u32[]{:S(2)}) collective-permute-start(bf16[5,56,128]{2,1,0:T(8,128)(2,1)S(1)} %collective-permute-done.1.refs_1_), channel_id=1, source_target_pairs={{0,2},{2,0},{1,3},{3,1},{4,6},{6,4},{5,7},{7,5},{8,10},{10,8},{9,1... | collective-permute-start | bytes 215048 | tf_op jit(solution)/shard_map/ppermute | solution.py:248
  17.8 3.6 %collective-permute-start.14 = (bf16[5,56,128]{2,1,0:T(8,128)(2,1)S(1)}, bf16[5,56,128]{2,1,0:T(8,128)(2,1)S(1)}, u32[]{:S(2)}, u32[]{:S(2)}) collective-permute-start(bf16[5,56,128]{2,1,0:T(8,128)(2,1)S(1)} %collective-permute-done.3.refs_5_), channel_id=1, source_target_pairs={{0,1},{1,0},{2,3},{3,2},{4,5},{5,4},{6,7},{7,6},{8,9},{9,8},{10,11... | collective-permute-start | bytes 215048 | tf_op jit(solution)/shard_map/ppermute | solution.py:248
  17.8 4.2 %collective-permute-start.9 = (bf16[5,56,128]{2,1,0:T(8,128)(2,1)S(1)}, bf16[5,56,128]{2,1,0:T(8,128)(2,1)S(1)}, u32[]{:S(2)}, u32[]{:S(2)}) collective-permute-start(bf16[5,56,128]{2,1,0:T(8,128)(2,1)S(1)} %collective-permute-done.refs_0_), channel_id=1, source_target_pairs={{0,1},{1,0},{2,3},{3,2},{4,5},{5,4},{6,7},{7,6},{8,9},{9,8},{10,11... | collective-permute-start | bytes 215048 | tf_op jit(solution)/shard_map/ppermute | solution.py:248
  18.3 3.6 %collective-permute-start.10 = (bf16[5,56,128]{2,1,0:T(8,128)(2,1)S(1)}, bf16[5,56,128]{2,1,0:T(8,128)(2,1)S(1)}, u32[]{:S(2)}, u32[]{:S(2)}) collective-permute-start(bf16[5,56,128]{2,1,0:T(8,128)(2,1)S(1)} %collective-permute-done.1.refs_1_), channel_id=1, source_target_pairs={{0,1},{1,0},{2,3},{3,2},{4,5},{5,4},{6,7},{7,6},{8,9},{9,8},{10,11... | collective-permute-start | bytes 215048 | tf_op jit(solution)/shard_map/ppermute | solution.py:248
  20.7 1.3 %collective-permute-start.11 = (bf16[5,56,128]{2,1,0:T(8,128)(2,1)S(1)}, bf16[5,56,128]{2,1,0:T(8,128)(2,1)S(1)}, u32[]{:S(2)}, u32[]{:S(2)}) collective-permute-start(bf16[5,56,128]{2,1,0:T(8,128)(2,1)S(1)} %collective-permute-done.2.refs_2_), channel_id=1, source_target_pairs={{0,1},{1,0},{2,3},{3,2},{4,5},{5,4},{6,7},{7,6},{8,9},{9,8},{10,11... | collective-permute-start | bytes 215048 | tf_op jit(solution)/shard_map/ppermute | solution.py:248
  21.4 1.3 %collective-permute-start.12 = (bf16[5,56,128]{2,1,0:T(8,128)(2,1)S(1)}, bf16[5,56,128]{2,1,0:T(8,128)(2,1)S(1)}, u32[]{:S(2)}, u32[]{:S(2)}) collective-permute-start(bf16[5,56,128]{2,1,0:T(8,128)(2,1)S(1)} %collective-permute-done.4.refs_3_), channel_id=1, source_target_pairs={{0,1},{1,0},{2,3},{3,2},{4,5},{5,4},{6,7},{7,6},{8,9},{9,8},{10,11... | collective-permute-start | bytes 215048 | tf_op jit(solution)/shard_map/ppermute | solution.py:248
  21.4 1.4 %collective-permute-start.13 = (bf16[5,56,128]{2,1,0:T(8,128)(2,1)S(1)}, bf16[5,56,128]{2,1,0:T(8,128)(2,1)S(1)}, u32[]{:S(2)}, u32[]{:S(2)}) collective-permute-start(bf16[5,56,128]{2,1,0:T(8,128)(2,1)S(1)} %collective-permute-done.5.refs_4_), channel_id=1, source_target_pairs={{0,1},{1,0},{2,3},{3,2},{4,5},{5,4},{6,7},{7,6},{8,9},{9,8},{10,11... | collective-permute-start | bytes 215048 | tf_op jit(solution)/shard_map/ppermute | solution.py:248
  25.2 1.4 %collective-permute-start.15 = (bf16[2,5,56,128]{3,2,1,0:T(8,128)(2,1)S(1)}, bf16[2,5,56,128]{3,2,1,0:T(8,128)(2,1)S(1)}, u32[]{:S(2)}, u32[]{:S(2)}) collective-permute-start(bf16[2,5,56,128]{3,2,1,0:T(8,128)(2,1)S(1)} %get-tuple-element.62), channel_id=1, source_target_pairs={{0,1},{1,0},{2,3},{3,2},{4,5},{5,4},{6,7},{7,6},{8,9},{9,8},{10,11... | collective-permute-start | bytes 430088 | tf_op jit(solution)/shard_map/ppermute | solution.py:248
  25.7 2.1 %collective-permute-start.18 = (bf16[2,5,56,128]{3,2,1,0:T(8,128)(2,1)S(1)}, bf16[2,5,56,128]{3,2,1,0:T(8,128)(2,1)S(1)}, u32[]{:S(2)}, u32[]{:S(2)}) collective-permute-start(bf16[2,5,56,128]{3,2,1,0:T(8,128)(2,1)S(1)} %get-tuple-element.68), channel_id=1, source_target_pairs={{0,1},{1,0},{2,3},{3,2},{4,5},{5,4},{6,7},{7,6},{8,9},{9,8},{10,11... | collective-permute-start | bytes 430088 | tf_op jit(solution)/shard_map/ppermute | solution.py:248
  25.8 11.2 %collective-permute-start.21 = (bf16[2,8,56,128]{3,2,1,0:T(8,128)(2,1)S(1)}, bf16[2,8,56,128]{3,2,1,0:T(8,128)(2,1)S(1)}, u32[]{:S(2)}, u32[]{:S(2)}) collective-permute-start(bf16[2,8,56,128]{3,2,1,0:T(8,128)(2,1)S(1)} %get-tuple-element.74), channel_id=1, source_target_pairs={{0,1},{1,0},{2,3},{3,2},{4,5},{5,4},{6,7},{7,6},{8,9},{9,8},{10,11... | collective-permute-start | bytes 688136 | tf_op jit(solution)/shard_map/ppermute | solution.py:248
  26.2 8.0 %collective-permute-start.24 = (bf16[2,5,56,128]{3,2,1,0:T(8,128)(2,1)S(1)}, bf16[2,5,56,128]{3,2,1,0:T(8,128)(2,1)S(1)}, u32[]{:S(2)}, u32[]{:S(2)}) collective-permute-start(bf16[2,5,56,128]{3,2,1,0:T(8,128)(2,1)S(1)} %get-tuple-element.82), channel_id=1, source_target_pairs={{0,1},{1,0},{2,3},{3,2},{4,5},{5,4},{6,7},{7,6},{8,9},{9,8},{10,11... | collective-permute-start | bytes 430088 | tf_op jit(solution)/shard_map/ppermute | solution.py:248
  26.7 5.1 %collective-permute-start.16 = (bf16[5,56,128]{2,1,0:T(8,128)(2,1)S(1)}, bf16[5,56,128]{2,1,0:T(8,128)(2,1)S(1)}, u32[]{:S(2)}, u32[]{:S(2)}) collective-permute-start(bf16[5,56,128]{2,1,0:T(8,128)(2,1)S(1)} %get-tuple-element.66), channel_id=1, source_target_pairs={{0,2},{2,0},{1,3},{3,1},{4,6},{6,4},{5,7},{7,5},{8,10},{10,8},{9,1... | collective-permute-start | bytes 215048 | tf_op jit(solution)/shard_map/ppermute | solution.py:248
  27.8 6.4 %collective-permute-start.19 = (bf16[5,56,128]{2,1,0:T(8,128)(2,1)S(1)}, bf16[5,56,128]{2,1,0:T(8,128)(2,1)S(1)}, u32[]{:S(2)}, u32[]{:S(2)}) collective-permute-start(bf16[5,56,128]{2,1,0:T(8,128)(2,1)S(1)} %get-tuple-element.72), channel_id=1, source_target_pairs={{0,2},{2,0},{1,3},{3,1},{4,6},{6,4},{5,7},{7,5},{8,10},{10,8},{9,1... | collective-permute-start | bytes 215048 | tf_op jit(solution)/shard_map/ppermute | solution.py:248
  31.9 6.6 %collective-permute-start.17 = (bf16[5,56,128]{2,1,0:T(8,128)(2,1)S(1)}, bf16[5,56,128]{2,1,0:T(8,128)(2,1)S(1)}, u32[]{:S(2)}, u32[]{:S(2)}) collective-permute-start(bf16[5,56,128]{2,1,0:T(8,128)(2,1)S(1)} %narrow_sum.2), channel_id=1, source_target_pairs={{0,12},{4,8},{8,4},{12,0},{1,13},{5,9},{9,5},{13,1},{2,14},{6,10},... | collective-permute-start | bytes 215048 | tf_op jit(solution)/shard_map/ppermute | solution.py:248
  34.2 6.4 %collective-permute-start.20 = (bf16[5,56,128]{2,1,0:T(8,128)(2,1)S(1)}, bf16[5,56,128]{2,1,0:T(8,128)(2,1)S(1)}, u32[]{:S(2)}, u32[]{:S(2)}) collective-permute-start(bf16[5,56,128]{2,1,0:T(8,128)(2,1)S(1)} %narrow_sum.3), channel_id=1, source_target_pairs={{0,8},{4,12},{8,0},{12,4},{1,9},{5,13},{9,1},{13,5},{2,10},{6,14},... | collective-permute-start | bytes 215048 | tf_op jit(solution)/shard_map/ppermute | solution.py:248
  34.6 6.5 %collective-permute-start.25 = (bf16[5,56,128]{2,1,0:T(8,128)(2,1)S(1)}, bf16[5,56,128]{2,1,0:T(8,128)(2,1)S(1)}, u32[]{:S(2)}, u32[]{:S(2)}) collective-permute-start(bf16[5,56,128]{2,1,0:T(8,128)(2,1)S(1)} %get-tuple-element.85), channel_id=1, source_target_pairs={{0,4},{2,6},{4,0},{6,2},{8,12},{10,14},{12,8},{14,10},{1,5},{3,7},... | collective-permute-start | bytes 215048 | tf_op jit(solution)/shard_map/ppermute | solution.py:248
  36.5 5.8 %collective-permute-start.26 = (bf16[5,56,128]{2,1,0:T(8,128)(2,1)S(1)}, bf16[5,56,128]{2,1,0:T(8,128)(2,1)S(1)}, u32[]{:S(2)}, u32[]{:S(2)}) collective-permute-start(bf16[5,56,128]{2,1,0:T(8,128)(2,1)S(1)} %get-tuple-element.86), channel_id=1, source_target_pairs={{0,6},{2,4},{4,2},{6,0},{8,14},{10,12},{12,10},{14,8},{1,7},{3,5},... | collective-permute-start | bytes 215048 | tf_op jit(solution)/shard_map/ppermute | solution.py:248
  37.1 5.2 %collective-permute-start.22 = (bf16[4,56,128]{2,1,0:T(8,128)(2,1)S(1)}, bf16[4,56,128]{2,1,0:T(8,128)(2,1)S(1)}, u32[]{:S(2)}, u32[]{:S(2)}) collective-permute-start(bf16[4,56,128]{2,1,0:T(8,128)(2,1)S(1)} %get-tuple-element.78), channel_id=1, source_target_pairs={{0,2},{2,0},{1,3},{3,1},{4,6},{6,4},{5,7},{7,5},{8,10},{10,8},{9,1... | collective-permute-start | bytes 172040 | tf_op jit(solution)/shard_map/ppermute | solution.py:248
  38.4 4.5 %collective-permute-start.23 = (bf16[4,56,128]{2,1,0:T(8,128)(2,1)S(1)}, bf16[4,56,128]{2,1,0:T(8,128)(2,1)S(1)}, u32[]{:S(2)}, u32[]{:S(2)}) collective-permute-start(bf16[4,56,128]{2,1,0:T(8,128)(2,1)S(1)} %get-tuple-element.80), channel_id=1, source_target_pairs={{0,2},{2,0},{1,3},{3,1},{4,6},{6,4},{5,7},{7,5},{8,10},{10,8},{9,1... | collective-permute-start | bytes 172040 | tf_op jit(solution)/shard_map/ppermute | solution.py:248
  (1 other events, 14.9 us)

commit v8 on v7

--- a/solution.py
+++ b/solution.py
@@ -206,7 +206,7 @@
     far, (total, stage) = refs[: len(order)], refs[-2:]
     topk, rows = route.shape
     tall = stage.shape[1]
-    stage[: 2 * CAP] = jnp.zeros((2 * CAP, tall, LANES), F32)
+    stage[:CAP] = jnp.zeros((CAP, tall, LANES), F32)
     for k, ref in zip(order, far):
         stage[k * CAP : (k + 1) * CAP] = ref[...].astype(F32)
     for t in range(rows):
@@ -216,26 +216,15 @@
         total[t] = value
 
 
-def combine_kernel(n_narrow, route, gains, far, *refs):
-    near, direct = refs[: HALVES * n_narrow], refs[HALVES * n_narrow : -3]
-    out, total, stage = refs[-3:]
+def combine_kernel(n_narrow, far, *refs):
+    near, (out, total) = refs[:-2], refs[-2:]
     rows, features = out.shape
     tall = features // LANES
-    topk = route.shape[0]
-    stage[0] = jnp.zeros((tall, LANES), F32)
-    arrived = direct[0][...].astype(F32)
-    for ref in direct[1:]:
-        arrived = arrived + ref[...].astype(F32)
-    stage[1:] = arrived
     for t in range(rows):
         value = far[t]
         cut, row = divmod(t, rows // HALVES)
         for ref in near[cut * n_narrow : (cut + 1) * n_narrow]:
             value = value + ref[row].astype(F32)
-        for k in range(topk):
-            slot = route[k, t] - CAP
-            slot = jnp.where((slot >= 0) & (slot < CAP), slot + 1, 0)
-            value = value + gains[k, t] * stage[slot]
         total[t * tall : (t + 1) * tall, :] = value
     for b in range(tall):
         out[:, b * LANES : (b + 1) * LANES] = total[
@@ -399,9 +388,9 @@
     def send_narrow(parts):
         return [parts[0]] + [swap(parts[j], "narrow", j) for j in range(1, n_narrow)]
 
-    far_back = []
-    for k in range(per - 1):
-        far_back += call(
+    sums = []
+    for k in range(per):
+        sums += call(
             functools.partial(narrow_sum_kernel, n_narrow),
             "narrow_sum",
             send_narrow(reduce_pair(far_out[k::per])),
@@ -410,16 +399,12 @@
             [],
             limit=limit,
         )
-    sums = far_back
-    far_back = [swap(value, "wide", k) for k, value in zip(order, far_back)]
-    direct_back = reduce_pair(far_out[per - 1 :: per])
+    order.append(1)
+    far_back = [swap(value, "wide", k) for k, value in zip(order, sums)]
     near_parts = reduce_pair(near_out, cuts=HALVES)
     near_back = []
     for cut in range(HALVES):
         near_back += send_narrow(near_parts[cut::HALVES])
-    direct_back = [
-        swap(value, across, n_narrow + j) for j, value in enumerate(direct_back)
-    ]
     far_sum = call(
         functools.partial(far_combine_kernel, order),
         "far_combine",
@@ -431,10 +416,10 @@
     return call(
         functools.partial(combine_kernel, n_narrow),
         "combine",
-        [route, gains, far_sum] + near_back + direct_back,
-        [SSPEC] * 2 + [VSPEC] * (1 + (HALVES + 1) * n_narrow),
+        [far_sum] + near_back,
+        [VSPEC] * (1 + HALVES * n_narrow),
         jax.ShapeDtypeStruct((tokens, features), BF16),
-        [VMEM((tokens * tall, LANES), F32), VMEM((CAP + 1, tall, LANES), F32)],
+        [VMEM((tokens * tall, LANES), F32)],
     )
 
 

time: 43.8 us -> 42.7 us (0.975)
  waiting for transfers between devices: 13.7 us -> 12.1 us
    ppermute x27, waiting for transfers between devices: 13.7 us -> 12.1 us  [swap(): return lax.ppermute(value, axis, [(i, i ^ offset) for i in range(size)])]
    pallas_call x11 -> x12, Pallas kernels: 6.81 us -> 6.79 us  [call(): pl.pallas_call(kernel, out_shape=outs, in_specs=specs, out_specs=jax.tree...]
  transfers between devices with their start and end apart: 27 -> 27, of which waited for: 15 -> 12; matrix products, arithmetic and copies ran while one was open for 0% -> 0% of each run, Pallas kernels for 5% -> 5%
where the time goes in v8:
time: 42.7 us; the launch traced here: 42.5 us
  starting transfers between devices  23.5 us (55%)
  waiting for transfers between devices  12.1 us (28%)
  Pallas kernels  6.79 us (16%)
    ppermute x27, starting transfers between devices, swap(): return lax.ppermute(value, axis, [(i, i ^ offset) for i in range(size)])  23.5 us
    ppermute x27, waiting for transfers between devices, swap(): return lax.ppermute(value, axis, [(i, i ^ offset) for i in range(size)])  12.1 us
    pallas_call x12, Pallas kernels, call(): pl.pallas_call(kernel, out_shape=outs, in_specs=specs, out_specs=jax.tree...  6.79 us
  transfers between devices with their start and end apart: 27, of which 12 were waited for; matrix products, arithmetic and copies ran while one was open for 0% of the time, Pallas kernels for 5%

profile of v8, /device:TPU:0, one launch (start us, length us, event | category | flops | bytes accessed | tf_op | source)
XLA Modules:
  0.0 42.5 jit_solution(10988543904557543158)
XLA Ops:
  0.0 1.4 %dispatch.1 = (bf16[9,56,128]{2,1,0:T(8,128)(2,1)S(1)}, bf16[5,56,128]{2,1,0:T(8,128)(2,1)S(1)}, bf16[5,56,128]{2,1,0:T(8,128)(2,1)S(1)}, bf16[5,56,128]{2,1,0:T...) custom-call(s32[2,8]{1,0:T(2,128)} %bitcast.14, s32[4]{0:T(128)} %place_in.1, f32[2,8]{1,0:T(2,128)} %bitcast.15, ...), custom_call_target="tpu_custom_call" | custom-call | tf_op jit(solution)/shard_map/dispatch/pallas_call | solution.py:249
  1.4 3.0 %collective-permute-start.6 = (bf16[9,56,128]{2,1,0:T(8,128)(2,1)S(1)}, bf16[9,56,128]{2,1,0:T(8,128)(2,1)S(1)}, u32[]{:S(2)}, u32[]{:S(2)}) collective-permute-start(bf16[9,56,128]{2,1,0:T(8,128)(2,1)S(1)} %get-tuple-element.54.refs_0_), channel_id=1, source_target_pairs={{0,2},{2,0},{1,3},{3,1},{4,6},{6,4},{5,7},{7,5},{8,10},{10,8},{9,1... | collective-permute-start | bytes 387080 | tf_op jit(solution)/shard_map/ppermute | solution.py:237
  4.4 3.6 %collective-permute-start = (bf16[5,56,128]{2,1,0:T(8,128)(2,1)S(1)}, bf16[5,56,128]{2,1,0:T(8,128)(2,1)S(1)}, u32[]{:S(2)}, u32[]{:S(2)}) collective-permute-start(bf16[5,56,128]{2,1,0:T(8,128)(2,1)S(1)} %get-tuple-element.48), channel_id=1, source_target_pairs={{0,12},{4,8},{8,4},{12,0},{1,13},{5,9},{9,5},{13,1},{2,14},{6,10},... | collective-permute-start | bytes 215048 | tf_op jit(solution)/shard_map/ppermute | solution.py:237
  8.0 0.5 %collective-permute-start.3 = (bf16[5,56,128]{2,1,0:T(8,128)(2,1)S(1)}, bf16[5,56,128]{2,1,0:T(8,128)(2,1)S(1)}, u32[]{:S(2)}, u32[]{:S(2)}) collective-permute-start(bf16[5,56,128]{2,1,0:T(8,128)(2,1)S(1)} %get-tuple-element.50), channel_id=1, source_target_pairs={{0,6},{2,4},{4,2},{6,0},{8,14},{10,12},{12,10},{14,8},{1,7},{3,5},... | collective-permute-start | bytes 215048 | tf_op jit(solution)/shard_map/ppermute | solution.py:237
  8.5 1.5 %collective-permute-start.2 = (bf16[5,56,128]{2,1,0:T(8,128)(2,1)S(1)}, bf16[5,56,128]{2,1,0:T(8,128)(2,1)S(1)}, u32[]{:S(2)}, u32[]{:S(2)}) collective-permute-start(bf16[5,56,128]{2,1,0:T(8,128)(2,1)S(1)} %get-tuple-element.50), channel_id=1, source_target_pairs={{0,4},{2,6},{4,0},{6,2},{8,12},{10,14},{12,8},{14,10},{1,5},{3,7},... | collective-permute-start | bytes 215048 | tf_op jit(solution)/shard_map/ppermute | solution.py:237
  10.1 1.3 %collective-permute-done.refs_0_ = bf16[5,56,128]{2,1,0:T(8,128)(2,1)S(1)} collective-permute-done((bf16[5,56,128]{2,1,0:T(8,128)(2,1)S(1)}, bf16[5,56,128]{2,1,0:T(8,128)(2,1)S(1)}, u32[]{:S(2)}, u32[]{:S(2)}) %collective-permute-start) | collective-permute-done | bytes 71712 | tf_op jit(solution)/shard_map/ppermute | solution.py:237
  11.4 2.4 %collective-permute-done.1.refs_1_ = bf16[5,56,128]{2,1,0:T(8,128)(2,1)S(1)} collective-permute-done((bf16[5,56,128]{2,1,0:T(8,128)(2,1)S(1)}, bf16[5,56,128]{2,1,0:T(8,128)(2,1)S(1)}, u32[]{:S(2)}, u32[]{:S(2)}) %collective-permute-start.1) | collective-permute-done | bytes 71712 | tf_op jit(solution)/shard_map/ppermute | solution.py:237
  13.8 0.9 %collective-permute-done.3.refs_5_ = bf16[5,56,128]{2,1,0:T(8,128)(2,1)S(1)} collective-permute-done((bf16[5,56,128]{2,1,0:T(8,128)(2,1)S(1)}, bf16[5,56,128]{2,1,0:T(8,128)(2,1)S(1)}, u32[]{:S(2)}, u32[]{:S(2)}) %collective-permute-start.3) | collective-permute-done | bytes 71712 | tf_op jit(solution)/shard_map/ppermute | solution.py:237
  14.7 0.6 %collective-permute-done.2.refs_2_ = bf16[5,56,128]{2,1,0:T(8,128)(2,1)S(1)} collective-permute-done((bf16[5,56,128]{2,1,0:T(8,128)(2,1)S(1)}, bf16[5,56,128]{2,1,0:T(8,128)(2,1)S(1)}, u32[]{:S(2)}, u32[]{:S(2)}) %collective-permute-start.2) | collective-permute-done | bytes 71712 | tf_op jit(solution)/shard_map/ppermute | solution.py:237
  15.3 0.5 %collective-permute-start.8 = (bf16[9,56,128]{2,1,0:T(8,128)(2,1)S(1)}, bf16[9,56,128]{2,1,0:T(8,128)(2,1)S(1)}, u32[]{:S(2)}, u32[]{:S(2)}) collective-permute-start(bf16[9,56,128]{2,1,0:T(8,128)(2,1)S(1)} %collective-permute-done.6.refs_1_), channel_id=1, source_target_pairs={{0,1},{1,0},{2,3},{3,2},{4,5},{5,4},{6,7},{7,6},{8,9},{9,8},{10,11... | collective-permute-start | bytes 387080 | tf_op jit(solution)/shard_map/ppermute | solution.py:237
  15.8 0.8 %collective-permute-start.4 = (bf16[5,56,128]{2,1,0:T(8,128)(2,1)S(1)}, bf16[5,56,128]{2,1,0:T(8,128)(2,1)S(1)}, u32[]{:S(2)}, u32[]{:S(2)}) collective-permute-start(bf16[5,56,128]{2,1,0:T(8,128)(2,1)S(1)} %collective-permute-done.refs_0_), channel_id=1, source_target_pairs={{0,2},{2,0},{1,3},{3,1},{4,6},{6,4},{5,7},{7,5},{8,10},{10,8},{9,1... | collective-permute-start | bytes 215048 | tf_op jit(solution)/shard_map/ppermute | solution.py:237
  16.5 1.3 %collective-permute-start.5 = (bf16[5,56,128]{2,1,0:T(8,128)(2,1)S(1)}, bf16[5,56,128]{2,1,0:T(8,128)(2,1)S(1)}, u32[]{:S(2)}, u32[]{:S(2)}) collective-permute-start(bf16[5,56,128]{2,1,0:T(8,128)(2,1)S(1)} %collective-permute-done.1.refs_1_), channel_id=1, source_target_pairs={{0,2},{2,0},{1,3},{3,1},{4,6},{6,4},{5,7},{7,5},{8,10},{10,8},{9,1... | collective-permute-start | bytes 215048 | tf_op jit(solution)/shard_map/ppermute | solution.py:237
  17.8 0.5 %collective-permute-start.9 = (bf16[5,56,128]{2,1,0:T(8,128)(2,1)S(1)}, bf16[5,56,128]{2,1,0:T(8,128)(2,1)S(1)}, u32[]{:S(2)}, u32[]{:S(2)}) collective-permute-start(bf16[5,56,128]{2,1,0:T(8,128)(2,1)S(1)} %collective-permute-done.refs_0_), channel_id=1, source_target_pairs={{0,1},{1,0},{2,3},{3,2},{4,5},{5,4},{6,7},{7,6},{8,9},{9,8},{10,11... | collective-permute-start | bytes 215048 | tf_op jit(solution)/shard_map/ppermute | solution.py:237
  18.4 2.0 %near_shared.1 = (bf16[32,7168]{1,0:T(8,128)(2,1)S(1)}, f32[32,128]{1,0:T(8,128)S(1)}, f32[32,7168]{1,0:T(8,128)S(1)}) custom-call(bf16[9,56,128]{2,1,0:T(8,128)(2,1)S(1)} %get-tuple-element.54.refs_0_, bf16[9,56,128]{2,1,0:T(8,128)(2,1)S(1)} %collective-permute-done.6.refs_1_, bf16[9,56,128]{2,1,0:T(8,128)(2,1)S(1)} %collective-permute-done.7.refs_2_, ...), custom_call_target="tpu_custom_call" | custom-call | flops 352321536 | bytes 11010048 | tf_op jit(solution)/shard_map/near_shared/pallas_call | solution.py:249
  20.9 0.5 %collective-permute-done.5.refs_4_ = bf16[5,56,128]{2,1,0:T(8,128)(2,1)S(1)} collective-permute-done((bf16[5,56,128]{2,1,0:T(8,128)(2,1)S(1)}, bf16[5,56,128]{2,1,0:T(8,128)(2,1)S(1)}, u32[]{:S(2)}, u32[]{:S(2)}) %collective-permute-start.5) | collective-permute-done | bytes 71712 | tf_op jit(solution)/shard_map/ppermute | solution.py:237
  21.4 0.5 %collective-permute-start.13 = (bf16[5,56,128]{2,1,0:T(8,128)(2,1)S(1)}, bf16[5,56,128]{2,1,0:T(8,128)(2,1)S(1)}, u32[]{:S(2)}, u32[]{:S(2)}) collective-permute-start(bf16[5,56,128]{2,1,0:T(8,128)(2,1)S(1)} %collective-permute-done.5.refs_4_), channel_id=1, source_target_pairs={{0,1},{1,0},{2,3},{3,2},{4,5},{5,4},{6,7},{7,6},{8,9},{9,8},{10,11... | collective-permute-start | bytes 215048 | tf_op jit(solution)/shard_map/ppermute | solution.py:237
  22.0 0.7 %collective-permute-done.12.refs_9_ = bf16[5,56,128]{2,1,0:T(8,128)(2,1)S(1)} collective-permute-done((bf16[5,56,128]{2,1,0:T(8,128)(2,1)S(1)}, bf16[5,56,128]{2,1,0:T(8,128)(2,1)S(1)}, u32[]{:S(2)}, u32[]{:S(2)}) %collective-permute-start.12) | collective-permute-done | bytes 71712 | tf_op jit(solution)/shard_map/ppermute | solution.py:237
  22.9 2.4 %routed.1 = (bf16[2,8,56,128]{3,2,1,0:T(8,128)(2,1)S(1)}, bf16[2,8,56,128]{3,2,1,0:T(8,128)(2,1)S(1)}, bf16[2,5,56,128]{3,2,1,0:T(8,128)(2,1)S(1)}, bf16[2,5,56,...) custom-call(bf16[5,56,128]{2,1,0:T(8,128)(2,1)S(1)} %collective-perm, ...), custom_call_target="tpu_custom_call" | custom-call | flops 1012924416 | bytes 11010048 | tf_op jit(solution)/shard_map/routed/pallas_call | solution.py:249
  25.3 0.4 collective-permute-start.15
  25.8 0.4 collective-permute-start.21
  26.3 0.3 collective-permute-done.15.refs_1_
  26.7 1.0 %collective-permute-start.16 = (bf16[5,56,128]{2,1,0:T(8,128)(2,1)S(1)}, bf16[5,56,128]{2,1,0:T(8,128)(2,1)S(1)}, u32[]{:S(2)}, u32[]{:S(2)}) collective-permute-start(bf16[5,56,128]{2,1,0:T(8,128)(2,1)S(1)} %get-tuple-element.66), channel_id=1, source_target_pairs={{0,2},{2,0},{1,3},{3,1},{4,6},{6,4},{5,7},{7,5},{8,10},{10,8},{9,1... | collective-permute-start | bytes 215048 | tf_op jit(solution)/shard_map/ppermute | solution.py:237
  27.8 1.1 %collective-permute-start.19 = (bf16[5,56,128]{2,1,0:T(8,128)(2,1)S(1)}, bf16[5,56,128]{2,1,0:T(8,128)(2,1)S(1)}, u32[]{:S(2)}, u32[]{:S(2)}) collective-permute-start(bf16[5,56,128]{2,1,0:T(8,128)(2,1)S(1)} %get-tuple-element.72), channel_id=1, source_target_pairs={{0,2},{2,0},{1,3},{3,1},{4,6},{6,4},{5,7},{7,5},{8,10},{10,8},{9,1... | collective-permute-start | bytes 215048 | tf_op jit(solution)/shard_map/ppermute | solution.py:237
  29.0 1.0 %collective-permute-start.22 = (bf16[5,56,128]{2,1,0:T(8,128)(2,1)S(1)}, bf16[5,56,128]{2,1,0:T(8,128)(2,1)S(1)}, u32[]{:S(2)}, u32[]{:S(2)}) collective-permute-start(bf16[5,56,128]{2,1,0:T(8,128)(2,1)S(1)} %get-tuple-element.78), channel_id=1, source_target_pairs={{0,2},{2,0},{1,3},{3,1},{4,6},{6,4},{5,7},{7,5},{8,10},{10,8},{9,1... | collective-permute-start | bytes 215048 | tf_op jit(solution)/shard_map/ppermute | solution.py:237
  30.0 1.8 %collective-permute-done.16.refs_1_ = bf16[5,56,128]{2,1,0:T(8,128)(2,1)S(1)} collective-permute-done((bf16[5,56,128]{2,1,0:T(8,128)(2,1)S(1)}, bf16[5,56,128]{2,1,0:T(8,128)(2,1)S(1)}, u32[]{:S(2)}, u32[]{:S(2)}) %collective-permute-start.16) | collective-permute-done | bytes 71712 | tf_op jit(solution)/shard_map/ppermute | solution.py:237
  31.9 2.4 %collective-permute-start.17 = (bf16[5,56,128]{2,1,0:T(8,128)(2,1)S(1)}, bf16[5,56,128]{2,1,0:T(8,128)(2,1)S(1)}, u32[]{:S(2)}, u32[]{:S(2)}) collective-permute-start(bf16[5,56,128]{2,1,0:T(8,128)(2,1)S(1)} %narrow_sum.3), channel_id=1, source_target_pairs={{0,12},{4,8},{8,4},{12,0},{1,13},{5,9},{9,5},{13,1},{2,14},{6,10},... | collective-permute-start | bytes 215048 | tf_op jit(solution)/shard_map/ppermute | solution.py:237
  34.6 1.9 %collective-permute-start.23 = (bf16[5,56,128]{2,1,0:T(8,128)(2,1)S(1)}, bf16[5,56,128]{2,1,0:T(8,128)(2,1)S(1)}, u32[]{:S(2)}, u32[]{:S(2)}) collective-permute-start(bf16[5,56,128]{2,1,0:T(8,128)(2,1)S(1)} %narrow_sum.5), channel_id=1, source_target_pairs={{0,4},{4,0},{8,12},{12,8},{1,5},{5,1},{9,13},{13,9},{2,6},{6,2},{1... | collective-permute-start | bytes 215048 | tf_op jit(solution)/shard_map/ppermute | solution.py:237
  36.6 1.1 %collective-permute-start.25 = (bf16[4,56,128]{2,1,0:T(8,128)(2,1)S(1)}, bf16[4,56,128]{2,1,0:T(8,128)(2,1)S(1)}, u32[]{:S(2)}, u32[]{:S(2)}) collective-permute-start(bf16[4,56,128]{2,1,0:T(8,128)(2,1)S(1)} %get-tuple-element.84), channel_id=1, source_target_pairs={{0,2},{2,0},{1,3},{3,1},{4,6},{6,4},{5,7},{7,5},{8,10},{10,8},{9,1... | collective-permute-start | bytes 172040 | tf_op jit(solution)/shard_map/ppermute | solution.py:237
  37.6 1.0 %collective-permute-start.26 = (bf16[4,56,128]{2,1,0:T(8,128)(2,1)S(1)}, bf16[4,56,128]{2,1,0:T(8,128)(2,1)S(1)}, u32[]{:S(2)}, u32[]{:S(2)}) collective-permute-start(bf16[4,56,128]{2,1,0:T(8,128)(2,1)S(1)} %get-tuple-element.86), channel_id=1, source_target_pairs={{0,2},{2,0},{1,3},{3,1},{4,6},{6,4},{5,7},{7,5},{8,10},{10,8},{9,1... | collective-permute-start | bytes 172040 | tf_op jit(solution)/shard_map/ppermute | solution.py:237
  38.7 2.0 %collective-permute-done.20.refs_1_ = bf16[5,56,128]{2,1,0:T(8,128)(2,1)S(1)} collective-permute-done((bf16[5,56,128]{2,1,0:T(8,128)(2,1)S(1)}, bf16[5,56,128]{2,1,0:T(8,128)(2,1)S(1)}, u32[]{:S(2)}, u32[]{:S(2)}) %collective-permute-start.20) | collective-permute-done | bytes 71712 | tf_op jit(solution)/shard_map/ppermute | solution.py:237
  40.8 1.0 %collective-permute-done.26.refs_3_ = bf16[4,56,128]{2,1,0:T(8,128)(2,1)S(1)} collective-permute-done((bf16[4,56,128]{2,1,0:T(8,128)(2,1)S(1)}, bf16[4,56,128]{2,1,0:T(8,128)(2,1)S(1)}, u32[]{:S(2)}, u32[]{:S(2)}) %collective-permute-start.26) | collective-permute-done | bytes 57376 | tf_op jit(solution)/shard_map/ppermute | solution.py:237
  41.8 0.7 %combine.1 = bf16[8,7168]{1,0:T(8,128)(2,1)} custom-call(f32[8,56,128]{2,1,0:T(8,128)S(1)} %far_combine.1.far, bf16[4,56,128]{2,1,0:T(8,128)(2,1)S(1)} %get-tuple-element.83.refs_0_, bf16[4,56,128]{2,1,0:T(8,128)(2,1)S(1)} %collective-permute-done.25.refs_1_, bf16[4,56,128]{2,1,0:T(8,128)(2,1)S(1)} %get-tuple-element.85.refs_2_, ...), custom_call_target="tpu_custom_call" | custom-call | tf_op jit(solution)/shard_map/combine/pallas_call | solution.py:249
  (46 shorter events, 1.8 us)
Async XLA Ops:
  0.0 18.4 %copy-start = (bf16[7168,256]{1,0:T(8,128)(2,1)S(1)}, bf16[7168,256]{1,0:T(8,128)(2,1)}, u32[]{:S(2)}) copy-start(bf16[7168,256]{1,0:T(8,128)(2,1)} %refs_3_.1) | copy-start | bytes 11010052
  0.0 18.4 %copy-start.1 = (bf16[7168,256]{1,0:T(8,128)(2,1)S(1)}, bf16[7168,256]{1,0:T(8,128)(2,1)}, u32[]{:S(2)}) copy-start(bf16[7168,256]{1,0:T(8,128)(2,1)} %refs_4_.3) | copy-start | bytes 11010052
  0.0 18.4 %copy-start.2 = (bf16[256,7168]{1,0:T(8,128)(2,1)S(1)}, bf16[256,7168]{1,0:T(8,128)(2,1)}, u32[]{:S(2)}) copy-start(bf16[256,7168]{1,0:T(8,128)(2,1)} %refs_5_.3) | copy-start | bytes 11010052
  1.4 13.9 %collective-permute-start.6 = (bf16[9,56,128]{2,1,0:T(8,128)(2,1)S(1)}, bf16[9,56,128]{2,1,0:T(8,128)(2,1)S(1)}, u32[]{:S(2)}, u32[]{:S(2)}) collective-permute-start(bf16[9,56,128]{2,1,0:T(8,128)(2,1)S(1)} %get-tuple-element.54.refs_0_), channel_id=1, source_target_pairs={{0,2},{2,0},{1,3},{3,1},{4,6},{6,4},{5,7},{7,5},{8,10},{10,8},{9,1... | collective-permute-start | bytes 387080 | tf_op jit(solution)/shard_map/ppermute | solution.py:237
  4.4 7.0 %collective-permute-start = (bf16[5,56,128]{2,1,0:T(8,128)(2,1)S(1)}, bf16[5,56,128]{2,1,0:T(8,128)(2,1)S(1)}, u32[]{:S(2)}, u32[]{:S(2)}) collective-permute-start(bf16[5,56,128]{2,1,0:T(8,128)(2,1)S(1)} %get-tuple-element.48), channel_id=1, source_target_pairs={{0,12},{4,8},{8,4},{12,0},{1,13},{5,9},{9,5},{13,1},{2,14},{6,10},... | collective-permute-start | bytes 215048 | tf_op jit(solution)/shard_map/ppermute | solution.py:237
  8.0 5.8 %collective-permute-start.1 = (bf16[5,56,128]{2,1,0:T(8,128)(2,1)S(1)}, bf16[5,56,128]{2,1,0:T(8,128)(2,1)S(1)}, u32[]{:S(2)}, u32[]{:S(2)}) collective-permute-start(bf16[5,56,128]{2,1,0:T(8,128)(2,1)S(1)} %get-tuple-element.49), channel_id=1, source_target_pairs={{0,8},{4,12},{8,0},{12,4},{1,9},{5,13},{9,1},{13,5},{2,10},{6,14},... | collective-permute-start | bytes 215048 | tf_op jit(solution)/shard_map/ppermute | solution.py:237
  8.0 14.9 %copy-start.4 = (bf16[1,7168,256]{2,1,0:T(8,128)(2,1)S(1)}, bf16[1,7168,256]{2,1,0:T(8,128)(2,1)}, u32[]{:S(2)}) copy-start(bf16[1,7168,256]{2,1,0:T(8,128)(2,1)} %param.17) | copy-start | bytes 11010052
  8.0 14.9 %copy-start.5 = (bf16[1,256,7168]{2,1,0:T(8,128)(2,1)S(1)}, bf16[1,256,7168]{2,1,0:T(8,128)(2,1)}, u32[]{:S(2)}) copy-start(bf16[1,256,7168]{2,1,0:T(8,128)(2,1)} %param.18) | copy-start | bytes 11010052
  8.0 6.7 %collective-permute-start.3 = (bf16[5,56,128]{2,1,0:T(8,128)(2,1)S(1)}, bf16[5,56,128]{2,1,0:T(8,128)(2,1)S(1)}, u32[]{:S(2)}, u32[]{:S(2)}) collective-permute-start(bf16[5,56,128]{2,1,0:T(8,128)(2,1)S(1)} %get-tuple-element.50), channel_id=1, source_target_pairs={{0,6},{2,4},{4,2},{6,0},{8,14},{10,12},{12,10},{14,8},{1,7},{3,5},... | collective-permute-start | bytes 215048 | tf_op jit(solution)/shard_map/ppermute | solution.py:237
  8.5 6.7 %collective-permute-start.2 = (bf16[5,56,128]{2,1,0:T(8,128)(2,1)S(1)}, bf16[5,56,128]{2,1,0:T(8,128)(2,1)S(1)}, u32[]{:S(2)}, u32[]{:S(2)}) collective-permute-start(bf16[5,56,128]{2,1,0:T(8,128)(2,1)S(1)} %get-tuple-element.50), channel_id=1, source_target_pairs={{0,4},{2,6},{4,0},{6,2},{8,12},{10,14},{12,8},{14,10},{1,5},{3,7},... | collective-permute-start | bytes 215048 | tf_op jit(solution)/shard_map/ppermute | solution.py:237
  15.3 2.5 %collective-permute-start.7 = (bf16[9,56,128]{2,1,0:T(8,128)(2,1)S(1)}, bf16[9,56,128]{2,1,0:T(8,128)(2,1)S(1)}, u32[]{:S(2)}, u32[]{:S(2)}) collective-permute-start(bf16[9,56,128]{2,1,0:T(8,128)(2,1)S(1)} %get-tuple-element.54.refs_0_), channel_id=1, source_target_pairs={{0,1},{1,0},{2,3},{3,2},{4,5},{5,4},{6,7},{7,6},{8,9},{9,8},{10,11... | collective-permute-start | bytes 387080 | tf_op jit(solution)/shard_map/ppermute | solution.py:237
  15.3 3.1 %collective-permute-start.8 = (bf16[9,56,128]{2,1,0:T(8,128)(2,1)S(1)}, bf16[9,56,128]{2,1,0:T(8,128)(2,1)S(1)}, u32[]{:S(2)}, u32[]{:S(2)}) collective-permute-start(bf16[9,56,128]{2,1,0:T(8,128)(2,1)S(1)} %collective-permute-done.6.refs_1_), channel_id=1, source_target_pairs={{0,1},{1,0},{2,3},{3,2},{4,5},{5,4},{6,7},{7,6},{8,9},{9,8},{10,11... | collective-permute-start | bytes 387080 | tf_op jit(solution)/shard_map/ppermute | solution.py:237
  15.8 4.9 %collective-permute-start.4 = (bf16[5,56,128]{2,1,0:T(8,128)(2,1)S(1)}, bf16[5,56,128]{2,1,0:T(8,128)(2,1)S(1)}, u32[]{:S(2)}, u32[]{:S(2)}) collective-permute-start(bf16[5,56,128]{2,1,0:T(8,128)(2,1)S(1)} %collective-permute-done.refs_0_), channel_id=1, source_target_pairs={{0,2},{2,0},{1,3},{3,1},{4,6},{6,4},{5,7},{7,5},{8,10},{10,8},{9,1... | collective-permute-start | bytes 215048 | tf_op jit(solution)/shard_map/ppermute | solution.py:237
  16.5 4.9 %collective-permute-start.5 = (bf16[5,56,128]{2,1,0:T(8,128)(2,1)S(1)}, bf16[5,56,128]{2,1,0:T(8,128)(2,1)S(1)}, u32[]{:S(2)}, u32[]{:S(2)}) collective-permute-start(bf16[5,56,128]{2,1,0:T(8,128)(2,1)S(1)} %collective-permute-done.1.refs_1_), channel_id=1, source_target_pairs={{0,2},{2,0},{1,3},{3,1},{4,6},{6,4},{5,7},{7,5},{8,10},{10,8},{9,1... | collective-permute-start | bytes 215048 | tf_op jit(solution)/shard_map/ppermute | solution.py:237
  17.8 3.6 %collective-permute-start.14 = (bf16[5,56,128]{2,1,0:T(8,128)(2,1)S(1)}, bf16[5,56,128]{2,1,0:T(8,128)(2,1)S(1)}, u32[]{:S(2)}, u32[]{:S(2)}) collective-permute-start(bf16[5,56,128]{2,1,0:T(8,128)(2,1)S(1)} %collective-permute-done.3.refs_5_), channel_id=1, source_target_pairs={{0,1},{1,0},{2,3},{3,2},{4,5},{5,4},{6,7},{7,6},{8,9},{9,8},{10,11... | collective-permute-start | bytes 215048 | tf_op jit(solution)/shard_map/ppermute | solution.py:237
  17.8 4.2 %collective-permute-start.9 = (bf16[5,56,128]{2,1,0:T(8,128)(2,1)S(1)}, bf16[5,56,128]{2,1,0:T(8,128)(2,1)S(1)}, u32[]{:S(2)}, u32[]{:S(2)}) collective-permute-start(bf16[5,56,128]{2,1,0:T(8,128)(2,1)S(1)} %collective-permute-done.refs_0_), channel_id=1, source_target_pairs={{0,1},{1,0},{2,3},{3,2},{4,5},{5,4},{6,7},{7,6},{8,9},{9,8},{10,11... | collective-permute-start | bytes 215048 | tf_op jit(solution)/shard_map/ppermute | solution.py:237
  18.3 3.6 %collective-permute-start.10 = (bf16[5,56,128]{2,1,0:T(8,128)(2,1)S(1)}, bf16[5,56,128]{2,1,0:T(8,128)(2,1)S(1)}, u32[]{:S(2)}, u32[]{:S(2)}) collective-permute-start(bf16[5,56,128]{2,1,0:T(8,128)(2,1)S(1)} %collective-permute-done.1.refs_1_), channel_id=1, source_target_pairs={{0,1},{1,0},{2,3},{3,2},{4,5},{5,4},{6,7},{7,6},{8,9},{9,8},{10,11... | collective-permute-start | bytes 215048 | tf_op jit(solution)/shard_map/ppermute | solution.py:237
  20.7 1.3 %collective-permute-start.11 = (bf16[5,56,128]{2,1,0:T(8,128)(2,1)S(1)}, bf16[5,56,128]{2,1,0:T(8,128)(2,1)S(1)}, u32[]{:S(2)}, u32[]{:S(2)}) collective-permute-start(bf16[5,56,128]{2,1,0:T(8,128)(2,1)S(1)} %collective-permute-done.2.refs_2_), channel_id=1, source_target_pairs={{0,1},{1,0},{2,3},{3,2},{4,5},{5,4},{6,7},{7,6},{8,9},{9,8},{10,11... | collective-permute-start | bytes 215048 | tf_op jit(solution)/shard_map/ppermute | solution.py:237
  21.4 1.3 %collective-permute-start.12 = (bf16[5,56,128]{2,1,0:T(8,128)(2,1)S(1)}, bf16[5,56,128]{2,1,0:T(8,128)(2,1)S(1)}, u32[]{:S(2)}, u32[]{:S(2)}) collective-permute-start(bf16[5,56,128]{2,1,0:T(8,128)(2,1)S(1)} %collective-permute-done.4.refs_3_), channel_id=1, source_target_pairs={{0,1},{1,0},{2,3},{3,2},{4,5},{5,4},{6,7},{7,6},{8,9},{9,8},{10,11... | collective-permute-start | bytes 215048 | tf_op jit(solution)/shard_map/ppermute | solution.py:237
  21.4 1.4 %collective-permute-start.13 = (bf16[5,56,128]{2,1,0:T(8,128)(2,1)S(1)}, bf16[5,56,128]{2,1,0:T(8,128)(2,1)S(1)}, u32[]{:S(2)}, u32[]{:S(2)}) collective-permute-start(bf16[5,56,128]{2,1,0:T(8,128)(2,1)S(1)} %collective-permute-done.5.refs_4_), channel_id=1, source_target_pairs={{0,1},{1,0},{2,3},{3,2},{4,5},{5,4},{6,7},{7,6},{8,9},{9,8},{10,11... | collective-permute-start | bytes 215048 | tf_op jit(solution)/shard_map/ppermute | solution.py:237
  25.3 1.4 %collective-permute-start.15 = (bf16[2,5,56,128]{3,2,1,0:T(8,128)(2,1)S(1)}, bf16[2,5,56,128]{3,2,1,0:T(8,128)(2,1)S(1)}, u32[]{:S(2)}, u32[]{:S(2)}) collective-permute-start(bf16[2,5,56,128]{3,2,1,0:T(8,128)(2,1)S(1)} %get-tuple-element.62), channel_id=1, source_target_pairs={{0,1},{1,0},{2,3},{3,2},{4,5},{5,4},{6,7},{7,6},{8,9},{9,8},{10,11... | collective-permute-start | bytes 430088 | tf_op jit(solution)/shard_map/ppermute | solution.py:237
  25.7 2.1 %collective-permute-start.18 = (bf16[2,5,56,128]{3,2,1,0:T(8,128)(2,1)S(1)}, bf16[2,5,56,128]{3,2,1,0:T(8,128)(2,1)S(1)}, u32[]{:S(2)}, u32[]{:S(2)}) collective-permute-start(bf16[2,5,56,128]{3,2,1,0:T(8,128)(2,1)S(1)} %get-tuple-element.68), channel_id=1, source_target_pairs={{0,1},{1,0},{2,3},{3,2},{4,5},{5,4},{6,7},{7,6},{8,9},{9,8},{10,11... | collective-permute-start | bytes 430088 | tf_op jit(solution)/shard_map/ppermute | solution.py:237
  25.8 3.1 %collective-permute-start.21 = (bf16[2,5,56,128]{3,2,1,0:T(8,128)(2,1)S(1)}, bf16[2,5,56,128]{3,2,1,0:T(8,128)(2,1)S(1)}, u32[]{:S(2)}, u32[]{:S(2)}) collective-permute-start(bf16[2,5,56,128]{3,2,1,0:T(8,128)(2,1)S(1)} %get-tuple-element.74), channel_id=1, source_target_pairs={{0,1},{1,0},{2,3},{3,2},{4,5},{5,4},{6,7},{7,6},{8,9},{9,8},{10,11... | collective-permute-start | bytes 430088 | tf_op jit(solution)/shard_map/ppermute | solution.py:237
  26.2 10.3 %collective-permute-start.24 = (bf16[2,8,56,128]{3,2,1,0:T(8,128)(2,1)S(1)}, bf16[2,8,56,128]{3,2,1,0:T(8,128)(2,1)S(1)}, u32[]{:S(2)}, u32[]{:S(2)}) collective-permute-start(bf16[2,8,56,128]{3,2,1,0:T(8,128)(2,1)S(1)} %get-tuple-element.80), channel_id=1, source_target_pairs={{0,1},{1,0},{2,3},{3,2},{4,5},{5,4},{6,7},{7,6},{8,9},{9,8},{10,11... | collective-permute-start | bytes 688136 | tf_op jit(solution)/shard_map/ppermute | solution.py:237
  26.7 5.1 %collective-permute-start.16 = (bf16[5,56,128]{2,1,0:T(8,128)(2,1)S(1)}, bf16[5,56,128]{2,1,0:T(8,128)(2,1)S(1)}, u32[]{:S(2)}, u32[]{:S(2)}) collective-permute-start(bf16[5,56,128]{2,1,0:T(8,128)(2,1)S(1)} %get-tuple-element.66), channel_id=1, source_target_pairs={{0,2},{2,0},{1,3},{3,1},{4,6},{6,4},{5,7},{7,5},{8,10},{10,8},{9,1... | collective-permute-start | bytes 215048 | tf_op jit(solution)/shard_map/ppermute | solution.py:237
  27.8 6.4 %collective-permute-start.19 = (bf16[5,56,128]{2,1,0:T(8,128)(2,1)S(1)}, bf16[5,56,128]{2,1,0:T(8,128)(2,1)S(1)}, u32[]{:S(2)}, u32[]{:S(2)}) collective-permute-start(bf16[5,56,128]{2,1,0:T(8,128)(2,1)S(1)} %get-tuple-element.72), channel_id=1, source_target_pairs={{0,2},{2,0},{1,3},{3,1},{4,6},{6,4},{5,7},{7,5},{8,10},{10,8},{9,1... | collective-permute-start | bytes 215048 | tf_op jit(solution)/shard_map/ppermute | solution.py:237
  29.0 5.6 %collective-permute-start.22 = (bf16[5,56,128]{2,1,0:T(8,128)(2,1)S(1)}, bf16[5,56,128]{2,1,0:T(8,128)(2,1)S(1)}, u32[]{:S(2)}, u32[]{:S(2)}) collective-permute-start(bf16[5,56,128]{2,1,0:T(8,128)(2,1)S(1)} %get-tuple-element.78), channel_id=1, source_target_pairs={{0,2},{2,0},{1,3},{3,1},{4,6},{6,4},{5,7},{7,5},{8,10},{10,8},{9,1... | collective-permute-start | bytes 215048 | tf_op jit(solution)/shard_map/ppermute | solution.py:237
  31.9 6.8 %collective-permute-start.17 = (bf16[5,56,128]{2,1,0:T(8,128)(2,1)S(1)}, bf16[5,56,128]{2,1,0:T(8,128)(2,1)S(1)}, u32[]{:S(2)}, u32[]{:S(2)}) collective-permute-start(bf16[5,56,128]{2,1,0:T(8,128)(2,1)S(1)} %narrow_sum.3), channel_id=1, source_target_pairs={{0,12},{4,8},{8,4},{12,0},{1,13},{5,9},{9,5},{13,1},{2,14},{6,10},... | collective-permute-start | bytes 215048 | tf_op jit(solution)/shard_map/ppermute | solution.py:237
  34.2 6.4 %collective-permute-start.20 = (bf16[5,56,128]{2,1,0:T(8,128)(2,1)S(1)}, bf16[5,56,128]{2,1,0:T(8,128)(2,1)S(1)}, u32[]{:S(2)}, u32[]{:S(2)}) collective-permute-start(bf16[5,56,128]{2,1,0:T(8,128)(2,1)S(1)} %narrow_sum.4), channel_id=1, source_target_pairs={{0,8},{4,12},{8,0},{12,4},{1,9},{5,13},{9,1},{13,5},{2,10},{6,14},... | collective-permute-start | bytes 215048 | tf_op jit(solution)/shard_map/ppermute | solution.py:237
  34.6 6.1 %collective-permute-start.23 = (bf16[5,56,128]{2,1,0:T(8,128)(2,1)S(1)}, bf16[5,56,128]{2,1,0:T(8,128)(2,1)S(1)}, u32[]{:S(2)}, u32[]{:S(2)}) collective-permute-start(bf16[5,56,128]{2,1,0:T(8,128)(2,1)S(1)} %narrow_sum.5), channel_id=1, source_target_pairs={{0,4},{4,0},{8,12},{12,8},{1,5},{5,1},{9,13},{13,9},{2,6},{6,2},{1... | collective-permute-start | bytes 215048 | tf_op jit(solution)/shard_map/ppermute | solution.py:237
  36.6 4.2 %collective-permute-start.25 = (bf16[4,56,128]{2,1,0:T(8,128)(2,1)S(1)}, bf16[4,56,128]{2,1,0:T(8,128)(2,1)S(1)}, u32[]{:S(2)}, u32[]{:S(2)}) collective-permute-start(bf16[4,56,128]{2,1,0:T(8,128)(2,1)S(1)} %get-tuple-element.84), channel_id=1, source_target_pairs={{0,2},{2,0},{1,3},{3,1},{4,6},{6,4},{5,7},{7,5},{8,10},{10,8},{9,1... | collective-permute-start | bytes 172040 | tf_op jit(solution)/shard_map/ppermute | solution.py:237
  37.6 4.2 %collective-permute-start.26 = (bf16[4,56,128]{2,1,0:T(8,128)(2,1)S(1)}, bf16[4,56,128]{2,1,0:T(8,128)(2,1)S(1)}, u32[]{:S(2)}, u32[]{:S(2)}) collective-permute-start(bf16[4,56,128]{2,1,0:T(8,128)(2,1)S(1)} %get-tuple-element.86), channel_id=1, source_target_pairs={{0,2},{2,0},{1,3},{3,1},{4,6},{6,4},{5,7},{7,5},{8,10},{10,8},{9,1... | collective-permute-start | bytes 172040 | tf_op jit(solution)/shard_map/ppermute | solution.py:237
  (1 other events, 14.9 us)

commit v9 on v8

--- a/solution.py
+++ b/solution.py
@@ -102,6 +102,12 @@
         ].astype(BF16)
 
 
+def gather_kernel(count, *refs):
+    out = refs[-1]
+    for i, ref in enumerate(refs[:count]):
+        out[i * CAP : (i + 1) * CAP] = ref[...]
+
+
 def silu_mul(gate, up):
     return (gate / (1.0 + jnp.exp(-gate)) * up).astype(BF16)
 
@@ -131,9 +137,17 @@
         value[:, at] = jnp.dot(hidden, down_w[:, at], preferred_element_type=F32)
 
 
-def routed_kernel(n_narrow, n_pair, per, *refs):
+def routed_kernel(n_narrow, n_pair, per, n_direct, *refs):
     count = n_narrow * n_pair * per
-    arrived, rest = refs[:count], refs[count:]
+    n_lines = n_narrow * (per - n_direct)
+    arrived = []
+    for c in range(n_pair):
+        *lines, gathered = refs[c * (n_lines + 1) : (c + 1) * (n_lines + 1)]
+        for j in range(n_narrow):
+            arrived += lines[j * (per - n_direct) : (j + 1) * (per - n_direct)]
+            for i in range(n_direct):
+                arrived.append(gathered.at[pl.ds((i * n_narrow + j) * CAP, CAP)])
+    rest = refs[n_pair * (n_lines + 1) :]
     near, weight, value, gate_w, up_w, down_w = rest[:6]
     near_outs, outs = rest[6 : 6 + n_pair], rest[6 + n_pair : -2]
     flat, inputs = rest[-2:]
@@ -202,26 +216,35 @@
         at += out.shape[0]
 
 
-def far_combine_kernel(order, route, gains, *refs):
-    far, (total, stage) = refs[: len(order)], refs[-2:]
-    topk, rows = route.shape
-    tall = stage.shape[1]
-    stage[:CAP] = jnp.zeros((CAP, tall, LANES), F32)
+def weigh(route, gains, stage, t):
+    value = gains[0, t] * stage[route[0, t]]
+    for k in range(1, route.shape[0]):
+        value = value + gains[k, t] * stage[route[k, t]]
+    return value
+
+
+def direct_combine_kernel(n_narrow, order, route, gains, *refs):
+    direct, (total, stage) = refs[: n_narrow * len(order)], refs[-2:]
+    stage[...] = jnp.zeros_like(stage)
+    for i, k in enumerate(order):
+        arrived = direct[i * n_narrow][...].astype(F32)
+        for ref in direct[i * n_narrow + 1 : (i + 1) * n_narrow]:
+            arrived = arrived + ref[...].astype(F32)
+        stage[k * CAP : (k + 1) * CAP] = arrived
+    for t in range(route.shape[1]):
+        total[t] = weigh(route, gains, stage, t)
+
+
+def combine_kernel(n_narrow, order, route, gains, direct, *refs):
+    near, far = refs[: HALVES * n_narrow], refs[HALVES * n_narrow : -3]
+    out, total, stage = refs[-3:]
+    rows, features = out.shape
+    tall = features // LANES
+    stage[...] = jnp.zeros_like(stage)
     for k, ref in zip(order, far):
         stage[k * CAP : (k + 1) * CAP] = ref[...].astype(F32)
     for t in range(rows):
-        value = gains[0, t] * stage[route[0, t]]
-        for k in range(1, topk):
-            value = value + gains[k, t] * stage[route[k, t]]
-        total[t] = value
-
-
-def combine_kernel(n_narrow, far, *refs):
-    near, (out, total) = refs[:-2], refs[-2:]
-    rows, features = out.shape
-    tall = features // LANES
-    for t in range(rows):
-        value = far[t]
+        value = direct[t] + weigh(route, gains, stage, t)
         cut, row = divmod(t, rows // HALVES)
         for ref in near[cut * n_narrow : (cut + 1) * n_narrow]:
             value = value + ref[row].astype(F32)
@@ -313,19 +336,23 @@
         ],
     )
     far, (route, gains) = far[:-2], far[-2:]
-    order = list(range(n_wide - 1, 1, -1))
+    directly = [k for k in (3, 1) if k < n_wide]
+    order = [k for k in range(n_wide - 1, 0, -1) if k not in directly]
     across = ("wide", "narrow")
     bundles = [swap(far[k - 1], "wide", k) for k in order]
-    direct = [swap(far[0], across, n_narrow + j) for j in range(n_narrow)]
+    direct = [
+        swap(far[k - 1], across, k * n_narrow + j)
+        for k in directly
+        for j in range(n_narrow)
+    ]
     near_line = [near] + [swap(near, "narrow", j) for j in range(1, n_narrow)]
-    bundles = after(bundles, *direct)
     if n_wide > 4:
         bundles = [jnp.concatenate(bundles, axis=0)]
     lines = [list(bundles)]
     for j in range(1, n_narrow):
         lines.append([swap(value, "narrow", j) for value in bundles])
-    per = len(bundles) + 1
-    slots = [value.shape[0] for value in bundles] + [CAP]
+    per = len(bundles) + len(directly)
+    slots = [value.shape[0] for value in bundles] + [CAP] * len(directly)
     near_line = after(near_line, *bundles)
     near_all = list(near_line)
     for c in range(1, n_pair):
@@ -348,10 +375,16 @@
         limit=limit,
     )
     side = after([value for line in lines[1:] for value in line], near_mid[1])
-    far_line = []
-    for j in range(n_narrow):
-        far_line += lines[0] if j == 0 else side[(j - 1) * (per - 1) : j * (per - 1)]
-        far_line.append(direct[j])
+    direct = after(direct, *side)
+    gathered = call(
+        functools.partial(gather_kernel, len(direct)),
+        "gather",
+        direct,
+        [VSPEC] * len(direct),
+        block(CAP * len(direct)),
+        [],
+    )
+    far_line = lines[0] + side + [gathered]
     far_all = list(far_line)
     for c in range(1, n_pair):
         far_all += [swap(value, "pair", c) for value in far_line]
@@ -360,10 +393,10 @@
     pass_rows = far_rows if far_rows <= MAX_ROWS else sum(slots)
     pass_rows = near_rows + -(-pass_rows // 16) * 16
     outs = call(
-        functools.partial(routed_kernel, n_narrow, n_pair, per),
+        functools.partial(routed_kernel, n_narrow, n_pair, per, len(directly)),
         "routed",
         far_all + list(near_mid) + routed,
-        [VSPEC] * (n_narrow * n_pair * per + 6),
+        [VSPEC] * (len(far_all) + 6),
         [block(n_narrow, tokens)] * n_pair
         + [block(n_narrow, count) for count in slots] * n_pair,
         [VMEM((pass_rows * tall, LANES), F32), VMEM((pass_rows, features), BF16)],
@@ -389,7 +422,7 @@
         return [parts[0]] + [swap(parts[j], "narrow", j) for j in range(1, n_narrow)]
 
     sums = []
-    for k in range(per):
+    for k in range(len(bundles)):
         sums += call(
             functools.partial(narrow_sum_kernel, n_narrow),
             "narrow_sum",
@@ -399,27 +432,35 @@
             [],
             limit=limit,
         )
-    order.append(1)
+    direct_back = []
+    for i, k in enumerate(directly):
+        parts = reduce_pair(far_out[len(bundles) + i :: per])
+        direct_back += [
+            swap(value, across, k * n_narrow + j) for j, value in enumerate(parts)
+        ]
     far_back = [swap(value, "wide", k) for k, value in zip(order, sums)]
     near_parts = reduce_pair(near_out, cuts=HALVES)
     near_back = []
     for cut in range(HALVES):
         near_back += send_narrow(near_parts[cut::HALVES])
-    far_sum = call(
-        functools.partial(far_combine_kernel, order),
-        "far_combine",
-        [route, gains] + far_back + in_hbm(*shared, *routed),
-        [SSPEC] * 2 + [VSPEC] * len(order) + [ASPEC] * 6,
+    direct_sum = call(
+        functools.partial(direct_combine_kernel, n_narrow, directly),
+        "direct_combine",
+        [route, gains] + direct_back + in_hbm(*shared, *routed),
+        [SSPEC] * 2 + [VSPEC] * len(direct_back) + [ASPEC] * 6,
         jax.ShapeDtypeStruct((tokens, tall, LANES), F32),
         [VMEM((n_wide * CAP, tall, LANES), F32)],
     )
     return call(
-        functools.partial(combine_kernel, n_narrow),
+        functools.partial(combine_kernel, n_narrow, order),
         "combine",
-        [far_sum] + near_back,
-        [VSPEC] * (1 + HALVES * n_narrow),
+        [route, gains, direct_sum] + near_back + far_back,
+        [SSPEC] * 2 + [VSPEC] * (1 + HALVES * n_narrow + len(far_back)),
         jax.ShapeDtypeStruct((tokens, features), BF16),
-        [VMEM((tokens * tall, LANES), F32)],
+        [
+            VMEM((tokens * tall, LANES), F32),
+            VMEM((n_wide * CAP, tall, LANES), F32),
+        ],
     )
 
 

time: 42.7 us -> 45.8 us (1.073)
  starting transfers between devices: 23.5 us -> 27.4 us
  waiting for transfers between devices: 12.1 us -> 11.3 us
    ppermute x27 -> x24, starting transfers between devices: 23.5 us -> 27.4 us  [swap(): return lax.ppermute(value, axis, [(i, i ^ offset) for i in range(size)])]
    ppermute x27 -> x24, waiting for transfers between devices: 12.1 us -> 11.3 us  [swap(): return lax.ppermute(value, axis, [(i, i ^ offset) for i in range(size)])]
    pallas_call x12 -> x11, Pallas kernels: 6.79 us -> 6.83 us  [call(): pl.pallas_call(kernel, out_shape=outs, in_specs=specs, out_specs=jax.tree...]
  transfers between devices with their start and end apart: 27 -> 24, of which waited for: 12 -> 12; matrix products, arithmetic and copies ran while one was open for 0% -> 0% of each run, Pallas kernels for 5% -> 5%
where the time goes in v9:
time: 45.8 us; the launch traced here: 45.7 us
  starting transfers between devices  27.4 us (60%)
  waiting for transfers between devices  11.3 us (25%)
  Pallas kernels  6.83 us (15%)
    ppermute x24, starting transfers between devices, swap(): return lax.ppermute(value, axis, [(i, i ^ offset) for i in range(size)])  27.4 us
    ppermute x24, waiting for transfers between devices, swap(): return lax.ppermute(value, axis, [(i, i ^ offset) for i in range(size)])  11.3 us
    pallas_call x11, Pallas kernels, call(): pl.pallas_call(kernel, out_shape=outs, in_specs=specs, out_specs=jax.tree...  6.83 us
  transfers between devices with their start and end apart: 24, of which 12 were waited for; matrix products, arithmetic and copies ran while one was open for 0% of the time, Pallas kernels for 5%

profile of v9, /device:TPU:0, one launch (start us, length us, event | category | flops | bytes accessed | tf_op | source)
XLA Modules:
  0.0 45.7 jit_solution(10898821587140035610)
XLA Ops:
  0.0 1.4 %dispatch.1 = (bf16[9,56,128]{2,1,0:T(8,128)(2,1)S(1)}, bf16[5,56,128]{2,1,0:T(8,128)(2,1)S(1)}, bf16[5,56,128]{2,1,0:T(8,128)(2,1)S(1)}, bf16[5,56,128]{2,1,0:T...) custom-call(s32[2,8]{1,0:T(2,128)} %bitcast.14, s32[4]{0:T(128)} %place_in.1, f32[2,8]{1,0:T(2,128)} %bitcast.15, ...), custom_call_target="tpu_custom_call" | custom-call | tf_op jit(solution)/shard_map/dispatch/pallas_call | solution.py:272
  1.4 3.0 %collective-permute-start.2 = (bf16[9,56,128]{2,1,0:T(8,128)(2,1)S(1)}, bf16[9,56,128]{2,1,0:T(8,128)(2,1)S(1)}, u32[]{:S(2)}, u32[]{:S(2)}) collective-permute-start(bf16[9,56,128]{2,1,0:T(8,128)(2,1)S(1)} %get-tuple-element.51.refs_0_), channel_id=1, source_target_pairs={{0,2},{2,0},{1,3},{3,1},{4,6},{6,4},{5,7},{7,5},{8,10},{10,8},{9,1... | collective-permute-start | bytes 387080 | tf_op jit(solution)/shard_map/ppermute | solution.py:260
  4.4 2.6 %collective-permute-start = (bf16[5,56,128]{2,1,0:T(8,128)(2,1)S(1)}, bf16[5,56,128]{2,1,0:T(8,128)(2,1)S(1)}, u32[]{:S(2)}, u32[]{:S(2)}) collective-permute-start(bf16[5,56,128]{2,1,0:T(8,128)(2,1)S(1)} %get-tuple-element.49), channel_id=1, source_target_pairs={{0,8},{4,12},{8,0},{12,4},{1,9},{5,13},{9,1},{13,5},{2,10},{6,14},... | collective-permute-start | bytes 215048 | tf_op jit(solution)/shard_map/ppermute | solution.py:260
  7.0 3.8 %collective-permute-done.refs_0_ = bf16[5,56,128]{2,1,0:T(8,128)(2,1)S(1)} collective-permute-done((bf16[5,56,128]{2,1,0:T(8,128)(2,1)S(1)}, bf16[5,56,128]{2,1,0:T(8,128)(2,1)S(1)}, u32[]{:S(2)}, u32[]{:S(2)}) %collective-permute-start) | collective-permute-done | bytes 71712 | tf_op jit(solution)/shard_map/ppermute | solution.py:260
  10.8 0.5 %collective-permute-start.4 = (bf16[9,56,128]{2,1,0:T(8,128)(2,1)S(1)}, bf16[9,56,128]{2,1,0:T(8,128)(2,1)S(1)}, u32[]{:S(2)}, u32[]{:S(2)}) collective-permute-start(bf16[9,56,128]{2,1,0:T(8,128)(2,1)S(1)} %collective-permute-done.2.refs_1_), channel_id=1, source_target_pairs={{0,1},{1,0},{2,3},{3,2},{4,5},{5,4},{6,7},{7,6},{8,9},{9,8},{10,11... | collective-permute-start | bytes 387080 | tf_op jit(solution)/shard_map/ppermute | solution.py:260
  11.3 0.5 %collective-permute-start.1 = (bf16[5,56,128]{2,1,0:T(8,128)(2,1)S(1)}, bf16[5,56,128]{2,1,0:T(8,128)(2,1)S(1)}, u32[]{:S(2)}, u32[]{:S(2)}) collective-permute-start(bf16[5,56,128]{2,1,0:T(8,128)(2,1)S(1)} %collective-permute-done.refs_0_), channel_id=1, source_target_pairs={{0,2},{2,0},{1,3},{3,1},{4,6},{6,4},{5,7},{7,5},{8,10},{10,8},{9,1... | collective-permute-start | bytes 215048 | tf_op jit(solution)/shard_map/ppermute | solution.py:260
  11.8 4.2 %collective-permute-start.6 = (bf16[5,56,128]{2,1,0:T(8,128)(2,1)S(1)}, bf16[5,56,128]{2,1,0:T(8,128)(2,1)S(1)}, u32[]{:S(2)}, u32[]{:S(2)}) collective-permute-start(bf16[5,56,128]{2,1,0:T(8,128)(2,1)S(1)} %get-tuple-element.55), channel_id=1, source_target_pairs={{0,14},{2,12},{4,10},{6,8},{8,6},{10,4},{12,2},{14,0},{1,15},{3,13... | collective-permute-start | bytes 215048 | tf_op jit(solution)/shard_map/ppermute | solution.py:260
  16.0 0.6 %collective-permute-start.5 = (bf16[5,56,128]{2,1,0:T(8,128)(2,1)S(1)}, bf16[5,56,128]{2,1,0:T(8,128)(2,1)S(1)}, u32[]{:S(2)}, u32[]{:S(2)}) collective-permute-start(bf16[5,56,128]{2,1,0:T(8,128)(2,1)S(1)} %get-tuple-element.55), channel_id=1, source_target_pairs={{0,12},{2,14},{4,8},{6,10},{8,4},{10,6},{12,0},{14,2},{1,13},{3,15... | collective-permute-start | bytes 215048 | tf_op jit(solution)/shard_map/ppermute | solution.py:260
  16.7 2.0 %collective-permute-start.7 = (bf16[5,56,128]{2,1,0:T(8,128)(2,1)S(1)}, bf16[5,56,128]{2,1,0:T(8,128)(2,1)S(1)}, u32[]{:S(2)}, u32[]{:S(2)}) collective-permute-start(bf16[5,56,128]{2,1,0:T(8,128)(2,1)S(1)} %get-tuple-element.56), channel_id=1, source_target_pairs={{0,4},{2,6},{4,0},{6,2},{8,12},{10,14},{12,8},{14,10},{1,5},{3,7},... | collective-permute-start | bytes 215048 | tf_op jit(solution)/shard_map/ppermute | solution.py:260
  18.6 2.0 %near_shared.1 = (bf16[32,7168]{1,0:T(8,128)(2,1)S(1)}, f32[32,128]{1,0:T(8,128)S(1)}, f32[32,7168]{1,0:T(8,128)S(1)}) custom-call(bf16[9,56,128]{2,1,0:T(8,128)(2,1)S(1)} %get-tuple-element.51.refs_0_, bf16[9,56,128]{2,1,0:T(8,128)(2,1)S(1)} %collective-permute-done.2.refs_1_, bf16[9,56,128]{2,1,0:T(8,128)(2,1)S(1)} %collective-permute-done.3.refs_2_, ...), custom_call_target="tpu_custom_call" | custom-call | flops 352321536 | bytes 11010048 | tf_op jit(solution)/shard_map/near_shared/pallas_call | solution.py:272
  20.7 2.3 %collective-permute-done.5.refs_0_ = bf16[5,56,128]{2,1,0:T(8,128)(2,1)S(1)} collective-permute-done((bf16[5,56,128]{2,1,0:T(8,128)(2,1)S(1)}, bf16[5,56,128]{2,1,0:T(8,128)(2,1)S(1)}, u32[]{:S(2)}, u32[]{:S(2)}) %collective-permute-start.5) | collective-permute-done | bytes 71712 | tf_op jit(solution)/shard_map/ppermute | solution.py:260
  23.1 0.3 collective-permute-done.7.refs_2_
  23.6 0.5 %collective-permute-start.9 = (bf16[5,56,128]{2,1,0:T(8,128)(2,1)S(1)}, bf16[5,56,128]{2,1,0:T(8,128)(2,1)S(1)}, u32[]{:S(2)}, u32[]{:S(2)}) collective-permute-start(bf16[5,56,128]{2,1,0:T(8,128)(2,1)S(1)} %collective-permute-done.refs_0_), channel_id=1, source_target_pairs={{0,1},{1,0},{2,3},{3,2},{4,5},{5,4},{6,7},{7,6},{8,9},{9,8},{10,11... | collective-permute-start | bytes 215048 | tf_op jit(solution)/shard_map/ppermute | solution.py:260
  24.1 1.1 %collective-permute-done.9.refs_3_ = bf16[5,56,128]{2,1,0:T(8,128)(2,1)S(1)} collective-permute-done((bf16[5,56,128]{2,1,0:T(8,128)(2,1)S(1)}, bf16[5,56,128]{2,1,0:T(8,128)(2,1)S(1)}, u32[]{:S(2)}, u32[]{:S(2)}) %collective-permute-start.9) | collective-permute-done | bytes 71712 | tf_op jit(solution)/shard_map/ppermute | solution.py:260
  25.4 2.4 %routed.1 = (bf16[2,8,56,128]{3,2,1,0:T(8,128)(2,1)S(1)}, bf16[2,8,56,128]{3,2,1,0:T(8,128)(2,1)S(1)}, bf16[2,5,56,128]{3,2,1,0:T(8,128)(2,1)S(1)}, bf16[2,5,56,...) custom-call(bf16[5,56,128]{2,1,0:T(8,128)(2,1)S(1)} %collective-perm, ...), custom_call_target="tpu_custom_call" | custom-call | flops 1012924416 | bytes 11010048 | tf_op jit(solution)/shard_map/routed/pallas_call | solution.py:272
  27.7 0.2 collective-permute-start.18
  27.9 0.4 collective-permute-start.21
  28.3 0.1 collective-permute-start.12
  28.4 0.4 collective-permute-start.15
  28.8 0.7 %collective-permute-done.21.refs_1_ = bf16[2,5,56,128]{3,2,1,0:T(8,128)(2,1)S(1)} collective-permute-done((bf16[2,5,56,128]{3,2,1,0:T(8,128)(2,1)S(1)}, bf16[2,5,56,128]{3,2,1,0:T(8,128)(2,1)S(1)}, u32[]{:S(2)}, u32[]{:S(2)}) %collective-permute-start.21) | collective-permute-done | bytes 143392 | tf_op jit(solution)/shard_map/ppermute | solution.py:260
  29.5 1.1 %collective-permute-start.22 = (bf16[5,56,128]{2,1,0:T(8,128)(2,1)S(1)}, bf16[5,56,128]{2,1,0:T(8,128)(2,1)S(1)}, u32[]{:S(2)}, u32[]{:S(2)}) collective-permute-start(bf16[5,56,128]{2,1,0:T(8,128)(2,1)S(1)} %get-tuple-element.88), channel_id=1, source_target_pairs={{0,2},{2,0},{1,3},{3,1},{4,6},{6,4},{5,7},{7,5},{8,10},{10,8},{9,1... | collective-permute-start | bytes 215048 | tf_op jit(solution)/shard_map/ppermute | solution.py:260
  30.6 2.7 %collective-permute-start.13 = (bf16[5,56,128]{2,1,0:T(8,128)(2,1)S(1)}, bf16[5,56,128]{2,1,0:T(8,128)(2,1)S(1)}, u32[]{:S(2)}, u32[]{:S(2)}) collective-permute-start(bf16[5,56,128]{2,1,0:T(8,128)(2,1)S(1)} %get-tuple-element.67), channel_id=1, source_target_pairs={{0,12},{2,14},{4,8},{6,10},{8,4},{10,6},{12,0},{14,2},{1,13},{3,15... | collective-permute-start | bytes 215048 | tf_op jit(solution)/shard_map/ppermute | solution.py:260
  33.3 1.6 %collective-permute-start.14 = (bf16[5,56,128]{2,1,0:T(8,128)(2,1)S(1)}, bf16[5,56,128]{2,1,0:T(8,128)(2,1)S(1)}, u32[]{:S(2)}, u32[]{:S(2)}) collective-permute-start(bf16[5,56,128]{2,1,0:T(8,128)(2,1)S(1)} %get-tuple-element.68), channel_id=1, source_target_pairs={{0,14},{2,12},{4,10},{6,8},{8,6},{10,4},{12,2},{14,0},{1,15},{3,13... | collective-permute-start | bytes 215048 | tf_op jit(solution)/shard_map/ppermute | solution.py:260
  35.1 2.4 %collective-permute-start.17 = (bf16[5,56,128]{2,1,0:T(8,128)(2,1)S(1)}, bf16[5,56,128]{2,1,0:T(8,128)(2,1)S(1)}, u32[]{:S(2)}, u32[]{:S(2)}) collective-permute-start(bf16[5,56,128]{2,1,0:T(8,128)(2,1)S(1)} %get-tuple-element.74), channel_id=1, source_target_pairs={{0,6},{2,4},{4,2},{6,0},{8,14},{10,12},{12,10},{14,8},{1,7},{3,5},... | collective-permute-start | bytes 215048 | tf_op jit(solution)/shard_map/ppermute | solution.py:260
  37.6 1.3 %collective-permute-start.23 = (bf16[5,56,128]{2,1,0:T(8,128)(2,1)S(1)}, bf16[5,56,128]{2,1,0:T(8,128)(2,1)S(1)}, u32[]{:S(2)}, u32[]{:S(2)}) collective-permute-start(bf16[5,56,128]{2,1,0:T(8,128)(2,1)S(1)} %narrow_sum.1), channel_id=1, source_target_pairs={{0,8},{4,12},{8,0},{12,4},{1,9},{5,13},{9,1},{13,5},{2,10},{6,14},... | collective-permute-start | bytes 215048 | tf_op jit(solution)/shard_map/ppermute | solution.py:260
  39.0 1.3 %collective-permute-start.19 = (bf16[4,56,128]{2,1,0:T(8,128)(2,1)S(1)}, bf16[4,56,128]{2,1,0:T(8,128)(2,1)S(1)}, u32[]{:S(2)}, u32[]{:S(2)}) collective-permute-start(bf16[4,56,128]{2,1,0:T(8,128)(2,1)S(1)} %get-tuple-element.80), channel_id=1, source_target_pairs={{0,2},{2,0},{1,3},{3,1},{4,6},{6,4},{5,7},{7,5},{8,10},{10,8},{9,1... | collective-permute-start | bytes 172040 | tf_op jit(solution)/shard_map/ppermute | solution.py:260
  40.3 0.4 collective-permute-done.14.refs_1_
  40.7 1.7 %collective-permute-start.20 = (bf16[4,56,128]{2,1,0:T(8,128)(2,1)S(1)}, bf16[4,56,128]{2,1,0:T(8,128)(2,1)S(1)}, u32[]{:S(2)}, u32[]{:S(2)}) collective-permute-start(bf16[4,56,128]{2,1,0:T(8,128)(2,1)S(1)} %get-tuple-element.82), channel_id=1, source_target_pairs={{0,2},{2,0},{1,3},{3,1},{4,6},{6,4},{5,7},{7,5},{8,10},{10,8},{9,1... | collective-permute-start | bytes 172040 | tf_op jit(solution)/shard_map/ppermute | solution.py:260
  42.4 0.7 %collective-permute-done.17.refs_3_ = bf16[5,56,128]{2,1,0:T(8,128)(2,1)S(1)} collective-permute-done((bf16[5,56,128]{2,1,0:T(8,128)(2,1)S(1)}, bf16[5,56,128]{2,1,0:T(8,128)(2,1)S(1)}, u32[]{:S(2)}, u32[]{:S(2)}) %collective-permute-start.17) | collective-permute-done | bytes 71712 | tf_op jit(solution)/shard_map/ppermute | solution.py:260
  43.3 0.4 collective-permute-done.19.refs_1_
  43.7 1.2 %collective-permute-done.20.refs_3_ = bf16[4,56,128]{2,1,0:T(8,128)(2,1)S(1)} collective-permute-done((bf16[4,56,128]{2,1,0:T(8,128)(2,1)S(1)}, bf16[4,56,128]{2,1,0:T(8,128)(2,1)S(1)}, u32[]{:S(2)}, u32[]{:S(2)}) %collective-permute-start.20) | collective-permute-done | bytes 57376 | tf_op jit(solution)/shard_map/ppermute | solution.py:260
  44.9 0.8 %combine.1 = bf16[8,7168]{1,0:T(8,128)(2,1)} custom-call(s32[2,8]{1,0:T(2,128)S(4)} %get-tuple-element.47.route, f32[2,8]{1,0:T(2,128)S(4)} %get-tuple-element.48.gains, f32[8,56,128]{2,1,0:T(8,128)S(1)} %direct_combine.1.direct, bf16[4,56,128]{2,1,0:T(8,128)(2,1)S(1)} %get-tuple-element.79.refs_0_, bf16[4,56,128]{2,1,0:T(8,128)(2,1)S(1)} %collective-permute-done.19.refs_1_, ...), custom_call_target="tpu_custom_call" | custom-call | tf_op jit(solution)/shard_map/combine/pallas_call | solution.py:272
  (39 shorter events, 1.0 us)
Async XLA Ops:
  0.0 18.6 %copy-start = (bf16[7168,256]{1,0:T(8,128)(2,1)S(1)}, bf16[7168,256]{1,0:T(8,128)(2,1)}, u32[]{:S(2)}) copy-start(bf16[7168,256]{1,0:T(8,128)(2,1)} %refs_4_.3) | copy-start | bytes 11010052
  0.0 18.6 %copy-start.1 = (bf16[7168,256]{1,0:T(8,128)(2,1)S(1)}, bf16[7168,256]{1,0:T(8,128)(2,1)}, u32[]{:S(2)}) copy-start(bf16[7168,256]{1,0:T(8,128)(2,1)} %refs_5_.3) | copy-start | bytes 11010052
  0.0 18.6 %copy-start.2 = (bf16[256,7168]{1,0:T(8,128)(2,1)S(1)}, bf16[256,7168]{1,0:T(8,128)(2,1)}, u32[]{:S(2)}) copy-start(bf16[256,7168]{1,0:T(8,128)(2,1)} %refs_6_.3) | copy-start | bytes 11010052
  1.4 9.4 %collective-permute-start.2 = (bf16[9,56,128]{2,1,0:T(8,128)(2,1)S(1)}, bf16[9,56,128]{2,1,0:T(8,128)(2,1)S(1)}, u32[]{:S(2)}, u32[]{:S(2)}) collective-permute-start(bf16[9,56,128]{2,1,0:T(8,128)(2,1)S(1)} %get-tuple-element.51.refs_0_), channel_id=1, source_target_pairs={{0,2},{2,0},{1,3},{3,1},{4,6},{6,4},{5,7},{7,5},{8,10},{10,8},{9,1... | collective-permute-start | bytes 387080 | tf_op jit(solution)/shard_map/ppermute | solution.py:260
  4.4 6.4 %collective-permute-start = (bf16[5,56,128]{2,1,0:T(8,128)(2,1)S(1)}, bf16[5,56,128]{2,1,0:T(8,128)(2,1)S(1)}, u32[]{:S(2)}, u32[]{:S(2)}) collective-permute-start(bf16[5,56,128]{2,1,0:T(8,128)(2,1)S(1)} %get-tuple-element.49), channel_id=1, source_target_pairs={{0,8},{4,12},{8,0},{12,4},{1,9},{5,13},{9,1},{13,5},{2,10},{6,14},... | collective-permute-start | bytes 215048 | tf_op jit(solution)/shard_map/ppermute | solution.py:260
  10.7 5.8 %collective-permute-start.3 = (bf16[9,56,128]{2,1,0:T(8,128)(2,1)S(1)}, bf16[9,56,128]{2,1,0:T(8,128)(2,1)S(1)}, u32[]{:S(2)}, u32[]{:S(2)}) collective-permute-start(bf16[9,56,128]{2,1,0:T(8,128)(2,1)S(1)} %get-tuple-element.51.refs_0_), channel_id=1, source_target_pairs={{0,1},{1,0},{2,3},{3,2},{4,5},{5,4},{6,7},{7,6},{8,9},{9,8},{10,11... | collective-permute-start | bytes 387080 | tf_op jit(solution)/shard_map/ppermute | solution.py:260
  10.8 5.9 %collective-permute-start.4 = (bf16[9,56,128]{2,1,0:T(8,128)(2,1)S(1)}, bf16[9,56,128]{2,1,0:T(8,128)(2,1)S(1)}, u32[]{:S(2)}, u32[]{:S(2)}) collective-permute-start(bf16[9,56,128]{2,1,0:T(8,128)(2,1)S(1)} %collective-permute-done.2.refs_1_), channel_id=1, source_target_pairs={{0,1},{1,0},{2,3},{3,2},{4,5},{5,4},{6,7},{7,6},{8,9},{9,8},{10,11... | collective-permute-start | bytes 387080 | tf_op jit(solution)/shard_map/ppermute | solution.py:260
  11.3 9.4 %collective-permute-start.1 = (bf16[5,56,128]{2,1,0:T(8,128)(2,1)S(1)}, bf16[5,56,128]{2,1,0:T(8,128)(2,1)S(1)}, u32[]{:S(2)}, u32[]{:S(2)}) collective-permute-start(bf16[5,56,128]{2,1,0:T(8,128)(2,1)S(1)} %collective-permute-done.refs_0_), channel_id=1, source_target_pairs={{0,2},{2,0},{1,3},{3,1},{4,6},{6,4},{5,7},{7,5},{8,10},{10,8},{9,1... | collective-permute-start | bytes 215048 | tf_op jit(solution)/shard_map/ppermute | solution.py:260
  11.8 8.9 %collective-permute-start.6 = (bf16[5,56,128]{2,1,0:T(8,128)(2,1)S(1)}, bf16[5,56,128]{2,1,0:T(8,128)(2,1)S(1)}, u32[]{:S(2)}, u32[]{:S(2)}) collective-permute-start(bf16[5,56,128]{2,1,0:T(8,128)(2,1)S(1)} %get-tuple-element.55), channel_id=1, source_target_pairs={{0,14},{2,12},{4,10},{6,8},{8,6},{10,4},{12,2},{14,0},{1,15},{3,13... | collective-permute-start | bytes 215048 | tf_op jit(solution)/shard_map/ppermute | solution.py:260
  16.0 7.0 %collective-permute-start.5 = (bf16[5,56,128]{2,1,0:T(8,128)(2,1)S(1)}, bf16[5,56,128]{2,1,0:T(8,128)(2,1)S(1)}, u32[]{:S(2)}, u32[]{:S(2)}) collective-permute-start(bf16[5,56,128]{2,1,0:T(8,128)(2,1)S(1)} %get-tuple-element.55), channel_id=1, source_target_pairs={{0,12},{2,14},{4,8},{6,10},{8,4},{10,6},{12,0},{14,2},{1,13},{3,15... | collective-permute-start | bytes 215048 | tf_op jit(solution)/shard_map/ppermute | solution.py:260
  16.6 8.8 %copy-start.3 = (bf16[1,7168,256]{2,1,0:T(8,128)(2,1)S(1)}, bf16[1,7168,256]{2,1,0:T(8,128)(2,1)}, u32[]{:S(2)}) copy-start(bf16[1,7168,256]{2,1,0:T(8,128)(2,1)} %param.16) | copy-start | bytes 11010052
  16.6 8.8 %copy-start.4 = (bf16[1,7168,256]{2,1,0:T(8,128)(2,1)S(1)}, bf16[1,7168,256]{2,1,0:T(8,128)(2,1)}, u32[]{:S(2)}) copy-start(bf16[1,7168,256]{2,1,0:T(8,128)(2,1)} %param.17) | copy-start | bytes 11010052
  16.6 8.8 %copy-start.5 = (bf16[1,256,7168]{2,1,0:T(8,128)(2,1)S(1)}, bf16[1,256,7168]{2,1,0:T(8,128)(2,1)}, u32[]{:S(2)}) copy-start(bf16[1,256,7168]{2,1,0:T(8,128)(2,1)} %param.18) | copy-start | bytes 11010052
  16.6 6.6 %collective-permute-start.8 = (bf16[5,56,128]{2,1,0:T(8,128)(2,1)S(1)}, bf16[5,56,128]{2,1,0:T(8,128)(2,1)S(1)}, u32[]{:S(2)}, u32[]{:S(2)}) collective-permute-start(bf16[5,56,128]{2,1,0:T(8,128)(2,1)S(1)} %get-tuple-element.56), channel_id=1, source_target_pairs={{0,6},{2,4},{4,2},{6,0},{8,14},{10,12},{12,10},{14,8},{1,7},{3,5},... | collective-permute-start | bytes 215048 | tf_op jit(solution)/shard_map/ppermute | solution.py:260
  16.7 6.8 %collective-permute-start.7 = (bf16[5,56,128]{2,1,0:T(8,128)(2,1)S(1)}, bf16[5,56,128]{2,1,0:T(8,128)(2,1)S(1)}, u32[]{:S(2)}, u32[]{:S(2)}) collective-permute-start(bf16[5,56,128]{2,1,0:T(8,128)(2,1)S(1)} %get-tuple-element.56), channel_id=1, source_target_pairs={{0,4},{2,6},{4,0},{6,2},{8,12},{10,14},{12,8},{14,10},{1,5},{3,7},... | collective-permute-start | bytes 215048 | tf_op jit(solution)/shard_map/ppermute | solution.py:260
  23.5 1.8 %collective-permute-start.11 = (bf16[20,56,128]{2,1,0:T(8,128)(2,1)S(1)}, bf16[20,56,128]{2,1,0:T(8,128)(2,1)S(1)}, u32[]{:S(2)}, u32[]{:S(2)}) collective-permute-start(bf16[20,56,128]{2,1,0:T(8,128)(2,1)S(1)} %gather.1.refs_2_), channel_id=1, source_target_pairs={{0,1},{1,0},{2,3},{3,2},{4,5},{5,4},{6,7},{7,6},{8,9},{9,8},{10,11... | collective-permute-start | bytes 860168 | tf_op jit(solution)/shard_map/ppermute | solution.py:260
  23.6 1.7 %collective-permute-start.9 = (bf16[5,56,128]{2,1,0:T(8,128)(2,1)S(1)}, bf16[5,56,128]{2,1,0:T(8,128)(2,1)S(1)}, u32[]{:S(2)}, u32[]{:S(2)}) collective-permute-start(bf16[5,56,128]{2,1,0:T(8,128)(2,1)S(1)} %collective-permute-done.refs_0_), channel_id=1, source_target_pairs={{0,1},{1,0},{2,3},{3,2},{4,5},{5,4},{6,7},{7,6},{8,9},{9,8},{10,11... | collective-permute-start | bytes 215048 | tf_op jit(solution)/shard_map/ppermute | solution.py:260
  24.1 1.3 %collective-permute-start.10 = (bf16[5,56,128]{2,1,0:T(8,128)(2,1)S(1)}, bf16[5,56,128]{2,1,0:T(8,128)(2,1)S(1)}, u32[]{:S(2)}, u32[]{:S(2)}) collective-permute-start(bf16[5,56,128]{2,1,0:T(8,128)(2,1)S(1)} %collective-permute-done.1.refs_1_), channel_id=1, source_target_pairs={{0,1},{1,0},{2,3},{3,2},{4,5},{5,4},{6,7},{7,6},{8,9},{9,8},{10,11... | collective-permute-start | bytes 215048 | tf_op jit(solution)/shard_map/ppermute | solution.py:260
  27.7 9.9 %collective-permute-start.18 = (bf16[2,8,56,128]{3,2,1,0:T(8,128)(2,1)S(1)}, bf16[2,8,56,128]{3,2,1,0:T(8,128)(2,1)S(1)}, u32[]{:S(2)}, u32[]{:S(2)}) collective-permute-start(bf16[2,8,56,128]{3,2,1,0:T(8,128)(2,1)S(1)} %get-tuple-element.76), channel_id=1, source_target_pairs={{0,1},{1,0},{2,3},{3,2},{4,5},{5,4},{6,7},{7,6},{8,9},{9,8},{10,11... | collective-permute-start | bytes 688136 | tf_op jit(solution)/shard_map/ppermute | solution.py:260
  27.9 1.5 %collective-permute-start.21 = (bf16[2,5,56,128]{3,2,1,0:T(8,128)(2,1)S(1)}, bf16[2,5,56,128]{3,2,1,0:T(8,128)(2,1)S(1)}, u32[]{:S(2)}, u32[]{:S(2)}) collective-permute-start(bf16[2,5,56,128]{3,2,1,0:T(8,128)(2,1)S(1)} %get-tuple-element.84), channel_id=1, source_target_pairs={{0,1},{1,0},{2,3},{3,2},{4,5},{5,4},{6,7},{7,6},{8,9},{9,8},{10,11... | collective-permute-start | bytes 430088 | tf_op jit(solution)/shard_map/ppermute | solution.py:260
  28.3 2.3 %collective-permute-start.12 = (bf16[2,5,56,128]{3,2,1,0:T(8,128)(2,1)S(1)}, bf16[2,5,56,128]{3,2,1,0:T(8,128)(2,1)S(1)}, u32[]{:S(2)}, u32[]{:S(2)}) collective-permute-start(bf16[2,5,56,128]{3,2,1,0:T(8,128)(2,1)S(1)} %get-tuple-element.64), channel_id=1, source_target_pairs={{0,1},{1,0},{2,3},{3,2},{4,5},{5,4},{6,7},{7,6},{8,9},{9,8},{10,11... | collective-permute-start | bytes 430088 | tf_op jit(solution)/shard_map/ppermute | solution.py:260
  28.4 6.5 %collective-permute-start.15 = (bf16[2,5,56,128]{3,2,1,0:T(8,128)(2,1)S(1)}, bf16[2,5,56,128]{3,2,1,0:T(8,128)(2,1)S(1)}, u32[]{:S(2)}, u32[]{:S(2)}) collective-permute-start(bf16[2,5,56,128]{3,2,1,0:T(8,128)(2,1)S(1)} %get-tuple-element.70), channel_id=1, source_target_pairs={{0,1},{1,0},{2,3},{3,2},{4,5},{5,4},{6,7},{7,6},{8,9},{9,8},{10,11... | collective-permute-start | bytes 430088 | tf_op jit(solution)/shard_map/ppermute | solution.py:260
  29.5 5.6 %collective-permute-start.22 = (bf16[5,56,128]{2,1,0:T(8,128)(2,1)S(1)}, bf16[5,56,128]{2,1,0:T(8,128)(2,1)S(1)}, u32[]{:S(2)}, u32[]{:S(2)}) collective-permute-start(bf16[5,56,128]{2,1,0:T(8,128)(2,1)S(1)} %get-tuple-element.88), channel_id=1, source_target_pairs={{0,2},{2,0},{1,3},{3,1},{4,6},{6,4},{5,7},{7,5},{8,10},{10,8},{9,1... | collective-permute-start | bytes 215048 | tf_op jit(solution)/shard_map/ppermute | solution.py:260
  30.6 8.4 %collective-permute-start.13 = (bf16[5,56,128]{2,1,0:T(8,128)(2,1)S(1)}, bf16[5,56,128]{2,1,0:T(8,128)(2,1)S(1)}, u32[]{:S(2)}, u32[]{:S(2)}) collective-permute-start(bf16[5,56,128]{2,1,0:T(8,128)(2,1)S(1)} %get-tuple-element.67), channel_id=1, source_target_pairs={{0,12},{2,14},{4,8},{6,10},{8,4},{10,6},{12,0},{14,2},{1,13},{3,15... | collective-permute-start | bytes 215048 | tf_op jit(solution)/shard_map/ppermute | solution.py:260
  33.3 7.4 %collective-permute-start.14 = (bf16[5,56,128]{2,1,0:T(8,128)(2,1)S(1)}, bf16[5,56,128]{2,1,0:T(8,128)(2,1)S(1)}, u32[]{:S(2)}, u32[]{:S(2)}) collective-permute-start(bf16[5,56,128]{2,1,0:T(8,128)(2,1)S(1)} %get-tuple-element.68), channel_id=1, source_target_pairs={{0,14},{2,12},{4,10},{6,8},{8,6},{10,4},{12,2},{14,0},{1,15},{3,13... | collective-permute-start | bytes 215048 | tf_op jit(solution)/shard_map/ppermute | solution.py:260
  35.0 7.3 %collective-permute-start.16 = (bf16[5,56,128]{2,1,0:T(8,128)(2,1)S(1)}, bf16[5,56,128]{2,1,0:T(8,128)(2,1)S(1)}, u32[]{:S(2)}, u32[]{:S(2)}) collective-permute-start(bf16[5,56,128]{2,1,0:T(8,128)(2,1)S(1)} %get-tuple-element.73), channel_id=1, source_target_pairs={{0,4},{2,6},{4,0},{6,2},{8,12},{10,14},{12,8},{14,10},{1,5},{3,7},... | collective-permute-start | bytes 215048 | tf_op jit(solution)/shard_map/ppermute | solution.py:260
  35.1 8.0 %collective-permute-start.17 = (bf16[5,56,128]{2,1,0:T(8,128)(2,1)S(1)}, bf16[5,56,128]{2,1,0:T(8,128)(2,1)S(1)}, u32[]{:S(2)}, u32[]{:S(2)}) collective-permute-start(bf16[5,56,128]{2,1,0:T(8,128)(2,1)S(1)} %get-tuple-element.74), channel_id=1, source_target_pairs={{0,6},{2,4},{4,2},{6,0},{8,14},{10,12},{12,10},{14,8},{1,7},{3,5},... | collective-permute-start | bytes 215048 | tf_op jit(solution)/shard_map/ppermute | solution.py:260
  37.6 5.7 %collective-permute-start.23 = (bf16[5,56,128]{2,1,0:T(8,128)(2,1)S(1)}, bf16[5,56,128]{2,1,0:T(8,128)(2,1)S(1)}, u32[]{:S(2)}, u32[]{:S(2)}) collective-permute-start(bf16[5,56,128]{2,1,0:T(8,128)(2,1)S(1)} %narrow_sum.1), channel_id=1, source_target_pairs={{0,8},{4,12},{8,0},{12,4},{1,9},{5,13},{9,1},{13,5},{2,10},{6,14},... | collective-permute-start | bytes 215048 | tf_op jit(solution)/shard_map/ppermute | solution.py:260
  39.0 4.7 %collective-permute-start.19 = (bf16[4,56,128]{2,1,0:T(8,128)(2,1)S(1)}, bf16[4,56,128]{2,1,0:T(8,128)(2,1)S(1)}, u32[]{:S(2)}, u32[]{:S(2)}) collective-permute-start(bf16[4,56,128]{2,1,0:T(8,128)(2,1)S(1)} %get-tuple-element.80), channel_id=1, source_target_pairs={{0,2},{2,0},{1,3},{3,1},{4,6},{6,4},{5,7},{7,5},{8,10},{10,8},{9,1... | collective-permute-start | bytes 172040 | tf_op jit(solution)/shard_map/ppermute | solution.py:260
  40.7 4.2 %collective-permute-start.20 = (bf16[4,56,128]{2,1,0:T(8,128)(2,1)S(1)}, bf16[4,56,128]{2,1,0:T(8,128)(2,1)S(1)}, u32[]{:S(2)}, u32[]{:S(2)}) collective-permute-start(bf16[4,56,128]{2,1,0:T(8,128)(2,1)S(1)} %get-tuple-element.82), channel_id=1, source_target_pairs={{0,2},{2,0},{1,3},{3,1},{4,6},{6,4},{5,7},{7,5},{8,10},{10,8},{9,1... | collective-permute-start | bytes 172040 | tf_op jit(solution)/shard_map/ppermute | solution.py:260

commit v10 on v8

--- a/solution.py
+++ b/solution.py
@@ -10,7 +10,7 @@
 CAP = 5
 LANES = 128
 SPAN = 7
-HALVES = 2
+HALVES = 1
 MAX_ROWS = 128
 
 VMEM = pltpu.VMEM
@@ -408,8 +408,8 @@
     far_sum = call(
         functools.partial(far_combine_kernel, order),
         "far_combine",
-        [route, gains] + far_back + in_hbm(*shared, *routed),
-        [SSPEC] * 2 + [VSPEC] * len(order) + [ASPEC] * 6,
+        [route, gains] + far_back,
+        [SSPEC] * 2 + [VSPEC] * len(order),
         jax.ShapeDtypeStruct((tokens, tall, LANES), F32),
         [VMEM((n_wide * CAP, tall, LANES), F32)],
     )

time: 42.7 us -> 41.9 us (0.981)
  starting transfers between devices: 23.5 us -> 22.2 us
  waiting for transfers between devices: 12.1 us -> 12.7 us
    ppermute x27 -> x26, starting transfers between devices: 23.5 us -> 22.2 us  [swap(): return lax.ppermute(value, axis, [(i, i ^ offset) for i in range(size)])]
    ppermute x27 -> x26, waiting for transfers between devices: 12.1 us -> 12.7 us  [swap(): return lax.ppermute(value, axis, [(i, i ^ offset) for i in range(size)])]
  transfers between devices with their start and end apart: 27 -> 26, of which waited for: 12 -> 13; matrix products, arithmetic and copies ran while one was open for 0% -> 0% of each run, Pallas kernels for 5% -> 6%
where the time goes in v10:
time: 41.9 us; the launch traced here: 41.7 us
  starting transfers between devices  22.2 us (53%)
  waiting for transfers between devices  12.7 us (30%)
  Pallas kernels  6.73 us (16%)
    ppermute x26, starting transfers between devices, swap(): return lax.ppermute(value, axis, [(i, i ^ offset) for i in range(size)])  22.2 us
    ppermute x26, waiting for transfers between devices, swap(): return lax.ppermute(value, axis, [(i, i ^ offset) for i in range(size)])  12.7 us
    pallas_call x12, Pallas kernels, call(): pl.pallas_call(kernel, out_shape=outs, in_specs=specs, out_specs=jax.tree...  6.73 us
  transfers between devices with their start and end apart: 26, of which 13 were waited for; matrix products, arithmetic and copies ran while one was open for 0% of the time, Pallas kernels for 6%

profile of v10, /device:TPU:0, one launch (start us, length us, event | category | flops | bytes accessed | tf_op | source)
XLA Modules:
  0.0 41.7 jit_solution(17063427899769140988)
XLA Ops:
  0.0 1.4 %dispatch.1 = (bf16[9,56,128]{2,1,0:T(8,128)(2,1)S(1)}, bf16[5,56,128]{2,1,0:T(8,128)(2,1)S(1)}, bf16[5,56,128]{2,1,0:T(8,128)(2,1)S(1)}, bf16[5,56,128]{2,1,0:T...) custom-call(s32[2,8]{1,0:T(2,128)} %bitcast.11, s32[4]{0:T(128)} %place_in.1, f32[2,8]{1,0:T(2,128)} %bitcast.12, ...), custom_call_target="tpu_custom_call" | custom-call | tf_op jit(solution)/shard_map/dispatch/pallas_call | solution.py:249
  1.4 3.0 %collective-permute-start.6 = (bf16[9,56,128]{2,1,0:T(8,128)(2,1)S(1)}, bf16[9,56,128]{2,1,0:T(8,128)(2,1)S(1)}, u32[]{:S(2)}, u32[]{:S(2)}) collective-permute-start(bf16[9,56,128]{2,1,0:T(8,128)(2,1)S(1)} %get-tuple-element.52.refs_0_), channel_id=1, source_target_pairs={{0,2},{2,0},{1,3},{3,1},{4,6},{6,4},{5,7},{7,5},{8,10},{10,8},{9,1... | collective-permute-start | bytes 387080 | tf_op jit(solution)/shard_map/ppermute | solution.py:237
  4.4 3.6 %collective-permute-start = (bf16[5,56,128]{2,1,0:T(8,128)(2,1)S(1)}, bf16[5,56,128]{2,1,0:T(8,128)(2,1)S(1)}, u32[]{:S(2)}, u32[]{:S(2)}) collective-permute-start(bf16[5,56,128]{2,1,0:T(8,128)(2,1)S(1)} %get-tuple-element.46), channel_id=1, source_target_pairs={{0,12},{4,8},{8,4},{12,0},{1,13},{5,9},{9,5},{13,1},{2,14},{6,10},... | collective-permute-start | bytes 215048 | tf_op jit(solution)/shard_map/ppermute | solution.py:237
  8.0 0.5 %collective-permute-start.3 = (bf16[5,56,128]{2,1,0:T(8,128)(2,1)S(1)}, bf16[5,56,128]{2,1,0:T(8,128)(2,1)S(1)}, u32[]{:S(2)}, u32[]{:S(2)}) collective-permute-start(bf16[5,56,128]{2,1,0:T(8,128)(2,1)S(1)} %get-tuple-element.48), channel_id=1, source_target_pairs={{0,6},{2,4},{4,2},{6,0},{8,14},{10,12},{12,10},{14,8},{1,7},{3,5},... | collective-permute-start | bytes 215048 | tf_op jit(solution)/shard_map/ppermute | solution.py:237
  8.5 1.5 %collective-permute-start.2 = (bf16[5,56,128]{2,1,0:T(8,128)(2,1)S(1)}, bf16[5,56,128]{2,1,0:T(8,128)(2,1)S(1)}, u32[]{:S(2)}, u32[]{:S(2)}) collective-permute-start(bf16[5,56,128]{2,1,0:T(8,128)(2,1)S(1)} %get-tuple-element.48), channel_id=1, source_target_pairs={{0,4},{2,6},{4,0},{6,2},{8,12},{10,14},{12,8},{14,10},{1,5},{3,7},... | collective-permute-start | bytes 215048 | tf_op jit(solution)/shard_map/ppermute | solution.py:237
  10.1 1.3 %collective-permute-done.refs_0_ = bf16[5,56,128]{2,1,0:T(8,128)(2,1)S(1)} collective-permute-done((bf16[5,56,128]{2,1,0:T(8,128)(2,1)S(1)}, bf16[5,56,128]{2,1,0:T(8,128)(2,1)S(1)}, u32[]{:S(2)}, u32[]{:S(2)}) %collective-permute-start) | collective-permute-done | bytes 71712 | tf_op jit(solution)/shard_map/ppermute | solution.py:237
  11.4 2.4 %collective-permute-done.1.refs_1_ = bf16[5,56,128]{2,1,0:T(8,128)(2,1)S(1)} collective-permute-done((bf16[5,56,128]{2,1,0:T(8,128)(2,1)S(1)}, bf16[5,56,128]{2,1,0:T(8,128)(2,1)S(1)}, u32[]{:S(2)}, u32[]{:S(2)}) %collective-permute-start.1) | collective-permute-done | bytes 71712 | tf_op jit(solution)/shard_map/ppermute | solution.py:237
  13.8 0.9 %collective-permute-done.3.refs_5_ = bf16[5,56,128]{2,1,0:T(8,128)(2,1)S(1)} collective-permute-done((bf16[5,56,128]{2,1,0:T(8,128)(2,1)S(1)}, bf16[5,56,128]{2,1,0:T(8,128)(2,1)S(1)}, u32[]{:S(2)}, u32[]{:S(2)}) %collective-permute-start.3) | collective-permute-done | bytes 71712 | tf_op jit(solution)/shard_map/ppermute | solution.py:237
  14.7 0.6 %collective-permute-done.2.refs_2_ = bf16[5,56,128]{2,1,0:T(8,128)(2,1)S(1)} collective-permute-done((bf16[5,56,128]{2,1,0:T(8,128)(2,1)S(1)}, bf16[5,56,128]{2,1,0:T(8,128)(2,1)S(1)}, u32[]{:S(2)}, u32[]{:S(2)}) %collective-permute-start.2) | collective-permute-done | bytes 71712 | tf_op jit(solution)/shard_map/ppermute | solution.py:237
  15.3 0.5 %collective-permute-start.8 = (bf16[9,56,128]{2,1,0:T(8,128)(2,1)S(1)}, bf16[9,56,128]{2,1,0:T(8,128)(2,1)S(1)}, u32[]{:S(2)}, u32[]{:S(2)}) collective-permute-start(bf16[9,56,128]{2,1,0:T(8,128)(2,1)S(1)} %collective-permute-done.6.refs_1_), channel_id=1, source_target_pairs={{0,1},{1,0},{2,3},{3,2},{4,5},{5,4},{6,7},{7,6},{8,9},{9,8},{10,11... | collective-permute-start | bytes 387080 | tf_op jit(solution)/shard_map/ppermute | solution.py:237
  15.8 0.8 %collective-permute-start.4 = (bf16[5,56,128]{2,1,0:T(8,128)(2,1)S(1)}, bf16[5,56,128]{2,1,0:T(8,128)(2,1)S(1)}, u32[]{:S(2)}, u32[]{:S(2)}) collective-permute-start(bf16[5,56,128]{2,1,0:T(8,128)(2,1)S(1)} %collective-permute-done.refs_0_), channel_id=1, source_target_pairs={{0,2},{2,0},{1,3},{3,1},{4,6},{6,4},{5,7},{7,5},{8,10},{10,8},{9,1... | collective-permute-start | bytes 215048 | tf_op jit(solution)/shard_map/ppermute | solution.py:237
  16.5 1.3 %collective-permute-start.5 = (bf16[5,56,128]{2,1,0:T(8,128)(2,1)S(1)}, bf16[5,56,128]{2,1,0:T(8,128)(2,1)S(1)}, u32[]{:S(2)}, u32[]{:S(2)}) collective-permute-start(bf16[5,56,128]{2,1,0:T(8,128)(2,1)S(1)} %collective-permute-done.1.refs_1_), channel_id=1, source_target_pairs={{0,2},{2,0},{1,3},{3,1},{4,6},{6,4},{5,7},{7,5},{8,10},{10,8},{9,1... | collective-permute-start | bytes 215048 | tf_op jit(solution)/shard_map/ppermute | solution.py:237
  17.8 0.5 %collective-permute-start.9 = (bf16[5,56,128]{2,1,0:T(8,128)(2,1)S(1)}, bf16[5,56,128]{2,1,0:T(8,128)(2,1)S(1)}, u32[]{:S(2)}, u32[]{:S(2)}) collective-permute-start(bf16[5,56,128]{2,1,0:T(8,128)(2,1)S(1)} %collective-permute-done.refs_0_), channel_id=1, source_target_pairs={{0,1},{1,0},{2,3},{3,2},{4,5},{5,4},{6,7},{7,6},{8,9},{9,8},{10,11... | collective-permute-start | bytes 215048 | tf_op jit(solution)/shard_map/ppermute | solution.py:237
  18.4 2.0 %near_shared.1 = (bf16[32,7168]{1,0:T(8,128)(2,1)S(1)}, f32[32,128]{1,0:T(8,128)S(1)}, f32[32,7168]{1,0:T(8,128)S(1)}) custom-call(bf16[9,56,128]{2,1,0:T(8,128)(2,1)S(1)} %get-tuple-element.52.refs_0_, bf16[9,56,128]{2,1,0:T(8,128)(2,1)S(1)} %collective-permute-done.6.refs_1_, bf16[9,56,128]{2,1,0:T(8,128)(2,1)S(1)} %collective-permute-done.7.refs_2_, ...), custom_call_target="tpu_custom_call" | custom-call | flops 352321536 | bytes 11010048 | tf_op jit(solution)/shard_map/near_shared/pallas_call | solution.py:249
  21.0 0.5 %collective-permute-done.5.refs_4_ = bf16[5,56,128]{2,1,0:T(8,128)(2,1)S(1)} collective-permute-done((bf16[5,56,128]{2,1,0:T(8,128)(2,1)S(1)}, bf16[5,56,128]{2,1,0:T(8,128)(2,1)S(1)}, u32[]{:S(2)}, u32[]{:S(2)}) %collective-permute-start.5) | collective-permute-done | bytes 71712 | tf_op jit(solution)/shard_map/ppermute | solution.py:237
  21.4 0.5 %collective-permute-start.13 = (bf16[5,56,128]{2,1,0:T(8,128)(2,1)S(1)}, bf16[5,56,128]{2,1,0:T(8,128)(2,1)S(1)}, u32[]{:S(2)}, u32[]{:S(2)}) collective-permute-start(bf16[5,56,128]{2,1,0:T(8,128)(2,1)S(1)} %collective-permute-done.5.refs_4_), channel_id=1, source_target_pairs={{0,1},{1,0},{2,3},{3,2},{4,5},{5,4},{6,7},{7,6},{8,9},{9,8},{10,11... | collective-permute-start | bytes 215048 | tf_op jit(solution)/shard_map/ppermute | solution.py:237
  22.0 0.7 %collective-permute-done.12.refs_9_ = bf16[5,56,128]{2,1,0:T(8,128)(2,1)S(1)} collective-permute-done((bf16[5,56,128]{2,1,0:T(8,128)(2,1)S(1)}, bf16[5,56,128]{2,1,0:T(8,128)(2,1)S(1)}, u32[]{:S(2)}, u32[]{:S(2)}) %collective-permute-start.12) | collective-permute-done | bytes 71712 | tf_op jit(solution)/shard_map/ppermute | solution.py:237
  22.9 2.3 %routed.1 = (bf16[2,8,56,128]{3,2,1,0:T(8,128)(2,1)S(1)}, bf16[2,8,56,128]{3,2,1,0:T(8,128)(2,1)S(1)}, bf16[2,5,56,128]{3,2,1,0:T(8,128)(2,1)S(1)}, bf16[2,5,56,...) custom-call(bf16[5,56,128]{2,1,0:T(8,128)(2,1)S(1)} %collective-perm, ...), custom_call_target="tpu_custom_call" | custom-call | flops 1012924416 | bytes 11010048 | tf_op jit(solution)/shard_map/routed/pallas_call | solution.py:249
  25.2 0.4 %collective-permute-start.24 = (bf16[2,8,56,128]{3,2,1,0:T(8,128)(2,1)S(1)}, bf16[2,8,56,128]{3,2,1,0:T(8,128)(2,1)S(1)}, u32[]{:S(2)}, u32[]{:S(2)}) collective-permute-start(bf16[2,8,56,128]{3,2,1,0:T(8,128)(2,1)S(1)} %get-tuple-element.78), channel_id=1, source_target_pairs={{0,1},{1,0},{2,3},{3,2},{4,5},{5,4},{6,7},{7,6},{8,9},{9,8},{10,11... | collective-permute-start | bytes 688136 | tf_op jit(solution)/shard_map/ppermute | solution.py:237
  25.8 0.4 collective-permute-start.18
  26.3 0.7 %collective-permute-done.15.refs_1_ = bf16[2,5,56,128]{3,2,1,0:T(8,128)(2,1)S(1)} collective-permute-done((bf16[2,5,56,128]{3,2,1,0:T(8,128)(2,1)S(1)}, bf16[2,5,56,128]{3,2,1,0:T(8,128)(2,1)S(1)}, u32[]{:S(2)}, u32[]{:S(2)}) %collective-permute-start.15) | collective-permute-done | bytes 143392 | tf_op jit(solution)/shard_map/ppermute | solution.py:237
  27.0 1.0 %collective-permute-start.16 = (bf16[5,56,128]{2,1,0:T(8,128)(2,1)S(1)}, bf16[5,56,128]{2,1,0:T(8,128)(2,1)S(1)}, u32[]{:S(2)}, u32[]{:S(2)}) collective-permute-start(bf16[5,56,128]{2,1,0:T(8,128)(2,1)S(1)} %get-tuple-element.64), channel_id=1, source_target_pairs={{0,2},{2,0},{1,3},{3,1},{4,6},{6,4},{5,7},{7,5},{8,10},{10,8},{9,1... | collective-permute-start | bytes 215048 | tf_op jit(solution)/shard_map/ppermute | solution.py:237
  28.1 1.1 %collective-permute-start.19 = (bf16[5,56,128]{2,1,0:T(8,128)(2,1)S(1)}, bf16[5,56,128]{2,1,0:T(8,128)(2,1)S(1)}, u32[]{:S(2)}, u32[]{:S(2)}) collective-permute-start(bf16[5,56,128]{2,1,0:T(8,128)(2,1)S(1)} %get-tuple-element.70), channel_id=1, source_target_pairs={{0,2},{2,0},{1,3},{3,1},{4,6},{6,4},{5,7},{7,5},{8,10},{10,8},{9,1... | collective-permute-start | bytes 215048 | tf_op jit(solution)/shard_map/ppermute | solution.py:237
  29.3 1.0 %collective-permute-start.22 = (bf16[5,56,128]{2,1,0:T(8,128)(2,1)S(1)}, bf16[5,56,128]{2,1,0:T(8,128)(2,1)S(1)}, u32[]{:S(2)}, u32[]{:S(2)}) collective-permute-start(bf16[5,56,128]{2,1,0:T(8,128)(2,1)S(1)} %get-tuple-element.76), channel_id=1, source_target_pairs={{0,2},{2,0},{1,3},{3,1},{4,6},{6,4},{5,7},{7,5},{8,10},{10,8},{9,1... | collective-permute-start | bytes 215048 | tf_op jit(solution)/shard_map/ppermute | solution.py:237
  30.4 1.1 %collective-permute-start.25 = (bf16[8,56,128]{2,1,0:T(8,128)(2,1)S(1)}, bf16[8,56,128]{2,1,0:T(8,128)(2,1)S(1)}, u32[]{:S(2)}, u32[]{:S(2)}) collective-permute-start(bf16[8,56,128]{2,1,0:T(8,128)(2,1)S(1)} %get-tuple-element.82), channel_id=1, source_target_pairs={{0,2},{2,0},{1,3},{3,1},{4,6},{6,4},{5,7},{7,5},{8,10},{10,8},{9,1... | collective-permute-start | bytes 344072 | tf_op jit(solution)/shard_map/ppermute | solution.py:237
  31.5 0.6 %collective-permute-done.16.refs_1_ = bf16[5,56,128]{2,1,0:T(8,128)(2,1)S(1)} collective-permute-done((bf16[5,56,128]{2,1,0:T(8,128)(2,1)S(1)}, bf16[5,56,128]{2,1,0:T(8,128)(2,1)S(1)}, u32[]{:S(2)}, u32[]{:S(2)}) %collective-permute-start.16) | collective-permute-done | bytes 71712 | tf_op jit(solution)/shard_map/ppermute | solution.py:237
  32.1 2.3 %collective-permute-start.17 = (bf16[5,56,128]{2,1,0:T(8,128)(2,1)S(1)}, bf16[5,56,128]{2,1,0:T(8,128)(2,1)S(1)}, u32[]{:S(2)}, u32[]{:S(2)}) collective-permute-start(bf16[5,56,128]{2,1,0:T(8,128)(2,1)S(1)} %narrow_sum.3), channel_id=1, source_target_pairs={{0,12},{4,8},{8,4},{12,0},{1,13},{5,9},{9,5},{13,1},{2,14},{6,10},... | collective-permute-start | bytes 215048 | tf_op jit(solution)/shard_map/ppermute | solution.py:237
  34.8 0.4 collective-permute-done.22.refs_1_
  35.2 1.6 %collective-permute-start.23 = (bf16[5,56,128]{2,1,0:T(8,128)(2,1)S(1)}, bf16[5,56,128]{2,1,0:T(8,128)(2,1)S(1)}, u32[]{:S(2)}, u32[]{:S(2)}) collective-permute-start(bf16[5,56,128]{2,1,0:T(8,128)(2,1)S(1)} %narrow_sum.5), channel_id=1, source_target_pairs={{0,4},{4,0},{8,12},{12,8},{1,5},{5,1},{9,13},{13,9},{2,6},{6,2},{1... | collective-permute-start | bytes 215048 | tf_op jit(solution)/shard_map/ppermute | solution.py:237
  36.8 2.0 %collective-permute-done.17.refs_0_ = bf16[5,56,128]{2,1,0:T(8,128)(2,1)S(1)} collective-permute-done((bf16[5,56,128]{2,1,0:T(8,128)(2,1)S(1)}, bf16[5,56,128]{2,1,0:T(8,128)(2,1)S(1)}, u32[]{:S(2)}, u32[]{:S(2)}) %collective-permute-start.17) | collective-permute-done | bytes 71712 | tf_op jit(solution)/shard_map/ppermute | solution.py:237
  38.8 2.2 %collective-permute-done.20.refs_1_ = bf16[5,56,128]{2,1,0:T(8,128)(2,1)S(1)} collective-permute-done((bf16[5,56,128]{2,1,0:T(8,128)(2,1)S(1)}, bf16[5,56,128]{2,1,0:T(8,128)(2,1)S(1)}, u32[]{:S(2)}, u32[]{:S(2)}) %collective-permute-start.20) | collective-permute-done | bytes 71712 | tf_op jit(solution)/shard_map/ppermute | solution.py:237
  41.0 0.7 %combine.1 = bf16[8,7168]{1,0:T(8,128)(2,1)} custom-call(f32[8,56,128]{2,1,0:T(8,128)S(1)} %far_combine.1.far, bf16[8,56,128]{2,1,0:T(8,128)(2,1)S(1)} %get-tuple-element.81.refs_0_, bf16[8,56,128]{2,1,0:T(8,128)(2,1)S(1)} %collective-permute-done.25.refs_1_), custom_call_target="tpu_custom_call" | custom-call | tf_op jit(solution)/shard_map/combine/pallas_call | solution.py:249
  (44 shorter events, 1.7 us)
Async XLA Ops:
  0.0 18.4 %copy-start = (bf16[7168,256]{1,0:T(8,128)(2,1)S(1)}, bf16[7168,256]{1,0:T(8,128)(2,1)}, u32[]{:S(2)}) copy-start(bf16[7168,256]{1,0:T(8,128)(2,1)} %refs_4_.1) | copy-start | bytes 11010052
  0.0 18.4 %copy-start.1 = (bf16[7168,256]{1,0:T(8,128)(2,1)S(1)}, bf16[7168,256]{1,0:T(8,128)(2,1)}, u32[]{:S(2)}) copy-start(bf16[7168,256]{1,0:T(8,128)(2,1)} %refs_5_.1) | copy-start | bytes 11010052
  0.0 18.4 %copy-start.2 = (bf16[256,7168]{1,0:T(8,128)(2,1)S(1)}, bf16[256,7168]{1,0:T(8,128)(2,1)}, u32[]{:S(2)}) copy-start(bf16[256,7168]{1,0:T(8,128)(2,1)} %refs_6_.1) | copy-start | bytes 11010052
  1.4 13.9 %collective-permute-start.6 = (bf16[9,56,128]{2,1,0:T(8,128)(2,1)S(1)}, bf16[9,56,128]{2,1,0:T(8,128)(2,1)S(1)}, u32[]{:S(2)}, u32[]{:S(2)}) collective-permute-start(bf16[9,56,128]{2,1,0:T(8,128)(2,1)S(1)} %get-tuple-element.52.refs_0_), channel_id=1, source_target_pairs={{0,2},{2,0},{1,3},{3,1},{4,6},{6,4},{5,7},{7,5},{8,10},{10,8},{9,1... | collective-permute-start | bytes 387080 | tf_op jit(solution)/shard_map/ppermute | solution.py:237
  4.4 7.0 %collective-permute-start = (bf16[5,56,128]{2,1,0:T(8,128)(2,1)S(1)}, bf16[5,56,128]{2,1,0:T(8,128)(2,1)S(1)}, u32[]{:S(2)}, u32[]{:S(2)}) collective-permute-start(bf16[5,56,128]{2,1,0:T(8,128)(2,1)S(1)} %get-tuple-element.46), channel_id=1, source_target_pairs={{0,12},{4,8},{8,4},{12,0},{1,13},{5,9},{9,5},{13,1},{2,14},{6,10},... | collective-permute-start | bytes 215048 | tf_op jit(solution)/shard_map/ppermute | solution.py:237
  8.0 5.8 %collective-permute-start.1 = (bf16[5,56,128]{2,1,0:T(8,128)(2,1)S(1)}, bf16[5,56,128]{2,1,0:T(8,128)(2,1)S(1)}, u32[]{:S(2)}, u32[]{:S(2)}) collective-permute-start(bf16[5,56,128]{2,1,0:T(8,128)(2,1)S(1)} %get-tuple-element.47), channel_id=1, source_target_pairs={{0,8},{4,12},{8,0},{12,4},{1,9},{5,13},{9,1},{13,5},{2,10},{6,14},... | collective-permute-start | bytes 215048 | tf_op jit(solution)/shard_map/ppermute | solution.py:237
  8.0 14.9 %copy-start.3 = (bf16[1,7168,256]{2,1,0:T(8,128)(2,1)S(1)}, bf16[1,7168,256]{2,1,0:T(8,128)(2,1)}, u32[]{:S(2)}) copy-start(bf16[1,7168,256]{2,1,0:T(8,128)(2,1)} %param.16) | copy-start | bytes 11010052
  8.0 14.9 %copy-start.4 = (bf16[1,7168,256]{2,1,0:T(8,128)(2,1)S(1)}, bf16[1,7168,256]{2,1,0:T(8,128)(2,1)}, u32[]{:S(2)}) copy-start(bf16[1,7168,256]{2,1,0:T(8,128)(2,1)} %param.17) | copy-start | bytes 11010052
  8.0 14.9 %copy-start.5 = (bf16[1,256,7168]{2,1,0:T(8,128)(2,1)S(1)}, bf16[1,256,7168]{2,1,0:T(8,128)(2,1)}, u32[]{:S(2)}) copy-start(bf16[1,256,7168]{2,1,0:T(8,128)(2,1)} %param.18) | copy-start | bytes 11010052
  8.0 6.7 %collective-permute-start.3 = (bf16[5,56,128]{2,1,0:T(8,128)(2,1)S(1)}, bf16[5,56,128]{2,1,0:T(8,128)(2,1)S(1)}, u32[]{:S(2)}, u32[]{:S(2)}) collective-permute-start(bf16[5,56,128]{2,1,0:T(8,128)(2,1)S(1)} %get-tuple-element.48), channel_id=1, source_target_pairs={{0,6},{2,4},{4,2},{6,0},{8,14},{10,12},{12,10},{14,8},{1,7},{3,5},... | collective-permute-start | bytes 215048 | tf_op jit(solution)/shard_map/ppermute | solution.py:237
  8.5 6.7 %collective-permute-start.2 = (bf16[5,56,128]{2,1,0:T(8,128)(2,1)S(1)}, bf16[5,56,128]{2,1,0:T(8,128)(2,1)S(1)}, u32[]{:S(2)}, u32[]{:S(2)}) collective-permute-start(bf16[5,56,128]{2,1,0:T(8,128)(2,1)S(1)} %get-tuple-element.48), channel_id=1, source_target_pairs={{0,4},{2,6},{4,0},{6,2},{8,12},{10,14},{12,8},{14,10},{1,5},{3,7},... | collective-permute-start | bytes 215048 | tf_op jit(solution)/shard_map/ppermute | solution.py:237
  15.3 2.5 %collective-permute-start.7 = (bf16[9,56,128]{2,1,0:T(8,128)(2,1)S(1)}, bf16[9,56,128]{2,1,0:T(8,128)(2,1)S(1)}, u32[]{:S(2)}, u32[]{:S(2)}) collective-permute-start(bf16[9,56,128]{2,1,0:T(8,128)(2,1)S(1)} %get-tuple-element.52.refs_0_), channel_id=1, source_target_pairs={{0,1},{1,0},{2,3},{3,2},{4,5},{5,4},{6,7},{7,6},{8,9},{9,8},{10,11... | collective-permute-start | bytes 387080 | tf_op jit(solution)/shard_map/ppermute | solution.py:237
  15.3 3.1 %collective-permute-start.8 = (bf16[9,56,128]{2,1,0:T(8,128)(2,1)S(1)}, bf16[9,56,128]{2,1,0:T(8,128)(2,1)S(1)}, u32[]{:S(2)}, u32[]{:S(2)}) collective-permute-start(bf16[9,56,128]{2,1,0:T(8,128)(2,1)S(1)} %collective-permute-done.6.refs_1_), channel_id=1, source_target_pairs={{0,1},{1,0},{2,3},{3,2},{4,5},{5,4},{6,7},{7,6},{8,9},{9,8},{10,11... | collective-permute-start | bytes 387080 | tf_op jit(solution)/shard_map/ppermute | solution.py:237
  15.8 4.9 %collective-permute-start.4 = (bf16[5,56,128]{2,1,0:T(8,128)(2,1)S(1)}, bf16[5,56,128]{2,1,0:T(8,128)(2,1)S(1)}, u32[]{:S(2)}, u32[]{:S(2)}) collective-permute-start(bf16[5,56,128]{2,1,0:T(8,128)(2,1)S(1)} %collective-permute-done.refs_0_), channel_id=1, source_target_pairs={{0,2},{2,0},{1,3},{3,1},{4,6},{6,4},{5,7},{7,5},{8,10},{10,8},{9,1... | collective-permute-start | bytes 215048 | tf_op jit(solution)/shard_map/ppermute | solution.py:237
  16.5 4.9 %collective-permute-start.5 = (bf16[5,56,128]{2,1,0:T(8,128)(2,1)S(1)}, bf16[5,56,128]{2,1,0:T(8,128)(2,1)S(1)}, u32[]{:S(2)}, u32[]{:S(2)}) collective-permute-start(bf16[5,56,128]{2,1,0:T(8,128)(2,1)S(1)} %collective-permute-done.1.refs_1_), channel_id=1, source_target_pairs={{0,2},{2,0},{1,3},{3,1},{4,6},{6,4},{5,7},{7,5},{8,10},{10,8},{9,1... | collective-permute-start | bytes 215048 | tf_op jit(solution)/shard_map/ppermute | solution.py:237
  17.8 3.6 %collective-permute-start.14 = (bf16[5,56,128]{2,1,0:T(8,128)(2,1)S(1)}, bf16[5,56,128]{2,1,0:T(8,128)(2,1)S(1)}, u32[]{:S(2)}, u32[]{:S(2)}) collective-permute-start(bf16[5,56,128]{2,1,0:T(8,128)(2,1)S(1)} %collective-permute-done.3.refs_5_), channel_id=1, source_target_pairs={{0,1},{1,0},{2,3},{3,2},{4,5},{5,4},{6,7},{7,6},{8,9},{9,8},{10,11... | collective-permute-start | bytes 215048 | tf_op jit(solution)/shard_map/ppermute | solution.py:237
  17.8 4.2 %collective-permute-start.9 = (bf16[5,56,128]{2,1,0:T(8,128)(2,1)S(1)}, bf16[5,56,128]{2,1,0:T(8,128)(2,1)S(1)}, u32[]{:S(2)}, u32[]{:S(2)}) collective-permute-start(bf16[5,56,128]{2,1,0:T(8,128)(2,1)S(1)} %collective-permute-done.refs_0_), channel_id=1, source_target_pairs={{0,1},{1,0},{2,3},{3,2},{4,5},{5,4},{6,7},{7,6},{8,9},{9,8},{10,11... | collective-permute-start | bytes 215048 | tf_op jit(solution)/shard_map/ppermute | solution.py:237
  18.3 3.6 %collective-permute-start.10 = (bf16[5,56,128]{2,1,0:T(8,128)(2,1)S(1)}, bf16[5,56,128]{2,1,0:T(8,128)(2,1)S(1)}, u32[]{:S(2)}, u32[]{:S(2)}) collective-permute-start(bf16[5,56,128]{2,1,0:T(8,128)(2,1)S(1)} %collective-permute-done.1.refs_1_), channel_id=1, source_target_pairs={{0,1},{1,0},{2,3},{3,2},{4,5},{5,4},{6,7},{7,6},{8,9},{9,8},{10,11... | collective-permute-start | bytes 215048 | tf_op jit(solution)/shard_map/ppermute | solution.py:237
  20.7 1.3 %collective-permute-start.11 = (bf16[5,56,128]{2,1,0:T(8,128)(2,1)S(1)}, bf16[5,56,128]{2,1,0:T(8,128)(2,1)S(1)}, u32[]{:S(2)}, u32[]{:S(2)}) collective-permute-start(bf16[5,56,128]{2,1,0:T(8,128)(2,1)S(1)} %collective-permute-done.2.refs_2_), channel_id=1, source_target_pairs={{0,1},{1,0},{2,3},{3,2},{4,5},{5,4},{6,7},{7,6},{8,9},{9,8},{10,11... | collective-permute-start | bytes 215048 | tf_op jit(solution)/shard_map/ppermute | solution.py:237
  21.4 1.3 %collective-permute-start.12 = (bf16[5,56,128]{2,1,0:T(8,128)(2,1)S(1)}, bf16[5,56,128]{2,1,0:T(8,128)(2,1)S(1)}, u32[]{:S(2)}, u32[]{:S(2)}) collective-permute-start(bf16[5,56,128]{2,1,0:T(8,128)(2,1)S(1)} %collective-permute-done.4.refs_3_), channel_id=1, source_target_pairs={{0,1},{1,0},{2,3},{3,2},{4,5},{5,4},{6,7},{7,6},{8,9},{9,8},{10,11... | collective-permute-start | bytes 215048 | tf_op jit(solution)/shard_map/ppermute | solution.py:237
  21.4 1.4 %collective-permute-start.13 = (bf16[5,56,128]{2,1,0:T(8,128)(2,1)S(1)}, bf16[5,56,128]{2,1,0:T(8,128)(2,1)S(1)}, u32[]{:S(2)}, u32[]{:S(2)}) collective-permute-start(bf16[5,56,128]{2,1,0:T(8,128)(2,1)S(1)} %collective-permute-done.5.refs_4_), channel_id=1, source_target_pairs={{0,1},{1,0},{2,3},{3,2},{4,5},{5,4},{6,7},{7,6},{8,9},{9,8},{10,11... | collective-permute-start | bytes 215048 | tf_op jit(solution)/shard_map/ppermute | solution.py:237
  25.2 5.1 %collective-permute-start.24 = (bf16[2,8,56,128]{3,2,1,0:T(8,128)(2,1)S(1)}, bf16[2,8,56,128]{3,2,1,0:T(8,128)(2,1)S(1)}, u32[]{:S(2)}, u32[]{:S(2)}) collective-permute-start(bf16[2,8,56,128]{3,2,1,0:T(8,128)(2,1)S(1)} %get-tuple-element.78), channel_id=1, source_target_pairs={{0,1},{1,0},{2,3},{3,2},{4,5},{5,4},{6,7},{7,6},{8,9},{9,8},{10,11... | collective-permute-start | bytes 688136 | tf_op jit(solution)/shard_map/ppermute | solution.py:237
  25.6 1.4 %collective-permute-start.15 = (bf16[2,5,56,128]{3,2,1,0:T(8,128)(2,1)S(1)}, bf16[2,5,56,128]{3,2,1,0:T(8,128)(2,1)S(1)}, u32[]{:S(2)}, u32[]{:S(2)}) collective-permute-start(bf16[2,5,56,128]{3,2,1,0:T(8,128)(2,1)S(1)} %get-tuple-element.60), channel_id=1, source_target_pairs={{0,1},{1,0},{2,3},{3,2},{4,5},{5,4},{6,7},{7,6},{8,9},{9,8},{10,11... | collective-permute-start | bytes 430088 | tf_op jit(solution)/shard_map/ppermute | solution.py:237
  25.8 2.3 %collective-permute-start.18 = (bf16[2,5,56,128]{3,2,1,0:T(8,128)(2,1)S(1)}, bf16[2,5,56,128]{3,2,1,0:T(8,128)(2,1)S(1)}, u32[]{:S(2)}, u32[]{:S(2)}) collective-permute-start(bf16[2,5,56,128]{3,2,1,0:T(8,128)(2,1)S(1)} %get-tuple-element.66), channel_id=1, source_target_pairs={{0,1},{1,0},{2,3},{3,2},{4,5},{5,4},{6,7},{7,6},{8,9},{9,8},{10,11... | collective-permute-start | bytes 430088 | tf_op jit(solution)/shard_map/ppermute | solution.py:237
  26.1 3.1 %collective-permute-start.21 = (bf16[2,5,56,128]{3,2,1,0:T(8,128)(2,1)S(1)}, bf16[2,5,56,128]{3,2,1,0:T(8,128)(2,1)S(1)}, u32[]{:S(2)}, u32[]{:S(2)}) collective-permute-start(bf16[2,5,56,128]{3,2,1,0:T(8,128)(2,1)S(1)} %get-tuple-element.72), channel_id=1, source_target_pairs={{0,1},{1,0},{2,3},{3,2},{4,5},{5,4},{6,7},{7,6},{8,9},{9,8},{10,11... | collective-permute-start | bytes 430088 | tf_op jit(solution)/shard_map/ppermute | solution.py:237
  27.0 5.1 %collective-permute-start.16 = (bf16[5,56,128]{2,1,0:T(8,128)(2,1)S(1)}, bf16[5,56,128]{2,1,0:T(8,128)(2,1)S(1)}, u32[]{:S(2)}, u32[]{:S(2)}) collective-permute-start(bf16[5,56,128]{2,1,0:T(8,128)(2,1)S(1)} %get-tuple-element.64), channel_id=1, source_target_pairs={{0,2},{2,0},{1,3},{3,1},{4,6},{6,4},{5,7},{7,5},{8,10},{10,8},{9,1... | collective-permute-start | bytes 215048 | tf_op jit(solution)/shard_map/ppermute | solution.py:237
  28.1 6.4 %collective-permute-start.19 = (bf16[5,56,128]{2,1,0:T(8,128)(2,1)S(1)}, bf16[5,56,128]{2,1,0:T(8,128)(2,1)S(1)}, u32[]{:S(2)}, u32[]{:S(2)}) collective-permute-start(bf16[5,56,128]{2,1,0:T(8,128)(2,1)S(1)} %get-tuple-element.70), channel_id=1, source_target_pairs={{0,2},{2,0},{1,3},{3,1},{4,6},{6,4},{5,7},{7,5},{8,10},{10,8},{9,1... | collective-permute-start | bytes 215048 | tf_op jit(solution)/shard_map/ppermute | solution.py:237
  29.3 5.9 %collective-permute-start.22 = (bf16[5,56,128]{2,1,0:T(8,128)(2,1)S(1)}, bf16[5,56,128]{2,1,0:T(8,128)(2,1)S(1)}, u32[]{:S(2)}, u32[]{:S(2)}) collective-permute-start(bf16[5,56,128]{2,1,0:T(8,128)(2,1)S(1)} %get-tuple-element.76), channel_id=1, source_target_pairs={{0,2},{2,0},{1,3},{3,1},{4,6},{6,4},{5,7},{7,5},{8,10},{10,8},{9,1... | collective-permute-start | bytes 215048 | tf_op jit(solution)/shard_map/ppermute | solution.py:237
  30.4 10.6 %collective-permute-start.25 = (bf16[8,56,128]{2,1,0:T(8,128)(2,1)S(1)}, bf16[8,56,128]{2,1,0:T(8,128)(2,1)S(1)}, u32[]{:S(2)}, u32[]{:S(2)}) collective-permute-start(bf16[8,56,128]{2,1,0:T(8,128)(2,1)S(1)} %get-tuple-element.82), channel_id=1, source_target_pairs={{0,2},{2,0},{1,3},{3,1},{4,6},{6,4},{5,7},{7,5},{8,10},{10,8},{9,1... | collective-permute-start | bytes 344072 | tf_op jit(solution)/shard_map/ppermute | solution.py:237
  32.1 6.6 %collective-permute-start.17 = (bf16[5,56,128]{2,1,0:T(8,128)(2,1)S(1)}, bf16[5,56,128]{2,1,0:T(8,128)(2,1)S(1)}, u32[]{:S(2)}, u32[]{:S(2)}) collective-permute-start(bf16[5,56,128]{2,1,0:T(8,128)(2,1)S(1)} %narrow_sum.3), channel_id=1, source_target_pairs={{0,12},{4,8},{8,4},{12,0},{1,13},{5,9},{9,5},{13,1},{2,14},{6,10},... | collective-permute-start | bytes 215048 | tf_op jit(solution)/shard_map/ppermute | solution.py:237
  34.5 6.4 %collective-permute-start.20 = (bf16[5,56,128]{2,1,0:T(8,128)(2,1)S(1)}, bf16[5,56,128]{2,1,0:T(8,128)(2,1)S(1)}, u32[]{:S(2)}, u32[]{:S(2)}) collective-permute-start(bf16[5,56,128]{2,1,0:T(8,128)(2,1)S(1)} %narrow_sum.4), channel_id=1, source_target_pairs={{0,8},{4,12},{8,0},{12,4},{1,9},{5,13},{9,1},{13,5},{2,10},{6,14},... | collective-permute-start | bytes 215048 | tf_op jit(solution)/shard_map/ppermute | solution.py:237
  35.2 5.7 %collective-permute-start.23 = (bf16[5,56,128]{2,1,0:T(8,128)(2,1)S(1)}, bf16[5,56,128]{2,1,0:T(8,128)(2,1)S(1)}, u32[]{:S(2)}, u32[]{:S(2)}) collective-permute-start(bf16[5,56,128]{2,1,0:T(8,128)(2,1)S(1)} %narrow_sum.5), channel_id=1, source_target_pairs={{0,4},{4,0},{8,12},{12,8},{1,5},{5,1},{9,13},{13,9},{2,6},{6,2},{1... | collective-permute-start | bytes 215048 | tf_op jit(solution)/shard_map/ppermute | solution.py:237

commit v11 on v10

--- a/solution.py
+++ b/solution.py
@@ -313,19 +313,16 @@
         ],
     )
     far, (route, gains) = far[:-2], far[-2:]
-    order = list(range(n_wide - 1, 1, -1))
-    across = ("wide", "narrow")
+    order = list(range(n_wide - 1, 0, -1))
     bundles = [swap(far[k - 1], "wide", k) for k in order]
-    direct = [swap(far[0], across, n_narrow + j) for j in range(n_narrow)]
     near_line = [near] + [swap(near, "narrow", j) for j in range(1, n_narrow)]
-    bundles = after(bundles, *direct)
     if n_wide > 4:
         bundles = [jnp.concatenate(bundles, axis=0)]
     lines = [list(bundles)]
     for j in range(1, n_narrow):
         lines.append([swap(value, "narrow", j) for value in bundles])
-    per = len(bundles) + 1
-    slots = [value.shape[0] for value in bundles] + [CAP]
+    per = len(bundles)
+    slots = [value.shape[0] for value in bundles]
     near_line = after(near_line, *bundles)
     near_all = list(near_line)
     for c in range(1, n_pair):
@@ -350,8 +347,7 @@
     side = after([value for line in lines[1:] for value in line], near_mid[1])
     far_line = []
     for j in range(n_narrow):
-        far_line += lines[0] if j == 0 else side[(j - 1) * (per - 1) : j * (per - 1)]
-        far_line.append(direct[j])
+        far_line += lines[0] if j == 0 else side[(j - 1) * per : j * per]
     far_all = list(far_line)
     for c in range(1, n_pair):
         far_all += [swap(value, "pair", c) for value in far_line]
@@ -399,7 +395,6 @@
             [],
             limit=limit,
         )
-    order.append(1)
     far_back = [swap(value, "wide", k) for k, value in zip(order, sums)]
     near_parts = reduce_pair(near_out, cuts=HALVES)
     near_back = []

time: 41.9 us -> 42.2 us (level)
  waiting for transfers between devices: 12.7 us -> 13.8 us
  starting transfers between devices: 22.2 us -> 21.4 us
    ppermute x26, waiting for transfers between devices: 12.7 us -> 13.8 us  [swap(): return lax.ppermute(value, axis, [(i, i ^ offset) for i in range(size)])]
    ppermute x26, starting transfers between devices: 22.2 us -> 21.4 us  [swap(): return lax.ppermute(value, axis, [(i, i ^ offset) for i in range(size)])]
  transfers between devices with their start and end apart: 26 -> 26, of which waited for: 13 -> 14; matrix products, arithmetic and copies ran while one was open for 0% -> 0% of each run, Pallas kernels for 6% -> 6%
where the time goes in v11:
time: 42.2 us; the launch traced here: 42 us
  starting transfers between devices  21.4 us (51%)
  waiting for transfers between devices  13.8 us (33%)
  Pallas kernels  6.71 us (16%)
    ppermute x26, starting transfers between devices, swap(): return lax.ppermute(value, axis, [(i, i ^ offset) for i in range(size)])  21.4 us
    ppermute x26, waiting for transfers between devices, swap(): return lax.ppermute(value, axis, [(i, i ^ offset) for i in range(size)])  13.8 us
    pallas_call x12, Pallas kernels, call(): pl.pallas_call(kernel, out_shape=outs, in_specs=specs, out_specs=jax.tree...  6.71 us
  transfers between devices with their start and end apart: 26, of which 14 were waited for; matrix products, arithmetic and copies ran while one was open for 0% of the time, Pallas kernels for 6%

profile of v11, /device:TPU:0, one launch (start us, length us, event | category | flops | bytes accessed | tf_op | source)
XLA Modules:
  0.0 42.0 jit_solution(18184671939192365318)
XLA Ops:
  0.0 1.4 %dispatch.1 = (bf16[9,56,128]{2,1,0:T(8,128)(2,1)S(1)}, bf16[5,56,128]{2,1,0:T(8,128)(2,1)S(1)}, bf16[5,56,128]{2,1,0:T(8,128)(2,1)S(1)}, bf16[5,56,128]{2,1,0:T...) custom-call(s32[2,8]{1,0:T(2,128)} %bitcast.11, s32[4]{0:T(128)} %place_in.1, f32[2,8]{1,0:T(2,128)} %bitcast.12, ...), custom_call_target="tpu_custom_call" | custom-call | tf_op jit(solution)/shard_map/dispatch/pallas_call | solution.py:249
  1.4 3.0 %collective-permute-start.6 = (bf16[9,56,128]{2,1,0:T(8,128)(2,1)S(1)}, bf16[9,56,128]{2,1,0:T(8,128)(2,1)S(1)}, u32[]{:S(2)}, u32[]{:S(2)}) collective-permute-start(bf16[9,56,128]{2,1,0:T(8,128)(2,1)S(1)} %get-tuple-element.49.refs_0_), channel_id=1, source_target_pairs={{0,2},{2,0},{1,3},{3,1},{4,6},{6,4},{5,7},{7,5},{8,10},{10,8},{9,1... | collective-permute-start | bytes 387080 | tf_op jit(solution)/shard_map/ppermute | solution.py:237
  4.4 3.6 %collective-permute-start = (bf16[5,56,128]{2,1,0:T(8,128)(2,1)S(1)}, bf16[5,56,128]{2,1,0:T(8,128)(2,1)S(1)}, u32[]{:S(2)}, u32[]{:S(2)}) collective-permute-start(bf16[5,56,128]{2,1,0:T(8,128)(2,1)S(1)} %get-tuple-element.45), channel_id=1, source_target_pairs={{0,12},{4,8},{8,4},{12,0},{1,13},{5,9},{9,5},{13,1},{2,14},{6,10},... | collective-permute-start | bytes 215048 | tf_op jit(solution)/shard_map/ppermute | solution.py:237
  8.0 0.8 %collective-permute-start.2 = (bf16[5,56,128]{2,1,0:T(8,128)(2,1)S(1)}, bf16[5,56,128]{2,1,0:T(8,128)(2,1)S(1)}, u32[]{:S(2)}, u32[]{:S(2)}) collective-permute-start(bf16[5,56,128]{2,1,0:T(8,128)(2,1)S(1)} %get-tuple-element.47), channel_id=1, source_target_pairs={{0,4},{4,0},{8,12},{12,8},{1,5},{5,1},{9,13},{13,9},{2,6},{6,2},{1... | collective-permute-start | bytes 215048 | tf_op jit(solution)/shard_map/ppermute | solution.py:237
  8.8 2.6 %collective-permute-done.refs_0_ = bf16[5,56,128]{2,1,0:T(8,128)(2,1)S(1)} collective-permute-done((bf16[5,56,128]{2,1,0:T(8,128)(2,1)S(1)}, bf16[5,56,128]{2,1,0:T(8,128)(2,1)S(1)}, u32[]{:S(2)}, u32[]{:S(2)}) %collective-permute-start) | collective-permute-done | bytes 71712 | tf_op jit(solution)/shard_map/ppermute | solution.py:237
  11.4 2.4 %collective-permute-done.1.refs_1_ = bf16[5,56,128]{2,1,0:T(8,128)(2,1)S(1)} collective-permute-done((bf16[5,56,128]{2,1,0:T(8,128)(2,1)S(1)}, bf16[5,56,128]{2,1,0:T(8,128)(2,1)S(1)}, u32[]{:S(2)}, u32[]{:S(2)}) %collective-permute-start.1) | collective-permute-done | bytes 71712 | tf_op jit(solution)/shard_map/ppermute | solution.py:237
  13.9 0.5 %collective-permute-start.8 = (bf16[9,56,128]{2,1,0:T(8,128)(2,1)S(1)}, bf16[9,56,128]{2,1,0:T(8,128)(2,1)S(1)}, u32[]{:S(2)}, u32[]{:S(2)}) collective-permute-start(bf16[9,56,128]{2,1,0:T(8,128)(2,1)S(1)} %collective-permute-done.6.refs_1_), channel_id=1, source_target_pairs={{0,1},{1,0},{2,3},{3,2},{4,5},{5,4},{6,7},{7,6},{8,9},{9,8},{10,11... | collective-permute-start | bytes 387080 | tf_op jit(solution)/shard_map/ppermute | solution.py:237
  14.4 0.4 collective-permute-start.3
  14.9 1.6 %collective-permute-start.4 = (bf16[5,56,128]{2,1,0:T(8,128)(2,1)S(1)}, bf16[5,56,128]{2,1,0:T(8,128)(2,1)S(1)}, u32[]{:S(2)}, u32[]{:S(2)}) collective-permute-start(bf16[5,56,128]{2,1,0:T(8,128)(2,1)S(1)} %collective-permute-done.1.refs_1_), channel_id=1, source_target_pairs={{0,2},{2,0},{1,3},{3,1},{4,6},{6,4},{5,7},{7,5},{8,10},{10,8},{9,1... | collective-permute-start | bytes 215048 | tf_op jit(solution)/shard_map/ppermute | solution.py:237
  16.5 0.4 collective-permute-start.5
  16.9 0.5 %collective-permute-start.10 = (bf16[5,56,128]{2,1,0:T(8,128)(2,1)S(1)}, bf16[5,56,128]{2,1,0:T(8,128)(2,1)S(1)}, u32[]{:S(2)}, u32[]{:S(2)}) collective-permute-start(bf16[5,56,128]{2,1,0:T(8,128)(2,1)S(1)} %collective-permute-done.1.refs_1_), channel_id=1, source_target_pairs={{0,1},{1,0},{2,3},{3,2},{4,5},{5,4},{6,7},{7,6},{8,9},{9,8},{10,11... | collective-permute-start | bytes 215048 | tf_op jit(solution)/shard_map/ppermute | solution.py:237
  17.4 2.0 %near_shared.1 = (bf16[32,7168]{1,0:T(8,128)(2,1)S(1)}, f32[32,128]{1,0:T(8,128)S(1)}, f32[32,7168]{1,0:T(8,128)S(1)}) custom-call(bf16[9,56,128]{2,1,0:T(8,128)(2,1)S(1)} %get-tuple-element.49.refs_0_, bf16[9,56,128]{2,1,0:T(8,128)(2,1)S(1)} %collective-permute-done.6.refs_1_, bf16[9,56,128]{2,1,0:T(8,128)(2,1)S(1)} %collective-permute-done.7.refs_2_, ...), custom_call_target="tpu_custom_call" | custom-call | flops 352321536 | bytes 11010048 | tf_op jit(solution)/shard_map/near_shared/pallas_call | solution.py:249
  19.6 1.3 %collective-permute-done.4.refs_4_ = bf16[5,56,128]{2,1,0:T(8,128)(2,1)S(1)} collective-permute-done((bf16[5,56,128]{2,1,0:T(8,128)(2,1)S(1)}, bf16[5,56,128]{2,1,0:T(8,128)(2,1)S(1)}, u32[]{:S(2)}, u32[]{:S(2)}) %collective-permute-start.4) | collective-permute-done | bytes 71712 | tf_op jit(solution)/shard_map/ppermute | solution.py:237
  20.9 0.8 %collective-permute-done.5.refs_5_ = bf16[5,56,128]{2,1,0:T(8,128)(2,1)S(1)} collective-permute-done((bf16[5,56,128]{2,1,0:T(8,128)(2,1)S(1)}, bf16[5,56,128]{2,1,0:T(8,128)(2,1)S(1)}, u32[]{:S(2)}, u32[]{:S(2)}) %collective-permute-start.5) | collective-permute-done | bytes 71712 | tf_op jit(solution)/shard_map/ppermute | solution.py:237
  21.7 0.5 %collective-permute-start.13 = (bf16[5,56,128]{2,1,0:T(8,128)(2,1)S(1)}, bf16[5,56,128]{2,1,0:T(8,128)(2,1)S(1)}, u32[]{:S(2)}, u32[]{:S(2)}) collective-permute-start(bf16[5,56,128]{2,1,0:T(8,128)(2,1)S(1)} %collective-permute-done.4.refs_4_), channel_id=1, source_target_pairs={{0,1},{1,0},{2,3},{3,2},{4,5},{5,4},{6,7},{7,6},{8,9},{9,8},{10,11... | collective-permute-start | bytes 215048 | tf_op jit(solution)/shard_map/ppermute | solution.py:237
  22.2 0.7 %collective-permute-done.12.refs_9_ = bf16[5,56,128]{2,1,0:T(8,128)(2,1)S(1)} collective-permute-done((bf16[5,56,128]{2,1,0:T(8,128)(2,1)S(1)}, bf16[5,56,128]{2,1,0:T(8,128)(2,1)S(1)}, u32[]{:S(2)}, u32[]{:S(2)}) %collective-permute-start.12) | collective-permute-done | bytes 71712 | tf_op jit(solution)/shard_map/ppermute | solution.py:237
  23.1 0.4 collective-permute-done.14.refs_11_
  23.5 2.3 %routed.1 = (bf16[2,8,56,128]{3,2,1,0:T(8,128)(2,1)S(1)}, bf16[2,8,56,128]{3,2,1,0:T(8,128)(2,1)S(1)}, bf16[2,5,56,128]{3,2,1,0:T(8,128)(2,1)S(1)}, bf16[2,5,56,...) custom-call(bf16[5,56,128]{2,1,0:T(8,128)(2,1)S(1)} %collective-perm, ...), custom_call_target="tpu_custom_call" | custom-call | flops 1012924416 | bytes 11010048 | tf_op jit(solution)/shard_map/routed/pallas_call | solution.py:249
  26.0 0.4 collective-permute-start.15
  26.5 0.4 collective-permute-start.21
  26.8 0.7 %collective-permute-done.15.refs_1_ = bf16[2,5,56,128]{3,2,1,0:T(8,128)(2,1)S(1)} collective-permute-done((bf16[2,5,56,128]{3,2,1,0:T(8,128)(2,1)S(1)}, bf16[2,5,56,128]{3,2,1,0:T(8,128)(2,1)S(1)}, u32[]{:S(2)}, u32[]{:S(2)}) %collective-permute-start.15) | collective-permute-done | bytes 143392 | tf_op jit(solution)/shard_map/ppermute | solution.py:237
  27.5 0.7 %collective-permute-start.16 = (bf16[5,56,128]{2,1,0:T(8,128)(2,1)S(1)}, bf16[5,56,128]{2,1,0:T(8,128)(2,1)S(1)}, u32[]{:S(2)}, u32[]{:S(2)}) collective-permute-start(bf16[5,56,128]{2,1,0:T(8,128)(2,1)S(1)} %get-tuple-element.62), channel_id=1, source_target_pairs={{0,2},{2,0},{1,3},{3,1},{4,6},{6,4},{5,7},{7,5},{8,10},{10,8},{9,1... | collective-permute-start | bytes 215048 | tf_op jit(solution)/shard_map/ppermute | solution.py:237
  28.3 1.5 %collective-permute-start.19 = (bf16[5,56,128]{2,1,0:T(8,128)(2,1)S(1)}, bf16[5,56,128]{2,1,0:T(8,128)(2,1)S(1)}, u32[]{:S(2)}, u32[]{:S(2)}) collective-permute-start(bf16[5,56,128]{2,1,0:T(8,128)(2,1)S(1)} %get-tuple-element.68), channel_id=1, source_target_pairs={{0,2},{2,0},{1,3},{3,1},{4,6},{6,4},{5,7},{7,5},{8,10},{10,8},{9,1... | collective-permute-start | bytes 215048 | tf_op jit(solution)/shard_map/ppermute | solution.py:237
  29.8 0.7 %collective-permute-start.22 = (bf16[5,56,128]{2,1,0:T(8,128)(2,1)S(1)}, bf16[5,56,128]{2,1,0:T(8,128)(2,1)S(1)}, u32[]{:S(2)}, u32[]{:S(2)}) collective-permute-start(bf16[5,56,128]{2,1,0:T(8,128)(2,1)S(1)} %get-tuple-element.74), channel_id=1, source_target_pairs={{0,2},{2,0},{1,3},{3,1},{4,6},{6,4},{5,7},{7,5},{8,10},{10,8},{9,1... | collective-permute-start | bytes 215048 | tf_op jit(solution)/shard_map/ppermute | solution.py:237
  30.5 1.5 %collective-permute-start.25 = (bf16[8,56,128]{2,1,0:T(8,128)(2,1)S(1)}, bf16[8,56,128]{2,1,0:T(8,128)(2,1)S(1)}, u32[]{:S(2)}, u32[]{:S(2)}) collective-permute-start(bf16[8,56,128]{2,1,0:T(8,128)(2,1)S(1)} %get-tuple-element.80), channel_id=1, source_target_pairs={{0,2},{2,0},{1,3},{3,1},{4,6},{6,4},{5,7},{7,5},{8,10},{10,8},{9,1... | collective-permute-start | bytes 344072 | tf_op jit(solution)/shard_map/ppermute | solution.py:237
  32.0 0.7 %collective-permute-done.16.refs_1_ = bf16[5,56,128]{2,1,0:T(8,128)(2,1)S(1)} collective-permute-done((bf16[5,56,128]{2,1,0:T(8,128)(2,1)S(1)}, bf16[5,56,128]{2,1,0:T(8,128)(2,1)S(1)}, u32[]{:S(2)}, u32[]{:S(2)}) %collective-permute-start.16) | collective-permute-done | bytes 71712 | tf_op jit(solution)/shard_map/ppermute | solution.py:237
  32.7 2.6 %collective-permute-start.17 = (bf16[5,56,128]{2,1,0:T(8,128)(2,1)S(1)}, bf16[5,56,128]{2,1,0:T(8,128)(2,1)S(1)}, u32[]{:S(2)}, u32[]{:S(2)}) collective-permute-start(bf16[5,56,128]{2,1,0:T(8,128)(2,1)S(1)} %narrow_sum.3), channel_id=1, source_target_pairs={{0,12},{4,8},{8,4},{12,0},{1,13},{5,9},{9,5},{13,1},{2,14},{6,10},... | collective-permute-start | bytes 215048 | tf_op jit(solution)/shard_map/ppermute | solution.py:237
  35.3 0.3 collective-permute-start.20
  35.8 1.7 %collective-permute-start.23 = (bf16[5,56,128]{2,1,0:T(8,128)(2,1)S(1)}, bf16[5,56,128]{2,1,0:T(8,128)(2,1)S(1)}, u32[]{:S(2)}, u32[]{:S(2)}) collective-permute-start(bf16[5,56,128]{2,1,0:T(8,128)(2,1)S(1)} %narrow_sum.5), channel_id=1, source_target_pairs={{0,4},{4,0},{8,12},{12,8},{1,5},{5,1},{9,13},{13,9},{2,6},{6,2},{1... | collective-permute-start | bytes 215048 | tf_op jit(solution)/shard_map/ppermute | solution.py:237
  37.5 2.1 %collective-permute-done.17.refs_0_ = bf16[5,56,128]{2,1,0:T(8,128)(2,1)S(1)} collective-permute-done((bf16[5,56,128]{2,1,0:T(8,128)(2,1)S(1)}, bf16[5,56,128]{2,1,0:T(8,128)(2,1)S(1)}, u32[]{:S(2)}, u32[]{:S(2)}) %collective-permute-start.17) | collective-permute-done | bytes 71712 | tf_op jit(solution)/shard_map/ppermute | solution.py:237
  39.6 1.6 %collective-permute-done.20.refs_1_ = bf16[5,56,128]{2,1,0:T(8,128)(2,1)S(1)} collective-permute-done((bf16[5,56,128]{2,1,0:T(8,128)(2,1)S(1)}, bf16[5,56,128]{2,1,0:T(8,128)(2,1)S(1)}, u32[]{:S(2)}, u32[]{:S(2)}) %collective-permute-start.20) | collective-permute-done | bytes 71712 | tf_op jit(solution)/shard_map/ppermute | solution.py:237
  41.3 0.7 %combine.1 = bf16[8,7168]{1,0:T(8,128)(2,1)} custom-call(f32[8,56,128]{2,1,0:T(8,128)S(1)} %far_combine.1.far, bf16[8,56,128]{2,1,0:T(8,128)(2,1)S(1)} %get-tuple-element.79.refs_0_, bf16[8,56,128]{2,1,0:T(8,128)(2,1)S(1)} %collective-permute-done.25.refs_1_), custom_call_target="tpu_custom_call" | custom-call | tf_op jit(solution)/shard_map/combine/pallas_call | solution.py:249
  (44 shorter events, 1.3 us)
Async XLA Ops:
  0.0 17.4 %copy-start = (bf16[7168,256]{1,0:T(8,128)(2,1)S(1)}, bf16[7168,256]{1,0:T(8,128)(2,1)}, u32[]{:S(2)}) copy-start(bf16[7168,256]{1,0:T(8,128)(2,1)} %refs_4_.1) | copy-start | bytes 11010052
  0.0 17.4 %copy-start.1 = (bf16[7168,256]{1,0:T(8,128)(2,1)S(1)}, bf16[7168,256]{1,0:T(8,128)(2,1)}, u32[]{:S(2)}) copy-start(bf16[7168,256]{1,0:T(8,128)(2,1)} %refs_5_.1) | copy-start | bytes 11010052
  0.0 17.4 %copy-start.2 = (bf16[256,7168]{1,0:T(8,128)(2,1)S(1)}, bf16[256,7168]{1,0:T(8,128)(2,1)}, u32[]{:S(2)}) copy-start(bf16[256,7168]{1,0:T(8,128)(2,1)} %refs_6_.1) | copy-start | bytes 11010052
  1.4 12.6 %collective-permute-start.6 = (bf16[9,56,128]{2,1,0:T(8,128)(2,1)S(1)}, bf16[9,56,128]{2,1,0:T(8,128)(2,1)S(1)}, u32[]{:S(2)}, u32[]{:S(2)}) collective-permute-start(bf16[9,56,128]{2,1,0:T(8,128)(2,1)S(1)} %get-tuple-element.49.refs_0_), channel_id=1, source_target_pairs={{0,2},{2,0},{1,3},{3,1},{4,6},{6,4},{5,7},{7,5},{8,10},{10,8},{9,1... | collective-permute-start | bytes 387080 | tf_op jit(solution)/shard_map/ppermute | solution.py:237
  4.4 7.0 %collective-permute-start = (bf16[5,56,128]{2,1,0:T(8,128)(2,1)S(1)}, bf16[5,56,128]{2,1,0:T(8,128)(2,1)S(1)}, u32[]{:S(2)}, u32[]{:S(2)}) collective-permute-start(bf16[5,56,128]{2,1,0:T(8,128)(2,1)S(1)} %get-tuple-element.45), channel_id=1, source_target_pairs={{0,12},{4,8},{8,4},{12,0},{1,13},{5,9},{9,5},{13,1},{2,14},{6,10},... | collective-permute-start | bytes 215048 | tf_op jit(solution)/shard_map/ppermute | solution.py:237
  8.0 5.8 %collective-permute-start.1 = (bf16[5,56,128]{2,1,0:T(8,128)(2,1)S(1)}, bf16[5,56,128]{2,1,0:T(8,128)(2,1)S(1)}, u32[]{:S(2)}, u32[]{:S(2)}) collective-permute-start(bf16[5,56,128]{2,1,0:T(8,128)(2,1)S(1)} %get-tuple-element.46), channel_id=1, source_target_pairs={{0,8},{4,12},{8,0},{12,4},{1,9},{5,13},{9,1},{13,5},{2,10},{6,14},... | collective-permute-start | bytes 215048 | tf_op jit(solution)/shard_map/ppermute | solution.py:237
  8.0 15.5 %copy-start.3 = (bf16[1,7168,256]{2,1,0:T(8,128)(2,1)S(1)}, bf16[1,7168,256]{2,1,0:T(8,128)(2,1)}, u32[]{:S(2)}) copy-start(bf16[1,7168,256]{2,1,0:T(8,128)(2,1)} %param.16) | copy-start | bytes 11010052
  8.0 15.5 %copy-start.4 = (bf16[1,7168,256]{2,1,0:T(8,128)(2,1)S(1)}, bf16[1,7168,256]{2,1,0:T(8,128)(2,1)}, u32[]{:S(2)}) copy-start(bf16[1,7168,256]{2,1,0:T(8,128)(2,1)} %param.17) | copy-start | bytes 11010052
  8.0 15.5 %copy-start.5 = (bf16[1,256,7168]{2,1,0:T(8,128)(2,1)S(1)}, bf16[1,256,7168]{2,1,0:T(8,128)(2,1)}, u32[]{:S(2)}) copy-start(bf16[1,256,7168]{2,1,0:T(8,128)(2,1)} %param.18) | copy-start | bytes 11010052
  8.0 5.9 %collective-permute-start.2 = (bf16[5,56,128]{2,1,0:T(8,128)(2,1)S(1)}, bf16[5,56,128]{2,1,0:T(8,128)(2,1)S(1)}, u32[]{:S(2)}, u32[]{:S(2)}) collective-permute-start(bf16[5,56,128]{2,1,0:T(8,128)(2,1)S(1)} %get-tuple-element.47), channel_id=1, source_target_pairs={{0,4},{4,0},{8,12},{12,8},{1,5},{5,1},{9,13},{13,9},{2,6},{6,2},{1... | collective-permute-start | bytes 215048 | tf_op jit(solution)/shard_map/ppermute | solution.py:237
  13.9 2.9 %collective-permute-start.7 = (bf16[9,56,128]{2,1,0:T(8,128)(2,1)S(1)}, bf16[9,56,128]{2,1,0:T(8,128)(2,1)S(1)}, u32[]{:S(2)}, u32[]{:S(2)}) collective-permute-start(bf16[9,56,128]{2,1,0:T(8,128)(2,1)S(1)} %get-tuple-element.49.refs_0_), channel_id=1, source_target_pairs={{0,1},{1,0},{2,3},{3,2},{4,5},{5,4},{6,7},{7,6},{8,9},{9,8},{10,11... | collective-permute-start | bytes 387080 | tf_op jit(solution)/shard_map/ppermute | solution.py:237
  13.9 3.0 %collective-permute-start.8 = (bf16[9,56,128]{2,1,0:T(8,128)(2,1)S(1)}, bf16[9,56,128]{2,1,0:T(8,128)(2,1)S(1)}, u32[]{:S(2)}, u32[]{:S(2)}) collective-permute-start(bf16[9,56,128]{2,1,0:T(8,128)(2,1)S(1)} %collective-permute-done.6.refs_1_), channel_id=1, source_target_pairs={{0,1},{1,0},{2,3},{3,2},{4,5},{5,4},{6,7},{7,6},{8,9},{9,8},{10,11... | collective-permute-start | bytes 387080 | tf_op jit(solution)/shard_map/ppermute | solution.py:237
  14.4 5.1 %collective-permute-start.3 = (bf16[5,56,128]{2,1,0:T(8,128)(2,1)S(1)}, bf16[5,56,128]{2,1,0:T(8,128)(2,1)S(1)}, u32[]{:S(2)}, u32[]{:S(2)}) collective-permute-start(bf16[5,56,128]{2,1,0:T(8,128)(2,1)S(1)} %collective-permute-done.refs_0_), channel_id=1, source_target_pairs={{0,2},{2,0},{1,3},{3,1},{4,6},{6,4},{5,7},{7,5},{8,10},{10,8},{9,1... | collective-permute-start | bytes 215048 | tf_op jit(solution)/shard_map/ppermute | solution.py:237
  14.9 6.0 %collective-permute-start.4 = (bf16[5,56,128]{2,1,0:T(8,128)(2,1)S(1)}, bf16[5,56,128]{2,1,0:T(8,128)(2,1)S(1)}, u32[]{:S(2)}, u32[]{:S(2)}) collective-permute-start(bf16[5,56,128]{2,1,0:T(8,128)(2,1)S(1)} %collective-permute-done.1.refs_1_), channel_id=1, source_target_pairs={{0,2},{2,0},{1,3},{3,1},{4,6},{6,4},{5,7},{7,5},{8,10},{10,8},{9,1... | collective-permute-start | bytes 215048 | tf_op jit(solution)/shard_map/ppermute | solution.py:237
  16.5 5.2 %collective-permute-start.5 = (bf16[5,56,128]{2,1,0:T(8,128)(2,1)S(1)}, bf16[5,56,128]{2,1,0:T(8,128)(2,1)S(1)}, u32[]{:S(2)}, u32[]{:S(2)}) collective-permute-start(bf16[5,56,128]{2,1,0:T(8,128)(2,1)S(1)} %collective-permute-done.2.refs_2_), channel_id=1, source_target_pairs={{0,2},{2,0},{1,3},{3,1},{4,6},{6,4},{5,7},{7,5},{8,10},{10,8},{9,1... | collective-permute-start | bytes 215048 | tf_op jit(solution)/shard_map/ppermute | solution.py:237
  16.9 5.3 %collective-permute-start.9 = (bf16[5,56,128]{2,1,0:T(8,128)(2,1)S(1)}, bf16[5,56,128]{2,1,0:T(8,128)(2,1)S(1)}, u32[]{:S(2)}, u32[]{:S(2)}) collective-permute-start(bf16[5,56,128]{2,1,0:T(8,128)(2,1)S(1)} %collective-permute-done.refs_0_), channel_id=1, source_target_pairs={{0,1},{1,0},{2,3},{3,2},{4,5},{5,4},{6,7},{7,6},{8,9},{9,8},{10,11... | collective-permute-start | bytes 215048 | tf_op jit(solution)/shard_map/ppermute | solution.py:237
  16.9 5.3 %collective-permute-start.10 = (bf16[5,56,128]{2,1,0:T(8,128)(2,1)S(1)}, bf16[5,56,128]{2,1,0:T(8,128)(2,1)S(1)}, u32[]{:S(2)}, u32[]{:S(2)}) collective-permute-start(bf16[5,56,128]{2,1,0:T(8,128)(2,1)S(1)} %collective-permute-done.1.refs_1_), channel_id=1, source_target_pairs={{0,1},{1,0},{2,3},{3,2},{4,5},{5,4},{6,7},{7,6},{8,9},{9,8},{10,11... | collective-permute-start | bytes 215048 | tf_op jit(solution)/shard_map/ppermute | solution.py:237
  19.5 2.7 %collective-permute-start.11 = (bf16[5,56,128]{2,1,0:T(8,128)(2,1)S(1)}, bf16[5,56,128]{2,1,0:T(8,128)(2,1)S(1)}, u32[]{:S(2)}, u32[]{:S(2)}) collective-permute-start(bf16[5,56,128]{2,1,0:T(8,128)(2,1)S(1)} %collective-permute-done.2.refs_2_), channel_id=1, source_target_pairs={{0,1},{1,0},{2,3},{3,2},{4,5},{5,4},{6,7},{7,6},{8,9},{9,8},{10,11... | collective-permute-start | bytes 215048 | tf_op jit(solution)/shard_map/ppermute | solution.py:237
  21.7 1.3 %collective-permute-start.12 = (bf16[5,56,128]{2,1,0:T(8,128)(2,1)S(1)}, bf16[5,56,128]{2,1,0:T(8,128)(2,1)S(1)}, u32[]{:S(2)}, u32[]{:S(2)}) collective-permute-start(bf16[5,56,128]{2,1,0:T(8,128)(2,1)S(1)} %collective-permute-done.3.refs_3_), channel_id=1, source_target_pairs={{0,1},{1,0},{2,3},{3,2},{4,5},{5,4},{6,7},{7,6},{8,9},{9,8},{10,11... | collective-permute-start | bytes 215048 | tf_op jit(solution)/shard_map/ppermute | solution.py:237
  21.7 1.4 %collective-permute-start.13 = (bf16[5,56,128]{2,1,0:T(8,128)(2,1)S(1)}, bf16[5,56,128]{2,1,0:T(8,128)(2,1)S(1)}, u32[]{:S(2)}, u32[]{:S(2)}) collective-permute-start(bf16[5,56,128]{2,1,0:T(8,128)(2,1)S(1)} %collective-permute-done.4.refs_4_), channel_id=1, source_target_pairs={{0,1},{1,0},{2,3},{3,2},{4,5},{5,4},{6,7},{7,6},{8,9},{9,8},{10,11... | collective-permute-start | bytes 215048 | tf_op jit(solution)/shard_map/ppermute | solution.py:237
  22.2 1.3 %collective-permute-start.14 = (bf16[5,56,128]{2,1,0:T(8,128)(2,1)S(1)}, bf16[5,56,128]{2,1,0:T(8,128)(2,1)S(1)}, u32[]{:S(2)}, u32[]{:S(2)}) collective-permute-start(bf16[5,56,128]{2,1,0:T(8,128)(2,1)S(1)} %collective-permute-done.5.refs_5_), channel_id=1, source_target_pairs={{0,1},{1,0},{2,3},{3,2},{4,5},{5,4},{6,7},{7,6},{8,9},{9,8},{10,11... | collective-permute-start | bytes 215048 | tf_op jit(solution)/shard_map/ppermute | solution.py:237
  25.7 4.7 %collective-permute-start.24 = (bf16[2,8,56,128]{3,2,1,0:T(8,128)(2,1)S(1)}, bf16[2,8,56,128]{3,2,1,0:T(8,128)(2,1)S(1)}, u32[]{:S(2)}, u32[]{:S(2)}) collective-permute-start(bf16[2,8,56,128]{3,2,1,0:T(8,128)(2,1)S(1)} %get-tuple-element.76), channel_id=1, source_target_pairs={{0,1},{1,0},{2,3},{3,2},{4,5},{5,4},{6,7},{7,6},{8,9},{9,8},{10,11... | collective-permute-start | bytes 688136 | tf_op jit(solution)/shard_map/ppermute | solution.py:237
  26.0 1.5 %collective-permute-start.15 = (bf16[2,5,56,128]{3,2,1,0:T(8,128)(2,1)S(1)}, bf16[2,5,56,128]{3,2,1,0:T(8,128)(2,1)S(1)}, u32[]{:S(2)}, u32[]{:S(2)}) collective-permute-start(bf16[2,5,56,128]{3,2,1,0:T(8,128)(2,1)S(1)} %get-tuple-element.58), channel_id=1, source_target_pairs={{0,1},{1,0},{2,3},{3,2},{4,5},{5,4},{6,7},{7,6},{8,9},{9,8},{10,11... | collective-permute-start | bytes 430088 | tf_op jit(solution)/shard_map/ppermute | solution.py:237
  26.3 1.9 %collective-permute-start.18 = (bf16[2,5,56,128]{3,2,1,0:T(8,128)(2,1)S(1)}, bf16[2,5,56,128]{3,2,1,0:T(8,128)(2,1)S(1)}, u32[]{:S(2)}, u32[]{:S(2)}) collective-permute-start(bf16[2,5,56,128]{3,2,1,0:T(8,128)(2,1)S(1)} %get-tuple-element.64), channel_id=1, source_target_pairs={{0,1},{1,0},{2,3},{3,2},{4,5},{5,4},{6,7},{7,6},{8,9},{9,8},{10,11... | collective-permute-start | bytes 430088 | tf_op jit(solution)/shard_map/ppermute | solution.py:237
  26.5 3.3 %collective-permute-start.21 = (bf16[2,5,56,128]{3,2,1,0:T(8,128)(2,1)S(1)}, bf16[2,5,56,128]{3,2,1,0:T(8,128)(2,1)S(1)}, u32[]{:S(2)}, u32[]{:S(2)}) collective-permute-start(bf16[2,5,56,128]{3,2,1,0:T(8,128)(2,1)S(1)} %get-tuple-element.70), channel_id=1, source_target_pairs={{0,1},{1,0},{2,3},{3,2},{4,5},{5,4},{6,7},{7,6},{8,9},{9,8},{10,11... | collective-permute-start | bytes 430088 | tf_op jit(solution)/shard_map/ppermute | solution.py:237
  27.5 5.1 %collective-permute-start.16 = (bf16[5,56,128]{2,1,0:T(8,128)(2,1)S(1)}, bf16[5,56,128]{2,1,0:T(8,128)(2,1)S(1)}, u32[]{:S(2)}, u32[]{:S(2)}) collective-permute-start(bf16[5,56,128]{2,1,0:T(8,128)(2,1)S(1)} %get-tuple-element.62), channel_id=1, source_target_pairs={{0,2},{2,0},{1,3},{3,1},{4,6},{6,4},{5,7},{7,5},{8,10},{10,8},{9,1... | collective-permute-start | bytes 215048 | tf_op jit(solution)/shard_map/ppermute | solution.py:237
  28.3 7.1 %collective-permute-start.19 = (bf16[5,56,128]{2,1,0:T(8,128)(2,1)S(1)}, bf16[5,56,128]{2,1,0:T(8,128)(2,1)S(1)}, u32[]{:S(2)}, u32[]{:S(2)}) collective-permute-start(bf16[5,56,128]{2,1,0:T(8,128)(2,1)S(1)} %get-tuple-element.68), channel_id=1, source_target_pairs={{0,2},{2,0},{1,3},{3,1},{4,6},{6,4},{5,7},{7,5},{8,10},{10,8},{9,1... | collective-permute-start | bytes 215048 | tf_op jit(solution)/shard_map/ppermute | solution.py:237
  29.8 6.0 %collective-permute-start.22 = (bf16[5,56,128]{2,1,0:T(8,128)(2,1)S(1)}, bf16[5,56,128]{2,1,0:T(8,128)(2,1)S(1)}, u32[]{:S(2)}, u32[]{:S(2)}) collective-permute-start(bf16[5,56,128]{2,1,0:T(8,128)(2,1)S(1)} %get-tuple-element.74), channel_id=1, source_target_pairs={{0,2},{2,0},{1,3},{3,1},{4,6},{6,4},{5,7},{7,5},{8,10},{10,8},{9,1... | collective-permute-start | bytes 215048 | tf_op jit(solution)/shard_map/ppermute | solution.py:237
  30.5 10.8 %collective-permute-start.25 = (bf16[8,56,128]{2,1,0:T(8,128)(2,1)S(1)}, bf16[8,56,128]{2,1,0:T(8,128)(2,1)S(1)}, u32[]{:S(2)}, u32[]{:S(2)}) collective-permute-start(bf16[8,56,128]{2,1,0:T(8,128)(2,1)S(1)} %get-tuple-element.80), channel_id=1, source_target_pairs={{0,2},{2,0},{1,3},{3,1},{4,6},{6,4},{5,7},{7,5},{8,10},{10,8},{9,1... | collective-permute-start | bytes 344072 | tf_op jit(solution)/shard_map/ppermute | solution.py:237
  32.7 6.9 %collective-permute-start.17 = (bf16[5,56,128]{2,1,0:T(8,128)(2,1)S(1)}, bf16[5,56,128]{2,1,0:T(8,128)(2,1)S(1)}, u32[]{:S(2)}, u32[]{:S(2)}) collective-permute-start(bf16[5,56,128]{2,1,0:T(8,128)(2,1)S(1)} %narrow_sum.3), channel_id=1, source_target_pairs={{0,12},{4,8},{8,4},{12,0},{1,13},{5,9},{9,5},{13,1},{2,14},{6,10},... | collective-permute-start | bytes 215048 | tf_op jit(solution)/shard_map/ppermute | solution.py:237
  35.3 5.9 %collective-permute-start.20 = (bf16[5,56,128]{2,1,0:T(8,128)(2,1)S(1)}, bf16[5,56,128]{2,1,0:T(8,128)(2,1)S(1)}, u32[]{:S(2)}, u32[]{:S(2)}) collective-permute-start(bf16[5,56,128]{2,1,0:T(8,128)(2,1)S(1)} %narrow_sum.4), channel_id=1, source_target_pairs={{0,8},{4,12},{8,0},{12,4},{1,9},{5,13},{9,1},{13,5},{2,10},{6,14},... | collective-permute-start | bytes 215048 | tf_op jit(solution)/shard_map/ppermute | solution.py:237
  35.8 5.4 %collective-permute-start.23 = (bf16[5,56,128]{2,1,0:T(8,128)(2,1)S(1)}, bf16[5,56,128]{2,1,0:T(8,128)(2,1)S(1)}, u32[]{:S(2)}, u32[]{:S(2)}) collective-permute-start(bf16[5,56,128]{2,1,0:T(8,128)(2,1)S(1)} %narrow_sum.5), channel_id=1, source_target_pairs={{0,4},{4,0},{8,12},{12,8},{1,5},{5,1},{9,13},{13,9},{2,6},{6,2},{1... | collective-permute-start | bytes 215048 | tf_op jit(solution)/shard_map/ppermute | solution.py:237

commit v12 on v10

--- a/solution.py
+++ b/solution.py
@@ -10,7 +10,6 @@
 CAP = 5
 LANES = 128
 SPAN = 7
-HALVES = 1
 MAX_ROWS = 128
 
 VMEM = pltpu.VMEM
@@ -135,7 +134,7 @@
     count = n_narrow * n_pair * per
     arrived, rest = refs[:count], refs[count:]
     near, weight, value, gate_w, up_w, down_w = rest[:6]
-    near_outs, outs = rest[6 : 6 + n_pair], rest[6 + n_pair : -2]
+    first_outs, outs = rest[6 : 6 + n_pair], rest[6 + n_pair : -2]
     flat, inputs = rest[-2:]
     tall = arrived[0].shape[1]
     near_rows = near.shape[0]
@@ -169,25 +168,33 @@
         if head:
             for c in range(n_pair):
                 part = flat[c * each * tall : (c + 1) * each * tall, :]
-                near_outs[c][...] = part.reshape(near_outs[c].shape).astype(BF16)
+                part = part.reshape(n_narrow, each // n_narrow, tall, LANES)
+                outs[c][:, outs[c].shape[1] - part.shape[1] :] = part.astype(BF16)
         at = head
         for i, slots in enumerate(group):
             line, k = divmod(first + i, per)
             c, j = divmod(line, n_narrow)
             part = flat[at * tall : (at + slots) * tall, :]
-            outs[c * per + k][j] = part.reshape(slots, tall, LANES).astype(BF16)
+            part = part.reshape(slots, tall, LANES).astype(BF16)
+            if k == 0:
+                first_outs[c][j] = part
+            else:
+                start = sum(blocks[1:k])
+                outs[c][j, start : start + slots] = part
             at += slots
 
 
-def pair_sum_kernel(n_pair, cuts, *refs):
+def pair_sum_kernel(n_pair, n_narrow, *refs):
     parts, outs = refs[:n_pair], refs[n_pair:]
-    for i, out in enumerate(outs):
-        j, cut = divmod(i, cuts)
-        rows = slice(cut * out.shape[0], (cut + 1) * out.shape[0])
-        total = parts[0][j, rows].astype(F32)
-        for ref in parts[1:]:
-            total = total + ref[j, rows].astype(F32)
-        out[...] = total.astype(BF16)
+    at = 0
+    for first in range(0, len(outs), n_narrow):
+        rows = slice(at, at + outs[first].shape[0])
+        for j in range(n_narrow):
+            total = parts[0][j, rows].astype(F32)
+            for ref in parts[1:]:
+                total = total + ref[j, rows].astype(F32)
+            outs[first + j][...] = total.astype(BF16)
+        at = rows.stop
 
 
 def narrow_sum_kernel(n_narrow, *refs):
@@ -216,15 +223,14 @@
         total[t] = value
 
 
-def combine_kernel(n_narrow, far, *refs):
+def combine_kernel(far, *refs):
     near, (out, total) = refs[:-2], refs[-2:]
     rows, features = out.shape
     tall = features // LANES
     for t in range(rows):
         value = far[t]
-        cut, row = divmod(t, rows // HALVES)
-        for ref in near[cut * n_narrow : (cut + 1) * n_narrow]:
-            value = value + ref[row].astype(F32)
+        for ref in near:
+            value = value + ref[t].astype(F32)
         total[t * tall : (t + 1) * tall, :] = value
     for b in range(tall):
         out[:, b * LANES : (b + 1) * LANES] = total[
@@ -364,36 +370,36 @@
         "routed",
         far_all + list(near_mid) + routed,
         [VSPEC] * (n_narrow * n_pair * per + 6),
-        [block(n_narrow, tokens)] * n_pair
-        + [block(n_narrow, count) for count in slots] * n_pair,
+        [block(n_narrow, slots[0])] * n_pair
+        + [block(n_narrow, sum(slots[1:]) + tokens)] * n_pair,
         [VMEM((pass_rows * tall, LANES), F32), VMEM((pass_rows, features), BF16)],
         flops=6 * (near_rows + far_rows) * features * hidden,
         moved=6 * features * hidden,
         limit=limit,
     )
-    near_out, far_out = outs[:n_pair], outs[n_pair:]
-
-    def reduce_pair(parts, *first, cuts=1):
-        rows = parts[0].shape[1]
-        return call(
-            functools.partial(pair_sum_kernel, n_pair, cuts),
+    def reduce_pair(parts, pieces):
+        outs = call(
+            functools.partial(pair_sum_kernel, n_pair, n_narrow),
             "pair_sum",
-            after([parts[0]] + [swap(parts[c], "pair", c) for c in range(1, n_pair)], *first),
+            [parts[0]] + [swap(parts[c], "pair", c) for c in range(1, n_pair)],
             [VSPEC] * n_pair,
-            [block(rows // cuts)] * (n_narrow * cuts),
+            [block(rows) for rows in pieces for _ in range(n_narrow)],
             [],
             limit=limit,
         )
+        return [outs[i : i + n_narrow] for i in range(0, len(outs), n_narrow)]
 
     def send_narrow(parts):
         return [parts[0]] + [swap(parts[j], "narrow", j) for j in range(1, n_narrow)]
 
+    reduced = reduce_pair(outs[:n_pair], slots[:1])
+    reduced += reduce_pair(outs[n_pair:], slots[1:] + [tokens])
     sums = []
     for k in range(per):
         sums += call(
             functools.partial(narrow_sum_kernel, n_narrow),
             "narrow_sum",
-            send_narrow(reduce_pair(far_out[k::per])),
+            send_narrow(reduced[k]),
             [VSPEC] * n_narrow,
             [block(CAP)] * (slots[k] // CAP),
             [],
@@ -401,10 +407,7 @@
         )
     order.append(1)
     far_back = [swap(value, "wide", k) for k, value in zip(order, sums)]
-    near_parts = reduce_pair(near_out, cuts=HALVES)
-    near_back = []
-    for cut in range(HALVES):
-        near_back += send_narrow(near_parts[cut::HALVES])
+    near_back = send_narrow(reduced[per])
     far_sum = call(
         functools.partial(far_combine_kernel, order),
         "far_combine",
@@ -414,10 +417,10 @@
         [VMEM((n_wide * CAP, tall, LANES), F32)],
     )
     return call(
-        functools.partial(combine_kernel, n_narrow),
+        combine_kernel,
         "combine",
         [far_sum] + near_back,
-        [VSPEC] * (1 + HALVES * n_narrow),
+        [VSPEC] * (1 + n_narrow),
         jax.ShapeDtypeStruct((tokens, features), BF16),
         [VMEM((tokens * tall, LANES), F32)],
     )

time: 41.9 us -> 42.3 us (level)
  waiting for transfers between devices: 12.7 us -> 13.7 us
  starting transfers between devices: 22.2 us -> 21.6 us
    ppermute x26 -> x24, waiting for transfers between devices: 12.7 us -> 13.7 us  [swap(): return lax.ppermute(value, axis, [(i, i ^ offset) for i in range(size)])]
    ppermute x26 -> x24, starting transfers between devices: 22.2 us -> 21.6 us  [swap(): return lax.ppermute(value, axis, [(i, i ^ offset) for i in range(size)])]
    pallas_call x12 -> x10, Pallas kernels: 6.73 us -> 6.73 us  [call(): pl.pallas_call(kernel, out_shape=outs, in_specs=specs, out_specs=jax.tree...]
  transfers between devices with their start and end apart: 26 -> 24, of which waited for: 13 -> 13; matrix products, arithmetic and copies ran while one was open for 0% -> 0% of each run, Pallas kernels for 6% -> 6%
where the time goes in v12:
time: 42.3 us; the launch traced here: 42.2 us
  starting transfers between devices  21.6 us (51%)
  waiting for transfers between devices  13.7 us (32%)
  Pallas kernels  6.73 us (16%)
    ppermute x24, starting transfers between devices, swap(): return lax.ppermute(value, axis, [(i, i ^ offset) for i in range(size)])  21.6 us
    ppermute x24, waiting for transfers between devices, swap(): return lax.ppermute(value, axis, [(i, i ^ offset) for i in range(size)])  13.7 us
    pallas_call x10, Pallas kernels, call(): pl.pallas_call(kernel, out_shape=outs, in_specs=specs, out_specs=jax.tree...  6.73 us
  transfers between devices with their start and end apart: 24, of which 13 were waited for; matrix products, arithmetic and copies ran while one was open for 0% of the time, Pallas kernels for 6%

profile of v12, /device:TPU:0, one launch (start us, length us, event | category | flops | bytes accessed | tf_op | source)
XLA Modules:
  0.0 42.2 jit_solution(1157162951587348651)
XLA Ops:
  0.0 1.4 %dispatch.1 = (bf16[9,56,128]{2,1,0:T(8,128)(2,1)S(1)}, bf16[5,56,128]{2,1,0:T(8,128)(2,1)S(1)}, bf16[5,56,128]{2,1,0:T(8,128)(2,1)S(1)}, bf16[5,56,128]{2,1,0:T...) custom-call(s32[2,8]{1,0:T(2,128)} %bitcast.11, s32[4]{0:T(128)} %place_in.1, f32[2,8]{1,0:T(2,128)} %bitcast.12, ...), custom_call_target="tpu_custom_call" | custom-call | tf_op jit(solution)/shard_map/dispatch/pallas_call | solution.py:255
  1.4 3.0 %collective-permute-start.6 = (bf16[9,56,128]{2,1,0:T(8,128)(2,1)S(1)}, bf16[9,56,128]{2,1,0:T(8,128)(2,1)S(1)}, u32[]{:S(2)}, u32[]{:S(2)}) collective-permute-start(bf16[9,56,128]{2,1,0:T(8,128)(2,1)S(1)} %get-tuple-element.40.refs_0_), channel_id=1, source_target_pairs={{0,2},{2,0},{1,3},{3,1},{4,6},{6,4},{5,7},{7,5},{8,10},{10,8},{9,1... | collective-permute-start | bytes 387080 | tf_op jit(solution)/shard_map/ppermute | solution.py:243
  4.4 3.6 %collective-permute-start = (bf16[5,56,128]{2,1,0:T(8,128)(2,1)S(1)}, bf16[5,56,128]{2,1,0:T(8,128)(2,1)S(1)}, u32[]{:S(2)}, u32[]{:S(2)}) collective-permute-start(bf16[5,56,128]{2,1,0:T(8,128)(2,1)S(1)} %get-tuple-element.34), channel_id=1, source_target_pairs={{0,12},{4,8},{8,4},{12,0},{1,13},{5,9},{9,5},{13,1},{2,14},{6,10},... | collective-permute-start | bytes 215048 | tf_op jit(solution)/shard_map/ppermute | solution.py:243
  8.0 0.5 %collective-permute-start.3 = (bf16[5,56,128]{2,1,0:T(8,128)(2,1)S(1)}, bf16[5,56,128]{2,1,0:T(8,128)(2,1)S(1)}, u32[]{:S(2)}, u32[]{:S(2)}) collective-permute-start(bf16[5,56,128]{2,1,0:T(8,128)(2,1)S(1)} %get-tuple-element.36), channel_id=1, source_target_pairs={{0,6},{2,4},{4,2},{6,0},{8,14},{10,12},{12,10},{14,8},{1,7},{3,5},... | collective-permute-start | bytes 215048 | tf_op jit(solution)/shard_map/ppermute | solution.py:243
  8.5 1.5 %collective-permute-start.2 = (bf16[5,56,128]{2,1,0:T(8,128)(2,1)S(1)}, bf16[5,56,128]{2,1,0:T(8,128)(2,1)S(1)}, u32[]{:S(2)}, u32[]{:S(2)}) collective-permute-start(bf16[5,56,128]{2,1,0:T(8,128)(2,1)S(1)} %get-tuple-element.36), channel_id=1, source_target_pairs={{0,4},{2,6},{4,0},{6,2},{8,12},{10,14},{12,8},{14,10},{1,5},{3,7},... | collective-permute-start | bytes 215048 | tf_op jit(solution)/shard_map/ppermute | solution.py:243
  10.1 1.3 %collective-permute-done.refs_0_ = bf16[5,56,128]{2,1,0:T(8,128)(2,1)S(1)} collective-permute-done((bf16[5,56,128]{2,1,0:T(8,128)(2,1)S(1)}, bf16[5,56,128]{2,1,0:T(8,128)(2,1)S(1)}, u32[]{:S(2)}, u32[]{:S(2)}) %collective-permute-start) | collective-permute-done | bytes 71712 | tf_op jit(solution)/shard_map/ppermute | solution.py:243
  11.4 2.4 %collective-permute-done.1.refs_1_ = bf16[5,56,128]{2,1,0:T(8,128)(2,1)S(1)} collective-permute-done((bf16[5,56,128]{2,1,0:T(8,128)(2,1)S(1)}, bf16[5,56,128]{2,1,0:T(8,128)(2,1)S(1)}, u32[]{:S(2)}, u32[]{:S(2)}) %collective-permute-start.1) | collective-permute-done | bytes 71712 | tf_op jit(solution)/shard_map/ppermute | solution.py:243
  13.8 0.9 %collective-permute-done.3.refs_5_ = bf16[5,56,128]{2,1,0:T(8,128)(2,1)S(1)} collective-permute-done((bf16[5,56,128]{2,1,0:T(8,128)(2,1)S(1)}, bf16[5,56,128]{2,1,0:T(8,128)(2,1)S(1)}, u32[]{:S(2)}, u32[]{:S(2)}) %collective-permute-start.3) | collective-permute-done | bytes 71712 | tf_op jit(solution)/shard_map/ppermute | solution.py:243
  14.7 0.6 %collective-permute-done.2.refs_2_ = bf16[5,56,128]{2,1,0:T(8,128)(2,1)S(1)} collective-permute-done((bf16[5,56,128]{2,1,0:T(8,128)(2,1)S(1)}, bf16[5,56,128]{2,1,0:T(8,128)(2,1)S(1)}, u32[]{:S(2)}, u32[]{:S(2)}) %collective-permute-start.2) | collective-permute-done | bytes 71712 | tf_op jit(solution)/shard_map/ppermute | solution.py:243
  15.3 0.5 %collective-permute-start.8 = (bf16[9,56,128]{2,1,0:T(8,128)(2,1)S(1)}, bf16[9,56,128]{2,1,0:T(8,128)(2,1)S(1)}, u32[]{:S(2)}, u32[]{:S(2)}) collective-permute-start(bf16[9,56,128]{2,1,0:T(8,128)(2,1)S(1)} %collective-permute-done.6.refs_1_), channel_id=1, source_target_pairs={{0,1},{1,0},{2,3},{3,2},{4,5},{5,4},{6,7},{7,6},{8,9},{9,8},{10,11... | collective-permute-start | bytes 387080 | tf_op jit(solution)/shard_map/ppermute | solution.py:243
  15.8 0.8 %collective-permute-start.4 = (bf16[5,56,128]{2,1,0:T(8,128)(2,1)S(1)}, bf16[5,56,128]{2,1,0:T(8,128)(2,1)S(1)}, u32[]{:S(2)}, u32[]{:S(2)}) collective-permute-start(bf16[5,56,128]{2,1,0:T(8,128)(2,1)S(1)} %collective-permute-done.refs_0_), channel_id=1, source_target_pairs={{0,2},{2,0},{1,3},{3,1},{4,6},{6,4},{5,7},{7,5},{8,10},{10,8},{9,1... | collective-permute-start | bytes 215048 | tf_op jit(solution)/shard_map/ppermute | solution.py:243
  16.5 1.3 %collective-permute-start.5 = (bf16[5,56,128]{2,1,0:T(8,128)(2,1)S(1)}, bf16[5,56,128]{2,1,0:T(8,128)(2,1)S(1)}, u32[]{:S(2)}, u32[]{:S(2)}) collective-permute-start(bf16[5,56,128]{2,1,0:T(8,128)(2,1)S(1)} %collective-permute-done.1.refs_1_), channel_id=1, source_target_pairs={{0,2},{2,0},{1,3},{3,1},{4,6},{6,4},{5,7},{7,5},{8,10},{10,8},{9,1... | collective-permute-start | bytes 215048 | tf_op jit(solution)/shard_map/ppermute | solution.py:243
  17.8 0.5 %collective-permute-start.9 = (bf16[5,56,128]{2,1,0:T(8,128)(2,1)S(1)}, bf16[5,56,128]{2,1,0:T(8,128)(2,1)S(1)}, u32[]{:S(2)}, u32[]{:S(2)}) collective-permute-start(bf16[5,56,128]{2,1,0:T(8,128)(2,1)S(1)} %collective-permute-done.refs_0_), channel_id=1, source_target_pairs={{0,1},{1,0},{2,3},{3,2},{4,5},{5,4},{6,7},{7,6},{8,9},{9,8},{10,11... | collective-permute-start | bytes 215048 | tf_op jit(solution)/shard_map/ppermute | solution.py:243
  18.4 2.0 %near_shared.1 = (bf16[32,7168]{1,0:T(8,128)(2,1)S(1)}, f32[32,128]{1,0:T(8,128)S(1)}, f32[32,7168]{1,0:T(8,128)S(1)}) custom-call(bf16[9,56,128]{2,1,0:T(8,128)(2,1)S(1)} %get-tuple-element.40.refs_0_, bf16[9,56,128]{2,1,0:T(8,128)(2,1)S(1)} %collective-permute-done.6.refs_1_, bf16[9,56,128]{2,1,0:T(8,128)(2,1)S(1)} %collective-permute-done.7.refs_2_, ...), custom_call_target="tpu_custom_call" | custom-call | flops 352321536 | bytes 11010048 | tf_op jit(solution)/shard_map/near_shared/pallas_call | solution.py:255
  21.0 0.5 %collective-permute-done.5.refs_4_ = bf16[5,56,128]{2,1,0:T(8,128)(2,1)S(1)} collective-permute-done((bf16[5,56,128]{2,1,0:T(8,128)(2,1)S(1)}, bf16[5,56,128]{2,1,0:T(8,128)(2,1)S(1)}, u32[]{:S(2)}, u32[]{:S(2)}) %collective-permute-start.5) | collective-permute-done | bytes 71712 | tf_op jit(solution)/shard_map/ppermute | solution.py:243
  21.4 0.5 %collective-permute-start.13 = (bf16[5,56,128]{2,1,0:T(8,128)(2,1)S(1)}, bf16[5,56,128]{2,1,0:T(8,128)(2,1)S(1)}, u32[]{:S(2)}, u32[]{:S(2)}) collective-permute-start(bf16[5,56,128]{2,1,0:T(8,128)(2,1)S(1)} %collective-permute-done.5.refs_4_), channel_id=1, source_target_pairs={{0,1},{1,0},{2,3},{3,2},{4,5},{5,4},{6,7},{7,6},{8,9},{9,8},{10,11... | collective-permute-start | bytes 215048 | tf_op jit(solution)/shard_map/ppermute | solution.py:243
  22.0 0.7 %collective-permute-done.12.refs_9_ = bf16[5,56,128]{2,1,0:T(8,128)(2,1)S(1)} collective-permute-done((bf16[5,56,128]{2,1,0:T(8,128)(2,1)S(1)}, bf16[5,56,128]{2,1,0:T(8,128)(2,1)S(1)}, u32[]{:S(2)}, u32[]{:S(2)}) %collective-permute-start.12) | collective-permute-done | bytes 71712 | tf_op jit(solution)/shard_map/ppermute | solution.py:243
  22.9 2.3 %routed.1 = (bf16[2,5,56,128]{3,2,1,0:T(8,128)(2,1)S(1)}, bf16[2,5,56,128]{3,2,1,0:T(8,128)(2,1)S(1)}, bf16[2,18,56,128]{3,2,1,0:T(8,128)(2,1)S(1)}, bf16[2,18,56,128]{3,2,1,0:T(8,128)(2,1)S(1)}) custom-call(bf16[5,56,128]{2,1,0:T(8,128)(2,1)S(1)} %collective-permute-done.refs_0_, bf16[5,56,128]{2,1,0:T(8,128)(2,1)S(1)} %collective-permute-done.1.refs_1_, ...), custom_call_target="tpu_custom_call" | custom-call | flops 1012924416 | bytes 11010048 | tf_op jit(solution)/shard_map/routed/pallas_call | solution.py:255
  25.2 0.4 %collective-permute-start.18 = (bf16[2,18,56,128]{3,2,1,0:T(8,128)(2,1)S(1)}, bf16[2,18,56,128]{3,2,1,0:T(8,128)(2,1)S(1)}, u32[]{:S(2)}, u32[]{:S(2)}) collective-permute-start(bf16[2,18,56,128]{3,2,1,0:T(8,128)(2,1)S(1)} %get-tuple-element.52), channel_id=1, source_target_pairs={{0,1},{1,0},{2,3},{3,2},{4,5},{5,4},{6,7},{7,6},{8,9},{9,8},{10,11... | collective-permute-start | bytes 1548296 | tf_op jit(solution)/shard_map/ppermute | solution.py:243
  25.8 1.6 %collective-permute-done.15.refs_1_ = bf16[2,5,56,128]{3,2,1,0:T(8,128)(2,1)S(1)} collective-permute-done((bf16[2,5,56,128]{3,2,1,0:T(8,128)(2,1)S(1)}, bf16[2,5,56,128]{3,2,1,0:T(8,128)(2,1)S(1)}, u32[]{:S(2)}, u32[]{:S(2)}) %collective-permute-start.15) | collective-permute-done | bytes 143392 | tf_op jit(solution)/shard_map/ppermute | solution.py:243
  27.4 1.0 %collective-permute-start.16 = (bf16[5,56,128]{2,1,0:T(8,128)(2,1)S(1)}, bf16[5,56,128]{2,1,0:T(8,128)(2,1)S(1)}, u32[]{:S(2)}, u32[]{:S(2)}) collective-permute-start(bf16[5,56,128]{2,1,0:T(8,128)(2,1)S(1)} %get-tuple-element.50), channel_id=1, source_target_pairs={{0,2},{2,0},{1,3},{3,1},{4,6},{6,4},{5,7},{7,5},{8,10},{10,8},{9,1... | collective-permute-start | bytes 215048 | tf_op jit(solution)/shard_map/ppermute | solution.py:243
  28.6 1.1 %collective-permute-start.19 = (bf16[5,56,128]{2,1,0:T(8,128)(2,1)S(1)}, bf16[5,56,128]{2,1,0:T(8,128)(2,1)S(1)}, u32[]{:S(2)}, u32[]{:S(2)}) collective-permute-start(bf16[5,56,128]{2,1,0:T(8,128)(2,1)S(1)} %get-tuple-element.54), channel_id=1, source_target_pairs={{0,2},{2,0},{1,3},{3,1},{4,6},{6,4},{5,7},{7,5},{8,10},{10,8},{9,1... | collective-permute-start | bytes 215048 | tf_op jit(solution)/shard_map/ppermute | solution.py:243
  29.7 1.0 %collective-permute-start.21 = (bf16[5,56,128]{2,1,0:T(8,128)(2,1)S(1)}, bf16[5,56,128]{2,1,0:T(8,128)(2,1)S(1)}, u32[]{:S(2)}, u32[]{:S(2)}) collective-permute-start(bf16[5,56,128]{2,1,0:T(8,128)(2,1)S(1)} %get-tuple-element.56), channel_id=1, source_target_pairs={{0,2},{2,0},{1,3},{3,1},{4,6},{6,4},{5,7},{7,5},{8,10},{10,8},{9,1... | collective-permute-start | bytes 215048 | tf_op jit(solution)/shard_map/ppermute | solution.py:243
  30.7 1.1 %collective-permute-start.23 = (bf16[8,56,128]{2,1,0:T(8,128)(2,1)S(1)}, bf16[8,56,128]{2,1,0:T(8,128)(2,1)S(1)}, u32[]{:S(2)}, u32[]{:S(2)}) collective-permute-start(bf16[8,56,128]{2,1,0:T(8,128)(2,1)S(1)} %get-tuple-element.58), channel_id=1, source_target_pairs={{0,2},{2,0},{1,3},{3,1},{4,6},{6,4},{5,7},{7,5},{8,10},{10,8},{9,1... | collective-permute-start | bytes 344072 | tf_op jit(solution)/shard_map/ppermute | solution.py:243
  31.7 0.8 %collective-permute-done.16.refs_1_ = bf16[5,56,128]{2,1,0:T(8,128)(2,1)S(1)} collective-permute-done((bf16[5,56,128]{2,1,0:T(8,128)(2,1)S(1)}, bf16[5,56,128]{2,1,0:T(8,128)(2,1)S(1)}, u32[]{:S(2)}, u32[]{:S(2)}) %collective-permute-start.16) | collective-permute-done | bytes 71712 | tf_op jit(solution)/shard_map/ppermute | solution.py:243
  32.6 2.3 %collective-permute-start.17 = (bf16[5,56,128]{2,1,0:T(8,128)(2,1)S(1)}, bf16[5,56,128]{2,1,0:T(8,128)(2,1)S(1)}, u32[]{:S(2)}, u32[]{:S(2)}) collective-permute-start(bf16[5,56,128]{2,1,0:T(8,128)(2,1)S(1)} %narrow_sum.3), channel_id=1, source_target_pairs={{0,12},{4,8},{8,4},{12,0},{1,13},{5,9},{9,5},{13,1},{2,14},{6,10},... | collective-permute-start | bytes 215048 | tf_op jit(solution)/shard_map/ppermute | solution.py:243
  34.9 0.3 collective-permute-start.20
  35.2 0.4 collective-permute-done.21.refs_1_
  35.6 1.6 %collective-permute-start.22 = (bf16[5,56,128]{2,1,0:T(8,128)(2,1)S(1)}, bf16[5,56,128]{2,1,0:T(8,128)(2,1)S(1)}, u32[]{:S(2)}, u32[]{:S(2)}) collective-permute-start(bf16[5,56,128]{2,1,0:T(8,128)(2,1)S(1)} %narrow_sum.5), channel_id=1, source_target_pairs={{0,4},{4,0},{8,12},{12,8},{1,5},{5,1},{9,13},{13,9},{2,6},{6,2},{1... | collective-permute-start | bytes 215048 | tf_op jit(solution)/shard_map/ppermute | solution.py:243
  37.2 1.9 %collective-permute-done.17.refs_0_ = bf16[5,56,128]{2,1,0:T(8,128)(2,1)S(1)} collective-permute-done((bf16[5,56,128]{2,1,0:T(8,128)(2,1)S(1)}, bf16[5,56,128]{2,1,0:T(8,128)(2,1)S(1)}, u32[]{:S(2)}, u32[]{:S(2)}) %collective-permute-start.17) | collective-permute-done | bytes 71712 | tf_op jit(solution)/shard_map/ppermute | solution.py:243
  39.1 2.2 %collective-permute-done.20.refs_1_ = bf16[5,56,128]{2,1,0:T(8,128)(2,1)S(1)} collective-permute-done((bf16[5,56,128]{2,1,0:T(8,128)(2,1)S(1)}, bf16[5,56,128]{2,1,0:T(8,128)(2,1)S(1)}, u32[]{:S(2)}, u32[]{:S(2)}) %collective-permute-start.20) | collective-permute-done | bytes 71712 | tf_op jit(solution)/shard_map/ppermute | solution.py:243
  41.4 0.7 %combine.1 = bf16[8,7168]{1,0:T(8,128)(2,1)} custom-call(f32[8,56,128]{2,1,0:T(8,128)S(1)} %far_combine.1.far, bf16[8,56,128]{2,1,0:T(8,128)(2,1)S(1)} %get-tuple-element.57.refs_0_, bf16[8,56,128]{2,1,0:T(8,128)(2,1)S(1)} %collective-permute-done.23.refs_1_), custom_call_target="tpu_custom_call" | custom-call | tf_op jit(solution)/shard_map/combine/pallas_call | solution.py:255
  (38 shorter events, 1.2 us)
Async XLA Ops:
  0.0 18.4 %copy-start = (bf16[7168,256]{1,0:T(8,128)(2,1)S(1)}, bf16[7168,256]{1,0:T(8,128)(2,1)}, u32[]{:S(2)}) copy-start(bf16[7168,256]{1,0:T(8,128)(2,1)} %refs_4_.1) | copy-start | bytes 11010052
  0.0 18.4 %copy-start.1 = (bf16[7168,256]{1,0:T(8,128)(2,1)S(1)}, bf16[7168,256]{1,0:T(8,128)(2,1)}, u32[]{:S(2)}) copy-start(bf16[7168,256]{1,0:T(8,128)(2,1)} %refs_5_.1) | copy-start | bytes 11010052
  0.0 18.4 %copy-start.2 = (bf16[256,7168]{1,0:T(8,128)(2,1)S(1)}, bf16[256,7168]{1,0:T(8,128)(2,1)}, u32[]{:S(2)}) copy-start(bf16[256,7168]{1,0:T(8,128)(2,1)} %refs_6_.1) | copy-start | bytes 11010052
  1.4 13.9 %collective-permute-start.6 = (bf16[9,56,128]{2,1,0:T(8,128)(2,1)S(1)}, bf16[9,56,128]{2,1,0:T(8,128)(2,1)S(1)}, u32[]{:S(2)}, u32[]{:S(2)}) collective-permute-start(bf16[9,56,128]{2,1,0:T(8,128)(2,1)S(1)} %get-tuple-element.40.refs_0_), channel_id=1, source_target_pairs={{0,2},{2,0},{1,3},{3,1},{4,6},{6,4},{5,7},{7,5},{8,10},{10,8},{9,1... | collective-permute-start | bytes 387080 | tf_op jit(solution)/shard_map/ppermute | solution.py:243
  4.4 7.0 %collective-permute-start = (bf16[5,56,128]{2,1,0:T(8,128)(2,1)S(1)}, bf16[5,56,128]{2,1,0:T(8,128)(2,1)S(1)}, u32[]{:S(2)}, u32[]{:S(2)}) collective-permute-start(bf16[5,56,128]{2,1,0:T(8,128)(2,1)S(1)} %get-tuple-element.34), channel_id=1, source_target_pairs={{0,12},{4,8},{8,4},{12,0},{1,13},{5,9},{9,5},{13,1},{2,14},{6,10},... | collective-permute-start | bytes 215048 | tf_op jit(solution)/shard_map/ppermute | solution.py:243
  8.0 5.8 %collective-permute-start.1 = (bf16[5,56,128]{2,1,0:T(8,128)(2,1)S(1)}, bf16[5,56,128]{2,1,0:T(8,128)(2,1)S(1)}, u32[]{:S(2)}, u32[]{:S(2)}) collective-permute-start(bf16[5,56,128]{2,1,0:T(8,128)(2,1)S(1)} %get-tuple-element.35), channel_id=1, source_target_pairs={{0,8},{4,12},{8,0},{12,4},{1,9},{5,13},{9,1},{13,5},{2,10},{6,14},... | collective-permute-start | bytes 215048 | tf_op jit(solution)/shard_map/ppermute | solution.py:243
  8.0 14.9 %copy-start.3 = (bf16[1,7168,256]{2,1,0:T(8,128)(2,1)S(1)}, bf16[1,7168,256]{2,1,0:T(8,128)(2,1)}, u32[]{:S(2)}) copy-start(bf16[1,7168,256]{2,1,0:T(8,128)(2,1)} %param.16) | copy-start | bytes 11010052
  8.0 14.9 %copy-start.4 = (bf16[1,7168,256]{2,1,0:T(8,128)(2,1)S(1)}, bf16[1,7168,256]{2,1,0:T(8,128)(2,1)}, u32[]{:S(2)}) copy-start(bf16[1,7168,256]{2,1,0:T(8,128)(2,1)} %param.17) | copy-start | bytes 11010052
  8.0 14.9 %copy-start.5 = (bf16[1,256,7168]{2,1,0:T(8,128)(2,1)S(1)}, bf16[1,256,7168]{2,1,0:T(8,128)(2,1)}, u32[]{:S(2)}) copy-start(bf16[1,256,7168]{2,1,0:T(8,128)(2,1)} %param.18) | copy-start | bytes 11010052
  8.0 6.7 %collective-permute-start.3 = (bf16[5,56,128]{2,1,0:T(8,128)(2,1)S(1)}, bf16[5,56,128]{2,1,0:T(8,128)(2,1)S(1)}, u32[]{:S(2)}, u32[]{:S(2)}) collective-permute-start(bf16[5,56,128]{2,1,0:T(8,128)(2,1)S(1)} %get-tuple-element.36), channel_id=1, source_target_pairs={{0,6},{2,4},{4,2},{6,0},{8,14},{10,12},{12,10},{14,8},{1,7},{3,5},... | collective-permute-start | bytes 215048 | tf_op jit(solution)/shard_map/ppermute | solution.py:243
  8.5 6.7 %collective-permute-start.2 = (bf16[5,56,128]{2,1,0:T(8,128)(2,1)S(1)}, bf16[5,56,128]{2,1,0:T(8,128)(2,1)S(1)}, u32[]{:S(2)}, u32[]{:S(2)}) collective-permute-start(bf16[5,56,128]{2,1,0:T(8,128)(2,1)S(1)} %get-tuple-element.36), channel_id=1, source_target_pairs={{0,4},{2,6},{4,0},{6,2},{8,12},{10,14},{12,8},{14,10},{1,5},{3,7},... | collective-permute-start | bytes 215048 | tf_op jit(solution)/shard_map/ppermute | solution.py:243
  15.3 2.5 %collective-permute-start.7 = (bf16[9,56,128]{2,1,0:T(8,128)(2,1)S(1)}, bf16[9,56,128]{2,1,0:T(8,128)(2,1)S(1)}, u32[]{:S(2)}, u32[]{:S(2)}) collective-permute-start(bf16[9,56,128]{2,1,0:T(8,128)(2,1)S(1)} %get-tuple-element.40.refs_0_), channel_id=1, source_target_pairs={{0,1},{1,0},{2,3},{3,2},{4,5},{5,4},{6,7},{7,6},{8,9},{9,8},{10,11... | collective-permute-start | bytes 387080 | tf_op jit(solution)/shard_map/ppermute | solution.py:243
  15.3 3.1 %collective-permute-start.8 = (bf16[9,56,128]{2,1,0:T(8,128)(2,1)S(1)}, bf16[9,56,128]{2,1,0:T(8,128)(2,1)S(1)}, u32[]{:S(2)}, u32[]{:S(2)}) collective-permute-start(bf16[9,56,128]{2,1,0:T(8,128)(2,1)S(1)} %collective-permute-done.6.refs_1_), channel_id=1, source_target_pairs={{0,1},{1,0},{2,3},{3,2},{4,5},{5,4},{6,7},{7,6},{8,9},{9,8},{10,11... | collective-permute-start | bytes 387080 | tf_op jit(solution)/shard_map/ppermute | solution.py:243
  15.8 4.9 %collective-permute-start.4 = (bf16[5,56,128]{2,1,0:T(8,128)(2,1)S(1)}, bf16[5,56,128]{2,1,0:T(8,128)(2,1)S(1)}, u32[]{:S(2)}, u32[]{:S(2)}) collective-permute-start(bf16[5,56,128]{2,1,0:T(8,128)(2,1)S(1)} %collective-permute-done.refs_0_), channel_id=1, source_target_pairs={{0,2},{2,0},{1,3},{3,1},{4,6},{6,4},{5,7},{7,5},{8,10},{10,8},{9,1... | collective-permute-start | bytes 215048 | tf_op jit(solution)/shard_map/ppermute | solution.py:243
  16.5 4.9 %collective-permute-start.5 = (bf16[5,56,128]{2,1,0:T(8,128)(2,1)S(1)}, bf16[5,56,128]{2,1,0:T(8,128)(2,1)S(1)}, u32[]{:S(2)}, u32[]{:S(2)}) collective-permute-start(bf16[5,56,128]{2,1,0:T(8,128)(2,1)S(1)} %collective-permute-done.1.refs_1_), channel_id=1, source_target_pairs={{0,2},{2,0},{1,3},{3,1},{4,6},{6,4},{5,7},{7,5},{8,10},{10,8},{9,1... | collective-permute-start | bytes 215048 | tf_op jit(solution)/shard_map/ppermute | solution.py:243
  17.8 3.6 %collective-permute-start.14 = (bf16[5,56,128]{2,1,0:T(8,128)(2,1)S(1)}, bf16[5,56,128]{2,1,0:T(8,128)(2,1)S(1)}, u32[]{:S(2)}, u32[]{:S(2)}) collective-permute-start(bf16[5,56,128]{2,1,0:T(8,128)(2,1)S(1)} %collective-permute-done.3.refs_5_), channel_id=1, source_target_pairs={{0,1},{1,0},{2,3},{3,2},{4,5},{5,4},{6,7},{7,6},{8,9},{9,8},{10,11... | collective-permute-start | bytes 215048 | tf_op jit(solution)/shard_map/ppermute | solution.py:243
  17.8 4.2 %collective-permute-start.9 = (bf16[5,56,128]{2,1,0:T(8,128)(2,1)S(1)}, bf16[5,56,128]{2,1,0:T(8,128)(2,1)S(1)}, u32[]{:S(2)}, u32[]{:S(2)}) collective-permute-start(bf16[5,56,128]{2,1,0:T(8,128)(2,1)S(1)} %collective-permute-done.refs_0_), channel_id=1, source_target_pairs={{0,1},{1,0},{2,3},{3,2},{4,5},{5,4},{6,7},{7,6},{8,9},{9,8},{10,11... | collective-permute-start | bytes 215048 | tf_op jit(solution)/shard_map/ppermute | solution.py:243
  18.3 3.6 %collective-permute-start.10 = (bf16[5,56,128]{2,1,0:T(8,128)(2,1)S(1)}, bf16[5,56,128]{2,1,0:T(8,128)(2,1)S(1)}, u32[]{:S(2)}, u32[]{:S(2)}) collective-permute-start(bf16[5,56,128]{2,1,0:T(8,128)(2,1)S(1)} %collective-permute-done.1.refs_1_), channel_id=1, source_target_pairs={{0,1},{1,0},{2,3},{3,2},{4,5},{5,4},{6,7},{7,6},{8,9},{9,8},{10,11... | collective-permute-start | bytes 215048 | tf_op jit(solution)/shard_map/ppermute | solution.py:243
  20.7 1.3 %collective-permute-start.11 = (bf16[5,56,128]{2,1,0:T(8,128)(2,1)S(1)}, bf16[5,56,128]{2,1,0:T(8,128)(2,1)S(1)}, u32[]{:S(2)}, u32[]{:S(2)}) collective-permute-start(bf16[5,56,128]{2,1,0:T(8,128)(2,1)S(1)} %collective-permute-done.2.refs_2_), channel_id=1, source_target_pairs={{0,1},{1,0},{2,3},{3,2},{4,5},{5,4},{6,7},{7,6},{8,9},{9,8},{10,11... | collective-permute-start | bytes 215048 | tf_op jit(solution)/shard_map/ppermute | solution.py:243
  21.4 1.3 %collective-permute-start.12 = (bf16[5,56,128]{2,1,0:T(8,128)(2,1)S(1)}, bf16[5,56,128]{2,1,0:T(8,128)(2,1)S(1)}, u32[]{:S(2)}, u32[]{:S(2)}) collective-permute-start(bf16[5,56,128]{2,1,0:T(8,128)(2,1)S(1)} %collective-permute-done.4.refs_3_), channel_id=1, source_target_pairs={{0,1},{1,0},{2,3},{3,2},{4,5},{5,4},{6,7},{7,6},{8,9},{9,8},{10,11... | collective-permute-start | bytes 215048 | tf_op jit(solution)/shard_map/ppermute | solution.py:243
  21.4 1.4 %collective-permute-start.13 = (bf16[5,56,128]{2,1,0:T(8,128)(2,1)S(1)}, bf16[5,56,128]{2,1,0:T(8,128)(2,1)S(1)}, u32[]{:S(2)}, u32[]{:S(2)}) collective-permute-start(bf16[5,56,128]{2,1,0:T(8,128)(2,1)S(1)} %collective-permute-done.5.refs_4_), channel_id=1, source_target_pairs={{0,1},{1,0},{2,3},{3,2},{4,5},{5,4},{6,7},{7,6},{8,9},{9,8},{10,11... | collective-permute-start | bytes 215048 | tf_op jit(solution)/shard_map/ppermute | solution.py:243
  25.2 3.3 %collective-permute-start.18 = (bf16[2,18,56,128]{3,2,1,0:T(8,128)(2,1)S(1)}, bf16[2,18,56,128]{3,2,1,0:T(8,128)(2,1)S(1)}, u32[]{:S(2)}, u32[]{:S(2)}) collective-permute-start(bf16[2,18,56,128]{3,2,1,0:T(8,128)(2,1)S(1)} %get-tuple-element.52), channel_id=1, source_target_pairs={{0,1},{1,0},{2,3},{3,2},{4,5},{5,4},{6,7},{7,6},{8,9},{9,8},{10,11... | collective-permute-start | bytes 1548296 | tf_op jit(solution)/shard_map/ppermute | solution.py:243
  25.6 1.7 %collective-permute-start.15 = (bf16[2,5,56,128]{3,2,1,0:T(8,128)(2,1)S(1)}, bf16[2,5,56,128]{3,2,1,0:T(8,128)(2,1)S(1)}, u32[]{:S(2)}, u32[]{:S(2)}) collective-permute-start(bf16[2,5,56,128]{3,2,1,0:T(8,128)(2,1)S(1)} %get-tuple-element.48), channel_id=1, source_target_pairs={{0,1},{1,0},{2,3},{3,2},{4,5},{5,4},{6,7},{7,6},{8,9},{9,8},{10,11... | collective-permute-start | bytes 430088 | tf_op jit(solution)/shard_map/ppermute | solution.py:243
  27.4 5.1 %collective-permute-start.16 = (bf16[5,56,128]{2,1,0:T(8,128)(2,1)S(1)}, bf16[5,56,128]{2,1,0:T(8,128)(2,1)S(1)}, u32[]{:S(2)}, u32[]{:S(2)}) collective-permute-start(bf16[5,56,128]{2,1,0:T(8,128)(2,1)S(1)} %get-tuple-element.50), channel_id=1, source_target_pairs={{0,2},{2,0},{1,3},{3,1},{4,6},{6,4},{5,7},{7,5},{8,10},{10,8},{9,1... | collective-permute-start | bytes 215048 | tf_op jit(solution)/shard_map/ppermute | solution.py:243
  28.6 6.3 %collective-permute-start.19 = (bf16[5,56,128]{2,1,0:T(8,128)(2,1)S(1)}, bf16[5,56,128]{2,1,0:T(8,128)(2,1)S(1)}, u32[]{:S(2)}, u32[]{:S(2)}) collective-permute-start(bf16[5,56,128]{2,1,0:T(8,128)(2,1)S(1)} %get-tuple-element.54), channel_id=1, source_target_pairs={{0,2},{2,0},{1,3},{3,1},{4,6},{6,4},{5,7},{7,5},{8,10},{10,8},{9,1... | collective-permute-start | bytes 215048 | tf_op jit(solution)/shard_map/ppermute | solution.py:243
  29.7 5.9 %collective-permute-start.21 = (bf16[5,56,128]{2,1,0:T(8,128)(2,1)S(1)}, bf16[5,56,128]{2,1,0:T(8,128)(2,1)S(1)}, u32[]{:S(2)}, u32[]{:S(2)}) collective-permute-start(bf16[5,56,128]{2,1,0:T(8,128)(2,1)S(1)} %get-tuple-element.56), channel_id=1, source_target_pairs={{0,2},{2,0},{1,3},{3,1},{4,6},{6,4},{5,7},{7,5},{8,10},{10,8},{9,1... | collective-permute-start | bytes 215048 | tf_op jit(solution)/shard_map/ppermute | solution.py:243
  30.7 10.8 %collective-permute-start.23 = (bf16[8,56,128]{2,1,0:T(8,128)(2,1)S(1)}, bf16[8,56,128]{2,1,0:T(8,128)(2,1)S(1)}, u32[]{:S(2)}, u32[]{:S(2)}) collective-permute-start(bf16[8,56,128]{2,1,0:T(8,128)(2,1)S(1)} %get-tuple-element.58), channel_id=1, source_target_pairs={{0,2},{2,0},{1,3},{3,1},{4,6},{6,4},{5,7},{7,5},{8,10},{10,8},{9,1... | collective-permute-start | bytes 344072 | tf_op jit(solution)/shard_map/ppermute | solution.py:243
  32.6 6.6 %collective-permute-start.17 = (bf16[5,56,128]{2,1,0:T(8,128)(2,1)S(1)}, bf16[5,56,128]{2,1,0:T(8,128)(2,1)S(1)}, u32[]{:S(2)}, u32[]{:S(2)}) collective-permute-start(bf16[5,56,128]{2,1,0:T(8,128)(2,1)S(1)} %narrow_sum.3), channel_id=1, source_target_pairs={{0,12},{4,8},{8,4},{12,0},{1,13},{5,9},{9,5},{13,1},{2,14},{6,10},... | collective-permute-start | bytes 215048 | tf_op jit(solution)/shard_map/ppermute | solution.py:243
  34.9 6.4 %collective-permute-start.20 = (bf16[5,56,128]{2,1,0:T(8,128)(2,1)S(1)}, bf16[5,56,128]{2,1,0:T(8,128)(2,1)S(1)}, u32[]{:S(2)}, u32[]{:S(2)}) collective-permute-start(bf16[5,56,128]{2,1,0:T(8,128)(2,1)S(1)} %narrow_sum.4), channel_id=1, source_target_pairs={{0,8},{4,12},{8,0},{12,4},{1,9},{5,13},{9,1},{13,5},{2,10},{6,14},... | collective-permute-start | bytes 215048 | tf_op jit(solution)/shard_map/ppermute | solution.py:243
  35.6 5.7 %collective-permute-start.22 = (bf16[5,56,128]{2,1,0:T(8,128)(2,1)S(1)}, bf16[5,56,128]{2,1,0:T(8,128)(2,1)S(1)}, u32[]{:S(2)}, u32[]{:S(2)}) collective-permute-start(bf16[5,56,128]{2,1,0:T(8,128)(2,1)S(1)} %narrow_sum.5), channel_id=1, source_target_pairs={{0,4},{4,0},{8,12},{12,8},{1,5},{5,1},{9,13},{13,9},{2,6},{6,2},{1... | collective-permute-start | bytes 215048 | tf_op jit(solution)/shard_map/ppermute | solution.py:243

commit v13 on v12

--- a/solution.py
+++ b/solution.py
@@ -393,7 +393,8 @@
         return [parts[0]] + [swap(parts[j], "narrow", j) for j in range(1, n_narrow)]
 
     reduced = reduce_pair(outs[:n_pair], slots[:1])
-    reduced += reduce_pair(outs[n_pair:], slots[1:] + [tokens])
+    later = list(outs[n_pair : n_pair + 1]) + after(outs[n_pair + 1 :], reduced[0][0])
+    reduced += reduce_pair(later, slots[1:] + [tokens])
     sums = []
     for k in range(per):
         sums += call(

time: 42.3 us -> 42.1 us (level)
  waiting for transfers between devices: 13.7 us -> 13.1 us
  starting transfers between devices: 21.6 us -> 22.1 us
    ppermute x24, waiting for transfers between devices: 13.7 us -> 13.1 us  [swap(): return lax.ppermute(value, axis, [(i, i ^ offset) for i in range(size)])]
    ppermute x24, starting transfers between devices: 21.6 us -> 22.1 us  [swap(): return lax.ppermute(value, axis, [(i, i ^ offset) for i in range(size)])]
  transfers between devices with their start and end apart: 24 -> 24, of which waited for: 13 -> 13; matrix products, arithmetic and copies ran while one was open for 0% -> 0% of each run, Pallas kernels for 6% -> 5%
where the time goes in v13:
time: 42.1 us; the launch traced here: 42 us
  starting transfers between devices  22.1 us (52%)
  waiting for transfers between devices  13.1 us (31%)
  Pallas kernels  6.73 us (16%)
    ppermute x24, starting transfers between devices, swap(): return lax.ppermute(value, axis, [(i, i ^ offset) for i in range(size)])  22.1 us
    ppermute x24, waiting for transfers between devices, swap(): return lax.ppermute(value, axis, [(i, i ^ offset) for i in range(size)])  13.1 us
    pallas_call x10, Pallas kernels, call(): pl.pallas_call(kernel, out_shape=outs, in_specs=specs, out_specs=jax.tree...  6.73 us
  transfers between devices with their start and end apart: 24, of which 13 were waited for; matrix products, arithmetic and copies ran while one was open for 0% of the time, Pallas kernels for 5%

profile of v13, /device:TPU:0, one launch (start us, length us, event | category | flops | bytes accessed | tf_op | source)
XLA Modules:
  0.0 42.0 jit_solution(9021214782052706135)
XLA Ops:
  0.0 1.4 %dispatch.1 = (bf16[9,56,128]{2,1,0:T(8,128)(2,1)S(1)}, bf16[5,56,128]{2,1,0:T(8,128)(2,1)S(1)}, bf16[5,56,128]{2,1,0:T(8,128)(2,1)S(1)}, bf16[5,56,128]{2,1,0:T...) custom-call(s32[2,8]{1,0:T(2,128)} %bitcast.11, s32[4]{0:T(128)} %place_in.1, f32[2,8]{1,0:T(2,128)} %bitcast.12, ...), custom_call_target="tpu_custom_call" | custom-call | tf_op jit(solution)/shard_map/dispatch/pallas_call | solution.py:255
  1.4 3.0 %collective-permute-start.6 = (bf16[9,56,128]{2,1,0:T(8,128)(2,1)S(1)}, bf16[9,56,128]{2,1,0:T(8,128)(2,1)S(1)}, u32[]{:S(2)}, u32[]{:S(2)}) collective-permute-start(bf16[9,56,128]{2,1,0:T(8,128)(2,1)S(1)} %get-tuple-element.41.refs_0_), channel_id=1, source_target_pairs={{0,2},{2,0},{1,3},{3,1},{4,6},{6,4},{5,7},{7,5},{8,10},{10,8},{9,1... | collective-permute-start | bytes 387080 | tf_op jit(solution)/shard_map/ppermute | solution.py:243
  4.4 3.6 %collective-permute-start = (bf16[5,56,128]{2,1,0:T(8,128)(2,1)S(1)}, bf16[5,56,128]{2,1,0:T(8,128)(2,1)S(1)}, u32[]{:S(2)}, u32[]{:S(2)}) collective-permute-start(bf16[5,56,128]{2,1,0:T(8,128)(2,1)S(1)} %get-tuple-element.35), channel_id=1, source_target_pairs={{0,12},{4,8},{8,4},{12,0},{1,13},{5,9},{9,5},{13,1},{2,14},{6,10},... | collective-permute-start | bytes 215048 | tf_op jit(solution)/shard_map/ppermute | solution.py:243
  8.0 0.5 %collective-permute-start.3 = (bf16[5,56,128]{2,1,0:T(8,128)(2,1)S(1)}, bf16[5,56,128]{2,1,0:T(8,128)(2,1)S(1)}, u32[]{:S(2)}, u32[]{:S(2)}) collective-permute-start(bf16[5,56,128]{2,1,0:T(8,128)(2,1)S(1)} %get-tuple-element.37), channel_id=1, source_target_pairs={{0,6},{2,4},{4,2},{6,0},{8,14},{10,12},{12,10},{14,8},{1,7},{3,5},... | collective-permute-start | bytes 215048 | tf_op jit(solution)/shard_map/ppermute | solution.py:243
  8.5 1.5 %collective-permute-start.2 = (bf16[5,56,128]{2,1,0:T(8,128)(2,1)S(1)}, bf16[5,56,128]{2,1,0:T(8,128)(2,1)S(1)}, u32[]{:S(2)}, u32[]{:S(2)}) collective-permute-start(bf16[5,56,128]{2,1,0:T(8,128)(2,1)S(1)} %get-tuple-element.37), channel_id=1, source_target_pairs={{0,4},{2,6},{4,0},{6,2},{8,12},{10,14},{12,8},{14,10},{1,5},{3,7},... | collective-permute-start | bytes 215048 | tf_op jit(solution)/shard_map/ppermute | solution.py:243
  10.1 1.3 %collective-permute-done.refs_0_ = bf16[5,56,128]{2,1,0:T(8,128)(2,1)S(1)} collective-permute-done((bf16[5,56,128]{2,1,0:T(8,128)(2,1)S(1)}, bf16[5,56,128]{2,1,0:T(8,128)(2,1)S(1)}, u32[]{:S(2)}, u32[]{:S(2)}) %collective-permute-start) | collective-permute-done | bytes 71712 | tf_op jit(solution)/shard_map/ppermute | solution.py:243
  11.4 2.4 %collective-permute-done.1.refs_1_ = bf16[5,56,128]{2,1,0:T(8,128)(2,1)S(1)} collective-permute-done((bf16[5,56,128]{2,1,0:T(8,128)(2,1)S(1)}, bf16[5,56,128]{2,1,0:T(8,128)(2,1)S(1)}, u32[]{:S(2)}, u32[]{:S(2)}) %collective-permute-start.1) | collective-permute-done | bytes 71712 | tf_op jit(solution)/shard_map/ppermute | solution.py:243
  13.8 0.9 %collective-permute-done.3.refs_5_ = bf16[5,56,128]{2,1,0:T(8,128)(2,1)S(1)} collective-permute-done((bf16[5,56,128]{2,1,0:T(8,128)(2,1)S(1)}, bf16[5,56,128]{2,1,0:T(8,128)(2,1)S(1)}, u32[]{:S(2)}, u32[]{:S(2)}) %collective-permute-start.3) | collective-permute-done | bytes 71712 | tf_op jit(solution)/shard_map/ppermute | solution.py:243
  14.7 0.6 %collective-permute-done.2.refs_2_ = bf16[5,56,128]{2,1,0:T(8,128)(2,1)S(1)} collective-permute-done((bf16[5,56,128]{2,1,0:T(8,128)(2,1)S(1)}, bf16[5,56,128]{2,1,0:T(8,128)(2,1)S(1)}, u32[]{:S(2)}, u32[]{:S(2)}) %collective-permute-start.2) | collective-permute-done | bytes 71712 | tf_op jit(solution)/shard_map/ppermute | solution.py:243
  15.3 0.5 %collective-permute-start.8 = (bf16[9,56,128]{2,1,0:T(8,128)(2,1)S(1)}, bf16[9,56,128]{2,1,0:T(8,128)(2,1)S(1)}, u32[]{:S(2)}, u32[]{:S(2)}) collective-permute-start(bf16[9,56,128]{2,1,0:T(8,128)(2,1)S(1)} %collective-permute-done.6.refs_1_), channel_id=1, source_target_pairs={{0,1},{1,0},{2,3},{3,2},{4,5},{5,4},{6,7},{7,6},{8,9},{9,8},{10,11... | collective-permute-start | bytes 387080 | tf_op jit(solution)/shard_map/ppermute | solution.py:243
  15.8 0.8 %collective-permute-start.4 = (bf16[5,56,128]{2,1,0:T(8,128)(2,1)S(1)}, bf16[5,56,128]{2,1,0:T(8,128)(2,1)S(1)}, u32[]{:S(2)}, u32[]{:S(2)}) collective-permute-start(bf16[5,56,128]{2,1,0:T(8,128)(2,1)S(1)} %collective-permute-done.refs_0_), channel_id=1, source_target_pairs={{0,2},{2,0},{1,3},{3,1},{4,6},{6,4},{5,7},{7,5},{8,10},{10,8},{9,1... | collective-permute-start | bytes 215048 | tf_op jit(solution)/shard_map/ppermute | solution.py:243
  16.5 1.3 %collective-permute-start.5 = (bf16[5,56,128]{2,1,0:T(8,128)(2,1)S(1)}, bf16[5,56,128]{2,1,0:T(8,128)(2,1)S(1)}, u32[]{:S(2)}, u32[]{:S(2)}) collective-permute-start(bf16[5,56,128]{2,1,0:T(8,128)(2,1)S(1)} %collective-permute-done.1.refs_1_), channel_id=1, source_target_pairs={{0,2},{2,0},{1,3},{3,1},{4,6},{6,4},{5,7},{7,5},{8,10},{10,8},{9,1... | collective-permute-start | bytes 215048 | tf_op jit(solution)/shard_map/ppermute | solution.py:243
  17.8 0.5 %collective-permute-start.9 = (bf16[5,56,128]{2,1,0:T(8,128)(2,1)S(1)}, bf16[5,56,128]{2,1,0:T(8,128)(2,1)S(1)}, u32[]{:S(2)}, u32[]{:S(2)}) collective-permute-start(bf16[5,56,128]{2,1,0:T(8,128)(2,1)S(1)} %collective-permute-done.refs_0_), channel_id=1, source_target_pairs={{0,1},{1,0},{2,3},{3,2},{4,5},{5,4},{6,7},{7,6},{8,9},{9,8},{10,11... | collective-permute-start | bytes 215048 | tf_op jit(solution)/shard_map/ppermute | solution.py:243
  18.4 2.0 %near_shared.1 = (bf16[32,7168]{1,0:T(8,128)(2,1)S(1)}, f32[32,128]{1,0:T(8,128)S(1)}, f32[32,7168]{1,0:T(8,128)S(1)}) custom-call(bf16[9,56,128]{2,1,0:T(8,128)(2,1)S(1)} %get-tuple-element.41.refs_0_, bf16[9,56,128]{2,1,0:T(8,128)(2,1)S(1)} %collective-permute-done.6.refs_1_, bf16[9,56,128]{2,1,0:T(8,128)(2,1)S(1)} %collective-permute-done.7.refs_2_, ...), custom_call_target="tpu_custom_call" | custom-call | flops 352321536 | bytes 11010048 | tf_op jit(solution)/shard_map/near_shared/pallas_call | solution.py:255
  21.0 0.5 %collective-permute-done.5.refs_4_ = bf16[5,56,128]{2,1,0:T(8,128)(2,1)S(1)} collective-permute-done((bf16[5,56,128]{2,1,0:T(8,128)(2,1)S(1)}, bf16[5,56,128]{2,1,0:T(8,128)(2,1)S(1)}, u32[]{:S(2)}, u32[]{:S(2)}) %collective-permute-start.5) | collective-permute-done | bytes 71712 | tf_op jit(solution)/shard_map/ppermute | solution.py:243
  21.4 0.5 %collective-permute-start.13 = (bf16[5,56,128]{2,1,0:T(8,128)(2,1)S(1)}, bf16[5,56,128]{2,1,0:T(8,128)(2,1)S(1)}, u32[]{:S(2)}, u32[]{:S(2)}) collective-permute-start(bf16[5,56,128]{2,1,0:T(8,128)(2,1)S(1)} %collective-permute-done.5.refs_4_), channel_id=1, source_target_pairs={{0,1},{1,0},{2,3},{3,2},{4,5},{5,4},{6,7},{7,6},{8,9},{9,8},{10,11... | collective-permute-start | bytes 215048 | tf_op jit(solution)/shard_map/ppermute | solution.py:243
  22.0 0.7 %collective-permute-done.12.refs_9_ = bf16[5,56,128]{2,1,0:T(8,128)(2,1)S(1)} collective-permute-done((bf16[5,56,128]{2,1,0:T(8,128)(2,1)S(1)}, bf16[5,56,128]{2,1,0:T(8,128)(2,1)S(1)}, u32[]{:S(2)}, u32[]{:S(2)}) %collective-permute-start.12) | collective-permute-done | bytes 71712 | tf_op jit(solution)/shard_map/ppermute | solution.py:243
  22.9 2.3 %routed.1 = (bf16[2,5,56,128]{3,2,1,0:T(8,128)(2,1)S(1)}, bf16[2,5,56,128]{3,2,1,0:T(8,128)(2,1)S(1)}, bf16[2,18,56,128]{3,2,1,0:T(8,128)(2,1)S(1)}, bf16[2,18,56,128]{3,2,1,0:T(8,128)(2,1)S(1)}) custom-call(bf16[5,56,128]{2,1,0:T(8,128)(2,1)S(1)} %collective-permute-done.refs_0_, bf16[5,56,128]{2,1,0:T(8,128)(2,1)S(1)} %collective-permute-done.1.refs_1_, ...), custom_call_target="tpu_custom_call" | custom-call | flops 1012924416 | bytes 11010048 | tf_op jit(solution)/shard_map/routed/pallas_call | solution.py:255
  25.2 0.4 %collective-permute-start.15 = (bf16[2,5,56,128]{3,2,1,0:T(8,128)(2,1)S(1)}, bf16[2,5,56,128]{3,2,1,0:T(8,128)(2,1)S(1)}, u32[]{:S(2)}, u32[]{:S(2)}) collective-permute-start(bf16[2,5,56,128]{3,2,1,0:T(8,128)(2,1)S(1)} %get-tuple-element.49), channel_id=1, source_target_pairs={{0,1},{1,0},{2,3},{3,2},{4,5},{5,4},{6,7},{7,6},{8,9},{9,8},{10,11... | collective-permute-start | bytes 430088 | tf_op jit(solution)/shard_map/ppermute | solution.py:243
  25.6 1.0 %collective-permute-done.15.refs_1_ = bf16[2,5,56,128]{3,2,1,0:T(8,128)(2,1)S(1)} collective-permute-done((bf16[2,5,56,128]{3,2,1,0:T(8,128)(2,1)S(1)}, bf16[2,5,56,128]{3,2,1,0:T(8,128)(2,1)S(1)}, u32[]{:S(2)}, u32[]{:S(2)}) %collective-permute-start.15) | collective-permute-done | bytes 143392 | tf_op jit(solution)/shard_map/ppermute | solution.py:243
  26.7 0.4 %collective-permute-start.18 = (bf16[2,18,56,128]{3,2,1,0:T(8,128)(2,1)S(1)}, bf16[2,18,56,128]{3,2,1,0:T(8,128)(2,1)S(1)}, u32[]{:S(2)}, u32[]{:S(2)}) collective-permute-start(bf16[2,18,56,128]{3,2,1,0:T(8,128)(2,1)S(1)} %get-tuple-element.54), channel_id=1, source_target_pairs={{0,1},{1,0},{2,3},{3,2},{4,5},{5,4},{6,7},{7,6},{8,9},{9,8},{10,11... | collective-permute-start | bytes 1548296 | tf_op jit(solution)/shard_map/ppermute | solution.py:243
  27.1 1.0 %collective-permute-start.16 = (bf16[5,56,128]{2,1,0:T(8,128)(2,1)S(1)}, bf16[5,56,128]{2,1,0:T(8,128)(2,1)S(1)}, u32[]{:S(2)}, u32[]{:S(2)}) collective-permute-start(bf16[5,56,128]{2,1,0:T(8,128)(2,1)S(1)} %get-tuple-element.51), channel_id=1, source_target_pairs={{0,2},{2,0},{1,3},{3,1},{4,6},{6,4},{5,7},{7,5},{8,10},{10,8},{9,1... | collective-permute-start | bytes 215048 | tf_op jit(solution)/shard_map/ppermute | solution.py:243
  28.1 0.6 %collective-permute-done.18.refs_1_ = bf16[2,18,56,128]{3,2,1,0:T(8,128)(2,1)S(1)} collective-permute-done((bf16[2,18,56,128]{3,2,1,0:T(8,128)(2,1)S(1)}, bf16[2,18,56,128]{3,2,1,0:T(8,128)(2,1)S(1)}, u32[]{:S(2)}, u32[]{:S(2)}) %collective-permute-start.18) | collective-permute-done | bytes 516128 | tf_op jit(solution)/shard_map/ppermute | solution.py:243
  28.8 1.0 %collective-permute-start.19 = (bf16[5,56,128]{2,1,0:T(8,128)(2,1)S(1)}, bf16[5,56,128]{2,1,0:T(8,128)(2,1)S(1)}, u32[]{:S(2)}, u32[]{:S(2)}) collective-permute-start(bf16[5,56,128]{2,1,0:T(8,128)(2,1)S(1)} %get-tuple-element.56), channel_id=1, source_target_pairs={{0,2},{2,0},{1,3},{3,1},{4,6},{6,4},{5,7},{7,5},{8,10},{10,8},{9,1... | collective-permute-start | bytes 215048 | tf_op jit(solution)/shard_map/ppermute | solution.py:243
  29.8 1.1 %collective-permute-start.21 = (bf16[5,56,128]{2,1,0:T(8,128)(2,1)S(1)}, bf16[5,56,128]{2,1,0:T(8,128)(2,1)S(1)}, u32[]{:S(2)}, u32[]{:S(2)}) collective-permute-start(bf16[5,56,128]{2,1,0:T(8,128)(2,1)S(1)} %get-tuple-element.58), channel_id=1, source_target_pairs={{0,2},{2,0},{1,3},{3,1},{4,6},{6,4},{5,7},{7,5},{8,10},{10,8},{9,1... | collective-permute-start | bytes 215048 | tf_op jit(solution)/shard_map/ppermute | solution.py:243
  30.9 1.0 %collective-permute-start.23 = (bf16[8,56,128]{2,1,0:T(8,128)(2,1)S(1)}, bf16[8,56,128]{2,1,0:T(8,128)(2,1)S(1)}, u32[]{:S(2)}, u32[]{:S(2)}) collective-permute-start(bf16[8,56,128]{2,1,0:T(8,128)(2,1)S(1)} %get-tuple-element.60), channel_id=1, source_target_pairs={{0,2},{2,0},{1,3},{3,1},{4,6},{6,4},{5,7},{7,5},{8,10},{10,8},{9,1... | collective-permute-start | bytes 344072 | tf_op jit(solution)/shard_map/ppermute | solution.py:243
  31.9 2.3 %collective-permute-start.17 = (bf16[5,56,128]{2,1,0:T(8,128)(2,1)S(1)}, bf16[5,56,128]{2,1,0:T(8,128)(2,1)S(1)}, u32[]{:S(2)}, u32[]{:S(2)}) collective-permute-start(bf16[5,56,128]{2,1,0:T(8,128)(2,1)S(1)} %narrow_sum.3), channel_id=1, source_target_pairs={{0,12},{4,8},{8,4},{12,0},{1,13},{5,9},{9,5},{13,1},{2,14},{6,10},... | collective-permute-start | bytes 215048 | tf_op jit(solution)/shard_map/ppermute | solution.py:243
  34.2 0.9 %collective-permute-start.20 = (bf16[5,56,128]{2,1,0:T(8,128)(2,1)S(1)}, bf16[5,56,128]{2,1,0:T(8,128)(2,1)S(1)}, u32[]{:S(2)}, u32[]{:S(2)}) collective-permute-start(bf16[5,56,128]{2,1,0:T(8,128)(2,1)S(1)} %narrow_sum.4), channel_id=1, source_target_pairs={{0,8},{4,12},{8,0},{12,4},{1,9},{5,13},{9,1},{13,5},{2,10},{6,14},... | collective-permute-start | bytes 215048 | tf_op jit(solution)/shard_map/ppermute | solution.py:243
  35.4 1.5 %collective-permute-start.22 = (bf16[5,56,128]{2,1,0:T(8,128)(2,1)S(1)}, bf16[5,56,128]{2,1,0:T(8,128)(2,1)S(1)}, u32[]{:S(2)}, u32[]{:S(2)}) collective-permute-start(bf16[5,56,128]{2,1,0:T(8,128)(2,1)S(1)} %narrow_sum.5), channel_id=1, source_target_pairs={{0,4},{4,0},{8,12},{12,8},{1,5},{5,1},{9,13},{13,9},{2,6},{6,2},{1... | collective-permute-start | bytes 215048 | tf_op jit(solution)/shard_map/ppermute | solution.py:243
  36.9 1.8 %collective-permute-done.17.refs_0_ = bf16[5,56,128]{2,1,0:T(8,128)(2,1)S(1)} collective-permute-done((bf16[5,56,128]{2,1,0:T(8,128)(2,1)S(1)}, bf16[5,56,128]{2,1,0:T(8,128)(2,1)S(1)}, u32[]{:S(2)}, u32[]{:S(2)}) %collective-permute-start.17) | collective-permute-done | bytes 71712 | tf_op jit(solution)/shard_map/ppermute | solution.py:243
  38.7 2.5 %collective-permute-done.20.refs_1_ = bf16[5,56,128]{2,1,0:T(8,128)(2,1)S(1)} collective-permute-done((bf16[5,56,128]{2,1,0:T(8,128)(2,1)S(1)}, bf16[5,56,128]{2,1,0:T(8,128)(2,1)S(1)}, u32[]{:S(2)}, u32[]{:S(2)}) %collective-permute-start.20) | collective-permute-done | bytes 71712 | tf_op jit(solution)/shard_map/ppermute | solution.py:243
  41.3 0.7 %combine.1 = bf16[8,7168]{1,0:T(8,128)(2,1)} custom-call(f32[8,56,128]{2,1,0:T(8,128)S(1)} %far_combine.1.far, bf16[8,56,128]{2,1,0:T(8,128)(2,1)S(1)} %get-tuple-element.59.refs_0_, bf16[8,56,128]{2,1,0:T(8,128)(2,1)S(1)} %collective-permute-done.23.refs_1_), custom_call_target="tpu_custom_call" | custom-call | tf_op jit(solution)/shard_map/combine/pallas_call | solution.py:255
  (38 shorter events, 1.4 us)
Async XLA Ops:
  0.0 18.4 %copy-start = (bf16[7168,256]{1,0:T(8,128)(2,1)S(1)}, bf16[7168,256]{1,0:T(8,128)(2,1)}, u32[]{:S(2)}) copy-start(bf16[7168,256]{1,0:T(8,128)(2,1)} %refs_4_.1) | copy-start | bytes 11010052
  0.0 18.4 %copy-start.1 = (bf16[7168,256]{1,0:T(8,128)(2,1)S(1)}, bf16[7168,256]{1,0:T(8,128)(2,1)}, u32[]{:S(2)}) copy-start(bf16[7168,256]{1,0:T(8,128)(2,1)} %refs_5_.1) | copy-start | bytes 11010052
  0.0 18.4 %copy-start.2 = (bf16[256,7168]{1,0:T(8,128)(2,1)S(1)}, bf16[256,7168]{1,0:T(8,128)(2,1)}, u32[]{:S(2)}) copy-start(bf16[256,7168]{1,0:T(8,128)(2,1)} %refs_6_.1) | copy-start | bytes 11010052
  1.4 13.9 %collective-permute-start.6 = (bf16[9,56,128]{2,1,0:T(8,128)(2,1)S(1)}, bf16[9,56,128]{2,1,0:T(8,128)(2,1)S(1)}, u32[]{:S(2)}, u32[]{:S(2)}) collective-permute-start(bf16[9,56,128]{2,1,0:T(8,128)(2,1)S(1)} %get-tuple-element.41.refs_0_), channel_id=1, source_target_pairs={{0,2},{2,0},{1,3},{3,1},{4,6},{6,4},{5,7},{7,5},{8,10},{10,8},{9,1... | collective-permute-start | bytes 387080 | tf_op jit(solution)/shard_map/ppermute | solution.py:243
  4.4 7.0 %collective-permute-start = (bf16[5,56,128]{2,1,0:T(8,128)(2,1)S(1)}, bf16[5,56,128]{2,1,0:T(8,128)(2,1)S(1)}, u32[]{:S(2)}, u32[]{:S(2)}) collective-permute-start(bf16[5,56,128]{2,1,0:T(8,128)(2,1)S(1)} %get-tuple-element.35), channel_id=1, source_target_pairs={{0,12},{4,8},{8,4},{12,0},{1,13},{5,9},{9,5},{13,1},{2,14},{6,10},... | collective-permute-start | bytes 215048 | tf_op jit(solution)/shard_map/ppermute | solution.py:243
  8.0 5.8 %collective-permute-start.1 = (bf16[5,56,128]{2,1,0:T(8,128)(2,1)S(1)}, bf16[5,56,128]{2,1,0:T(8,128)(2,1)S(1)}, u32[]{:S(2)}, u32[]{:S(2)}) collective-permute-start(bf16[5,56,128]{2,1,0:T(8,128)(2,1)S(1)} %get-tuple-element.36), channel_id=1, source_target_pairs={{0,8},{4,12},{8,0},{12,4},{1,9},{5,13},{9,1},{13,5},{2,10},{6,14},... | collective-permute-start | bytes 215048 | tf_op jit(solution)/shard_map/ppermute | solution.py:243
  8.0 14.9 %copy-start.3 = (bf16[1,7168,256]{2,1,0:T(8,128)(2,1)S(1)}, bf16[1,7168,256]{2,1,0:T(8,128)(2,1)}, u32[]{:S(2)}) copy-start(bf16[1,7168,256]{2,1,0:T(8,128)(2,1)} %param.16) | copy-start | bytes 11010052
  8.0 14.9 %copy-start.4 = (bf16[1,7168,256]{2,1,0:T(8,128)(2,1)S(1)}, bf16[1,7168,256]{2,1,0:T(8,128)(2,1)}, u32[]{:S(2)}) copy-start(bf16[1,7168,256]{2,1,0:T(8,128)(2,1)} %param.17) | copy-start | bytes 11010052
  8.0 14.9 %copy-start.5 = (bf16[1,256,7168]{2,1,0:T(8,128)(2,1)S(1)}, bf16[1,256,7168]{2,1,0:T(8,128)(2,1)}, u32[]{:S(2)}) copy-start(bf16[1,256,7168]{2,1,0:T(8,128)(2,1)} %param.18) | copy-start | bytes 11010052
  8.0 6.7 %collective-permute-start.3 = (bf16[5,56,128]{2,1,0:T(8,128)(2,1)S(1)}, bf16[5,56,128]{2,1,0:T(8,128)(2,1)S(1)}, u32[]{:S(2)}, u32[]{:S(2)}) collective-permute-start(bf16[5,56,128]{2,1,0:T(8,128)(2,1)S(1)} %get-tuple-element.37), channel_id=1, source_target_pairs={{0,6},{2,4},{4,2},{6,0},{8,14},{10,12},{12,10},{14,8},{1,7},{3,5},... | collective-permute-start | bytes 215048 | tf_op jit(solution)/shard_map/ppermute | solution.py:243
  8.5 6.7 %collective-permute-start.2 = (bf16[5,56,128]{2,1,0:T(8,128)(2,1)S(1)}, bf16[5,56,128]{2,1,0:T(8,128)(2,1)S(1)}, u32[]{:S(2)}, u32[]{:S(2)}) collective-permute-start(bf16[5,56,128]{2,1,0:T(8,128)(2,1)S(1)} %get-tuple-element.37), channel_id=1, source_target_pairs={{0,4},{2,6},{4,0},{6,2},{8,12},{10,14},{12,8},{14,10},{1,5},{3,7},... | collective-permute-start | bytes 215048 | tf_op jit(solution)/shard_map/ppermute | solution.py:243
  15.3 2.5 %collective-permute-start.7 = (bf16[9,56,128]{2,1,0:T(8,128)(2,1)S(1)}, bf16[9,56,128]{2,1,0:T(8,128)(2,1)S(1)}, u32[]{:S(2)}, u32[]{:S(2)}) collective-permute-start(bf16[9,56,128]{2,1,0:T(8,128)(2,1)S(1)} %get-tuple-element.41.refs_0_), channel_id=1, source_target_pairs={{0,1},{1,0},{2,3},{3,2},{4,5},{5,4},{6,7},{7,6},{8,9},{9,8},{10,11... | collective-permute-start | bytes 387080 | tf_op jit(solution)/shard_map/ppermute | solution.py:243
  15.3 3.1 %collective-permute-start.8 = (bf16[9,56,128]{2,1,0:T(8,128)(2,1)S(1)}, bf16[9,56,128]{2,1,0:T(8,128)(2,1)S(1)}, u32[]{:S(2)}, u32[]{:S(2)}) collective-permute-start(bf16[9,56,128]{2,1,0:T(8,128)(2,1)S(1)} %collective-permute-done.6.refs_1_), channel_id=1, source_target_pairs={{0,1},{1,0},{2,3},{3,2},{4,5},{5,4},{6,7},{7,6},{8,9},{9,8},{10,11... | collective-permute-start | bytes 387080 | tf_op jit(solution)/shard_map/ppermute | solution.py:243
  15.8 4.9 %collective-permute-start.4 = (bf16[5,56,128]{2,1,0:T(8,128)(2,1)S(1)}, bf16[5,56,128]{2,1,0:T(8,128)(2,1)S(1)}, u32[]{:S(2)}, u32[]{:S(2)}) collective-permute-start(bf16[5,56,128]{2,1,0:T(8,128)(2,1)S(1)} %collective-permute-done.refs_0_), channel_id=1, source_target_pairs={{0,2},{2,0},{1,3},{3,1},{4,6},{6,4},{5,7},{7,5},{8,10},{10,8},{9,1... | collective-permute-start | bytes 215048 | tf_op jit(solution)/shard_map/ppermute | solution.py:243
  16.5 4.9 %collective-permute-start.5 = (bf16[5,56,128]{2,1,0:T(8,128)(2,1)S(1)}, bf16[5,56,128]{2,1,0:T(8,128)(2,1)S(1)}, u32[]{:S(2)}, u32[]{:S(2)}) collective-permute-start(bf16[5,56,128]{2,1,0:T(8,128)(2,1)S(1)} %collective-permute-done.1.refs_1_), channel_id=1, source_target_pairs={{0,2},{2,0},{1,3},{3,1},{4,6},{6,4},{5,7},{7,5},{8,10},{10,8},{9,1... | collective-permute-start | bytes 215048 | tf_op jit(solution)/shard_map/ppermute | solution.py:243
  17.8 3.6 %collective-permute-start.14 = (bf16[5,56,128]{2,1,0:T(8,128)(2,1)S(1)}, bf16[5,56,128]{2,1,0:T(8,128)(2,1)S(1)}, u32[]{:S(2)}, u32[]{:S(2)}) collective-permute-start(bf16[5,56,128]{2,1,0:T(8,128)(2,1)S(1)} %collective-permute-done.3.refs_5_), channel_id=1, source_target_pairs={{0,1},{1,0},{2,3},{3,2},{4,5},{5,4},{6,7},{7,6},{8,9},{9,8},{10,11... | collective-permute-start | bytes 215048 | tf_op jit(solution)/shard_map/ppermute | solution.py:243
  17.8 4.2 %collective-permute-start.9 = (bf16[5,56,128]{2,1,0:T(8,128)(2,1)S(1)}, bf16[5,56,128]{2,1,0:T(8,128)(2,1)S(1)}, u32[]{:S(2)}, u32[]{:S(2)}) collective-permute-start(bf16[5,56,128]{2,1,0:T(8,128)(2,1)S(1)} %collective-permute-done.refs_0_), channel_id=1, source_target_pairs={{0,1},{1,0},{2,3},{3,2},{4,5},{5,4},{6,7},{7,6},{8,9},{9,8},{10,11... | collective-permute-start | bytes 215048 | tf_op jit(solution)/shard_map/ppermute | solution.py:243
  18.3 3.6 %collective-permute-start.10 = (bf16[5,56,128]{2,1,0:T(8,128)(2,1)S(1)}, bf16[5,56,128]{2,1,0:T(8,128)(2,1)S(1)}, u32[]{:S(2)}, u32[]{:S(2)}) collective-permute-start(bf16[5,56,128]{2,1,0:T(8,128)(2,1)S(1)} %collective-permute-done.1.refs_1_), channel_id=1, source_target_pairs={{0,1},{1,0},{2,3},{3,2},{4,5},{5,4},{6,7},{7,6},{8,9},{9,8},{10,11... | collective-permute-start | bytes 215048 | tf_op jit(solution)/shard_map/ppermute | solution.py:243
  20.7 1.3 %collective-permute-start.11 = (bf16[5,56,128]{2,1,0:T(8,128)(2,1)S(1)}, bf16[5,56,128]{2,1,0:T(8,128)(2,1)S(1)}, u32[]{:S(2)}, u32[]{:S(2)}) collective-permute-start(bf16[5,56,128]{2,1,0:T(8,128)(2,1)S(1)} %collective-permute-done.2.refs_2_), channel_id=1, source_target_pairs={{0,1},{1,0},{2,3},{3,2},{4,5},{5,4},{6,7},{7,6},{8,9},{9,8},{10,11... | collective-permute-start | bytes 215048 | tf_op jit(solution)/shard_map/ppermute | solution.py:243
  21.4 1.3 %collective-permute-start.12 = (bf16[5,56,128]{2,1,0:T(8,128)(2,1)S(1)}, bf16[5,56,128]{2,1,0:T(8,128)(2,1)S(1)}, u32[]{:S(2)}, u32[]{:S(2)}) collective-permute-start(bf16[5,56,128]{2,1,0:T(8,128)(2,1)S(1)} %collective-permute-done.4.refs_3_), channel_id=1, source_target_pairs={{0,1},{1,0},{2,3},{3,2},{4,5},{5,4},{6,7},{7,6},{8,9},{9,8},{10,11... | collective-permute-start | bytes 215048 | tf_op jit(solution)/shard_map/ppermute | solution.py:243
  21.4 1.4 %collective-permute-start.13 = (bf16[5,56,128]{2,1,0:T(8,128)(2,1)S(1)}, bf16[5,56,128]{2,1,0:T(8,128)(2,1)S(1)}, u32[]{:S(2)}, u32[]{:S(2)}) collective-permute-start(bf16[5,56,128]{2,1,0:T(8,128)(2,1)S(1)} %collective-permute-done.5.refs_4_), channel_id=1, source_target_pairs={{0,1},{1,0},{2,3},{3,2},{4,5},{5,4},{6,7},{7,6},{8,9},{9,8},{10,11... | collective-permute-start | bytes 215048 | tf_op jit(solution)/shard_map/ppermute | solution.py:243
  25.2 1.4 %collective-permute-start.15 = (bf16[2,5,56,128]{3,2,1,0:T(8,128)(2,1)S(1)}, bf16[2,5,56,128]{3,2,1,0:T(8,128)(2,1)S(1)}, u32[]{:S(2)}, u32[]{:S(2)}) collective-permute-start(bf16[2,5,56,128]{3,2,1,0:T(8,128)(2,1)S(1)} %get-tuple-element.49), channel_id=1, source_target_pairs={{0,1},{1,0},{2,3},{3,2},{4,5},{5,4},{6,7},{7,6},{8,9},{9,8},{10,11... | collective-permute-start | bytes 430088 | tf_op jit(solution)/shard_map/ppermute | solution.py:243
  26.7 2.0 %collective-permute-start.18 = (bf16[2,18,56,128]{3,2,1,0:T(8,128)(2,1)S(1)}, bf16[2,18,56,128]{3,2,1,0:T(8,128)(2,1)S(1)}, u32[]{:S(2)}, u32[]{:S(2)}) collective-permute-start(bf16[2,18,56,128]{3,2,1,0:T(8,128)(2,1)S(1)} %get-tuple-element.54), channel_id=1, source_target_pairs={{0,1},{1,0},{2,3},{3,2},{4,5},{5,4},{6,7},{7,6},{8,9},{9,8},{10,11... | collective-permute-start | bytes 1548296 | tf_op jit(solution)/shard_map/ppermute | solution.py:243
  27.1 4.7 %collective-permute-start.16 = (bf16[5,56,128]{2,1,0:T(8,128)(2,1)S(1)}, bf16[5,56,128]{2,1,0:T(8,128)(2,1)S(1)}, u32[]{:S(2)}, u32[]{:S(2)}) collective-permute-start(bf16[5,56,128]{2,1,0:T(8,128)(2,1)S(1)} %get-tuple-element.51), channel_id=1, source_target_pairs={{0,2},{2,0},{1,3},{3,1},{4,6},{6,4},{5,7},{7,5},{8,10},{10,8},{9,1... | collective-permute-start | bytes 215048 | tf_op jit(solution)/shard_map/ppermute | solution.py:243
  28.8 5.4 %collective-permute-start.19 = (bf16[5,56,128]{2,1,0:T(8,128)(2,1)S(1)}, bf16[5,56,128]{2,1,0:T(8,128)(2,1)S(1)}, u32[]{:S(2)}, u32[]{:S(2)}) collective-permute-start(bf16[5,56,128]{2,1,0:T(8,128)(2,1)S(1)} %get-tuple-element.56), channel_id=1, source_target_pairs={{0,2},{2,0},{1,3},{3,1},{4,6},{6,4},{5,7},{7,5},{8,10},{10,8},{9,1... | collective-permute-start | bytes 215048 | tf_op jit(solution)/shard_map/ppermute | solution.py:243
  29.8 5.6 %collective-permute-start.21 = (bf16[5,56,128]{2,1,0:T(8,128)(2,1)S(1)}, bf16[5,56,128]{2,1,0:T(8,128)(2,1)S(1)}, u32[]{:S(2)}, u32[]{:S(2)}) collective-permute-start(bf16[5,56,128]{2,1,0:T(8,128)(2,1)S(1)} %get-tuple-element.58), channel_id=1, source_target_pairs={{0,2},{2,0},{1,3},{3,1},{4,6},{6,4},{5,7},{7,5},{8,10},{10,8},{9,1... | collective-permute-start | bytes 215048 | tf_op jit(solution)/shard_map/ppermute | solution.py:243
  30.9 10.4 %collective-permute-start.23 = (bf16[8,56,128]{2,1,0:T(8,128)(2,1)S(1)}, bf16[8,56,128]{2,1,0:T(8,128)(2,1)S(1)}, u32[]{:S(2)}, u32[]{:S(2)}) collective-permute-start(bf16[8,56,128]{2,1,0:T(8,128)(2,1)S(1)} %get-tuple-element.60), channel_id=1, source_target_pairs={{0,2},{2,0},{1,3},{3,1},{4,6},{6,4},{5,7},{7,5},{8,10},{10,8},{9,1... | collective-permute-start | bytes 344072 | tf_op jit(solution)/shard_map/ppermute | solution.py:243
  31.9 6.9 %collective-permute-start.17 = (bf16[5,56,128]{2,1,0:T(8,128)(2,1)S(1)}, bf16[5,56,128]{2,1,0:T(8,128)(2,1)S(1)}, u32[]{:S(2)}, u32[]{:S(2)}) collective-permute-start(bf16[5,56,128]{2,1,0:T(8,128)(2,1)S(1)} %narrow_sum.3), channel_id=1, source_target_pairs={{0,12},{4,8},{8,4},{12,0},{1,13},{5,9},{9,5},{13,1},{2,14},{6,10},... | collective-permute-start | bytes 215048 | tf_op jit(solution)/shard_map/ppermute | solution.py:243
  34.2 7.0 %collective-permute-start.20 = (bf16[5,56,128]{2,1,0:T(8,128)(2,1)S(1)}, bf16[5,56,128]{2,1,0:T(8,128)(2,1)S(1)}, u32[]{:S(2)}, u32[]{:S(2)}) collective-permute-start(bf16[5,56,128]{2,1,0:T(8,128)(2,1)S(1)} %narrow_sum.4), channel_id=1, source_target_pairs={{0,8},{4,12},{8,0},{12,4},{1,9},{5,13},{9,1},{13,5},{2,10},{6,14},... | collective-permute-start | bytes 215048 | tf_op jit(solution)/shard_map/ppermute | solution.py:243
  35.4 5.8 %collective-permute-start.22 = (bf16[5,56,128]{2,1,0:T(8,128)(2,1)S(1)}, bf16[5,56,128]{2,1,0:T(8,128)(2,1)S(1)}, u32[]{:S(2)}, u32[]{:S(2)}) collective-permute-start(bf16[5,56,128]{2,1,0:T(8,128)(2,1)S(1)} %narrow_sum.5), channel_id=1, source_target_pairs={{0,4},{4,0},{8,12},{12,8},{1,5},{5,1},{9,13},{13,9},{2,6},{6,2},{1... | collective-permute-start | bytes 215048 | tf_op jit(solution)/shard_map/ppermute | solution.py:243
